TPU v7x, 32 devices: a whole 2x2x4 slice. The times are simulated.
32 devices in a mesh: dp: 16 (over z, y, core), mp: 2 (over x).
Axes of the slice: x: 2, y: 2, z: 4, core: 2. Of those that a mesh axis runs over, the one named last changes fastest.
Arguments:
- features: bfloat16 [1024, 4096], P('dp', 'mp'), may hold values from -6 to 6
- norm_gain: bfloat16 [4096], replicated, may hold values from 0.099609375 to 1.8984375
- w_key: bfloat16 [4096, 512], P('dp', 'mp'), may hold values from -0.09375 to 0.09375
- w_value: bfloat16 [4096, 512], P('dp', 'mp'), may hold values from -0.09375 to 0.09375
- queries: bfloat16 [1024, 2048], P('dp', 'mp'), may hold values from -150 to 150
- key_pool: bfloat16 [48, 128, 512], P('dp', None, 'mp'), may hold values from -5 to 5
- value_pool: bfloat16 [48, 128, 512], P('dp', None, 'mp'), may hold values from -5 to 5
- cache_lens: int32 [3], replicated, may hold values from 2 to 1920, as said below
- page_table: int32 [3, 25], replicated, may hold values from -1 to 47, as said below
- token_request: int32 [1024], replicated, may hold values from 0 to 2, as said below
Outputs:
- attended: bfloat16 [1024, 2048], P('dp', 'mp')
- keys_out: bfloat16 [48, 128, 512], P('dp', None, 'mp')
- values_out: bfloat16 [48, 128, 512], P('dp', None, 'mp')
Inputs may be any that keep to these rules, and one draw needn't show every extreme that they name: `cache_lens`: exactly one request has 1920 cached tokens, each other request has at most 512. `page_table`: row r lists the pool pages of request r in logical order: its first ceil(cache_lens[r] / 128) entries are pages among the first 2 slots of some device, the entries up to the page of its last new token are pages among the other slots of some device, later entries are -1; no pool page is listed twice. `token_request`: never falling along the new tokens; every request has 256 or more new tokens.
All inputs are finite; a program needn't handle non-finite values.
Results may differ from a plain program's by a relative error of at most 0.0068.
Values may be sent and summed in bfloat16 or wider, within the bound.
No kernel may reach another device: no remote copies, remote signals or barrier semaphores. Data moves between devices by JAX's collectives and lax.ppermute only.
A program may use at most 64 MiB of HBM per device.

v0:
```python
import math

import jax
import jax.numpy as jnp
from jax import lax
from jax.sharding import PartitionSpec as P

HD = 128
PAGE = 128
SHORT = 512
CTX_DEV = 120


THETA = 500000.0
NEG_FILL = -1e30


def rotate(values, positions, head_size):
    halfway = head_size // 2
    inverse = THETA ** (-(jnp.arange(halfway, dtype=jnp.float32) * 2.0) / head_size)
    angles = positions.astype(jnp.float32)[:, None] * inverse[None, :]
    cosine = jnp.cos(angles)[:, None, :]
    sine = jnp.sin(angles)[:, None, :]
    first_half = values[..., :halfway]
    second_half = values[..., halfway:]
    return jnp.concatenate(
        [first_half * cosine - second_half * sine, second_half * cosine + first_half * sine],
        axis=-1,
    )


def body(
    features,
    norm_gain,
    w_key,
    w_value,
    queries,
    key_pool,
    value_pool,
    cache_lens,
    page_table,
    token_request,
):
    gathered = lax.all_gather(features, "mp", axis=1, tiled=True)
    widened = gathered.astype(jnp.float32)
    mean_square = jnp.mean(widened * widened, axis=1, keepdims=True)
    normed = (widened * lax.rsqrt(mean_square + 1e-05) * norm_gain.astype(jnp.float32)).astype(
        jnp.bfloat16
    )
    tok_rows = features.shape[0]
    kv_width = w_key.shape[1]
    head_size = HD
    kv_heads = kv_width // head_size
    q_heads = queries.shape[1] // head_size
    group_size = q_heads // kv_heads
    scale = 1.0 / math.sqrt(head_size)
    pieces = (
        lax.all_gather(w_key, "dp", axis=0, tiled=True),
        lax.all_gather(w_value, "dp", axis=0, tiled=True),
    )
    key_sums = jnp.dot(normed, pieces[0], preferred_element_type=jnp.float32)
    value_sums = jnp.dot(normed, pieces[1], preferred_element_type=jnp.float32)
    total_new = token_request.shape[0]
    requests = cache_lens.shape[0]
    request_ids = jnp.arange(requests, dtype=jnp.int32)
    member = (token_request[:, None] == request_ids[None, :]).astype(jnp.int32)
    counts = jnp.sum(member, axis=0)
    starts = jnp.cumsum(counts) - counts
    token_index = jnp.arange(total_new, dtype=jnp.int32)
    token_pos = jnp.sum(member * (cache_lens - starts)[None, :], axis=1) + token_index
    dp_index = lax.axis_index("dp")
    dp_count = lax.axis_size("dp")
    first_token = dp_index * tok_rows
    my_request = lax.dynamic_slice_in_dim(token_request, first_token, tok_rows)
    my_pos = lax.dynamic_slice_in_dim(token_pos, first_token, tok_rows)
    key_heads = rotate(key_sums.reshape(tok_rows, kv_heads, head_size), my_pos, head_size)
    new_keys = key_heads.reshape(tok_rows, kv_width).astype(jnp.bfloat16)
    new_values = value_sums.astype(jnp.bfloat16)
    pages_dev = key_pool.shape[0]
    page_rows = key_pool.shape[1]
    max_pages = page_table.shape[1]
    slot_all = jnp.take(page_table.reshape(-1), token_request * max_pages + token_pos // page_rows)
    local_slot = slot_all - dp_index * pages_dev
    owned = (local_slot >= 0) & (local_slot < pages_dev)
    dest_all = jnp.where(
        owned, local_slot * page_rows + token_pos % page_rows, pages_dev * page_rows
    )
    long_pages = (CTX_DEV * dp_count + PAGE - 1) // PAGE
    old_dev = (long_pages + 2 * ((SHORT + PAGE - 1) // PAGE) + dp_count - 1) // dp_count
    old_total = old_dev * dp_count
    old_ids = jnp.arange(old_total, dtype=jnp.int32)
    old_phys = old_ids // old_dev * pages_dev + old_ids % old_dev
    matches = (page_table[None, :, :] == old_phys[:, None, None]).astype(jnp.int32)
    page_has = jnp.sum(matches, axis=(1, 2)) > 0
    page_request = jnp.sum(matches * request_ids[None, :, None], axis=(1, 2))
    page_logical = jnp.sum(
        matches * jnp.arange(max_pages, dtype=jnp.int32)[None, None, :], axis=(1, 2)
    )
    page_limit = jnp.sum(matches * cache_lens[None, :, None], axis=(1, 2))
    q_local = queries.reshape(tok_rows, kv_heads, group_size, head_size)

    def attend(att_state, keys_flat, values_flat, key_info):
        key_request, key_pos, key_ok = key_info
        visible = (
            key_ok[None, :]
            & (key_request[None, :] == my_request[:, None])
            & (key_pos[None, :] <= my_pos[:, None])
        )
        keys_shaped = keys_flat.reshape(keys_flat.shape[0], kv_heads, head_size)
        values_shaped = values_flat.reshape(values_flat.shape[0], kv_heads, head_size)
        running_max, running_sum, running_acc = att_state
        scores = (
            jnp.einsum("thgd,khd->thgk", q_local, keys_shaped, preferred_element_type=jnp.float32)
            * scale
        )
        mask_full = visible[:, None, None, :]
        masked = jnp.where(mask_full, scores, NEG_FILL)
        new_max = jnp.maximum(running_max, jnp.max(masked, axis=-1))
        factor = jnp.exp(running_max - new_max)
        soft_weights = jnp.where(mask_full, jnp.exp(masked - new_max[..., None]), 0.0)
        new_sum = running_sum * factor + jnp.sum(soft_weights, axis=-1)
        new_acc = running_acc * factor[..., None] + jnp.einsum(
            "thgk,khd->thgd",
            soft_weights.astype(jnp.bfloat16),
            values_shaped,
            preferred_element_type=jnp.float32,
        )
        return (new_max, new_sum, new_acc)

    def attend_rows(att_state, keys_flat, values_flat, key_info):
        row_count = keys_flat.shape[0]
        key_block = 2048
        if row_count > key_block and row_count % key_block == 0:
            blocks = row_count // key_block
            stacked = (
                keys_flat.reshape(blocks, key_block, kv_width),
                values_flat.reshape(blocks, key_block, kv_width),
                key_info[0].reshape(blocks, key_block),
                key_info[1].reshape(blocks, key_block),
                key_info[2].reshape(blocks, key_block),
            )

            def step_block(inner_state, slab_parts):
                return (
                    attend(
                        inner_state,
                        slab_parts[0],
                        slab_parts[1],
                        (slab_parts[2], slab_parts[3], slab_parts[4]),
                    ),
                    None,
                )

            att_state, unused = lax.scan(step_block, att_state, stacked)
            return att_state
        return attend(att_state, keys_flat, values_flat, key_info)

    start_state = (
        jnp.full((tok_rows, kv_heads, group_size), NEG_FILL, jnp.float32),
        jnp.zeros((tok_rows, kv_heads, group_size), jnp.float32),
        jnp.zeros((tok_rows, kv_heads, group_size, head_size), jnp.float32),
    )
    flat_keys = key_pool.reshape(pages_dev * page_rows, kv_width)
    flat_values = value_pool.reshape(pages_dev * page_rows, kv_width)
    old_keys = key_pool[:old_dev]
    old_values = value_pool[:old_dev]
    pieces = (
        lax.all_gather(old_keys, "dp", axis=0, tiled=True),
        lax.all_gather(old_values, "dp", axis=0, tiled=True),
    )
    page_count = pieces[0].shape[0]
    cached_keys = pieces[0].reshape(page_count * page_rows, kv_width)
    cached_values = pieces[1].reshape(page_count * page_rows, kv_width)
    row_ids = jnp.arange(page_rows, dtype=jnp.int32)[None, :]
    key_pos = page_logical[:, None] * page_rows + row_ids
    key_ok = page_has[:, None] & (key_pos < page_limit[:, None])
    key_request = jnp.broadcast_to(page_request[:, None], (page_count, page_rows))
    middle_state = attend_rows(
        start_state,
        cached_keys,
        cached_values,
        (key_request.reshape(-1), key_pos.reshape(-1), key_ok.reshape(-1)),
    )
    pieces = (
        lax.all_gather(new_keys, "dp", axis=0, tiled=True),
        lax.all_gather(new_values, "dp", axis=0, tiled=True),
    )
    att_state = middle_state
    pool_keys = flat_keys
    pool_values = flat_values
    key_request = token_request
    key_pos = token_pos
    att_state = attend_rows(
        att_state,
        pieces[0],
        pieces[1],
        (key_request, key_pos, jnp.ones((pieces[0].shape[0],), jnp.bool_)),
    )
    pool_keys, pool_values = (
        pool_keys.at[dest_all].set(pieces[0], mode="drop"),
        pool_values.at[dest_all].set(pieces[1], mode="drop"),
    )
    final_state, pool_keys, pool_values = (att_state, pool_keys, pool_values)
    final_max, final_sum, final_acc = final_state
    attended = (
        (final_acc / final_sum[..., None])
        .reshape(tok_rows, q_heads * head_size)
        .astype(jnp.bfloat16)
    )
    return (attended, pool_keys.reshape(key_pool.shape), pool_values.reshape(value_pool.shape))


def solution(mesh):
    in_specs = (
        P("dp", "mp"),
        P(),
        P("dp", "mp"),
        P("dp", "mp"),
        P("dp", "mp"),
        P("dp", None, "mp"),
        P("dp", None, "mp"),
        P(),
        P(),
        P(),
    )
    out_specs = (P("dp", "mp"), P("dp", None, "mp"), P("dp", None, "mp"))
    return jax.shard_map(body, mesh=mesh, in_specs=in_specs, out_specs=out_specs, check_vma=False)
```

profile of v0, /device:TPU:0, one launch (start us, length us, event | category | flops | bytes accessed | tf_op | source)
XLA Modules:
  0.0 226.2 jit_solution(3043117057913694723)
XLA Ops:
  7.2 0.9 copy.106
  8.1 0.9 copy.107
  11.2 0.8 convert_reduce_fusion
  12.9 0.8 select_reduce_fusion
  14.4 0.8 reshape.348
  15.1 0.8 dynamic_slice.24
  15.9 6.6 %gather_fusion = s32[1024]{0:T(1024)S(1)} fusion(s32[75]{0:T(128)S(1)} %reshape.348, s32[1024]{0:T(1024)S(1)} %broadcast_clamp_fusion), kind=kCustom, calls=%fused_computation | custom fusion | bytes 12288 | tf_op jit(solution)/shard_map/jit(_take)/gather | solution.py:82
  23.2 9.9 %all_gather.23 = bf16[64,4096]{1,0:T(8,128)(2,1)S(1)} all-gather(bf16[64,2048]{1,0:T(8,128)(2,1)S(1)} %copy-done.10), channel_id=1, replica_groups=mesh['dp'=16,'mp'=2] {'mp'}, dimensions={1}, use_global_device_ids=true | all-gather | bytes 786432 | tf_op jit(solution)/shard_map/all_gather | solution.py:44
  35.1 0.7 compare_and_fusion.1
  36.0 18.3 %all-gather.9.cloned.1.call-done = bf16[4096,256]{1,0:T(8,128)(2,1)} async-done(((bf16[256,256]{1,0:T(8,128)(2,1)}), bf16[4096,256]{1,0:T(8,128)(2,1)}) %all-gather.9.cloned.1.call-update) | async-done | bytes 2097168 | tf_op jit(solution)/shard_map/all_gather | solution.py:58
  54.3 2.1 fusion.32
  56.8 21.4 %all_gather.25 = bf16[1024,256]{1,0:T(8,128)(2,1)S(1)} all-gather(bf16[64,256]{1,0:T(8,128)(2,1)S(1)} %bitcast.141), channel_id=1, replica_groups=mesh['dp'=16,'mp'=2] {'dp'}, dimensions={0}, use_global_device_ids=true | all-gather | bytes 557056 | tf_op jit(solution)/shard_map/all_gather | solution.py:185
  78.2 1.0 copy.48
  79.2 18.9 %all-gather.5.cloned.1.call-done = bf16[32,128,256]{2,1,0:T(8,128)(2,1)} async-done(((bf16[2,128,256]{2,1,0:T(8,128)(2,1)}), bf16[32,128,256]{2,1,0:T(8,128)(2,1)}) %all-gather.5.cloned.1.call-update) | async-done | bytes 2097168 | tf_op jit(solution)/shard_map/all_gather | solution.py:168
  98.1 42.4 %all-gather.7.cloned.1.call-done = bf16[32,128,256]{2,1,0:T(8,128)(2,1)} async-done(((bf16[2,128,256]{2,1,0:T(8,128)(2,1)}), bf16[32,128,256]{2,1,0:T(8,128)(2,1)}) %all-gather.7.cloned.1.call-update) | async-done | bytes 2097168 | tf_op jit(solution)/shard_map/all_gather | solution.py:169
  140.5 31.7 %while.15 = (s32[]{:T(128)}, f32[64,2,4]{0,2,1:T(4,128)S(1)}, f32[64,2,4]{0,2,1:T(4,128)S(1)}, f32[64,2,4,128]{3,0,2,1:T(8,128)}, pred[2,2048]{1,0:T(4,128)(4,1)...) while((s32[]{:T(128)}, f32[64,2,4]{0,2,1:T(4,128)S(1)}, ...), condition=%wide.region_10.11_spmd.clone, body=%wide.region_7.10_spmd.clone.sunk | while | flops 551225856 | bytes 27225040 | solution.py:154
  140.6 0.9 compare_and_fusion.3
  141.4 1.7 constant_dynamic-slice_fusion.7
  143.8 3.8 %fusion.70 = (f32[64,2,4]{0,2,1:T(4,128)S(1)}, f32[2,2048,64,4]{1,2,3,0:T(8,128)}) fusion(pred[64,2048]{1,0:T(8,128)(4,1)} %compare_and_fusion.3, bf16[2048,2,128,1]{0,2,3,1:T(8,128)(2,1)S(1)} %bitcast.125, bf16[64,2,4,128]{3,0,2,1:T(8,128)(2,1)} %get-tuple-element.338), kind=kOutput, calls=%fused_computation.5.clone.1 | convolution fusion | flops 271580672 | bytes 5507072 | tf_op jit(solution)/shard_map/while/body/eval_jaxpr/thgd,khd->thgk/dot_general | solution.py:113
  147.6 3.5 %fusion.71 = f32[64,2,4]{0,2,1:T(4,128)S(1)} fusion(f32[2,2048,64,4]{1,2,3,0:T(8,128)} %get-tuple-element.296, f32[64,2,4]{0,2,1:T(4,128)S(1)} %select_maximum_fusion.2, pred[64,2048]{1,0:T(8,128)(4,1)S(1)} %copy-done.2), kind=kLoop, calls=%fused_computation.7.clone.1 | loop fusion | flops 5242368 | bytes 4329472 | tf_op jit(solution)/shard_map/while/body/eval_jaxpr/reduce_sum | solution.py:121
  152.1 3.5 %fusion.73 = f32[64,2,4,128]{3,0,2,1:T(8,128)S(1)} fusion(bf16[2048,2,128,1]{0,2,3,1:T(8,128)(2,1)S(1)} %bitcast.130, f32[2,2048,64,4]{1,2,3,0:T(8,128)} %get-tuple-element.296, f32[64,2,4]{0,2,1:T(4,128)S(1)} %select_maximum_fusion.2, pred[64,2048]{1,0:T(8,128)(4,1)S(1)} %copy-done.2, f32[64,2,4,128]{3,0,2,1:T(8,128)S(1)} %copy-done.27, ...), kind=kOutput, calls=%fused_computation.11.clone.1 | convolution fusion | flops 273874944 | bytes 5902337 | tf_op jit(solution)/shard_map/while/body/eval_jaxpr/thgk,khd->thgd/dot_general | solution.py:122
  156.4 0.9 compare_and_fusion.3
  157.3 1.7 constant_dynamic-slice_fusion.7
  159.7 3.8 %fusion.70 = (f32[64,2,4]{0,2,1:T(4,128)S(1)}, f32[2,2048,64,4]{1,2,3,0:T(8,128)}) fusion(pred[64,2048]{1,0:T(8,128)(4,1)} %compare_and_fusion.3, bf16[2048,2,128,1]{0,2,3,1:T(8,128)(2,1)S(1)} %bitcast.125, bf16[64,2,4,128]{3,0,2,1:T(8,128)(2,1)} %get-tuple-element.338), kind=kOutput, calls=%fused_computation.5.clone.1 | convolution fusion | flops 271580672 | bytes 5507072 | tf_op jit(solution)/shard_map/while/body/eval_jaxpr/thgd,khd->thgk/dot_general | solution.py:113
  163.5 3.5 %fusion.71 = f32[64,2,4]{0,2,1:T(4,128)S(1)} fusion(f32[2,2048,64,4]{1,2,3,0:T(8,128)} %get-tuple-element.296, f32[64,2,4]{0,2,1:T(4,128)S(1)} %select_maximum_fusion.2, pred[64,2048]{1,0:T(8,128)(4,1)S(1)} %copy-done.2), kind=kLoop, calls=%fused_computation.7.clone.1 | loop fusion | flops 5242368 | bytes 4329472 | tf_op jit(solution)/shard_map/while/body/eval_jaxpr/reduce_sum | solution.py:121
  167.9 3.5 %fusion.73 = f32[64,2,4,128]{3,0,2,1:T(8,128)S(1)} fusion(bf16[2048,2,128,1]{0,2,3,1:T(8,128)(2,1)S(1)} %bitcast.130, f32[2,2048,64,4]{1,2,3,0:T(8,128)} %get-tuple-element.296, f32[64,2,4]{0,2,1:T(4,128)S(1)} %select_maximum_fusion.2, pred[64,2048]{1,0:T(8,128)(4,1)S(1)} %copy-done.2, f32[64,2,4,128]{3,0,2,1:T(8,128)S(1)} %copy-done.27, ...), kind=kOutput, calls=%fused_computation.11.clone.1 | convolution fusion | flops 273874944 | bytes 5902337 | tf_op jit(solution)/shard_map/while/body/eval_jaxpr/thgk,khd->thgd/dot_general | solution.py:122
  172.2 10.5 %all-gather.11.cloned.1.call-done = bf16[4096,256]{1,0:T(8,128)(2,1)} async-done(((bf16[256,256]{1,0:T(8,128)(2,1)}), bf16[4096,256]{1,0:T(8,128)(2,1)}) %all-gather.11.cloned.1.call-update) | async-done | bytes 2097168 | tf_op jit(solution)/shard_map/all_gather | solution.py:59
  182.7 2.3 %convolution_convert_fusion = bf16[64,256]{1,0:T(8,128)(2,1)S(1)} fusion(bf16[4096,256]{1,0:T(8,128)(2,1)} %all-gather.11.cloned.1.call-done, bf16[64,4096]{1,0:T(8,128)(2,1)} %copy-done.3, f32[4096]{0:T(1024)} %copy-done.15, f32[64]{0:T(128)} %copy-done.25), kind=kOutput, calls=%fused_computation.37 | convolution fusion | flops 135282688 | bytes 2670848 | tf_op jit(solution)/shard_map/dot_general | solution.py:62
  185.0 20.6 %all_gather.27 = bf16[1024,256]{1,0:T(8,128)(2,1)S(1)} all-gather(bf16[64,256]{1,0:T(8,128)(2,1)S(1)} %convolution_convert_fusion), channel_id=1, replica_groups=mesh['dp'=16,'mp'=2] {'dp'}, dimensions={0}, use_global_device_ids=true | all-gather | bytes 557056 | tf_op jit(solution)/shard_map/all_gather | solution.py:186
  207.1 0.8 fusion.21
  208.7 5.2 %scatter_fusion = bf16[384,256]{1,0:T(8,128)(2,1)S(1)} fusion(bf16[384,256]{1,0:T(8,128)(2,1)S(1)} %bitcast.128, s32[1024]{0:T(1024)S(1)} %copy-done.18, bf16[1024,256]{1,0:T(8,128)(2,1)S(1)} %copy-done.5), kind=kCustom, calls=%fused_computation.1 | custom fusion | bytes 1576960 | tf_op jit(solution)/shard_map/scatter | solution.py:200
  213.9 5.0 %scatter_fusion.1 = bf16[384,256]{1,0:T(8,128)(2,1)S(1)} fusion(bf16[384,256]{1,0:T(8,128)(2,1)S(1)} %bitcast.126, s32[1024]{0:T(1024)S(1)} %copy-done.18, bf16[1024,256]{1,0:T(8,128)(2,1)S(1)} %all_gather.27), kind=kCustom, calls=%fused_computation.2 | custom fusion | bytes 1576960 | tf_op jit(solution)/shard_map/scatter | solution.py:201
  (146 shorter events, 14.4 us)
Async XLA Ops:
  7.2 47.1 %all-gather.9.cloned.1.call-start = ((), (), s32[]{:S(2)}) async-start(), calls=%async_computation.2 | async-start | bytes 2228224 | tf_op jit(solution)/shard_map/all_gather | solution.py:58
  9.1 89.0 %all-gather.5.cloned.1.call-start = ((), (), s32[]{:S(2)}) async-start(), calls=%async_computation | async-start | bytes 2228224 | tf_op jit(solution)/shard_map/all_gather | solution.py:168
  9.8 130.6 %all-gather.7.cloned.1.call-start = ((), (), s32[]{:S(2)}) async-start(), calls=%async_computation.1 | async-start | bytes 2228224 | tf_op jit(solution)/shard_map/all_gather | solution.py:169
  10.6 172.1 %all-gather.11.cloned.1.call-start = ((), (), s32[]{:S(2)}) async-start(), calls=%async_computation.3 | async-start | bytes 2228224 | tf_op jit(solution)/shard_map/all_gather | solution.py:59
  15.9 6.6 %copy-start.17 = (s32[1024]{0:T(1024)S(1)}, s32[1024]{0:T(1024)}, u32[]{:S(2)}) copy-start(s32[1024]{0:T(1024)} %param.21) | copy-start | bytes 12292
  15.9 7.3 %copy-start.10 = (bf16[64,2048]{1,0:T(8,128)(2,1)S(1)}, bf16[64,2048]{1,0:T(8,128)(2,1)}, u32[]{:S(2)}) copy-start(bf16[64,2048]{1,0:T(8,128)(2,1)} %param.12) | copy-start | bytes 786436
  15.9 17.4 %copy-start.23 = (bf16[4096]{0:T(1024)(128)(2,1)S(1)}, bf16[4096]{0:T(1024)(128)(2,1)}, u32[]{:S(2)}) copy-start(bf16[4096]{0:T(1024)(128)(2,1)} %param.13) | copy-start | bytes 24580
  15.9 17.5 %copy-start.16 = (bf16[64,1024]{1,0:T(8,128)(2,1)S(1)}, bf16[64,1024]{1,0:T(8,128)(2,1)}, u32[]{:S(2)}) copy-start(bf16[64,1024]{1,0:T(8,128)(2,1)} %param.16) | copy-start | bytes 393220
  15.9 17.6 %copy-start.24 = (s32[3,25]{1,0:T(4,128)S(1)}, s32[3,25]{1,0:T(4,128)}, u32[]{:S(2)}) copy-start(s32[3,25]{1,0:T(4,128)} %param.20) | copy-start | bytes 904
  15.9 17.6 %copy-start.26 = (s32[3]{0:T(128)S(1)}, s32[3]{0:T(128)}, u32[]{:S(2)}) copy-start(s32[3]{0:T(128)} %param.19) | copy-start | bytes 40
  33.1 23.4 %copy-start.3 = (bf16[64,4096]{1,0:T(8,128)(2,1)}, bf16[64,4096]{1,0:T(8,128)(2,1)S(1)}, u32[]{:S(2)}) copy-start(bf16[64,4096]{1,0:T(8,128)(2,1)S(1)} %all_gather.23) | copy-start | bytes 1572868
  33.3 21.0 %copy-start.25 = (f32[64]{0:T(128)}, f32[64]{0:T(128)S(1)}, u32[]{:S(2)}) copy-start(f32[64]{0:T(128)S(1)} %add_rsqrt_fusion) | copy-start | bytes 772
  33.4 20.9 %copy-start.15 = (f32[4096]{0:T(1024)}, f32[4096]{0:T(1024)S(1)}, u32[]{:S(2)}) copy-start(f32[4096]{0:T(1024)S(1)} %convert_element_type.40) | copy-start | bytes 49156
  33.5 44.7 %copy-start.7 = (bf16[64,2,4,128]{3,2,1,0:T(4,128)(2,1)}, bf16[64,2,4,128]{3,2,1,0:T(4,128)(2,1)S(1)}, u32[]{:S(2)}) copy-start(bf16[64,2,4,128]{3,2,1,0:T(4,128)(2,1)S(1)} %reshape.343) | copy-start | bytes 393220
  78.2 62.3 %copy-start.4 = (bf16[1024,256]{1,0:T(8,128)(2,1)}, bf16[1024,256]{1,0:T(8,128)(2,1)S(1)}, u32[]{:S(2)}) copy-start(bf16[1024,256]{1,0:T(8,128)(2,1)S(1)} %all_gather.25) | copy-start | bytes 1572868
  143.8 3.8 %copy-start.2 = (pred[64,2048]{1,0:T(8,128)(4,1)S(1)}, pred[64,2048]{1,0:T(8,128)(4,1)}, u32[]{:S(2)}) copy-start(pred[64,2048]{1,0:T(8,128)(4,1)} %compare_and_fusion.3) | copy-start | bytes 393220 | tf_op jit(solution)/shard_map/while
  152.1 4.2 %copy-start.12 = (s32[2,2048]{1,0:T(2,128)S(1)}, s32[2,2048]{1,0:T(2,128)}, u32[]{:S(2)}) copy-start(s32[2,2048]{1,0:T(2,128)} %copy-done.11) | copy-start | bytes 49156 | tf_op jit(solution)/shard_map/while
  152.1 4.2 %copy-start.14 = (s32[2,2048]{1,0:T(2,128)S(1)}, s32[2,2048]{1,0:T(2,128)}, u32[]{:S(2)}) copy-start(s32[2,2048]{1,0:T(2,128)} %copy-done.13) | copy-start | bytes 49156 | tf_op jit(solution)/shard_map/while
  152.1 4.2 %copy-start.20 = (s32[64]{0:T(128)S(1)}, s32[64]{0:T(128)}, u32[]{:S(2)}) copy-start(s32[64]{0:T(128)} %copy-done.19) | copy-start | bytes 772 | tf_op jit(solution)/shard_map/while
  152.1 4.2 %copy-start.22 = (s32[64]{0:T(128)S(1)}, s32[64]{0:T(128)}, u32[]{:S(2)}) copy-start(s32[64]{0:T(128)} %copy-done.21) | copy-start | bytes 772 | tf_op jit(solution)/shard_map/while
  159.7 3.8 %copy-start.2 = (pred[64,2048]{1,0:T(8,128)(4,1)S(1)}, pred[64,2048]{1,0:T(8,128)(4,1)}, u32[]{:S(2)}) copy-start(pred[64,2048]{1,0:T(8,128)(4,1)} %compare_and_fusion.3) | copy-start | bytes 393220 | tf_op jit(solution)/shard_map/while
  167.9 4.2 %copy-start.12 = (s32[2,2048]{1,0:T(2,128)S(1)}, s32[2,2048]{1,0:T(2,128)}, u32[]{:S(2)}) copy-start(s32[2,2048]{1,0:T(2,128)} %copy-done.11) | copy-start | bytes 49156 | tf_op jit(solution)/shard_map/while
  167.9 4.2 %copy-start.14 = (s32[2,2048]{1,0:T(2,128)S(1)}, s32[2,2048]{1,0:T(2,128)}, u32[]{:S(2)}) copy-start(s32[2,2048]{1,0:T(2,128)} %copy-done.13) | copy-start | bytes 49156 | tf_op jit(solution)/shard_map/while
  167.9 4.2 %copy-start.20 = (s32[64]{0:T(128)S(1)}, s32[64]{0:T(128)}, u32[]{:S(2)}) copy-start(s32[64]{0:T(128)} %copy-done.19) | copy-start | bytes 772 | tf_op jit(solution)/shard_map/while
  167.9 4.2 %copy-start.22 = (s32[64]{0:T(128)S(1)}, s32[64]{0:T(128)}, u32[]{:S(2)}) copy-start(s32[64]{0:T(128)} %copy-done.21) | copy-start | bytes 772 | tf_op jit(solution)/shard_map/while
  172.2 33.6 %copy-start.6 = (bf16[1024,256]{0,1:T(8,128)(2,1)S(1)}, bf16[1024,256]{0,1:T(8,128)(2,1)}, u32[]{:S(2)}) copy-start(bf16[1024,256]{0,1:T(8,128)(2,1)} %copy.48) | copy-start | bytes 1572868
  172.2 33.6 %copy-start.8 = (bf16[64,2,4,128]{3,2,1,0:T(4,128)(2,1)S(1)}, bf16[64,2,4,128]{3,2,1,0:T(4,128)(2,1)}, u32[]{:S(2)}) copy-start(bf16[64,2,4,128]{3,2,1,0:T(4,128)(2,1)} %copy-done.7) | copy-start | bytes 393220
  172.2 33.6 %copy-start.9 = (pred[64,1024]{1,0:T(8,128)(4,1)S(1)}, pred[64,1024]{1,0:T(8,128)(4,1)}, u32[]{:S(2)}) copy-start(pred[64,1024]{1,0:T(8,128)(4,1)} %compare_and_fusion.1) | copy-start | bytes 196612
  205.8 1.3 copy-start.29
  207.1 1.6 copy-start.5
  207.1 1.6 copy-start.18
  213.9 5.0 %copy-start.1 = (bf16[384,256]{1,0:T(8,128)(2,1)}, bf16[384,256]{1,0:T(8,128)(2,1)S(1)}, u32[]{:S(2)}) copy-start(bf16[384,256]{1,0:T(8,128)(2,1)S(1)} %scatter_fusion) | copy-start | bytes 589828
  (13 other events, 11.7 us)
Sparse Core Ops, SparseCore 0:
  10.2 44.0 all-gather.8
  57.0 41.0 all-gather.4
  100.3 40.1 all-gather.6
  142.5 40.1 all-gather.10
where the time goes:
time: 227 us; the launch traced here: 226 us
  waiting for transfers between devices  90.7 us (40%)
  blocking collectives  51.9 us (23%)
  local copies, waits for them, and re-layouts  33.7 us (15%)
  matrix products  20.4 us (9%)
  other arithmetic  15 us (7%)
  between operations  14.1 us (6%)
    all_gather x1, waiting for transfers between devices, body(): lax.all_gather(old_values, 'dp', axis=0, tiled=True)  42.4 us
    all_gather x1, blocking collectives, body(): lax.all_gather(new_keys, 'dp', axis=0, tiled=True)  21.4 us
    all_gather x1, blocking collectives, body(): lax.all_gather(new_values, 'dp', axis=0, tiled=True)  20.6 us
    all_gather x1, waiting for transfers between devices, body(): lax.all_gather(old_keys, 'dp', axis=0, tiled=True)  18.9 us
    all_gather x1, waiting for transfers between devices, body(): lax.all_gather(w_key, 'dp', axis=0, tiled=True)  18.3 us
    all_gather x1, waiting for transfers between devices, body(): lax.all_gather(w_value, 'dp', axis=0, tiled=True)  10.5 us
    all_gather x1, blocking collectives, body(): gathered = lax.all_gather(features, 'mp', axis=1, tiled=True)  9.9 us
    dot_general x3, matrix products, attend(): jnp.einsum('thgd,khd->thgk', q_local, keys_shaped, preferred_element_type...  8.2 us
  transfers between devices with their start and end apart: 4, of which 4 were waited for; matrix products, arithmetic and copies ran while one was open for 22% of the time, Pallas kernels for 0%

commit v1 on v0

--- a/solution.py
+++ b/solution.py
@@ -1,8 +1,12 @@
+import functools
 import math
 
 import jax
 import jax.numpy as jnp
+import numpy as np
 from jax import lax
+from jax.experimental import pallas as pl
+from jax.experimental.pallas import tpu as pltpu
 from jax.sharding import PartitionSpec as P
 
 HD = 128
@@ -13,6 +17,11 @@
 
 THETA = 500000.0
 NEG_FILL = -1e30
+NEG_START = -1e29
+LOG2E = 1.4426950408889634
+VMEM_LIMIT = 32 * 1024 * 1024
+SPLIT_LIMIT = 63 * 1024 * 1024
+STEP_PAGES = 4
 
 
 def rotate(values, positions, head_size):
@@ -29,7 +38,7 @@
     )
 
 
-def body(
+def general_body(
     features,
     norm_gain,
     w_key,
@@ -210,6 +219,583 @@
     return (attended, pool_keys.reshape(key_pool.shape), pool_values.reshape(value_pool.shape))
 
 
+def ring_chip(pos, chips):
+    pos = pos % chips
+    return jnp.where(pos < chips // 2, 2 * pos, 2 * chips - 1 - 2 * pos)
+
+
+def ring_place(chip, chips):
+    return jnp.where(chip % 2 == 0, chip // 2, (2 * chips - 1 - chip) // 2)
+
+
+def ring_pairs(chips, step, swap):
+    order = [2 * k if k < chips // 2 else 2 * chips - 1 - 2 * k for k in range(chips)]
+    return [
+        (2 * order[k] + core, 2 * order[(k + step) % chips] + (core ^ swap))
+        for k in range(chips)
+        for core in range(2)
+    ]
+
+
+def ring_offsets(chips):
+    return [0] + [o for d in range(1, chips // 2) for o in (d, -d)] + [chips // 2]
+
+
+def request_starts(tr_ref, requests):
+    tr = tr_ref[...]
+    starts = [jnp.int32(0)]
+    for r in range(1, requests):
+        starts.append(jnp.sum(jnp.where(tr < r, 1.0, 0.0)).astype(jnp.int32))
+    starts.append(jnp.int32(tr.shape[0] * tr.shape[1]))
+    return starts
+
+
+def pick(cond_starts, values, tokens):
+    out = jnp.zeros_like(tokens) + values[0]
+    for r in range(1, len(values)):
+        out = jnp.where(tokens >= cond_starts[r], values[r], out)
+    return out
+
+
+def chip_requests(chip, toks, starts):
+    first, last = jnp.int32(0), jnp.int32(0)
+    for start in starts[1:-1]:
+        first = first + (chip * toks >= start).astype(jnp.int32)
+        last = last + (chip * toks + toks - 1 >= start).astype(jnp.int32)
+    return first, last
+
+
+def split_kernel(old, f_ref, q_ref, kp_ref, vp_ref, xc_ref, xo_ref, qo_ref, kvc_ref, kvo_ref, sems):
+    core = lax.axis_index("dp") % 2
+    copies = []
+
+    def copy(source, target):
+        copies.append(pltpu.make_async_copy(source, target, sems.at[len(copies)]))
+        copies[-1].start()
+
+    for page_ref, first in ((kp_ref, 0), (vp_ref, old)):
+        for out_ref, head in ((kvo_ref, 1 - core), (kvc_ref, core)):
+            at = pl.ds(pl.multiple_of(head * HD, HD), HD)
+            copy(page_ref.at[pl.ds(0, old), :, at], out_ref.at[pl.ds(first, old)])
+    for out_ref, own in ((xo_ref, 1 - core), (xc_ref, core)):
+        for m in range(f_ref.shape[1] // 512):
+            at = pl.ds(pl.multiple_of((2 * m + own) * 256, 256), 256)
+            copy(f_ref.at[:, at], out_ref.at[:, pl.ds(m * 256, 256)])
+    half = q_ref.shape[1] // 2
+    copy(q_ref.at[:, pl.ds(pl.multiple_of((1 - core) * half, 128), half)], qo_ref)
+    for c in copies:
+        c.wait()
+
+
+def merge_kernel(kvm_ref, kvg_ref, q_ref, qg_ref, kv_ref, qs_ref):
+    core = lax.axis_index("dp") % 2
+    count = kvm_ref.shape[0]
+    kv_ref[:count] = kvm_ref[...]
+    kv_ref[count:] = kvg_ref[...]
+    rows, group = q_ref.shape[0], qg_ref.shape[1] // HD
+    for h in range(group):
+        mine = pl.ds(pl.multiple_of((2 * h + core) * rows, rows), rows)
+        other = pl.ds(pl.multiple_of((2 * h + 1 - core) * rows, rows), rows)
+        qs_ref[mine, :] = q_ref[:, pl.ds(pl.multiple_of((core * group + h) * HD, HD), HD)]
+        qs_ref[other, :] = qg_ref[:, h * HD : (h + 1) * HD]
+
+
+def scale_kernel(
+    chips, lens_ref, tr_ref, inv_ref, gain_ref, a_ref, b_ref, c_ref, d_ref, xs_ref, ss_ref, cos_ref, sin_ref
+):
+    dp = lax.axis_index("dp")
+    mp = lax.axis_index("mp")
+    chip, core = dp // 2, dp % 2
+    rows = a_ref.shape[0]
+    per_half = a_ref.shape[1] // 256
+    for first, second, owner in ((a_ref, b_ref, core), (c_ref, d_ref, 1 - core)):
+        at = pl.ds(pl.multiple_of(owner * rows, rows), rows)
+        total = jnp.zeros((rows, 256), jnp.float32)
+        for ref, half in ((first, mp), (second, 1 - mp)):
+            for m in range(per_half):
+                wide = ref[:, m * 256 : (m + 1) * 256].astype(jnp.float32)
+                block = half * (2 * per_half) + 2 * m + core
+                gain = gain_ref[:, pl.ds(pl.multiple_of(block * 256, 256), 256)].astype(jnp.float32)
+                total = total + wide * wide
+                xs_ref[half * per_half + m, at, :] = (wide * gain).astype(jnp.bfloat16)
+        ss_ref[at, :] = jnp.broadcast_to(jnp.sum(total, axis=1, keepdims=True), (rows, 128))
+    requests = lens_ref.shape[0]
+    starts = request_starts(tr_ref, requests)
+    tokens = chip * (2 * rows) + lax.broadcasted_iota(jnp.int32, (2 * rows, 128), 0)
+    shift = pick(starts, [lens_ref[r] - starts[r] for r in range(requests)], tokens)
+    angles = (tokens + shift).astype(jnp.float32) * inv_ref[...]
+    lane = lax.broadcasted_iota(jnp.int32, (2 * rows, 128), 1)
+    sine = jnp.sin(angles)
+    cos_ref[...] = jnp.cos(angles)
+    sin_ref[...] = jnp.where(lane < HD // 2, -sine, sine)
+
+
+def project_kernel(chips, xs_ref, ss_ref, *refs):
+    keys, values = refs[:chips], refs[chips : 2 * chips]
+    send_ref, keep_ref, acc_ref = refs[2 * chips :]
+    dp = lax.axis_index("dp")
+    chip, core = dp // 2, dp % 2
+    place = ring_place(chip, chips)
+    ksum = jnp.zeros((xs_ref.shape[1], 2 * HD), jnp.float32)
+    vsum = jnp.zeros((xs_ref.shape[1], 2 * HD), jnp.float32)
+    for n, offset in enumerate(ring_offsets(chips)):
+        x = xs_ref[ring_chip(place + offset + chips, chips)]
+        ksum = ksum + jnp.dot(x, keys[n][...], preferred_element_type=jnp.float32)
+        vsum = vsum + jnp.dot(x, values[n][...], preferred_element_type=jnp.float32)
+    acc_ref[:, : 2 * HD] = ksum
+    acc_ref[:, 2 * HD :] = vsum
+    for ref, head in ((send_ref, 1 - core), (keep_ref, core)):
+        ref[:, :HD] = acc_ref[:, pl.ds(pl.multiple_of(head * HD, HD), HD)]
+        ref[:, HD : 2 * HD] = acc_ref[:, pl.ds(pl.multiple_of((2 + head) * HD, HD), HD)]
+        ref[:, 2 * HD :] = ss_ref[...]
+
+
+def rotate_kernel(width, keep_ref, got_ref, cos_ref, sin_ref, out_ref):
+    total = keep_ref[...] + got_ref[...]
+    inverse = lax.rsqrt(total[:, 2 * HD :] * (1.0 / width) + 1e-05)
+    key = total[:, :HD] * inverse
+    rolled = pltpu.roll(key, HD // 2, 1)
+    out_ref[:, :HD] = (key * cos_ref[...] + rolled * sin_ref[...]).astype(jnp.bfloat16)
+    out_ref[:, HD:] = (total[:, HD : 2 * HD] * inverse).astype(jnp.bfloat16)
+
+
+def attend_block(qs_ref, keys, values, first, low, high, m_ref, l_ref, acc_ref):
+    scores = lax.dot_general(keys, qs_ref[...], (((1,), (1,)), ((), ())), preferred_element_type=jnp.float32)
+    ids = first + lax.broadcasted_iota(jnp.int32, scores.shape, 0)
+    scores = jnp.where((ids >= low) & (ids < high), scores * (LOG2E / math.sqrt(HD)), NEG_FILL)
+    before = m_ref[...]
+    top = jnp.maximum(before, jnp.max(scores, axis=0, keepdims=True))
+    shrink = jnp.exp2(before - top)
+    weights = jnp.exp2(scores - top)
+    m_ref[...] = top
+    l_ref[...] = l_ref[...] * shrink + jnp.sum(weights, axis=0, keepdims=True)
+    acc_ref[...] = acc_ref[...] * shrink + lax.dot_general(
+        values,
+        weights.astype(jnp.bfloat16),
+        (((0,), (0,)), ((), ())),
+        preferred_element_type=jnp.float32,
+    )
+
+
+def cached_part(
+    chips, pages_dev, old, offsets, blocks, starts, reqs, lens_ref, table_ref, qs_ref, kbuf, vbuf, slot_of, state
+):
+    dp = lax.axis_index("dp")
+    chip, core = dp // 2, dp % 2
+    place = ring_place(chip, chips)
+    requests = lens_ref.shape[0]
+    width = qs_ref.shape[0]
+    toks = starts[-1] // chips
+
+    def clear(i, carry):
+        slot_of[i] = -1
+        return carry
+
+    def held(page):
+        distance = (ring_place(page // (2 * pages_dev), chips) - place + chips) % chips
+        found = distance == offsets[0] % chips
+        for o in offsets[1:]:
+            found = found | (distance == o % chips)
+        return found
+
+    lax.fori_loop(0, slot_of.shape[0], clear, 0)
+    base = jnp.int32(0)
+    lows, highs = [], []
+    for r in range(requests):
+        length = lens_ref[r]
+        pages = (length + PAGE - 1) // PAGE
+        count = jnp.where((r >= reqs[0]) & (r <= reqs[1]), pages, 0)
+
+        def put(l, at, r=r):
+            page = table_ref[r, l]
+            here = held(page)
+
+            @pl.when(here)
+            def _():
+                slot_of[page] = at
+
+            return at + here.astype(jnp.int32)
+
+        end = lax.fori_loop(0, count, put, base)
+        last_here = (end > base) & held(table_ref[r, pages - 1])
+        lows.append(base * PAGE)
+        highs.append(end * PAGE - jnp.where(last_here, pages * PAGE - length, 0))
+        base = end
+
+    for offset, block in zip(offsets, blocks):
+        source = ring_chip(place + offset + chips, chips)
+        for part, owner in ((0, 2 * source + core), (2 * old, 2 * source + 1 - core)):
+            for s in range(old):
+                slot = slot_of[owner * pages_dev + s]
+
+                @pl.when(slot >= 0)
+                def _(block=block, part=part, s=s, slot=slot):
+                    at = pl.ds(pl.multiple_of(slot * PAGE, PAGE), PAGE)
+                    kbuf[at, :] = block[part + s]
+                    vbuf[at, :] = block[part + old + s]
+
+    size = STEP_PAGES * PAGE
+    pad = pl.ds(pl.multiple_of(base * PAGE, PAGE), size - PAGE)
+    kbuf[pad, :] = jnp.zeros((size - PAGE, HD), kbuf.dtype)
+    vbuf[pad, :] = jnp.zeros((size - PAGE, HD), vbuf.dtype)
+    tokens = chip * toks + lax.broadcasted_iota(jnp.int32, (1, width), 1) % toks
+    low = pick(starts, lows, tokens)
+    high = pick(starts, highs, tokens)
+
+    def step(i, carry):
+        at = pl.ds(pl.multiple_of(i * size, size), size)
+        attend_block(qs_ref, kbuf[at, :], vbuf[at, :], i * size, low, high, *state)
+        return carry
+
+    lax.fori_loop(0, (base + STEP_PAGES - 1) // STEP_PAGES, step, 0)
+
+
+def cached_kernel(chips, pages_dev, old, offsets, lens_ref, table_ref, tr_ref, qs_ref, *refs):
+    blocks = refs[: len(offsets)]
+    m_ref, l_ref, acc_ref, kbuf, vbuf, slot_of = refs[len(offsets) :]
+    chip = lax.axis_index("dp") // 2
+    starts = request_starts(tr_ref, lens_ref.shape[0])
+    reqs = chip_requests(chip, starts[-1] // chips, starts)
+    m_ref[...] = jnp.full(m_ref.shape, NEG_START, jnp.float32)
+    l_ref[...] = jnp.zeros(l_ref.shape, jnp.float32)
+    acc_ref[...] = jnp.zeros(acc_ref.shape, jnp.float32)
+    cached_part(
+        chips,
+        pages_dev,
+        old,
+        offsets,
+        blocks,
+        starts,
+        reqs,
+        lens_ref,
+        table_ref,
+        qs_ref,
+        kbuf,
+        vbuf,
+        slot_of,
+        (m_ref, l_ref, acc_ref),
+    )
+
+
+def fresh_kernel(
+    chips, pages_dev, old, offsets, lens_ref, table_ref, tr_ref, qs_ref, m0_ref, l0_ref, acc0_ref, *refs
+):
+    blocks, fresh = refs[: len(offsets)], refs[len(offsets) : len(offsets) + chips]
+    atto_ref, attc_ref, no_ref, nc_ref, info_ref = refs[len(offsets) + chips : len(offsets) + chips + 5]
+    (kbuf, vbuf, nbuf, m_ref, l_ref, acc_ref, out_ref, slot_of, new_at, new_lo, new_hi) = refs[
+        len(offsets) + chips + 5 :
+    ]
+    dp = lax.axis_index("dp")
+    chip, core = dp // 2, dp % 2
+    place = ring_place(chip, chips)
+    toks = fresh[0].shape[0]
+    rows = toks // 2
+    requests = lens_ref.shape[0]
+    width = qs_ref.shape[0]
+    group = width // toks
+    starts = request_starts(tr_ref, requests)
+    reqs = chip_requests(chip, toks, starts)
+    first_req = reqs[0]
+    m_ref[...] = m0_ref[...]
+    l_ref[...] = l0_ref[...]
+    acc_ref[...] = acc0_ref[...]
+    cached_part(
+        chips,
+        pages_dev,
+        old,
+        offsets,
+        blocks,
+        starts,
+        reqs,
+        lens_ref,
+        table_ref,
+        qs_ref,
+        kbuf,
+        vbuf,
+        slot_of,
+        (m_ref, l_ref, acc_ref),
+    )
+
+    def clear(i, carry):
+        new_lo[i] = 0
+        new_hi[i] = 0
+        return carry
+
+    lax.fori_loop(0, new_lo.shape[0], clear, 0)
+    for r in range(requests):
+        length = lens_ref[r]
+
+        def place_new(l, carry, r=r, length=length):
+            at = l * PAGE - length + starts[r]
+            page = table_ref[r, l]
+            new_at[page] = at
+            new_lo[page] = jnp.maximum(starts[r] - at, 0)
+            new_hi[page] = jnp.minimum(starts[r + 1] - at, PAGE)
+            return carry
+
+        end = (length + starts[r + 1] - starts[r] + PAGE - 1) // PAGE
+        lax.fori_loop(length // PAGE, end, place_new, 0)
+
+    for n, offset in enumerate(ring_offsets(chips)):
+        source = ring_chip(place + offset + chips, chips)
+        nbuf[pl.ds(pl.multiple_of((source + 1) * toks, toks), toks), :] = fresh[n][...]
+    nbuf[:toks, :] = jnp.zeros((toks, 2 * HD), nbuf.dtype)
+    nbuf[(chips + 1) * toks :, :] = jnp.zeros((toks, 2 * HD), nbuf.dtype)
+
+    tokens = chip * toks + lax.broadcasted_iota(jnp.int32, (1, width), 1) % toks
+    low = pick(starts, starts[:requests], tokens)
+    first_start = starts[0]
+    for r in range(1, requests):
+        first_start = jnp.where(first_req == r, starts[r], first_start)
+
+    def step(b, carry):
+        at = pl.ds(pl.multiple_of((b + 1) * toks, toks), toks)
+        attend_block(qs_ref, nbuf[at, :HD], nbuf[at, HD:], b * toks, low, tokens + 1, m_ref, l_ref, acc_ref)
+        return carry
+
+    lax.fori_loop(first_start // toks, chip + 1, step, 0)
+    result = acc_ref[...] / l_ref[...]
+    for h in range(group):
+        out_ref[:, h * HD : (h + 1) * HD] = result[:, h * toks : (h + 1) * toks].T.astype(jnp.bfloat16)
+    attc_ref[...] = out_ref[pl.ds(pl.multiple_of(core * rows, rows), rows), :]
+    atto_ref[...] = out_ref[pl.ds(pl.multiple_of((1 - core) * rows, rows), rows), :]
+
+    row = lax.broadcasted_iota(jnp.int32, (PAGE, 2 * toks), 0)
+    column = lax.broadcasted_iota(jnp.int32, (PAGE, 2 * toks), 1)
+    for ref, owner in ((no_ref, dp + 1 - 2 * core), (nc_ref, dp)):
+        for s in range(pages_dev):
+            page = owner * pages_dev + s
+            at, low_row, high_row = new_at[page], new_lo[page], new_hi[page]
+
+            @pl.when(high_row > low_row)
+            def _(ref=ref, s=s, at=at, low_row=low_row, high_row=high_row):
+                shifted = at + toks
+                first = pl.multiple_of(shifted // toks * toks, toks)
+                chosen = (column + first == row + shifted) & (row >= low_row) & (row < high_row)
+                ref[s] = jnp.dot(
+                    jnp.where(chosen, 1.0, 0.0).astype(jnp.bfloat16),
+                    nbuf[pl.ds(first, 2 * toks), :],
+                    preferred_element_type=jnp.float32,
+                ).astype(jnp.bfloat16)
+
+    for s in range(pages_dev):
+        info_ref[2 * s] = new_lo[dp * pages_dev + s]
+        info_ref[2 * s + 1] = new_hi[dp * pages_dev + s]
+
+
+def join_kernel(info_ref, attc_ref, attr_ref, nc_ref, nr_ref, kp_ref, vp_ref, att_ref, ko_ref, vo_ref):
+    core = lax.axis_index("dp") % 2
+    half = attc_ref.shape[1]
+    att_ref[:, pl.ds(pl.multiple_of(core * half, HD), half)] = attc_ref[...]
+    att_ref[:, pl.ds(pl.multiple_of((1 - core) * half, HD), half)] = attr_ref[...]
+    row = lax.broadcasted_iota(jnp.int32, (PAGE, HD), 0)
+    for s in range(kp_ref.shape[0]):
+        chosen = (row >= info_ref[2 * s]) & (row < info_ref[2 * s + 1])
+        for ref, head in ((nc_ref, core), (nr_ref, 1 - core)):
+            at = pl.ds(pl.multiple_of(head * HD, HD), HD)
+            ko_ref[s, :, at] = jnp.where(chosen, ref[s, :, :HD], kp_ref[s, :, at])
+            vo_ref[s, :, at] = jnp.where(chosen, ref[s, :, HD:], vp_ref[s, :, at])
+
+
+def call(
+    kernel, outs, scratch=(), ins=None, smem=(), far=(), out_smem=(), out_far=(), limit=VMEM_LIMIT, name=None
+):
+    vmem, sm = pl.BlockSpec(memory_space=pltpu.VMEM), pl.BlockSpec(memory_space=pltpu.SMEM)
+    hbm = pl.BlockSpec(memory_space=pl.ANY)
+    return pl.pallas_call(
+        kernel,
+        out_shape=[jax.ShapeDtypeStruct(s, d) for s, d in outs],
+        in_specs=[sm if n in smem else hbm if n in far else vmem for n in range(ins)],
+        out_specs=[sm if n in out_smem else hbm if n in out_far else vmem for n in range(len(outs))],
+        scratch_shapes=list(scratch),
+        compiler_params=pltpu.CompilerParams(vmem_limit_bytes=limit),
+        name=name,
+    )
+
+
+def ring_send(chips, arrays, step, swap=0):
+    return [lax.ppermute(a, "dp", ring_pairs(chips, step, swap * n)) for n, a in enumerate(arrays)]
+
+
+def ring_body(
+    dp_count,
+    features,
+    norm_gain,
+    w_key,
+    w_value,
+    queries,
+    key_pool,
+    value_pool,
+    cache_lens,
+    page_table,
+    token_request,
+):
+    bf, f32, i32 = jnp.bfloat16, jnp.float32, jnp.int32
+    chips = dp_count // 2
+    offsets = ring_offsets(chips)
+    rows, half_width = features.shape
+    width = norm_gain.shape[0]
+    toks = 2 * rows
+    pages_dev = key_pool.shape[0]
+    long_pages = (CTX_DEV * dp_count + PAGE - 1) // PAGE
+    old = (long_pages + 2 * ((SHORT + PAGE - 1) // PAGE) + dp_count - 1) // dp_count
+    group = queries.shape[1] // (2 * HD)
+    columns = group * toks
+    core_pairs = [(i, i ^ 1) for i in range(dp_count)]
+    mp_pairs = [(0, 1), (1, 0)]
+    both_pairs = [(2 * i + j, 2 * (i ^ 1) + (1 - j)) for i in range(dp_count) for j in range(2)]
+    requests_tile = token_request.reshape(-1, 128)
+
+    w_got = {0: [w_key, w_value]}
+    right, left = ring_send(chips, [w_key, w_value], 1), ring_send(chips, [w_key, w_value], -1)
+    w_got[-1], w_got[1] = right, left
+    x_mine, x_other, q_other, kv_mine, kv_other = call(
+        functools.partial(split_kernel, old),
+        [
+            ((rows, half_width // 2), bf),
+            ((rows, half_width // 2), bf),
+            ((rows, group * HD), bf),
+            ((2 * old, PAGE, HD), bf),
+            ((2 * old, PAGE, HD), bf),
+        ],
+        scratch=[pltpu.SemaphoreType.DMA((4 + 2 * (half_width // 512) + 1,))],
+        ins=4,
+        far=(0, 1, 2, 3),
+        limit=SPLIT_LIMIT,
+        name="split",
+    )(features, queries, key_pool, value_pool)
+    x_b = lax.ppermute(x_mine, "mp", mp_pairs)
+    x_c = lax.ppermute(x_other, "dp", core_pairs)
+    x_d = lax.ppermute(x_other, ("dp", "mp"), both_pairs)
+    q_got = lax.ppermute(q_other, "dp", core_pairs)
+    kv_got = lax.ppermute(kv_other, "dp", core_pairs)
+    early = (x_b, x_c, x_d, q_got, kv_got)
+    for d in range(2, chips // 2):
+        if d == chips // 2 - 1:
+            right, left, early = lax.optimization_barrier((right, left, early))
+            x_b, x_c, x_d, q_got, kv_got = early
+        right, left = ring_send(chips, right, 1), ring_send(chips, left, -1)
+        w_got[-d], w_got[d] = right, left
+
+    kv, q_rows = call(
+        merge_kernel,
+        [((4 * old, PAGE, HD), bf), ((columns, HD), bf)],
+        ins=4,
+        name="merge",
+    )(kv_mine, kv_got, queries, q_got)
+    inverse = (THETA ** (-(np.arange(HD) % (HD // 2)) * 2.0 / HD)).astype(np.float32)[None, :]
+    scaled, squares, cosine, sine = call(
+        functools.partial(scale_kernel, chips),
+        [((chips, toks, 256), bf), ((toks, 128), f32), ((toks, HD), f32), ((toks, HD), f32)],
+        ins=8,
+        smem=(0,),
+        name="scale",
+    )(
+        cache_lens,
+        requests_tile,
+        jnp.asarray(inverse),
+        norm_gain.reshape(1, -1),
+        x_mine,
+        x_b,
+        x_c,
+        x_d,
+    )
+    right, left, scaled, kv, q_rows = lax.optimization_barrier((right, left, scaled, kv, q_rows))
+    w_got[chips // 2] = ring_send(chips, right[:1], 1) + ring_send(chips, left[1:], -1)
+    part_send, part_keep = call(
+        functools.partial(project_kernel, chips),
+        [((toks, 3 * HD), f32), ((toks, 3 * HD), f32)],
+        scratch=[pltpu.VMEM((toks, 4 * HD), f32)],
+        ins=2 + 2 * chips,
+        name="project",
+    )(scaled, squares, *[w_got[o][0] for o in offsets], *[w_got[o][1] for o in offsets])
+    part_got = lax.ppermute(part_send, "dp", core_pairs)
+
+    kv_late, _ = lax.optimization_barrier((kv, part_send))
+    kv_got = {0: kv}
+    kv_got[-1], kv_got[1] = ring_send(chips, [kv_late], 1)[0], ring_send(chips, [kv_late], -1)[0]
+    (fresh,) = call(
+        functools.partial(rotate_kernel, width),
+        [((toks, 2 * HD), bf)],
+        ins=4,
+        name="rotary",
+    )(part_keep, part_got, cosine, sine)
+    new = {0: fresh}
+    new[-1], new[1] = ring_send(chips, [fresh], 1)[0], ring_send(chips, [fresh], -1)[0]
+    for d in range(2, chips // 2):
+        right, left, _ = lax.optimization_barrier((kv_got[1 - d], kv_got[d - 1], (new[1 - d], new[d - 1])))
+        new[-d], new[d] = ring_send(chips, [new[1 - d]], 1)[0], ring_send(chips, [new[d - 1]], -1)[0]
+        kv_got[-d], kv_got[d] = ring_send(chips, [right], 1)[0], ring_send(chips, [left], -1)[0]
+    last = chips // 2
+    (kv_got[last],) = ring_send(chips, [kv_got[1 - last]], 1)
+
+    first = [o for o in offsets if abs(o) <= last - 2]
+    rest = [o for o in offsets if abs(o) > last - 2]
+
+    def buffers(count):
+        slots = 2 * old * count + STEP_PAGES
+        return [pltpu.VMEM((slots * PAGE, HD), bf)] * 2
+
+    table = pltpu.SMEM((dp_count * pages_dev,), i32)
+    top, total, acc = call(
+        functools.partial(cached_kernel, chips, pages_dev, old, first),
+        [((1, columns), f32), ((1, columns), f32), ((HD, columns), f32)],
+        scratch=[*buffers(len(first)), table],
+        ins=4 + len(first),
+        smem=(0, 1),
+        name="attend_cached",
+    )(cache_lens, page_table, requests_tile, q_rows, *[kv_got[o] for o in first])
+    before, top, total, acc = lax.optimization_barrier((new[last - 1], top, total, acc))
+    (new[last],) = ring_send(chips, [before], -1)
+
+    att_other, att_mine, rows_other, rows_mine, info = call(
+        functools.partial(fresh_kernel, chips, pages_dev, old, rest),
+        [
+            ((rows, group * HD), bf),
+            ((rows, group * HD), bf),
+            ((pages_dev, PAGE, 2 * HD), bf),
+            ((pages_dev, PAGE, 2 * HD), bf),
+            ((2 * pages_dev,), i32),
+        ],
+        scratch=[
+            *buffers(len(rest)),
+            pltpu.VMEM(((chips + 2) * toks, 2 * HD), bf),
+            pltpu.VMEM((1, columns), f32),
+            pltpu.VMEM((1, columns), f32),
+            pltpu.VMEM((HD, columns), f32),
+            pltpu.VMEM((toks, group * HD), bf),
+            table,
+            table,
+            table,
+            table,
+        ],
+        ins=7 + len(rest) + chips,
+        smem=(0, 1),
+        out_smem=(4,),
+        name="attend_new",
+    )(
+        cache_lens,
+        page_table,
+        requests_tile,
+        q_rows,
+        top,
+        total,
+        acc,
+        *[kv_got[o] for o in rest],
+        *[new[o] for o in offsets],
+    )
+    rows_got = lax.ppermute(rows_other, "dp", core_pairs)
+    att_got = lax.ppermute(att_other, "dp", core_pairs)
+    attended, keys_out, values_out = call(
+        join_kernel,
+        [(queries.shape, bf), (key_pool.shape, bf), (value_pool.shape, bf)],
+        ins=7,
+        smem=(0,),
+        name="join",
+    )(info, att_mine, att_got, rows_mine, rows_got, key_pool, value_pool)
+    return attended, keys_out, values_out
+
+
 def solution(mesh):
     in_specs = (
         P("dp", "mp"),
@@ -224,4 +810,12 @@
         P(),
     )
     out_specs = (P("dp", "mp"), P("dp", None, "mp"), P("dp", None, "mp"))
+    dp_count, mp_count = mesh.shape["dp"], mesh.shape["mp"]
+
+    def body(*args):
+        even = mp_count == 2 and dp_count % 8 == 0 and dp_count & (dp_count - 1) == 0
+        if even and args[2].shape == (256, 2 * HD):
+            return ring_body(dp_count, *args)
+        return general_body(*args)
+
     return jax.shard_map(body, mesh=mesh, in_specs=in_specs, out_specs=out_specs, check_vma=False)

time: 227 us -> 86.8 us (0.38)
  waiting for transfers between devices: 90.7 us -> 38.3 us
  blocking collectives: 51.9 us -> 0 us
  starting transfers between devices: 0.16 us -> 33.4 us
  local copies, waits for them, and re-layouts: 33.7 us -> 1.78 us
  matrix products: 20.4 us -> 0 us
  other arithmetic: 15 us -> 0 us
  between operations: 14.1 us -> 0.82 us
  Pallas kernels: 0 us -> 11.3 us
    all_gather x4 -> x0, waiting for transfers between devices: 90.1 us -> none  [the longest x1 42.4 us: body(): lax.all_gather(old_values, 'dp', axis=0, tiled=True)]
    all_gather x3 -> x0, blocking collectives: 51.9 us -> none  [the longest x1 21.4 us: body(): lax.all_gather(new_keys, 'dp', axis=0, tiled=True)]
    ppermute x0 -> x36, waiting for transfers between devices: none -> 38.3 us  [the longest x28 37.2 us: ring_send(): lax.ppermute(a, 'dp', ring_pairs(chips, step, swap * n))]
    ppermute x0 -> x36, starting transfers between devices: none -> 33.4 us  [the longest x28 30.6 us: ring_send(): lax.ppermute(a, 'dp', ring_pairs(chips, step, swap * n))]
    dot_general x8 -> x0, matrix products: 20.4 us -> none  [the longest x3 8.2 us: attend(): jnp.einsum('thgd,khd->thgk', q_local, keys_shaped, preferred_element_type...]
    pallas_call x0 -> x8, Pallas kernels: none -> 11.3 us  [the longest x1 4.02 us: ring_body(): call(functools.partial(fresh_kernel, chips, pages_dev, old, rest), [((row...]
    scatter x2 -> x0, local copies, waits for them, and re-layouts: 10.2 us -> none  [the longest x1 5.18 us: body(): pool_keys.at[dest_all].set(pieces[0], mode='drop')]
    reduce_sum x7 -> x0, other arithmetic: 9.72 us -> none  [the longest x3 7.7 us: attend(): new_sum = running_sum * factor + jnp.sum(soft_weights, axis=-1)]
  transfers between devices with their start and end apart: 4 -> 36, of which waited for: 4 -> 18; matrix products, arithmetic and copies ran while one was open for 22% -> 0% of each run, Pallas kernels for 0% -> 6%
where the time goes in v1:
time: 86.8 us; the launch traced here: 85.6 us
  waiting for transfers between devices  38.3 us (44%)
  starting transfers between devices  33.4 us (38%)
  Pallas kernels  11.3 us (13%)
  local copies, waits for them, and re-layouts  1.78 us (2%)
    ppermute x28, waiting for transfers between devices, ring_send(): lax.ppermute(a, 'dp', ring_pairs(chips, step, swap * n))  37.2 us
    ppermute x28, starting transfers between devices, ring_send(): lax.ppermute(a, 'dp', ring_pairs(chips, step, swap * n))  30.6 us
    pallas_call x1, Pallas kernels, ring_body(): call(functools.partial(fresh_kernel, chips, pages_dev, old, rest), [((row...  4.02 us
    pallas_call x1, Pallas kernels, ring_body(): call(functools.partial(cached_kernel, chips, pages_dev, old, first), [((1...  2.2 us
    pallas_call x1, Pallas kernels, ring_body(): call(functools.partial(split_kernel, old), [((rows, half_width // 2), bf)...  2.02 us
    ppermute x1, starting transfers between devices, ring_body(): x_b = lax.ppermute(x_mine, 'mp', mp_pairs)  1.85 us
    unnamed x24, local copies, waits for them, and re-layouts  1.77 us
  transfers between devices with their start and end apart: 36, of which 18 were waited for; matrix products, arithmetic and copies ran while one was open for 0% of the time, Pallas kernels for 6%

profile of v1, /device:TPU:0, one launch (start us, length us, event | category | flops | bytes accessed | tf_op | source)
XLA Modules:
  0.0 85.6 jit_solution(10587523909906270194)
XLA Ops:
  0.7 3.1 %collective-permute-start = (bf16[256,256]{1,0:T(8,128)(2,1)}, bf16[256,256]{1,0:T(8,128)(2,1)S(1)}, u32[]{:S(2)}, u32[]{:S(2)}) collective-permute-start(bf16[256,256]{1,0:T(8,128)(2,1)} %refs_0_.1), channel_id=1, source_target_pairs={{0,8},{2,10},{8,16},{10,18},{16,24},{18,26},{24,28},{26,30},{28,20... | collective-permute-start | bytes 393224 | tf_op jit(solution)/shard_map/ppermute | solution.py:617
  3.7 2.0 %split.1 = (bf16[64,1024]{1,0:T(8,128)(2,1)}, bf16[64,1024]{1,0:T(8,128)(2,1)}, bf16[64,512]{1,0:T(8,128)(2,1)}, bf16[4,128,128]{2,1,0:T(8,128)(2,1)}, bf16[4,128,128]{2,1,0:T(8,128)(2,1)}) custom-call(bf16[64,2048]{1,0:T(8,128)(2,1)} %f_ref.1, bf16[64,1024]{1,0:T(8,128)(2,1)} %q_ref.3, bf16[3,128,256]{2,1,0:T(8,128)(2,1)} %kp_ref.3, bf16[3,128,256]{2,1,0:T(8,128)(2,1)} %vp_ref.3), custom_call_target="tpu_custom_call" | custom-call | tf_op jit(solution)/shard_map/split/pallas_call | solution.py:652
  5.9 2.1 %collective-permute-start.2 = (bf16[256,256]{1,0:T(8,128)(2,1)S(1)}, bf16[256,256]{1,0:T(8,128)(2,1)S(1)}, u32[]{:S(2)}, u32[]{:S(2)}) collective-permute-start(bf16[256,256]{1,0:T(8,128)(2,1)S(1)} %copy-done.6), channel_id=1, source_target_pairs={{0,8},{2,10},{8,16},{10,18},{16,24},{18,26},{24,28},{26,30},{28,20... | collective-permute-start | bytes 393224 | tf_op jit(solution)/shard_map/ppermute | solution.py:617
  8.1 1.8 %collective-permute-start.8 = (bf16[64,1024]{1,0:T(8,128)(2,1)}, bf16[64,1024]{1,0:T(8,128)(2,1)S(1)}, u32[]{:S(2)}, u32[]{:S(2)}) collective-permute-start(bf16[64,1024]{1,0:T(8,128)(2,1)} %get-tuple-element.47.a_ref), channel_id=1, source_target_pairs={{0,1},{1,0},{2,3},{3,2},{4,5},{5,4},{6,7},{7,6},{8,9},{9,8},{10,11... | collective-permute-start | bytes 393224 | tf_op jit(solution)/shard_map/ppermute | solution.py:667
  10.1 1.9 %collective-permute-done.2.refs_10_ = bf16[256,256]{1,0:T(8,128)(2,1)S(1)} collective-permute-done((bf16[256,256]{1,0:T(8,128)(2,1)S(1)}, bf16[256,256]{1,0:T(8,128)(2,1)S(1)}, u32[]{:S(2)}, u32[]{:S(2)}) %collective-permute-start.2) | collective-permute-done | bytes 131104 | tf_op jit(solution)/shard_map/ppermute | solution.py:617
  12.0 1.5 %collective-permute-done.6.refs_9_ = bf16[256,256]{1,0:T(8,128)(2,1)S(1)} collective-permute-done((bf16[256,256]{1,0:T(8,128)(2,1)S(1)}, bf16[256,256]{1,0:T(8,128)(2,1)S(1)}, u32[]{:S(2)}, u32[]{:S(2)}) %collective-permute-start.6) | collective-permute-done | bytes 131104 | tf_op jit(solution)/shard_map/ppermute | solution.py:617
  13.5 1.6 %collective-permute-start.1 = (bf16[256,256]{1,0:T(8,128)(2,1)S(1)}, bf16[256,256]{1,0:T(8,128)(2,1)S(1)}, u32[]{:S(2)}, u32[]{:S(2)}) collective-permute-start(bf16[256,256]{1,0:T(8,128)(2,1)S(1)} %collective-permute-done.refs_2_), channel_id=1, source_target_pairs={{0,8},{2,10},{8,16},{10,18},{16,24},{18,26},{24,28},{26,30},{28,20... | collective-permute-start | bytes 393224 | tf_op jit(solution)/shard_map/ppermute | solution.py:617
  15.5 1.6 %collective-permute-start.3 = (bf16[256,256]{1,0:T(8,128)(2,1)S(1)}, bf16[256,256]{1,0:T(8,128)(2,1)S(1)}, u32[]{:S(2)}, u32[]{:S(2)}) collective-permute-start(bf16[256,256]{1,0:T(8,128)(2,1)S(1)} %collective-permute-done.2.refs_10_), channel_id=1, source_target_pairs={{0,8},{2,10},{8,16},{10,18},{16,24},{18,26},{24,28},{26,30},{28,20... | collective-permute-start | bytes 393224 | tf_op jit(solution)/shard_map/ppermute | solution.py:617
  17.1 1.3 %collective-permute-start.7 = (bf16[256,256]{1,0:T(8,128)(2,1)S(1)}, bf16[256,256]{1,0:T(8,128)(2,1)S(1)}, u32[]{:S(2)}, u32[]{:S(2)}) collective-permute-start(bf16[256,256]{1,0:T(8,128)(2,1)S(1)} %collective-permute-done.6.refs_9_), channel_id=1, source_target_pairs={{0,4},{2,6},{8,0},{10,2},{16,8},{18,10},{24,16},{26,18},{28,24},{3... | collective-permute-start | bytes 393224 | tf_op jit(solution)/shard_map/ppermute | solution.py:617
  18.4 1.3 %collective-permute-done.1.refs_4_ = bf16[256,256]{1,0:T(8,128)(2,1)S(1)} collective-permute-done((bf16[256,256]{1,0:T(8,128)(2,1)S(1)}, bf16[256,256]{1,0:T(8,128)(2,1)S(1)}, u32[]{:S(2)}, u32[]{:S(2)}) %collective-permute-start.1) | collective-permute-done | bytes 131104 | tf_op jit(solution)/shard_map/ppermute | solution.py:617
  21.1 1.8 %collective-permute-done.7.refs_11_ = bf16[256,256]{1,0:T(8,128)(2,1)S(1)} collective-permute-done((bf16[256,256]{1,0:T(8,128)(2,1)S(1)}, bf16[256,256]{1,0:T(8,128)(2,1)S(1)}, u32[]{:S(2)}, u32[]{:S(2)}) %collective-permute-start.7) | collective-permute-done | bytes 131104 | tf_op jit(solution)/shard_map/ppermute | solution.py:617
  22.8 1.6 %collective-permute-start.13 = (bf16[256,256]{1,0:T(8,128)(2,1)S(1)}, bf16[256,256]{1,0:T(8,128)(2,1)S(1)}, u32[]{:S(2)}, u32[]{:S(2)}) collective-permute-start(bf16[256,256]{1,0:T(8,128)(2,1)S(1)} %collective-permute-done.1.refs_4_), channel_id=1, source_target_pairs={{0,8},{2,10},{8,16},{10,18},{16,24},{18,26},{24,28},{26,30},{28,20... | collective-permute-start | bytes 393224 | tf_op jit(solution)/shard_map/ppermute | solution.py:617
  24.4 1.6 %collective-permute-start.14 = (bf16[256,256]{1,0:T(8,128)(2,1)S(1)}, bf16[256,256]{1,0:T(8,128)(2,1)S(1)}, u32[]{:S(2)}, u32[]{:S(2)}) collective-permute-start(bf16[256,256]{1,0:T(8,128)(2,1)S(1)} %collective-permute-done.3.refs_12_), channel_id=1, source_target_pairs={{0,8},{2,10},{8,16},{10,18},{16,24},{18,26},{24,28},{26,30},{28,20... | collective-permute-start | bytes 393224 | tf_op jit(solution)/shard_map/ppermute | solution.py:617
  30.6 1.2 %collective-permute-done.15.refs_5_ = bf16[256,256]{1,0:T(8,128)(2,1)S(1)} collective-permute-done((bf16[256,256]{1,0:T(8,128)(2,1)S(1)}, bf16[256,256]{1,0:T(8,128)(2,1)S(1)}, u32[]{:S(2)}, u32[]{:S(2)}) %collective-permute-start.15) | collective-permute-done | bytes 131104 | tf_op jit(solution)/shard_map/ppermute | solution.py:617
  31.9 1.4 %collective-permute-done.16.refs_13_ = bf16[256,256]{1,0:T(8,128)(2,1)S(1)} collective-permute-done((bf16[256,256]{1,0:T(8,128)(2,1)S(1)}, bf16[256,256]{1,0:T(8,128)(2,1)S(1)}, u32[]{:S(2)}, u32[]{:S(2)}) %collective-permute-start.16) | collective-permute-done | bytes 131104 | tf_op jit(solution)/shard_map/ppermute | solution.py:617
  33.3 1.7 %collective-permute-start.17 = (bf16[256,256]{1,0:T(8,128)(2,1)S(1)}, bf16[256,256]{1,0:T(8,128)(2,1)S(1)}, u32[]{:S(2)}, u32[]{:S(2)}) collective-permute-start(bf16[256,256]{1,0:T(8,128)(2,1)S(1)} %collective-permute-done.13.refs_6_), channel_id=1, source_target_pairs={{0,8},{2,10},{8,16},{10,18},{16,24},{18,26},{24,28},{26,30},{28,20... | collective-permute-start | bytes 393224 | tf_op jit(solution)/shard_map/ppermute | solution.py:617
  35.3 2.9 %collective-permute-done.17.refs_7_ = bf16[256,256]{1,0:T(8,128)(2,1)S(1)} collective-permute-done((bf16[256,256]{1,0:T(8,128)(2,1)S(1)}, bf16[256,256]{1,0:T(8,128)(2,1)S(1)}, u32[]{:S(2)}, u32[]{:S(2)}) %collective-permute-start.17) | collective-permute-done | bytes 131104 | tf_op jit(solution)/shard_map/ppermute | solution.py:617
  38.3 1.7 %collective-permute-done.18.refs_15_ = bf16[256,256]{1,0:T(8,128)(2,1)S(1)} collective-permute-done((bf16[256,256]{1,0:T(8,128)(2,1)S(1)}, bf16[256,256]{1,0:T(8,128)(2,1)S(1)}, u32[]{:S(2)}, u32[]{:S(2)}) %collective-permute-start.18) | collective-permute-done | bytes 131104 | tf_op jit(solution)/shard_map/ppermute | solution.py:617
  40.6 1.6 %collective-permute-start.24 = (bf16[8,128,128]{2,1,0:T(8,128)(2,1)S(1)}, bf16[8,128,128]{2,1,0:T(8,128)(2,1)S(1)}, u32[]{:S(2)}, u32[]{:S(2)}) collective-permute-start(bf16[8,128,128]{2,1,0:T(8,128)(2,1)S(1)} %get-tuple-element.74.refs_0_), channel_id=1, source_target_pairs={{0,8},{2,10},{8,16},{10,18},{16,24},{18,26},{24,28},{26,30},{28,20... | collective-permute-start | bytes 786440 | tf_op jit(solution)/shard_map/ppermute | solution.py:617
  42.8 1.6 %collective-permute-start.25 = (bf16[128,256]{1,0:T(8,128)(2,1)S(1)}, bf16[128,256]{1,0:T(8,128)(2,1)S(1)}, u32[]{:S(2)}, u32[]{:S(2)}) collective-permute-start(bf16[128,256]{1,0:T(8,128)(2,1)S(1)} %rotary.1.refs_3_), channel_id=1, source_target_pairs={{0,8},{2,10},{8,16},{10,18},{16,24},{18,26},{24,28},{26,30},{28,20... | collective-permute-start | bytes 196616 | tf_op jit(solution)/shard_map/ppermute | solution.py:617
  44.8 5.8 %collective-permute-done.25.refs_5_ = bf16[128,256]{1,0:T(8,128)(2,1)S(1)} collective-permute-done((bf16[128,256]{1,0:T(8,128)(2,1)S(1)}, bf16[128,256]{1,0:T(8,128)(2,1)S(1)}, u32[]{:S(2)}, u32[]{:S(2)}) %collective-permute-start.25) | collective-permute-done | bytes 65568 | tf_op jit(solution)/shard_map/ppermute | solution.py:617
  52.4 1.5 %collective-permute-start.27 = (bf16[8,128,128]{2,1,0:T(8,128)(2,1)S(1)}, bf16[8,128,128]{2,1,0:T(8,128)(2,1)S(1)}, u32[]{:S(2)}, u32[]{:S(2)}) collective-permute-start(bf16[8,128,128]{2,1,0:T(8,128)(2,1)S(1)} %collective-permute-done.24.refs_2_), channel_id=1, source_target_pairs={{0,8},{2,10},{8,16},{10,18},{16,24},{18,26},{24,28},{26,30},{28,20... | collective-permute-start | bytes 786440 | tf_op jit(solution)/shard_map/ppermute | solution.py:617
  54.4 1.6 %collective-permute-start.21 = (bf16[128,256]{1,0:T(8,128)(2,1)S(1)}, bf16[128,256]{1,0:T(8,128)(2,1)S(1)}, u32[]{:S(2)}, u32[]{:S(2)}) collective-permute-start(bf16[128,256]{1,0:T(8,128)(2,1)S(1)} %collective-permute-done.20.refs_4_), channel_id=1, source_target_pairs={{0,4},{2,6},{8,0},{10,2},{16,8},{18,10},{24,16},{26,18},{28,24},{3... | collective-permute-start | bytes 196616 | tf_op jit(solution)/shard_map/ppermute | solution.py:617
  56.0 5.1 %collective-permute-done.28.refs_7_ = bf16[128,256]{1,0:T(8,128)(2,1)S(1)} collective-permute-done((bf16[128,256]{1,0:T(8,128)(2,1)S(1)}, bf16[128,256]{1,0:T(8,128)(2,1)S(1)}, u32[]{:S(2)}, u32[]{:S(2)}) %collective-permute-start.28) | collective-permute-done | bytes 65568 | tf_op jit(solution)/shard_map/ppermute | solution.py:617
  61.1 1.6 %collective-permute-start.30 = (bf16[8,128,128]{2,1,0:T(8,128)(2,1)S(1)}, bf16[8,128,128]{2,1,0:T(8,128)(2,1)S(1)}, u32[]{:S(2)}, u32[]{:S(2)}) collective-permute-start(bf16[8,128,128]{2,1,0:T(8,128)(2,1)S(1)} %collective-permute-done.27.refs_4_), channel_id=1, source_target_pairs={{0,8},{2,10},{8,16},{10,18},{16,24},{18,26},{24,28},{26,30},{28,20... | collective-permute-start | bytes 786440 | tf_op jit(solution)/shard_map/ppermute | solution.py:617
  63.2 4.7 %collective-permute-done.30.refs_1_ = bf16[8,128,128]{2,1,0:T(8,128)(2,1)S(1)} collective-permute-done((bf16[8,128,128]{2,1,0:T(8,128)(2,1)S(1)}, bf16[8,128,128]{2,1,0:T(8,128)(2,1)S(1)}, u32[]{:S(2)}, u32[]{:S(2)}) %collective-permute-start.30) | collective-permute-done | bytes 262176 | tf_op jit(solution)/shard_map/ppermute | solution.py:617
  67.9 1.5 %collective-permute-start.31 = (bf16[8,128,128]{2,1,0:T(8,128)(2,1)S(1)}, bf16[8,128,128]{2,1,0:T(8,128)(2,1)S(1)}, u32[]{:S(2)}, u32[]{:S(2)}) collective-permute-start(bf16[8,128,128]{2,1,0:T(8,128)(2,1)S(1)} %collective-permute-done.30.refs_1_), channel_id=1, source_target_pairs={{0,8},{2,10},{8,16},{10,18},{16,24},{18,26},{24,28},{26,30},{28,20... | collective-permute-start | bytes 786440 | tf_op jit(solution)/shard_map/ppermute | solution.py:617
  69.9 1.5 %collective-permute-start.32 = (bf16[128,256]{1,0:T(8,128)(2,1)S(1)}, bf16[128,256]{1,0:T(8,128)(2,1)S(1)}, u32[]{:S(2)}, u32[]{:S(2)}) collective-permute-start(bf16[128,256]{1,0:T(8,128)(2,1)S(1)} %collective-permute-done.28.refs_7_), channel_id=1, source_target_pairs={{0,8},{2,10},{8,16},{10,18},{16,24},{18,26},{24,28},{26,30},{28,20... | collective-permute-start | bytes 196616 | tf_op jit(solution)/shard_map/ppermute | solution.py:617
  71.5 2.2 %attend_cached.1 = (f32[1,512]{1,0:T(1,128)S(1)}, f32[1,512]{1,0:T(1,128)S(1)}, f32[128,512]{1,0:T(8,128)S(1)}) custom-call(s32[3]{0:T(128)S(1)} %copy-done.9, s32[3,25]{1,0:T(4,128)S(1)} %copy-done.8, s32[8,128]{1,0:T(8,128)S(1)} %bitcast.2, bf16[512,128]{1,0:T(8,128)(2,1)S(1)} %get-tuple-element.64.qs_ref, ...), custom_call_target="tpu_custom_call" | custom-call | tf_op jit(solution)/shard_map/attend_cached/pallas_call | solution.py:740
  75.0 3.6 %collective-permute-done.33.refs_10_ = bf16[128,256]{1,0:T(8,128)(2,1)S(1)} collective-permute-done((bf16[128,256]{1,0:T(8,128)(2,1)S(1)}, bf16[128,256]{1,0:T(8,128)(2,1)S(1)}, u32[]{:S(2)}, u32[]{:S(2)}) %collective-permute-start.33) | collective-permute-done | bytes 65568 | tf_op jit(solution)/shard_map/ppermute | solution.py:617
  78.5 4.0 %attend_new.1 = (bf16[64,512]{1,0:T(8,128)(2,1)S(1)}, bf16[64,512]{1,0:T(8,128)(2,1)S(1)}, bf16[3,128,256]{2,1,0:T(8,128)(2,1)S(1)}, bf16[3,128,256]{2,1,0:T(8,128)(2,1)S(1)}, s32[6]{0:T(128)S(1)}) custom-call(s32[3]{0:T(128)S(1)} %copy-done.9, s32[3,25]{1,0:T(4,128)S(1)} %copy-done.8, s32[8,128]{1,0:T(8,128)S(1)} %bitcast.3, ...), custom_call_target="tpu_custom_call" | custom-call | tf_op jit(solution)/shard_map/attend_new/pallas_call | solution.py:751
  84.2 1.5 %join.1 = (bf16[64,1024]{1,0:T(8,128)(2,1)}, bf16[3,128,256]{2,1,0:T(8,128)(2,1)}, bf16[3,128,256]{2,1,0:T(8,128)(2,1)}) custom-call(s32[6]{0:T(128)S(1)} %get-tuple-element.86.info_ref, bf16[64,512]{1,0:T(8,128)(2,1)S(1)} %get-tuple-element.87.attc_ref, bf16[64,512]{1,0:T(8,128)(2,1)S(1)} %collective-permute-done.34.attr_ref, ...), custom_call_target="tpu_custom_call" | custom-call | tf_op jit(solution)/shard_map/join/pallas_call | solution.py:789
  (73 shorter events, 14.9 us)
Async XLA Ops:
  0.7 7.4 %collective-permute-start = (bf16[256,256]{1,0:T(8,128)(2,1)}, bf16[256,256]{1,0:T(8,128)(2,1)S(1)}, u32[]{:S(2)}, u32[]{:S(2)}) collective-permute-start(bf16[256,256]{1,0:T(8,128)(2,1)} %refs_0_.1), channel_id=1, source_target_pairs={{0,8},{2,10},{8,16},{10,18},{16,24},{18,26},{24,28},{26,30},{28,20... | collective-permute-start | bytes 393224 | tf_op jit(solution)/shard_map/ppermute | solution.py:617
  3.7 6.2 %collective-permute-start.4 = (bf16[256,256]{1,0:T(8,128)(2,1)}, bf16[256,256]{1,0:T(8,128)(2,1)S(1)}, u32[]{:S(2)}, u32[]{:S(2)}) collective-permute-start(bf16[256,256]{1,0:T(8,128)(2,1)} %refs_0_.1), channel_id=1, source_target_pairs={{0,4},{2,6},{8,0},{10,2},{16,8},{18,10},{24,16},{26,18},{28,24},{3... | collective-permute-start | bytes 393224 | tf_op jit(solution)/shard_map/ppermute | solution.py:617
  5.9 6.1 %collective-permute-start.2 = (bf16[256,256]{1,0:T(8,128)(2,1)S(1)}, bf16[256,256]{1,0:T(8,128)(2,1)S(1)}, u32[]{:S(2)}, u32[]{:S(2)}) collective-permute-start(bf16[256,256]{1,0:T(8,128)(2,1)S(1)} %copy-done.6), channel_id=1, source_target_pairs={{0,8},{2,10},{8,16},{10,18},{16,24},{18,26},{24,28},{26,30},{28,20... | collective-permute-start | bytes 393224 | tf_op jit(solution)/shard_map/ppermute | solution.py:617
  7.9 5.6 %collective-permute-start.6 = (bf16[256,256]{1,0:T(8,128)(2,1)S(1)}, bf16[256,256]{1,0:T(8,128)(2,1)S(1)}, u32[]{:S(2)}, u32[]{:S(2)}) collective-permute-start(bf16[256,256]{1,0:T(8,128)(2,1)S(1)} %copy-done.6), channel_id=1, source_target_pairs={{0,4},{2,6},{8,0},{10,2},{16,8},{18,10},{24,16},{26,18},{28,24},{3... | collective-permute-start | bytes 393224 | tf_op jit(solution)/shard_map/ppermute | solution.py:617
  8.0 7.1 %collective-permute-start.12 = (bf16[4,128,128]{2,1,0:T(8,128)(2,1)}, bf16[4,128,128]{2,1,0:T(8,128)(2,1)S(1)}, u32[]{:S(2)}, u32[]{:S(2)}) collective-permute-start(bf16[4,128,128]{2,1,0:T(8,128)(2,1)} %get-tuple-element.50), channel_id=1, source_target_pairs={{0,2},{2,0},{4,6},{6,4},{8,10},{10,8},{12,14},{14,12},{16,18},{18,... | collective-permute-start | bytes 393224 | tf_op jit(solution)/shard_map/ppermute | solution.py:671
  8.1 7.4 %collective-permute-start.8 = (bf16[64,1024]{1,0:T(8,128)(2,1)}, bf16[64,1024]{1,0:T(8,128)(2,1)S(1)}, u32[]{:S(2)}, u32[]{:S(2)}) collective-permute-start(bf16[64,1024]{1,0:T(8,128)(2,1)} %get-tuple-element.47.a_ref), channel_id=1, source_target_pairs={{0,1},{1,0},{2,3},{3,2},{4,5},{5,4},{6,7},{7,6},{8,9},{9,8},{10,11... | collective-permute-start | bytes 393224 | tf_op jit(solution)/shard_map/ppermute | solution.py:667
  9.9 7.2 %collective-permute-start.10 = (bf16[64,1024]{1,0:T(8,128)(2,1)}, bf16[64,1024]{1,0:T(8,128)(2,1)S(1)}, u32[]{:S(2)}, u32[]{:S(2)}) collective-permute-start(bf16[64,1024]{1,0:T(8,128)(2,1)} %get-tuple-element.48), channel_id=1, source_target_pairs={{0,3},{1,2},{2,1},{3,0},{4,7},{5,6},{6,5},{7,4},{8,11},{9,10},{10,... | collective-permute-start | bytes 393224 | tf_op jit(solution)/shard_map/ppermute | solution.py:669
  12.0 6.4 %collective-permute-start.9 = (bf16[64,1024]{1,0:T(8,128)(2,1)}, bf16[64,1024]{1,0:T(8,128)(2,1)S(1)}, u32[]{:S(2)}, u32[]{:S(2)}) collective-permute-start(bf16[64,1024]{1,0:T(8,128)(2,1)} %get-tuple-element.48), channel_id=1, source_target_pairs={{0,2},{2,0},{4,6},{6,4},{8,10},{10,8},{12,14},{14,12},{16,18},{18,... | collective-permute-start | bytes 393224 | tf_op jit(solution)/shard_map/ppermute | solution.py:668
  13.5 6.2 %collective-permute-start.1 = (bf16[256,256]{1,0:T(8,128)(2,1)S(1)}, bf16[256,256]{1,0:T(8,128)(2,1)S(1)}, u32[]{:S(2)}, u32[]{:S(2)}) collective-permute-start(bf16[256,256]{1,0:T(8,128)(2,1)S(1)} %collective-permute-done.refs_2_), channel_id=1, source_target_pairs={{0,8},{2,10},{8,16},{10,18},{16,24},{18,26},{24,28},{26,30},{28,20... | collective-permute-start | bytes 393224 | tf_op jit(solution)/shard_map/ppermute | solution.py:617
  15.1 5.1 %collective-permute-start.5 = (bf16[256,256]{1,0:T(8,128)(2,1)S(1)}, bf16[256,256]{1,0:T(8,128)(2,1)S(1)}, u32[]{:S(2)}, u32[]{:S(2)}) collective-permute-start(bf16[256,256]{1,0:T(8,128)(2,1)S(1)} %collective-permute-done.4.refs_1_), channel_id=1, source_target_pairs={{0,4},{2,6},{8,0},{10,2},{16,8},{18,10},{24,16},{26,18},{28,24},{3... | collective-permute-start | bytes 393224 | tf_op jit(solution)/shard_map/ppermute | solution.py:617
  15.5 5.6 %collective-permute-start.3 = (bf16[256,256]{1,0:T(8,128)(2,1)S(1)}, bf16[256,256]{1,0:T(8,128)(2,1)S(1)}, u32[]{:S(2)}, u32[]{:S(2)}) collective-permute-start(bf16[256,256]{1,0:T(8,128)(2,1)S(1)} %collective-permute-done.2.refs_10_), channel_id=1, source_target_pairs={{0,8},{2,10},{8,16},{10,18},{16,24},{18,26},{24,28},{26,30},{28,20... | collective-permute-start | bytes 393224 | tf_op jit(solution)/shard_map/ppermute | solution.py:617
  17.1 5.7 %collective-permute-start.7 = (bf16[256,256]{1,0:T(8,128)(2,1)S(1)}, bf16[256,256]{1,0:T(8,128)(2,1)S(1)}, u32[]{:S(2)}, u32[]{:S(2)}) collective-permute-start(bf16[256,256]{1,0:T(8,128)(2,1)S(1)} %collective-permute-done.6.refs_9_), channel_id=1, source_target_pairs={{0,4},{2,6},{8,0},{10,2},{16,8},{18,10},{24,16},{26,18},{28,24},{3... | collective-permute-start | bytes 393224 | tf_op jit(solution)/shard_map/ppermute | solution.py:617
  22.8 6.9 %collective-permute-start.13 = (bf16[256,256]{1,0:T(8,128)(2,1)S(1)}, bf16[256,256]{1,0:T(8,128)(2,1)S(1)}, u32[]{:S(2)}, u32[]{:S(2)}) collective-permute-start(bf16[256,256]{1,0:T(8,128)(2,1)S(1)} %collective-permute-done.1.refs_4_), channel_id=1, source_target_pairs={{0,8},{2,10},{8,16},{10,18},{16,24},{18,26},{24,28},{26,30},{28,20... | collective-permute-start | bytes 393224 | tf_op jit(solution)/shard_map/ppermute | solution.py:617
  24.4 6.2 %collective-permute-start.14 = (bf16[256,256]{1,0:T(8,128)(2,1)S(1)}, bf16[256,256]{1,0:T(8,128)(2,1)S(1)}, u32[]{:S(2)}, u32[]{:S(2)}) collective-permute-start(bf16[256,256]{1,0:T(8,128)(2,1)S(1)} %collective-permute-done.3.refs_12_), channel_id=1, source_target_pairs={{0,8},{2,10},{8,16},{10,18},{16,24},{18,26},{24,28},{26,30},{28,20... | collective-permute-start | bytes 393224 | tf_op jit(solution)/shard_map/ppermute | solution.py:617
  26.0 5.9 %collective-permute-start.15 = (bf16[256,256]{1,0:T(8,128)(2,1)S(1)}, bf16[256,256]{1,0:T(8,128)(2,1)S(1)}, u32[]{:S(2)}, u32[]{:S(2)}) collective-permute-start(bf16[256,256]{1,0:T(8,128)(2,1)S(1)} %collective-permute-done.5.refs_3_), channel_id=1, source_target_pairs={{0,4},{2,6},{8,0},{10,2},{16,8},{18,10},{24,16},{26,18},{28,24},{3... | collective-permute-start | bytes 393224 | tf_op jit(solution)/shard_map/ppermute | solution.py:617
  26.4 6.8 %collective-permute-start.16 = (bf16[256,256]{1,0:T(8,128)(2,1)S(1)}, bf16[256,256]{1,0:T(8,128)(2,1)S(1)}, u32[]{:S(2)}, u32[]{:S(2)}) collective-permute-start(bf16[256,256]{1,0:T(8,128)(2,1)S(1)} %collective-permute-done.7.refs_11_), channel_id=1, source_target_pairs={{0,4},{2,6},{8,0},{10,2},{16,8},{18,10},{24,16},{26,18},{28,24},{3... | collective-permute-start | bytes 393224 | tf_op jit(solution)/shard_map/ppermute | solution.py:617
  33.3 5.0 %collective-permute-start.17 = (bf16[256,256]{1,0:T(8,128)(2,1)S(1)}, bf16[256,256]{1,0:T(8,128)(2,1)S(1)}, u32[]{:S(2)}, u32[]{:S(2)}) collective-permute-start(bf16[256,256]{1,0:T(8,128)(2,1)S(1)} %collective-permute-done.13.refs_6_), channel_id=1, source_target_pairs={{0,8},{2,10},{8,16},{10,18},{16,24},{18,26},{24,28},{26,30},{28,20... | collective-permute-start | bytes 393224 | tf_op jit(solution)/shard_map/ppermute | solution.py:617
  35.0 5.0 %collective-permute-start.18 = (bf16[256,256]{1,0:T(8,128)(2,1)S(1)}, bf16[256,256]{1,0:T(8,128)(2,1)S(1)}, u32[]{:S(2)}, u32[]{:S(2)}) collective-permute-start(bf16[256,256]{1,0:T(8,128)(2,1)S(1)} %collective-permute-done.16.refs_13_), channel_id=1, source_target_pairs={{0,4},{2,6},{8,0},{10,2},{16,8},{18,10},{24,16},{26,18},{28,24},{3... | collective-permute-start | bytes 393224 | tf_op jit(solution)/shard_map/ppermute | solution.py:617
  40.6 11.4 %collective-permute-start.24 = (bf16[8,128,128]{2,1,0:T(8,128)(2,1)S(1)}, bf16[8,128,128]{2,1,0:T(8,128)(2,1)S(1)}, u32[]{:S(2)}, u32[]{:S(2)}) collective-permute-start(bf16[8,128,128]{2,1,0:T(8,128)(2,1)S(1)} %get-tuple-element.74.refs_0_), channel_id=1, source_target_pairs={{0,8},{2,10},{8,16},{10,18},{16,24},{18,26},{24,28},{26,30},{28,20... | collective-permute-start | bytes 786440 | tf_op jit(solution)/shard_map/ppermute | solution.py:617
  42.1 9.8 %collective-permute-start.23 = (bf16[8,128,128]{2,1,0:T(8,128)(2,1)S(1)}, bf16[8,128,128]{2,1,0:T(8,128)(2,1)S(1)}, u32[]{:S(2)}, u32[]{:S(2)}) collective-permute-start(bf16[8,128,128]{2,1,0:T(8,128)(2,1)S(1)} %get-tuple-element.74.refs_0_), channel_id=1, source_target_pairs={{0,4},{2,6},{8,0},{10,2},{16,8},{18,10},{24,16},{26,18},{28,24},{3... | collective-permute-start | bytes 786440 | tf_op jit(solution)/shard_map/ppermute | solution.py:617
  42.8 7.9 %collective-permute-start.25 = (bf16[128,256]{1,0:T(8,128)(2,1)S(1)}, bf16[128,256]{1,0:T(8,128)(2,1)S(1)}, u32[]{:S(2)}, u32[]{:S(2)}) collective-permute-start(bf16[128,256]{1,0:T(8,128)(2,1)S(1)} %rotary.1.refs_3_), channel_id=1, source_target_pairs={{0,8},{2,10},{8,16},{10,18},{16,24},{18,26},{24,28},{26,30},{28,20... | collective-permute-start | bytes 196616 | tf_op jit(solution)/shard_map/ppermute | solution.py:617
  44.3 7.6 %collective-permute-start.20 = (bf16[128,256]{1,0:T(8,128)(2,1)S(1)}, bf16[128,256]{1,0:T(8,128)(2,1)S(1)}, u32[]{:S(2)}, u32[]{:S(2)}) collective-permute-start(bf16[128,256]{1,0:T(8,128)(2,1)S(1)} %rotary.1.refs_3_), channel_id=1, source_target_pairs={{0,4},{2,6},{8,0},{10,2},{16,8},{18,10},{24,16},{26,18},{28,24},{3... | collective-permute-start | bytes 196616 | tf_op jit(solution)/shard_map/ppermute | solution.py:617
  51.9 9.2 %collective-permute-start.26 = (bf16[8,128,128]{2,1,0:T(8,128)(2,1)S(1)}, bf16[8,128,128]{2,1,0:T(8,128)(2,1)S(1)}, u32[]{:S(2)}, u32[]{:S(2)}) collective-permute-start(bf16[8,128,128]{2,1,0:T(8,128)(2,1)S(1)} %collective-permute-done.23.refs_1_), channel_id=1, source_target_pairs={{0,4},{2,6},{8,0},{10,2},{16,8},{18,10},{24,16},{26,18},{28,24},{3... | collective-permute-start | bytes 786440 | tf_op jit(solution)/shard_map/ppermute | solution.py:617
  52.4 8.7 %collective-permute-start.27 = (bf16[8,128,128]{2,1,0:T(8,128)(2,1)S(1)}, bf16[8,128,128]{2,1,0:T(8,128)(2,1)S(1)}, u32[]{:S(2)}, u32[]{:S(2)}) collective-permute-start(bf16[8,128,128]{2,1,0:T(8,128)(2,1)S(1)} %collective-permute-done.24.refs_2_), channel_id=1, source_target_pairs={{0,8},{2,10},{8,16},{10,18},{16,24},{18,26},{24,28},{26,30},{28,20... | collective-permute-start | bytes 786440 | tf_op jit(solution)/shard_map/ppermute | solution.py:617
  54.0 7.2 %collective-permute-start.28 = (bf16[128,256]{1,0:T(8,128)(2,1)S(1)}, bf16[128,256]{1,0:T(8,128)(2,1)S(1)}, u32[]{:S(2)}, u32[]{:S(2)}) collective-permute-start(bf16[128,256]{1,0:T(8,128)(2,1)S(1)} %collective-permute-done.25.refs_5_), channel_id=1, source_target_pairs={{0,8},{2,10},{8,16},{10,18},{16,24},{18,26},{24,28},{26,30},{28,20... | collective-permute-start | bytes 196616 | tf_op jit(solution)/shard_map/ppermute | solution.py:617
  54.4 6.7 %collective-permute-start.21 = (bf16[128,256]{1,0:T(8,128)(2,1)S(1)}, bf16[128,256]{1,0:T(8,128)(2,1)S(1)}, u32[]{:S(2)}, u32[]{:S(2)}) collective-permute-start(bf16[128,256]{1,0:T(8,128)(2,1)S(1)} %collective-permute-done.20.refs_4_), channel_id=1, source_target_pairs={{0,4},{2,6},{8,0},{10,2},{16,8},{18,10},{24,16},{26,18},{28,24},{3... | collective-permute-start | bytes 196616 | tf_op jit(solution)/shard_map/ppermute | solution.py:617
  61.1 6.8 %collective-permute-start.30 = (bf16[8,128,128]{2,1,0:T(8,128)(2,1)S(1)}, bf16[8,128,128]{2,1,0:T(8,128)(2,1)S(1)}, u32[]{:S(2)}, u32[]{:S(2)}) collective-permute-start(bf16[8,128,128]{2,1,0:T(8,128)(2,1)S(1)} %collective-permute-done.27.refs_4_), channel_id=1, source_target_pairs={{0,8},{2,10},{8,16},{10,18},{16,24},{18,26},{24,28},{26,30},{28,20... | collective-permute-start | bytes 786440 | tf_op jit(solution)/shard_map/ppermute | solution.py:617
  62.7 15.8 %collective-permute-start.29 = (bf16[8,128,128]{2,1,0:T(8,128)(2,1)S(1)}, bf16[8,128,128]{2,1,0:T(8,128)(2,1)S(1)}, u32[]{:S(2)}, u32[]{:S(2)}) collective-permute-start(bf16[8,128,128]{2,1,0:T(8,128)(2,1)S(1)} %collective-permute-done.26.refs_3_), channel_id=1, source_target_pairs={{0,4},{2,6},{8,0},{10,2},{16,8},{18,10},{24,16},{26,18},{28,24},{3... | collective-permute-start | bytes 786440 | tf_op jit(solution)/shard_map/ppermute | solution.py:617
  67.9 10.7 %collective-permute-start.31 = (bf16[8,128,128]{2,1,0:T(8,128)(2,1)S(1)}, bf16[8,128,128]{2,1,0:T(8,128)(2,1)S(1)}, u32[]{:S(2)}, u32[]{:S(2)}) collective-permute-start(bf16[8,128,128]{2,1,0:T(8,128)(2,1)S(1)} %collective-permute-done.30.refs_1_), channel_id=1, source_target_pairs={{0,8},{2,10},{8,16},{10,18},{16,24},{18,26},{24,28},{26,30},{28,20... | collective-permute-start | bytes 786440 | tf_op jit(solution)/shard_map/ppermute | solution.py:617
  69.4 4.3 %collective-permute-start.22 = (bf16[128,256]{1,0:T(8,128)(2,1)S(1)}, bf16[128,256]{1,0:T(8,128)(2,1)S(1)}, u32[]{:S(2)}, u32[]{:S(2)}) collective-permute-start(bf16[128,256]{1,0:T(8,128)(2,1)S(1)} %collective-permute-done.21.refs_6_), channel_id=1, source_target_pairs={{0,4},{2,6},{8,0},{10,2},{16,8},{18,10},{24,16},{26,18},{28,24},{3... | collective-permute-start | bytes 196616 | tf_op jit(solution)/shard_map/ppermute | solution.py:617
  69.9 5.0 %collective-permute-start.32 = (bf16[128,256]{1,0:T(8,128)(2,1)S(1)}, bf16[128,256]{1,0:T(8,128)(2,1)S(1)}, u32[]{:S(2)}, u32[]{:S(2)}) collective-permute-start(bf16[128,256]{1,0:T(8,128)(2,1)S(1)} %collective-permute-done.28.refs_7_), channel_id=1, source_target_pairs={{0,8},{2,10},{8,16},{10,18},{16,24},{18,26},{24,28},{26,30},{28,20... | collective-permute-start | bytes 196616 | tf_op jit(solution)/shard_map/ppermute | solution.py:617
  73.7 4.8 %collective-permute-start.33 = (bf16[128,256]{1,0:T(8,128)(2,1)S(1)}, bf16[128,256]{1,0:T(8,128)(2,1)S(1)}, u32[]{:S(2)}, u32[]{:S(2)}) collective-permute-start(bf16[128,256]{1,0:T(8,128)(2,1)S(1)} %collective-permute-done.22.refs_8_), channel_id=1, source_target_pairs={{0,4},{2,6},{8,0},{10,2},{16,8},{18,10},{24,16},{26,18},{28,24},{3... | collective-permute-start | bytes 196616 | tf_op jit(solution)/shard_map/ppermute | solution.py:617
  (16 other events, 127.6 us)

commit v2 on v1

--- a/solution.py
+++ b/solution.py
@@ -287,11 +287,8 @@
         c.wait()
 
 
-def merge_kernel(kvm_ref, kvg_ref, q_ref, qg_ref, kv_ref, qs_ref):
+def merge_kernel(q_ref, qg_ref, qs_ref):
     core = lax.axis_index("dp") % 2
-    count = kvm_ref.shape[0]
-    kv_ref[:count] = kvm_ref[...]
-    kv_ref[count:] = kvg_ref[...]
     rows, group = q_ref.shape[0], qg_ref.shape[1] // HD
     for h in range(group):
         mine = pl.ds(pl.multiple_of((2 * h + core) * rows, rows), rows)
@@ -377,114 +374,103 @@
     )
 
 
-def cached_part(
-    chips, pages_dev, old, offsets, blocks, starts, reqs, lens_ref, table_ref, qs_ref, kbuf, vbuf, slot_of, state
-):
+def three_parts(x):
+    first = x.astype(jnp.bfloat16).astype(jnp.float32)
+    second = (x - first).astype(jnp.bfloat16).astype(jnp.float32)
+    return jnp.concatenate([first, second, x - first - second], axis=0)
+
+
+def cached_kernel(chips, pages_dev, old, away, lens_ref, table_ref, tr_ref, qs_ref, *refs):
+    members = chips // 2
+    near, far = refs[:members], refs[members : 2 * members]
+    outs, (kbuf, vbuf, m_ref, l_ref, acc_ref, slot_of) = refs[2 * members : -6], refs[-6:]
     dp = lax.axis_index("dp")
     chip, core = dp // 2, dp % 2
-    place = ring_place(chip, chips)
+    who = chip ^ away
     requests = lens_ref.shape[0]
     width = qs_ref.shape[0]
-    toks = starts[-1] // chips
+    toks = tr_ref.shape[0] * tr_ref.shape[1] // chips
+    starts = request_starts(tr_ref, requests)
+    first_req, last_req = chip_requests(who, toks, starts)
 
     def clear(i, carry):
         slot_of[i] = -1
         return carry
-
-    def held(page):
-        distance = (ring_place(page // (2 * pages_dev), chips) - place + chips) % chips
-        found = distance == offsets[0] % chips
-        for o in offsets[1:]:
-            found = found | (distance == o % chips)
-        return found
 
     lax.fori_loop(0, slot_of.shape[0], clear, 0)
     base = jnp.int32(0)
     lows, highs = [], []
     for r in range(requests):
         length = lens_ref[r]
-        pages = (length + PAGE - 1) // PAGE
-        count = jnp.where((r >= reqs[0]) & (r <= reqs[1]), pages, 0)
-
-        def put(l, at, r=r):
+        relevant = (r >= first_req) & (r <= last_req)
+        count = jnp.where(relevant, (length + PAGE - 1) // PAGE, 0)
+
+        def place(l, at, r=r):
             page = table_ref[r, l]
-            here = held(page)
-
-            @pl.when(here)
+            held = page // (2 * pages_dev * members) == chip // members
+
+            @pl.when(held)
             def _():
                 slot_of[page] = at
 
-            return at + here.astype(jnp.int32)
-
-        end = lax.fori_loop(0, count, put, base)
-        last_here = (end > base) & held(table_ref[r, pages - 1])
+            return at + held.astype(jnp.int32)
+
+        end = lax.fori_loop(0, count, place, base)
+        last_page = table_ref[r, (length + PAGE - 1) // PAGE - 1]
+        cut = jnp.where(
+            (end > base) & (last_page // (2 * pages_dev * members) == chip // members),
+            (length + PAGE - 1) // PAGE * PAGE - length,
+            0,
+        )
         lows.append(base * PAGE)
-        highs.append(end * PAGE - jnp.where(last_here, pages * PAGE - length, 0))
+        highs.append(end * PAGE - cut)
         base = end
 
-    for offset, block in zip(offsets, blocks):
-        source = ring_chip(place + offset + chips, chips)
-        for part, owner in ((0, 2 * source + core), (2 * old, 2 * source + 1 - core)):
+    for e in range(members):
+        source = chip ^ e
+        for block, owner in ((near[e], 2 * source + core), (far[e], 2 * source + 1 - core)):
             for s in range(old):
                 slot = slot_of[owner * pages_dev + s]
 
                 @pl.when(slot >= 0)
-                def _(block=block, part=part, s=s, slot=slot):
+                def _(block=block, s=s, slot=slot):
                     at = pl.ds(pl.multiple_of(slot * PAGE, PAGE), PAGE)
-                    kbuf[at, :] = block[part + s]
-                    vbuf[at, :] = block[part + old + s]
-
-    size = STEP_PAGES * PAGE
-    pad = pl.ds(pl.multiple_of(base * PAGE, PAGE), size - PAGE)
-    kbuf[pad, :] = jnp.zeros((size - PAGE, HD), kbuf.dtype)
-    vbuf[pad, :] = jnp.zeros((size - PAGE, HD), vbuf.dtype)
-    tokens = chip * toks + lax.broadcasted_iota(jnp.int32, (1, width), 1) % toks
+                    kbuf[at, :] = block[s]
+                    vbuf[at, :] = block[old + s]
+
+    step_pages = STEP_PAGES
+    pad = pl.ds(pl.multiple_of(base * PAGE, PAGE), (step_pages - 1) * PAGE)
+    kbuf[pad, :] = jnp.zeros(((step_pages - 1) * PAGE, HD), kbuf.dtype)
+    vbuf[pad, :] = jnp.zeros(((step_pages - 1) * PAGE, HD), vbuf.dtype)
+    tokens = who * toks + lax.broadcasted_iota(jnp.int32, (1, width), 1) % toks
     low = pick(starts, lows, tokens)
     high = pick(starts, highs, tokens)
-
-    def step(i, carry):
-        at = pl.ds(pl.multiple_of(i * size, size), size)
-        attend_block(qs_ref, kbuf[at, :], vbuf[at, :], i * size, low, high, *state)
-        return carry
-
-    lax.fori_loop(0, (base + STEP_PAGES - 1) // STEP_PAGES, step, 0)
-
-
-def cached_kernel(chips, pages_dev, old, offsets, lens_ref, table_ref, tr_ref, qs_ref, *refs):
-    blocks = refs[: len(offsets)]
-    m_ref, l_ref, acc_ref, kbuf, vbuf, slot_of = refs[len(offsets) :]
-    chip = lax.axis_index("dp") // 2
-    starts = request_starts(tr_ref, lens_ref.shape[0])
-    reqs = chip_requests(chip, starts[-1] // chips, starts)
     m_ref[...] = jnp.full(m_ref.shape, NEG_START, jnp.float32)
     l_ref[...] = jnp.zeros(l_ref.shape, jnp.float32)
     acc_ref[...] = jnp.zeros(acc_ref.shape, jnp.float32)
-    cached_part(
-        chips,
-        pages_dev,
-        old,
-        offsets,
-        blocks,
-        starts,
-        reqs,
-        lens_ref,
-        table_ref,
-        qs_ref,
-        kbuf,
-        vbuf,
-        slot_of,
-        (m_ref, l_ref, acc_ref),
-    )
+
+    def step(i, carry):
+        size = step_pages * PAGE
+        at = pl.ds(pl.multiple_of(i * size, size), size)
+        attend_block(qs_ref, kbuf[at, :], vbuf[at, :], i * size, low, high, m_ref, l_ref, acc_ref)
+        return carry
+
+    lax.fori_loop(0, (base + step_pages - 1) // step_pages, step, 0)
+    if away:
+        outs[0][:HD, :] = acc_ref[...].astype(jnp.bfloat16)
+        outs[0][HD:, :] = jnp.concatenate(
+            [three_parts(m_ref[...]), three_parts(l_ref[...]), jnp.zeros((10, width), jnp.float32)], axis=0
+        ).astype(jnp.bfloat16)
+    else:
+        outs[0][...], outs[1][...], outs[2][...] = m_ref[...], l_ref[...], acc_ref[...]
 
 
 def fresh_kernel(
-    chips, pages_dev, old, offsets, lens_ref, table_ref, tr_ref, qs_ref, m0_ref, l0_ref, acc0_ref, *refs
+    chips, pages_dev, lens_ref, table_ref, tr_ref, qs_ref, m0_ref, l0_ref, acc0_ref, back_ref, *refs
 ):
-    blocks, fresh = refs[: len(offsets)], refs[len(offsets) : len(offsets) + chips]
-    atto_ref, attc_ref, no_ref, nc_ref, info_ref = refs[len(offsets) + chips : len(offsets) + chips + 5]
-    (kbuf, vbuf, nbuf, m_ref, l_ref, acc_ref, out_ref, slot_of, new_at, new_lo, new_hi) = refs[
-        len(offsets) + chips + 5 :
-    ]
+    fresh = refs[:chips]
+    atto_ref, attc_ref, no_ref, nc_ref, info_ref = refs[chips : chips + 5]
+    nbuf, m_ref, l_ref, acc_ref, out_ref, new_at, new_lo, new_hi = refs[chips + 5 :]
     dp = lax.axis_index("dp")
     chip, core = dp // 2, dp % 2
     place = ring_place(chip, chips)
@@ -496,25 +482,13 @@
     starts = request_starts(tr_ref, requests)
     reqs = chip_requests(chip, toks, starts)
     first_req = reqs[0]
-    m_ref[...] = m0_ref[...]
-    l_ref[...] = l0_ref[...]
-    acc_ref[...] = acc0_ref[...]
-    cached_part(
-        chips,
-        pages_dev,
-        old,
-        offsets,
-        blocks,
-        starts,
-        reqs,
-        lens_ref,
-        table_ref,
-        qs_ref,
-        kbuf,
-        vbuf,
-        slot_of,
-        (m_ref, l_ref, acc_ref),
-    )
+    parts = back_ref[HD : HD + 6, :].astype(jnp.float32)
+    m0, m1 = m0_ref[...], parts[0:1] + parts[1:2] + parts[2:3]
+    top = jnp.maximum(m0, m1)
+    f0, f1 = jnp.exp2(m0 - top), jnp.exp2(m1 - top)
+    m_ref[...] = top
+    l_ref[...] = l0_ref[...] * f0 + (parts[3:4] + parts[4:5] + parts[5:6]) * f1
+    acc_ref[...] = acc0_ref[...] * f0 + back_ref[:HD, :].astype(jnp.float32) * f1
 
     def clear(i, carry):
         new_lo[i] = 0
@@ -646,6 +620,9 @@
     both_pairs = [(2 * i + j, 2 * (i ^ 1) + (1 - j)) for i in range(dp_count) for j in range(2)]
     requests_tile = token_request.reshape(-1, 128)
 
+    def exchange(array, e, swap=0):
+        return lax.ppermute(array, "dp", [(i, i ^ (2 * e) ^ swap) for i in range(dp_count)])
+
     w_got = {0: [w_key, w_value]}
     right, left = ring_send(chips, [w_key, w_value], 1), ring_send(chips, [w_key, w_value], -1)
     w_got[-1], w_got[1] = right, left
@@ -669,20 +646,21 @@
     x_d = lax.ppermute(x_other, ("dp", "mp"), both_pairs)
     q_got = lax.ppermute(q_other, "dp", core_pairs)
     kv_got = lax.ppermute(kv_other, "dp", core_pairs)
-    early = (x_b, x_c, x_d, q_got, kv_got)
+    z_near, z_far = exchange(kv_mine, 2), exchange(kv_other, 2, 1)
+    y_near, y_far = exchange(kv_mine, 1), exchange(kv_other, 1, 1)
     for d in range(2, chips // 2):
         if d == chips // 2 - 1:
-            right, left, early = lax.optimization_barrier((right, left, early))
-            x_b, x_c, x_d, q_got, kv_got = early
+            w_first, z_near, z_far, y_near, y_far, q_got = lax.optimization_barrier(
+                (right[0], z_near, z_far, y_near, y_far, q_got)
+            )
+            right = [w_first, right[1]]
         right, left = ring_send(chips, right, 1), ring_send(chips, left, -1)
         w_got[-d], w_got[d] = right, left
-
-    kv, q_rows = call(
-        merge_kernel,
-        [((4 * old, PAGE, HD), bf), ((columns, HD), bf)],
-        ins=4,
-        name="merge",
-    )(kv_mine, kv_got, queries, q_got)
+    near = [kv_mine, y_near, z_near, exchange(y_near, 2)]
+    far = [kv_got, y_far, z_far, exchange(z_far, 1)]
+
+    (q_rows,) = call(merge_kernel, [((columns, HD), bf)], ins=2, name="merge")(queries, q_got)
+    q_away = exchange(q_rows, chips // 2)
     inverse = (THETA ** (-(np.arange(HD) % (HD // 2)) * 2.0 / HD)).astype(np.float32)[None, :]
     scaled, squares, cosine, sine = call(
         functools.partial(scale_kernel, chips),
@@ -700,8 +678,8 @@
         x_c,
         x_d,
     )
-    right, left, scaled, kv, q_rows = lax.optimization_barrier((right, left, scaled, kv, q_rows))
     w_got[chips // 2] = ring_send(chips, right[:1], 1) + ring_send(chips, left[1:], -1)
+    scaled, near[3], far[3], q_away = lax.optimization_barrier((scaled, near[3], far[3], q_away))
     part_send, part_keep = call(
         functools.partial(project_kernel, chips),
         [((toks, 3 * HD), f32), ((toks, 3 * HD), f32)],
@@ -711,9 +689,6 @@
     )(scaled, squares, *[w_got[o][0] for o in offsets], *[w_got[o][1] for o in offsets])
     part_got = lax.ppermute(part_send, "dp", core_pairs)
 
-    kv_late, _ = lax.optimization_barrier((kv, part_send))
-    kv_got = {0: kv}
-    kv_got[-1], kv_got[1] = ring_send(chips, [kv_late], 1)[0], ring_send(chips, [kv_late], -1)[0]
     (fresh,) = call(
         functools.partial(rotate_kernel, width),
         [((toks, 2 * HD), bf)],
@@ -722,34 +697,40 @@
     )(part_keep, part_got, cosine, sine)
     new = {0: fresh}
     new[-1], new[1] = ring_send(chips, [fresh], 1)[0], ring_send(chips, [fresh], -1)[0]
+    slots = dp_count // 2 * old + STEP_PAGES
+    table = pltpu.SMEM((dp_count * pages_dev,), i32)
+
+    def cached(q, away, outs, name):
+        return call(
+            functools.partial(cached_kernel, chips, pages_dev, old, away),
+            outs,
+            scratch=[
+                pltpu.VMEM((slots * PAGE, HD), bf),
+                pltpu.VMEM((slots * PAGE, HD), bf),
+                pltpu.VMEM((1, columns), f32),
+                pltpu.VMEM((1, columns), f32),
+                pltpu.VMEM((HD, columns), f32),
+                table,
+            ],
+            ins=4 + chips,
+            smem=(0, 1),
+            name=name,
+        )(cache_lens, page_table, requests_tile, q, *near, *far)
+
+    (away,) = cached(q_away, chips // 2, [((HD + 16, columns), bf)], "attend_cached_away")
+    here = cached(
+        q_rows, 0, [((1, columns), f32), ((1, columns), f32), ((HD, columns), f32)], "attend_cached_here"
+    )
+    beside = {2: away, 3: here}
     for d in range(2, chips // 2):
-        right, left, _ = lax.optimization_barrier((kv_got[1 - d], kv_got[d - 1], (new[1 - d], new[d - 1])))
-        new[-d], new[d] = ring_send(chips, [new[1 - d]], 1)[0], ring_send(chips, [new[d - 1]], -1)[0]
-        kv_got[-d], kv_got[d] = ring_send(chips, [right], 1)[0], ring_send(chips, [left], -1)[0]
-    last = chips // 2
-    (kv_got[last],) = ring_send(chips, [kv_got[1 - last]], 1)
-
-    first = [o for o in offsets if abs(o) <= last - 2]
-    rest = [o for o in offsets if abs(o) > last - 2]
-
-    def buffers(count):
-        slots = 2 * old * count + STEP_PAGES
-        return [pltpu.VMEM((slots * PAGE, HD), bf)] * 2
-
-    table = pltpu.SMEM((dp_count * pages_dev,), i32)
-    top, total, acc = call(
-        functools.partial(cached_kernel, chips, pages_dev, old, first),
-        [((1, columns), f32), ((1, columns), f32), ((HD, columns), f32)],
-        scratch=[*buffers(len(first)), table],
-        ins=4 + len(first),
-        smem=(0, 1),
-        name="attend_cached",
-    )(cache_lens, page_table, requests_tile, q_rows, *[kv_got[o] for o in first])
-    before, top, total, acc = lax.optimization_barrier((new[last - 1], top, total, acc))
-    (new[last],) = ring_send(chips, [before], -1)
+        right, left, beside[d] = lax.optimization_barrier((new[1 - d], new[d - 1], beside[d]))
+        new[-d], new[d] = ring_send(chips, [right], 1)[0], ring_send(chips, [left], -1)[0]
+    (new[chips // 2],) = ring_send(chips, [new[1 - chips // 2]], 1)
+    back = exchange(beside[2], chips // 2)
+    top, total, acc = beside[3]
 
     att_other, att_mine, rows_other, rows_mine, info = call(
-        functools.partial(fresh_kernel, chips, pages_dev, old, rest),
+        functools.partial(fresh_kernel, chips, pages_dev),
         [
             ((rows, group * HD), bf),
             ((rows, group * HD), bf),
@@ -758,7 +739,6 @@
             ((2 * pages_dev,), i32),
         ],
         scratch=[
-            *buffers(len(rest)),
             pltpu.VMEM(((chips + 2) * toks, 2 * HD), bf),
             pltpu.VMEM((1, columns), f32),
             pltpu.VMEM((1, columns), f32),
@@ -767,9 +747,8 @@
             table,
             table,
             table,
-            table,
         ],
-        ins=7 + len(rest) + chips,
+        ins=8 + chips,
         smem=(0, 1),
         out_smem=(4,),
         name="attend_new",
@@ -781,7 +760,7 @@
         top,
         total,
         acc,
-        *[kv_got[o] for o in rest],
+        back,
         *[new[o] for o in offsets],
     )
     rows_got = lax.ppermute(rows_other, "dp", core_pairs)
@@ -813,7 +792,7 @@
     dp_count, mp_count = mesh.shape["dp"], mesh.shape["mp"]
 
     def body(*args):
-        even = mp_count == 2 and dp_count % 8 == 0 and dp_count & (dp_count - 1) == 0
+        even = mp_count == 2 and dp_count == 16
         if even and args[2].shape == (256, 2 * HD):
             return ring_body(dp_count, *args)
         return general_body(*args)

time: 86.8 us -> 75 us (0.86)
  waiting for transfers between devices: 38.3 us -> 15 us
  starting transfers between devices: 33.4 us -> 43.8 us
  Pallas kernels: 11.3 us -> 13.8 us
    ppermute x28 -> x21, waiting for transfers between devices: 37.2 us -> 9.12 us  [ring_send(): lax.ppermute(a, 'dp', ring_pairs(chips, step, swap * n))]
    ppermute x0 -> x8, starting transfers between devices: none -> 12.2 us  [exchange(): lax.ppermute(array, 'dp', [(i, i ^ 2 * e ^ swap) for i in range(dp_count)])]
    ppermute x28 -> x21, starting transfers between devices: 30.6 us -> 27.5 us  [ring_send(): lax.ppermute(a, 'dp', ring_pairs(chips, step, swap * n))]
    ppermute x0 -> x8, waiting for transfers between devices: none -> 2.79 us  [exchange(): lax.ppermute(array, 'dp', [(i, i ^ 2 * e ^ swap) for i in range(dp_count)])]
    pallas_call x3 -> x4, Pallas kernels: 6.27 us -> 8.71 us  [the longest x2 5.92 us: cached(): call(functools.partial(cached_kernel, chips, pages_dev, old, away), outs,...]
    ppermute x1, waiting for transfers between devices: 0.01 us -> 1.11 us  [ring_body(): q_got = lax.ppermute(q_other, 'dp', core_pairs)]
    ppermute x1, waiting for transfers between devices: 0.01 us -> 0.93 us  [ring_body(): part_got = lax.ppermute(part_send, 'dp', core_pairs)]
    ppermute x1, starting transfers between devices: 0.07 us -> 0.96 us  [ring_body(): q_got = lax.ppermute(q_other, 'dp', core_pairs)]
  transfers between devices with their start and end apart: 36 -> 37, of which waited for: 18 -> 12; matrix products, arithmetic and copies ran while one was open for 0% -> 0% of each run, Pallas kernels for 6% -> 9%
where the time goes in v2:
time: 75 us; the launch traced here: 74.5 us
  starting transfers between devices  43.8 us (58%)
  waiting for transfers between devices  15 us (20%)
  Pallas kernels  13.8 us (18%)
  local copies, waits for them, and re-layouts  1.03 us (1%)
  between operations  0.85 us (1%)
    ppermute x21, starting transfers between devices, ring_send(): lax.ppermute(a, 'dp', ring_pairs(chips, step, swap * n))  27.5 us
    ppermute x8, starting transfers between devices, exchange(): lax.ppermute(array, 'dp', [(i, i ^ 2 * e ^ swap) for i in range(dp_count)])  12.2 us
    ppermute x21, waiting for transfers between devices, ring_send(): lax.ppermute(a, 'dp', ring_pairs(chips, step, swap * n))  9.12 us
    pallas_call x2, Pallas kernels, cached(): call(functools.partial(cached_kernel, chips, pages_dev, old, away), outs,...  5.92 us
    ppermute x8, waiting for transfers between devices, exchange(): lax.ppermute(array, 'dp', [(i, i ^ 2 * e ^ swap) for i in range(dp_count)])  2.79 us
    pallas_call x1, Pallas kernels, ring_body(): call(functools.partial(fresh_kernel, chips, pages_dev), [((rows, group *...  2.75 us
    pallas_call x1, Pallas kernels, ring_body(): call(functools.partial(split_kernel, old), [((rows, half_width // 2), bf)...  2.1 us
  transfers between devices with their start and end apart: 37, of which 12 were waited for; matrix products, arithmetic and copies ran while one was open for 0% of the time, Pallas kernels for 9%

profile of v2, /device:TPU:0, one launch (start us, length us, event | category | flops | bytes accessed | tf_op | source)
XLA Modules:
  0.0 74.5 jit_solution(10854546236795598772)
XLA Ops:
  0.7 2.1 %split.1 = (bf16[64,1024]{1,0:T(8,128)(2,1)}, bf16[64,1024]{1,0:T(8,128)(2,1)}, bf16[64,512]{1,0:T(8,128)(2,1)}, bf16[4,128,128]{2,1,0:T(8,128)(2,1)}, bf16[4,128,128]{2,1,0:T(8,128)(2,1)}) custom-call(bf16[64,2048]{1,0:T(8,128)(2,1)} %f_ref.1, bf16[64,1024]{1,0:T(8,128)(2,1)} %q_ref.3, bf16[3,128,256]{2,1,0:T(8,128)(2,1)} %kp_ref.3, bf16[3,128,256]{2,1,0:T(8,128)(2,1)} %vp_ref.3), custom_call_target="tpu_custom_call" | custom-call | tf_op jit(solution)/shard_map/split/pallas_call | solution.py:629
  2.8 3.1 %collective-permute-start.2 = (bf16[4,128,128]{2,1,0:T(8,128)(2,1)}, bf16[4,128,128]{2,1,0:T(8,128)(2,1)S(1)}, u32[]{:S(2)}, u32[]{:S(2)}) collective-permute-start(bf16[4,128,128]{2,1,0:T(8,128)(2,1)} %get-tuple-element.40.refs_0_), channel_id=1, source_target_pairs={{0,8},{2,10},{4,12},{6,14},{8,0},{10,2},{12,4},{14,6},{16,24},{18,... | collective-permute-start | bytes 393224 | tf_op jit(solution)/shard_map/ppermute | solution.py:624
  5.9 1.5 %collective-permute-start.4 = (bf16[4,128,128]{2,1,0:T(8,128)(2,1)}, bf16[4,128,128]{2,1,0:T(8,128)(2,1)S(1)}, u32[]{:S(2)}, u32[]{:S(2)}) collective-permute-start(bf16[4,128,128]{2,1,0:T(8,128)(2,1)} %get-tuple-element.40.refs_0_), channel_id=1, source_target_pairs={{0,4},{2,6},{4,0},{6,2},{8,12},{10,14},{12,8},{14,10},{16,20},{18,... | collective-permute-start | bytes 393224 | tf_op jit(solution)/shard_map/ppermute | solution.py:624
  9.2 1.1 %collective-permute-done.6.qg_ref = bf16[64,512]{1,0:T(8,128)(2,1)S(1)} collective-permute-done((bf16[64,512]{1,0:T(8,128)(2,1)}, bf16[64,512]{1,0:T(8,128)(2,1)S(1)}, u32[]{:S(2)}, u32[]{:S(2)}) %collective-permute-start.6) | collective-permute-done | bytes 65568 | tf_op jit(solution)/shard_map/ppermute | solution.py:647
  10.8 1.5 %collective-permute-start.7 = (bf16[64,1024]{1,0:T(8,128)(2,1)}, bf16[64,1024]{1,0:T(8,128)(2,1)S(1)}, u32[]{:S(2)}, u32[]{:S(2)}) collective-permute-start(bf16[64,1024]{1,0:T(8,128)(2,1)} %get-tuple-element.44.a_ref), channel_id=1, source_target_pairs={{0,1},{1,0},{2,3},{3,2},{4,5},{5,4},{6,7},{7,6},{8,9},{9,8},{10,11... | collective-permute-start | bytes 393224 | tf_op jit(solution)/shard_map/ppermute | solution.py:644
  12.3 1.6 %collective-permute-start.18 = (bf16[256,256]{1,0:T(8,128)(2,1)S(1)}, bf16[256,256]{1,0:T(8,128)(2,1)S(1)}, u32[]{:S(2)}, u32[]{:S(2)}) collective-permute-start(bf16[256,256]{1,0:T(8,128)(2,1)S(1)} %copy-done.6), channel_id=1, source_target_pairs={{0,4},{2,6},{8,0},{10,2},{16,8},{18,10},{24,16},{26,18},{28,24},{3... | collective-permute-start | bytes 393224 | tf_op jit(solution)/shard_map/ppermute | solution.py:591
  13.8 1.6 %collective-permute-start.13 = (bf16[256,256]{1,0:T(8,128)(2,1)S(1)}, bf16[256,256]{1,0:T(8,128)(2,1)S(1)}, u32[]{:S(2)}, u32[]{:S(2)}) collective-permute-start(bf16[256,256]{1,0:T(8,128)(2,1)S(1)} %copy-done.5), channel_id=1, source_target_pairs={{0,4},{2,6},{8,0},{10,2},{16,8},{18,10},{24,16},{26,18},{28,24},{3... | collective-permute-start | bytes 393224 | tf_op jit(solution)/shard_map/ppermute | solution.py:591
  15.5 1.4 %collective-permute-start.1 = (bf16[256,256]{1,0:T(8,128)(2,1)S(1)}, bf16[256,256]{1,0:T(8,128)(2,1)S(1)}, u32[]{:S(2)}, u32[]{:S(2)}) collective-permute-start(bf16[256,256]{1,0:T(8,128)(2,1)S(1)} %collective-permute-done.refs_2_), channel_id=1, source_target_pairs={{0,8},{2,10},{8,16},{10,18},{16,24},{18,26},{24,28},{26,30},{28,20... | collective-permute-start | bytes 393224 | tf_op jit(solution)/shard_map/ppermute | solution.py:591
  19.2 1.2 %collective-permute-done.13.refs_1_ = bf16[256,256]{1,0:T(8,128)(2,1)S(1)} collective-permute-done((bf16[256,256]{1,0:T(8,128)(2,1)S(1)}, bf16[256,256]{1,0:T(8,128)(2,1)S(1)}, u32[]{:S(2)}, u32[]{:S(2)}) %collective-permute-start.13) | collective-permute-done | bytes 131104 | tf_op jit(solution)/shard_map/ppermute | solution.py:591
  20.4 2.1 %collective-permute-start.20 = (bf16[256,256]{1,0:T(8,128)(2,1)S(1)}, bf16[256,256]{1,0:T(8,128)(2,1)S(1)}, u32[]{:S(2)}, u32[]{:S(2)}) collective-permute-start(bf16[256,256]{1,0:T(8,128)(2,1)S(1)} %collective-permute-done.18.refs_9_), channel_id=1, source_target_pairs={{0,4},{2,6},{8,0},{10,2},{16,8},{18,10},{24,16},{26,18},{28,24},{3... | collective-permute-start | bytes 393224 | tf_op jit(solution)/shard_map/ppermute | solution.py:591
  22.5 1.1 %collective-permute-start.14 = (bf16[256,256]{1,0:T(8,128)(2,1)S(1)}, bf16[256,256]{1,0:T(8,128)(2,1)S(1)}, u32[]{:S(2)}, u32[]{:S(2)}) collective-permute-start(bf16[256,256]{1,0:T(8,128)(2,1)S(1)} %collective-permute-done.13.refs_1_), channel_id=1, source_target_pairs={{0,4},{2,6},{8,0},{10,2},{16,8},{18,10},{24,16},{26,18},{28,24},{3... | collective-permute-start | bytes 393224 | tf_op jit(solution)/shard_map/ppermute | solution.py:591
  23.6 1.4 %collective-permute-start.21 = (bf16[256,256]{1,0:T(8,128)(2,1)S(1)}, bf16[256,256]{1,0:T(8,128)(2,1)S(1)}, u32[]{:S(2)}, u32[]{:S(2)}) collective-permute-start(bf16[256,256]{1,0:T(8,128)(2,1)S(1)} %collective-permute-done.19.refs_10_), channel_id=1, source_target_pairs={{0,8},{2,10},{8,16},{10,18},{16,24},{18,26},{24,28},{26,30},{28,20... | collective-permute-start | bytes 393224 | tf_op jit(solution)/shard_map/ppermute | solution.py:591
  25.0 2.6 %collective-permute-start.12 = (bf16[512,128]{1,0:T(8,128)(2,1)S(1)}, bf16[512,128]{1,0:T(8,128)(2,1)S(1)}, u32[]{:S(2)}, u32[]{:S(2)}) collective-permute-start(bf16[512,128]{1,0:T(8,128)(2,1)S(1)} %merge.1.qs_ref), channel_id=1, source_target_pairs={{0,16},{2,18},{4,20},{6,22},{8,24},{10,26},{12,28},{14,30},{16,0},... | collective-permute-start | bytes 393224 | tf_op jit(solution)/shard_map/ppermute | solution.py:624
  28.0 1.6 %collective-permute-start.16 = (bf16[256,256]{1,0:T(8,128)(2,1)S(1)}, bf16[256,256]{1,0:T(8,128)(2,1)S(1)}, u32[]{:S(2)}, u32[]{:S(2)}) collective-permute-start(bf16[256,256]{1,0:T(8,128)(2,1)S(1)} %collective-permute-done.1.refs_4_), channel_id=1, source_target_pairs={{0,8},{2,10},{8,16},{10,18},{16,24},{18,26},{24,28},{26,30},{28,20... | collective-permute-start | bytes 393224 | tf_op jit(solution)/shard_map/ppermute | solution.py:591
  30.2 2.9 %collective-permute-start.11 = (bf16[4,128,128]{2,1,0:T(8,128)(2,1)S(1)}, bf16[4,128,128]{2,1,0:T(8,128)(2,1)S(1)}, u32[]{:S(2)}, u32[]{:S(2)}) collective-permute-start(bf16[4,128,128]{2,1,0:T(8,128)(2,1)S(1)} %collective-permute-done.3.refs_6_), channel_id=1, source_target_pairs={{0,4},{2,6},{4,0},{6,2},{8,12},{10,14},{12,8},{14,10},{16,20},{18,... | collective-permute-start | bytes 393224 | tf_op jit(solution)/shard_map/ppermute | solution.py:624
  33.2 2.8 %collective-permute-done.12.qs_ref = bf16[512,128]{1,0:T(8,128)(2,1)S(1)} collective-permute-done((bf16[512,128]{1,0:T(8,128)(2,1)S(1)}, bf16[512,128]{1,0:T(8,128)(2,1)S(1)}, u32[]{:S(2)}, u32[]{:S(2)}) %collective-permute-start.12) | collective-permute-done | bytes 131104 | tf_op jit(solution)/shard_map/ppermute | solution.py:624
  35.9 1.7 %collective-permute-start.15 = (bf16[256,256]{1,0:T(8,128)(2,1)S(1)}, bf16[256,256]{1,0:T(8,128)(2,1)S(1)}, u32[]{:S(2)}, u32[]{:S(2)}) collective-permute-start(bf16[256,256]{1,0:T(8,128)(2,1)S(1)} %collective-permute-done.14.refs_3_), channel_id=1, source_target_pairs={{0,4},{2,6},{8,0},{10,2},{16,8},{18,10},{24,16},{26,18},{28,24},{3... | collective-permute-start | bytes 393224 | tf_op jit(solution)/shard_map/ppermute | solution.py:591
  38.5 1.5 %collective-permute-start.24 = (bf16[256,256]{1,0:T(8,128)(2,1)S(1)}, bf16[256,256]{1,0:T(8,128)(2,1)S(1)}, u32[]{:S(2)}, u32[]{:S(2)}) collective-permute-start(bf16[256,256]{1,0:T(8,128)(2,1)S(1)} %collective-permute-done.22.refs_13_), channel_id=1, source_target_pairs={{0,4},{2,6},{8,0},{10,2},{16,8},{18,10},{24,16},{26,18},{28,24},{3... | collective-permute-start | bytes 393224 | tf_op jit(solution)/shard_map/ppermute | solution.py:591
  40.7 1.0 %scale.1 = (bf16[8,128,256]{2,1,0:T(8,128)(2,1)S(1)}, f32[128,128]{1,0:T(8,128)S(1)}, f32[128,128]{1,0:T(8,128)S(1)}, f32[128,128]{1,0:T(8,128)S(1)}) custom-call(s32[3]{0:T(128)S(1)} %copy-done.9, s32[8,128]{1,0:T(8,128)S(1)} %bitcast.1, f32[1,128]{1,0:T(1,128)S(1)} %copy-done.10, bf16[1,4096]{1,0:T(2,128)(2,1)S(1)} %reshape.13.gain_ref, ...), custom_call_target="tpu_custom_call" | custom-call | tf_op jit(solution)/shard_map/scale/pallas_call | solution.py:665
  42.6 1.4 %collective-permute-done.17.refs_7_ = bf16[256,256]{1,0:T(8,128)(2,1)S(1)} collective-permute-done((bf16[256,256]{1,0:T(8,128)(2,1)S(1)}, bf16[256,256]{1,0:T(8,128)(2,1)S(1)}, u32[]{:S(2)}, u32[]{:S(2)}) %collective-permute-start.17) | collective-permute-done | bytes 131104 | tf_op jit(solution)/shard_map/ppermute | solution.py:591
  46.1 1.5 %collective-permute-start.26 = (bf16[128,256]{1,0:T(8,128)(2,1)S(1)}, bf16[128,256]{1,0:T(8,128)(2,1)S(1)}, u32[]{:S(2)}, u32[]{:S(2)}) collective-permute-start(bf16[128,256]{1,0:T(8,128)(2,1)S(1)} %rotary.1.refs_0_), channel_id=1, source_target_pairs={{0,8},{2,10},{8,16},{10,18},{16,24},{18,26},{24,28},{26,30},{28,20... | collective-permute-start | bytes 196616 | tf_op jit(solution)/shard_map/ppermute | solution.py:591
  48.2 3.9 %attend_cached_away.1 = bf16[144,512]{1,0:T(8,128)(2,1)S(1)} custom-call(s32[3]{0:T(128)S(1)} %copy-done.9, s32[3,25]{1,0:T(4,128)S(1)} %copy-done.8, s32[8,128]{1,0:T(8,128)S(1)} %bitcast.2, bf16[512,128]{1,0:T(8,128)(2,1)S(1)} %collective-permute-done.12.qs_ref, bf16[4,128,128]{2,1,0:T(8,128)(2,1)S(1)} %copy-done.2, ...), custom_call_target="tpu_custom_call" | custom-call | tf_op jit(solution)/shard_map/attend_cached_away/pallas_call | solution.py:704
  52.1 1.8 %collective-permute-start.29 = (bf16[128,256]{1,0:T(8,128)(2,1)S(1)}, bf16[128,256]{1,0:T(8,128)(2,1)S(1)}, u32[]{:S(2)}, u32[]{:S(2)}) collective-permute-start(bf16[128,256]{1,0:T(8,128)(2,1)S(1)} %collective-permute-done.26.refs_2_), channel_id=1, source_target_pairs={{0,8},{2,10},{8,16},{10,18},{16,24},{18,26},{24,28},{26,30},{28,20... | collective-permute-start | bytes 196616 | tf_op jit(solution)/shard_map/ppermute | solution.py:591
  54.2 1.3 %collective-permute-start.31 = (bf16[144,512]{1,0:T(8,128)(2,1)S(1)}, bf16[144,512]{1,0:T(8,128)(2,1)S(1)}, u32[]{:S(2)}, u32[]{:S(2)}) collective-permute-start(bf16[144,512]{1,0:T(8,128)(2,1)S(1)} %attend_cached_away.1), channel_id=1, source_target_pairs={{0,16},{2,18},{4,20},{6,22},{8,24},{10,26},{12,28},{14,30},{16,0},... | collective-permute-start | bytes 442376 | tf_op jit(solution)/shard_map/ppermute | solution.py:624
  55.5 2.0 %attend_cached_here.1 = (f32[1,512]{1,0:T(1,128)S(1)}, f32[1,512]{1,0:T(1,128)S(1)}, f32[128,512]{1,0:T(8,128)S(1)}) custom-call(s32[3]{0:T(128)S(1)} %copy-done.9, s32[3,25]{1,0:T(4,128)S(1)} %copy-done.8, s32[8,128]{1,0:T(8,128)S(1)} %bitcast.3, bf16[512,128]{1,0:T(8,128)(2,1)S(1)} %merge.1.qs_ref, bf16[4,128,128]{2,1,0:T(8,128)(2,1)S(1)} %copy-done.2, ...), custom_call_target="tpu_custom_call" | custom-call | tf_op jit(solution)/shard_map/attend_cached_here/pallas_call | solution.py:704
  58.3 3.8 %collective-permute-start.33 = (bf16[128,256]{1,0:T(8,128)(2,1)S(1)}, bf16[128,256]{1,0:T(8,128)(2,1)S(1)}, u32[]{:S(2)}, u32[]{:S(2)}) collective-permute-start(bf16[128,256]{1,0:T(8,128)(2,1)S(1)} %collective-permute-done.29.refs_4_), channel_id=1, source_target_pairs={{0,8},{2,10},{8,16},{10,18},{16,24},{18,26},{24,28},{26,30},{28,20... | collective-permute-start | bytes 196616 | tf_op jit(solution)/shard_map/ppermute | solution.py:591
  62.1 2.2 %collective-permute-done.33.refs_6_ = bf16[128,256]{1,0:T(8,128)(2,1)S(1)} collective-permute-done((bf16[128,256]{1,0:T(8,128)(2,1)S(1)}, bf16[128,256]{1,0:T(8,128)(2,1)S(1)}, u32[]{:S(2)}, u32[]{:S(2)}) %collective-permute-start.33) | collective-permute-done | bytes 65568 | tf_op jit(solution)/shard_map/ppermute | solution.py:591
  64.3 2.5 %collective-permute-start.34 = (bf16[128,256]{1,0:T(8,128)(2,1)S(1)}, bf16[128,256]{1,0:T(8,128)(2,1)S(1)}, u32[]{:S(2)}, u32[]{:S(2)}) collective-permute-start(bf16[128,256]{1,0:T(8,128)(2,1)S(1)} %collective-permute-done.33.refs_6_), channel_id=1, source_target_pairs={{0,8},{2,10},{8,16},{10,18},{16,24},{18,26},{24,28},{26,30},{28,20... | collective-permute-start | bytes 196616 | tf_op jit(solution)/shard_map/ppermute | solution.py:591
  66.8 1.9 %collective-permute-done.34.refs_7_ = bf16[128,256]{1,0:T(8,128)(2,1)S(1)} collective-permute-done((bf16[128,256]{1,0:T(8,128)(2,1)S(1)}, bf16[128,256]{1,0:T(8,128)(2,1)S(1)}, u32[]{:S(2)}, u32[]{:S(2)}) %collective-permute-start.34) | collective-permute-done | bytes 65568 | tf_op jit(solution)/shard_map/ppermute | solution.py:591
  68.7 2.8 %attend_new.1 = (bf16[64,512]{1,0:T(8,128)(2,1)S(1)}, bf16[64,512]{1,0:T(8,128)(2,1)S(1)}, bf16[3,128,256]{2,1,0:T(8,128)(2,1)S(1)}, bf16[3,128,256]{2,1,0:T(8,128)(2,1)S(1)}, s32[6]{0:T(128)S(1)}) custom-call(s32[3]{0:T(128)S(1)} %copy-done.9, s32[3,25]{1,0:T(4,128)S(1)} %copy-done.8, s32[8,128]{1,0:T(8,128)S(1)} %bitcast.4, ...), custom_call_target="tpu_custom_call" | custom-call | tf_op jit(solution)/shard_map/attend_new/pallas_call | solution.py:732
  72.0 1.0 %collective-permute-done.35.attr_ref = bf16[64,512]{1,0:T(8,128)(2,1)S(1)} collective-permute-done((bf16[64,512]{1,0:T(8,128)(2,1)S(1)}, bf16[64,512]{1,0:T(8,128)(2,1)S(1)}, u32[]{:S(2)}, u32[]{:S(2)}) %collective-permute-start.35) | collective-permute-done | bytes 65568 | tf_op jit(solution)/shard_map/ppermute | solution.py:767
  73.1 1.5 %join.1 = (bf16[64,1024]{1,0:T(8,128)(2,1)}, bf16[3,128,256]{2,1,0:T(8,128)(2,1)}, bf16[3,128,256]{2,1,0:T(8,128)(2,1)}) custom-call(s32[6]{0:T(128)S(1)} %get-tuple-element.72.info_ref, bf16[64,512]{1,0:T(8,128)(2,1)S(1)} %get-tuple-element.73.attc_ref, bf16[64,512]{1,0:T(8,128)(2,1)S(1)} %collective-permute-done.35.attr_ref, ...), custom_call_target="tpu_custom_call" | custom-call | tf_op jit(solution)/shard_map/join/pallas_call | solution.py:768
  (78 shorter events, 12.4 us)
Async XLA Ops:
  2.8 8.0 %collective-permute-start.2 = (bf16[4,128,128]{2,1,0:T(8,128)(2,1)}, bf16[4,128,128]{2,1,0:T(8,128)(2,1)S(1)}, u32[]{:S(2)}, u32[]{:S(2)}) collective-permute-start(bf16[4,128,128]{2,1,0:T(8,128)(2,1)} %get-tuple-element.40.refs_0_), channel_id=1, source_target_pairs={{0,8},{2,10},{4,12},{6,14},{8,0},{10,2},{12,4},{14,6},{16,24},{18,... | collective-permute-start | bytes 393224 | tf_op jit(solution)/shard_map/ppermute | solution.py:624
  5.9 6.4 %collective-permute-start.4 = (bf16[4,128,128]{2,1,0:T(8,128)(2,1)}, bf16[4,128,128]{2,1,0:T(8,128)(2,1)S(1)}, u32[]{:S(2)}, u32[]{:S(2)}) collective-permute-start(bf16[4,128,128]{2,1,0:T(8,128)(2,1)} %get-tuple-element.40.refs_0_), channel_id=1, source_target_pairs={{0,4},{2,6},{4,0},{6,2},{8,12},{10,14},{12,8},{14,10},{16,20},{18,... | collective-permute-start | bytes 393224 | tf_op jit(solution)/shard_map/ppermute | solution.py:624
  7.4 6.5 %collective-permute-start.3 = (bf16[4,128,128]{2,1,0:T(8,128)(2,1)}, bf16[4,128,128]{2,1,0:T(8,128)(2,1)S(1)}, u32[]{:S(2)}, u32[]{:S(2)}) collective-permute-start(bf16[4,128,128]{2,1,0:T(8,128)(2,1)} %get-tuple-element.41), channel_id=1, source_target_pairs={{0,10},{2,8},{4,14},{6,12},{8,2},{10,0},{12,6},{14,4},{16,26},{18,... | collective-permute-start | bytes 393224 | tf_op jit(solution)/shard_map/ppermute | solution.py:624
  7.4 8.1 %collective-permute-start = (bf16[256,256]{1,0:T(8,128)(2,1)S(1)}, bf16[256,256]{1,0:T(8,128)(2,1)S(1)}, u32[]{:S(2)}, u32[]{:S(2)}) collective-permute-start(bf16[256,256]{1,0:T(8,128)(2,1)S(1)} %copy-done.5), channel_id=1, source_target_pairs={{0,8},{2,10},{8,16},{10,18},{16,24},{18,26},{24,28},{26,30},{28,20... | collective-permute-start | bytes 393224 | tf_op jit(solution)/shard_map/ppermute | solution.py:591
  10.4 6.6 %collective-permute-start.5 = (bf16[4,128,128]{2,1,0:T(8,128)(2,1)}, bf16[4,128,128]{2,1,0:T(8,128)(2,1)S(1)}, u32[]{:S(2)}, u32[]{:S(2)}) collective-permute-start(bf16[4,128,128]{2,1,0:T(8,128)(2,1)} %get-tuple-element.41), channel_id=1, source_target_pairs={{0,6},{2,4},{4,2},{6,0},{8,14},{10,12},{12,10},{14,8},{16,22},{18,... | collective-permute-start | bytes 393224 | tf_op jit(solution)/shard_map/ppermute | solution.py:624
  10.8 6.9 %collective-permute-start.7 = (bf16[64,1024]{1,0:T(8,128)(2,1)}, bf16[64,1024]{1,0:T(8,128)(2,1)S(1)}, u32[]{:S(2)}, u32[]{:S(2)}) collective-permute-start(bf16[64,1024]{1,0:T(8,128)(2,1)} %get-tuple-element.44.a_ref), channel_id=1, source_target_pairs={{0,1},{1,0},{2,3},{3,2},{4,5},{5,4},{6,7},{7,6},{8,9},{9,8},{10,11... | collective-permute-start | bytes 393224 | tf_op jit(solution)/shard_map/ppermute | solution.py:644
  12.3 6.4 %collective-permute-start.18 = (bf16[256,256]{1,0:T(8,128)(2,1)S(1)}, bf16[256,256]{1,0:T(8,128)(2,1)S(1)}, u32[]{:S(2)}, u32[]{:S(2)}) collective-permute-start(bf16[256,256]{1,0:T(8,128)(2,1)S(1)} %copy-done.6), channel_id=1, source_target_pairs={{0,4},{2,6},{8,0},{10,2},{16,8},{18,10},{24,16},{26,18},{28,24},{3... | collective-permute-start | bytes 393224 | tf_op jit(solution)/shard_map/ppermute | solution.py:591
  13.8 6.6 %collective-permute-start.13 = (bf16[256,256]{1,0:T(8,128)(2,1)S(1)}, bf16[256,256]{1,0:T(8,128)(2,1)S(1)}, u32[]{:S(2)}, u32[]{:S(2)}) collective-permute-start(bf16[256,256]{1,0:T(8,128)(2,1)S(1)} %copy-done.5), channel_id=1, source_target_pairs={{0,4},{2,6},{8,0},{10,2},{16,8},{18,10},{24,16},{26,18},{28,24},{3... | collective-permute-start | bytes 393224 | tf_op jit(solution)/shard_map/ppermute | solution.py:591
  15.5 7.0 %collective-permute-start.1 = (bf16[256,256]{1,0:T(8,128)(2,1)S(1)}, bf16[256,256]{1,0:T(8,128)(2,1)S(1)}, u32[]{:S(2)}, u32[]{:S(2)}) collective-permute-start(bf16[256,256]{1,0:T(8,128)(2,1)S(1)} %collective-permute-done.refs_2_), channel_id=1, source_target_pairs={{0,8},{2,10},{8,16},{10,18},{16,24},{18,26},{24,28},{26,30},{28,20... | collective-permute-start | bytes 393224 | tf_op jit(solution)/shard_map/ppermute | solution.py:591
  16.9 6.7 %collective-permute-start.19 = (bf16[256,256]{1,0:T(8,128)(2,1)S(1)}, bf16[256,256]{1,0:T(8,128)(2,1)S(1)}, u32[]{:S(2)}, u32[]{:S(2)}) collective-permute-start(bf16[256,256]{1,0:T(8,128)(2,1)S(1)} %copy-done.6), channel_id=1, source_target_pairs={{0,8},{2,10},{8,16},{10,18},{16,24},{18,26},{24,28},{26,30},{28,20... | collective-permute-start | bytes 393224 | tf_op jit(solution)/shard_map/ppermute | solution.py:591
  17.6 7.4 %collective-permute-start.8 = (bf16[64,1024]{1,0:T(8,128)(2,1)}, bf16[64,1024]{1,0:T(8,128)(2,1)S(1)}, u32[]{:S(2)}, u32[]{:S(2)}) collective-permute-start(bf16[64,1024]{1,0:T(8,128)(2,1)} %get-tuple-element.45), channel_id=1, source_target_pairs={{0,2},{2,0},{4,6},{6,4},{8,10},{10,8},{12,14},{14,12},{16,18},{18,... | collective-permute-start | bytes 393224 | tf_op jit(solution)/shard_map/ppermute | solution.py:645
  18.6 9.0 %collective-permute-start.9 = (bf16[64,1024]{1,0:T(8,128)(2,1)}, bf16[64,1024]{1,0:T(8,128)(2,1)S(1)}, u32[]{:S(2)}, u32[]{:S(2)}) collective-permute-start(bf16[64,1024]{1,0:T(8,128)(2,1)} %get-tuple-element.45), channel_id=1, source_target_pairs={{0,3},{1,2},{2,1},{3,0},{4,7},{5,6},{6,5},{7,4},{8,11},{9,10},{10,... | collective-permute-start | bytes 393224 | tf_op jit(solution)/shard_map/ppermute | solution.py:646
  20.4 7.6 %collective-permute-start.20 = (bf16[256,256]{1,0:T(8,128)(2,1)S(1)}, bf16[256,256]{1,0:T(8,128)(2,1)S(1)}, u32[]{:S(2)}, u32[]{:S(2)}) collective-permute-start(bf16[256,256]{1,0:T(8,128)(2,1)S(1)} %collective-permute-done.18.refs_9_), channel_id=1, source_target_pairs={{0,4},{2,6},{8,0},{10,2},{16,8},{18,10},{24,16},{26,18},{28,24},{3... | collective-permute-start | bytes 393224 | tf_op jit(solution)/shard_map/ppermute | solution.py:591
  22.5 7.1 %collective-permute-start.14 = (bf16[256,256]{1,0:T(8,128)(2,1)S(1)}, bf16[256,256]{1,0:T(8,128)(2,1)S(1)}, u32[]{:S(2)}, u32[]{:S(2)}) collective-permute-start(bf16[256,256]{1,0:T(8,128)(2,1)S(1)} %collective-permute-done.13.refs_1_), channel_id=1, source_target_pairs={{0,4},{2,6},{8,0},{10,2},{16,8},{18,10},{24,16},{26,18},{28,24},{3... | collective-permute-start | bytes 393224 | tf_op jit(solution)/shard_map/ppermute | solution.py:591
  23.6 6.6 %collective-permute-start.21 = (bf16[256,256]{1,0:T(8,128)(2,1)S(1)}, bf16[256,256]{1,0:T(8,128)(2,1)S(1)}, u32[]{:S(2)}, u32[]{:S(2)}) collective-permute-start(bf16[256,256]{1,0:T(8,128)(2,1)S(1)} %collective-permute-done.19.refs_10_), channel_id=1, source_target_pairs={{0,8},{2,10},{8,16},{10,18},{16,24},{18,26},{24,28},{26,30},{28,20... | collective-permute-start | bytes 393224 | tf_op jit(solution)/shard_map/ppermute | solution.py:591
  25.0 10.9 %collective-permute-start.12 = (bf16[512,128]{1,0:T(8,128)(2,1)S(1)}, bf16[512,128]{1,0:T(8,128)(2,1)S(1)}, u32[]{:S(2)}, u32[]{:S(2)}) collective-permute-start(bf16[512,128]{1,0:T(8,128)(2,1)S(1)} %merge.1.qs_ref), channel_id=1, source_target_pairs={{0,16},{2,18},{4,20},{6,22},{8,24},{10,26},{12,28},{14,30},{16,0},... | collective-permute-start | bytes 393224 | tf_op jit(solution)/shard_map/ppermute | solution.py:624
  27.6 10.0 %collective-permute-start.10 = (bf16[4,128,128]{2,1,0:T(8,128)(2,1)S(1)}, bf16[4,128,128]{2,1,0:T(8,128)(2,1)S(1)}, u32[]{:S(2)}, u32[]{:S(2)}) collective-permute-start(bf16[4,128,128]{2,1,0:T(8,128)(2,1)S(1)} %collective-permute-done.4.refs_1_), channel_id=1, source_target_pairs={{0,8},{2,10},{4,12},{6,14},{8,0},{10,2},{12,4},{14,6},{16,24},{18,... | collective-permute-start | bytes 393224 | tf_op jit(solution)/shard_map/ppermute | solution.py:624
  28.0 9.9 %collective-permute-start.16 = (bf16[256,256]{1,0:T(8,128)(2,1)S(1)}, bf16[256,256]{1,0:T(8,128)(2,1)S(1)}, u32[]{:S(2)}, u32[]{:S(2)}) collective-permute-start(bf16[256,256]{1,0:T(8,128)(2,1)S(1)} %collective-permute-done.1.refs_4_), channel_id=1, source_target_pairs={{0,8},{2,10},{8,16},{10,18},{16,24},{18,26},{24,28},{26,30},{28,20... | collective-permute-start | bytes 393224 | tf_op jit(solution)/shard_map/ppermute | solution.py:591
  29.7 8.8 %collective-permute-start.22 = (bf16[256,256]{1,0:T(8,128)(2,1)S(1)}, bf16[256,256]{1,0:T(8,128)(2,1)S(1)}, u32[]{:S(2)}, u32[]{:S(2)}) collective-permute-start(bf16[256,256]{1,0:T(8,128)(2,1)S(1)} %collective-permute-done.20.refs_11_), channel_id=1, source_target_pairs={{0,4},{2,6},{8,0},{10,2},{16,8},{18,10},{24,16},{26,18},{28,24},{3... | collective-permute-start | bytes 393224 | tf_op jit(solution)/shard_map/ppermute | solution.py:591
  30.2 11.5 %collective-permute-start.11 = (bf16[4,128,128]{2,1,0:T(8,128)(2,1)S(1)}, bf16[4,128,128]{2,1,0:T(8,128)(2,1)S(1)}, u32[]{:S(2)}, u32[]{:S(2)}) collective-permute-start(bf16[4,128,128]{2,1,0:T(8,128)(2,1)S(1)} %collective-permute-done.3.refs_6_), channel_id=1, source_target_pairs={{0,4},{2,6},{4,0},{6,2},{8,12},{10,14},{12,8},{14,10},{16,20},{18,... | collective-permute-start | bytes 393224 | tf_op jit(solution)/shard_map/ppermute | solution.py:624
  35.9 6.3 %collective-permute-start.15 = (bf16[256,256]{1,0:T(8,128)(2,1)S(1)}, bf16[256,256]{1,0:T(8,128)(2,1)S(1)}, u32[]{:S(2)}, u32[]{:S(2)}) collective-permute-start(bf16[256,256]{1,0:T(8,128)(2,1)S(1)} %collective-permute-done.14.refs_3_), channel_id=1, source_target_pairs={{0,4},{2,6},{8,0},{10,2},{16,8},{18,10},{24,16},{26,18},{28,24},{3... | collective-permute-start | bytes 393224 | tf_op jit(solution)/shard_map/ppermute | solution.py:591
  37.6 5.0 %collective-permute-start.23 = (bf16[256,256]{1,0:T(8,128)(2,1)S(1)}, bf16[256,256]{1,0:T(8,128)(2,1)S(1)}, u32[]{:S(2)}, u32[]{:S(2)}) collective-permute-start(bf16[256,256]{1,0:T(8,128)(2,1)S(1)} %collective-permute-done.21.refs_12_), channel_id=1, source_target_pairs={{0,8},{2,10},{8,16},{10,18},{16,24},{18,26},{24,28},{26,30},{28,20... | collective-permute-start | bytes 393224 | tf_op jit(solution)/shard_map/ppermute | solution.py:591
  38.0 6.0 %collective-permute-start.17 = (bf16[256,256]{1,0:T(8,128)(2,1)S(1)}, bf16[256,256]{1,0:T(8,128)(2,1)S(1)}, u32[]{:S(2)}, u32[]{:S(2)}) collective-permute-start(bf16[256,256]{1,0:T(8,128)(2,1)S(1)} %collective-permute-done.16.refs_6_), channel_id=1, source_target_pairs={{0,8},{2,10},{8,16},{10,18},{16,24},{18,26},{24,28},{26,30},{28,20... | collective-permute-start | bytes 393224 | tf_op jit(solution)/shard_map/ppermute | solution.py:591
  38.5 5.5 %collective-permute-start.24 = (bf16[256,256]{1,0:T(8,128)(2,1)S(1)}, bf16[256,256]{1,0:T(8,128)(2,1)S(1)}, u32[]{:S(2)}, u32[]{:S(2)}) collective-permute-start(bf16[256,256]{1,0:T(8,128)(2,1)S(1)} %collective-permute-done.22.refs_13_), channel_id=1, source_target_pairs={{0,4},{2,6},{8,0},{10,2},{16,8},{18,10},{24,16},{26,18},{28,24},{3... | collective-permute-start | bytes 393224 | tf_op jit(solution)/shard_map/ppermute | solution.py:591
  46.1 6.0 %collective-permute-start.26 = (bf16[128,256]{1,0:T(8,128)(2,1)S(1)}, bf16[128,256]{1,0:T(8,128)(2,1)S(1)}, u32[]{:S(2)}, u32[]{:S(2)}) collective-permute-start(bf16[128,256]{1,0:T(8,128)(2,1)S(1)} %rotary.1.refs_0_), channel_id=1, source_target_pairs={{0,8},{2,10},{8,16},{10,18},{16,24},{18,26},{24,28},{26,30},{28,20... | collective-permute-start | bytes 196616 | tf_op jit(solution)/shard_map/ppermute | solution.py:591
  47.6 4.5 %collective-permute-start.27 = (bf16[128,256]{1,0:T(8,128)(2,1)S(1)}, bf16[128,256]{1,0:T(8,128)(2,1)S(1)}, u32[]{:S(2)}, u32[]{:S(2)}) collective-permute-start(bf16[128,256]{1,0:T(8,128)(2,1)S(1)} %rotary.1.refs_0_), channel_id=1, source_target_pairs={{0,4},{2,6},{8,0},{10,2},{16,8},{18,10},{24,16},{26,18},{28,24},{3... | collective-permute-start | bytes 196616 | tf_op jit(solution)/shard_map/ppermute | solution.py:591
  52.1 5.4 %collective-permute-start.29 = (bf16[128,256]{1,0:T(8,128)(2,1)S(1)}, bf16[128,256]{1,0:T(8,128)(2,1)S(1)}, u32[]{:S(2)}, u32[]{:S(2)}) collective-permute-start(bf16[128,256]{1,0:T(8,128)(2,1)S(1)} %collective-permute-done.26.refs_2_), channel_id=1, source_target_pairs={{0,8},{2,10},{8,16},{10,18},{16,24},{18,26},{24,28},{26,30},{28,20... | collective-permute-start | bytes 196616 | tf_op jit(solution)/shard_map/ppermute | solution.py:591
  53.9 4.4 %collective-permute-start.30 = (bf16[128,256]{1,0:T(8,128)(2,1)S(1)}, bf16[128,256]{1,0:T(8,128)(2,1)S(1)}, u32[]{:S(2)}, u32[]{:S(2)}) collective-permute-start(bf16[128,256]{1,0:T(8,128)(2,1)S(1)} %collective-permute-done.27.refs_1_), channel_id=1, source_target_pairs={{0,4},{2,6},{8,0},{10,2},{16,8},{18,10},{24,16},{26,18},{28,24},{3... | collective-permute-start | bytes 196616 | tf_op jit(solution)/shard_map/ppermute | solution.py:591
  54.2 12.6 %collective-permute-start.31 = (bf16[144,512]{1,0:T(8,128)(2,1)S(1)}, bf16[144,512]{1,0:T(8,128)(2,1)S(1)}, u32[]{:S(2)}, u32[]{:S(2)}) collective-permute-start(bf16[144,512]{1,0:T(8,128)(2,1)S(1)} %attend_cached_away.1), channel_id=1, source_target_pairs={{0,16},{2,18},{4,20},{6,22},{8,24},{10,26},{12,28},{14,30},{16,0},... | collective-permute-start | bytes 442376 | tf_op jit(solution)/shard_map/ppermute | solution.py:624
  58.3 6.0 %collective-permute-start.33 = (bf16[128,256]{1,0:T(8,128)(2,1)S(1)}, bf16[128,256]{1,0:T(8,128)(2,1)S(1)}, u32[]{:S(2)}, u32[]{:S(2)}) collective-permute-start(bf16[128,256]{1,0:T(8,128)(2,1)S(1)} %collective-permute-done.29.refs_4_), channel_id=1, source_target_pairs={{0,8},{2,10},{8,16},{10,18},{16,24},{18,26},{24,28},{26,30},{28,20... | collective-permute-start | bytes 196616 | tf_op jit(solution)/shard_map/ppermute | solution.py:591
  62.1 4.7 %collective-permute-start.32 = (bf16[128,256]{1,0:T(8,128)(2,1)S(1)}, bf16[128,256]{1,0:T(8,128)(2,1)S(1)}, u32[]{:S(2)}, u32[]{:S(2)}) collective-permute-start(bf16[128,256]{1,0:T(8,128)(2,1)S(1)} %collective-permute-done.30.refs_3_), channel_id=1, source_target_pairs={{0,4},{2,6},{8,0},{10,2},{16,8},{18,10},{24,16},{26,18},{28,24},{3... | collective-permute-start | bytes 196616 | tf_op jit(solution)/shard_map/ppermute | solution.py:591
  64.3 4.4 %collective-permute-start.34 = (bf16[128,256]{1,0:T(8,128)(2,1)S(1)}, bf16[128,256]{1,0:T(8,128)(2,1)S(1)}, u32[]{:S(2)}, u32[]{:S(2)}) collective-permute-start(bf16[128,256]{1,0:T(8,128)(2,1)S(1)} %collective-permute-done.33.refs_6_), channel_id=1, source_target_pairs={{0,8},{2,10},{8,16},{10,18},{16,24},{18,26},{24,28},{26,30},{28,20... | collective-permute-start | bytes 196616 | tf_op jit(solution)/shard_map/ppermute | solution.py:591
  (18 other events, 133.0 us)

commit v3 on v2

--- a/solution.py
+++ b/solution.py
@@ -265,7 +265,7 @@
     return first, last
 
 
-def split_kernel(old, f_ref, q_ref, kp_ref, vp_ref, xc_ref, xo_ref, qo_ref, kvc_ref, kvo_ref, sems):
+def split_kernel(old, f_ref, q_ref, kp_ref, vp_ref, xm_ref, kvm_ref, out_ref, sems):
     core = lax.axis_index("dp") % 2
     copies = []
 
@@ -273,49 +273,78 @@
         copies.append(pltpu.make_async_copy(source, target, sems.at[len(copies)]))
         copies[-1].start()
 
-    for page_ref, first in ((kp_ref, 0), (vp_ref, old)):
-        for out_ref, head in ((kvo_ref, 1 - core), (kvc_ref, core)):
-            at = pl.ds(pl.multiple_of(head * HD, HD), HD)
-            copy(page_ref.at[pl.ds(0, old), :, at], out_ref.at[pl.ds(first, old)])
-    for out_ref, own in ((xo_ref, 1 - core), (xc_ref, core)):
-        for m in range(f_ref.shape[1] // 512):
-            at = pl.ds(pl.multiple_of((2 * m + own) * 256, 256), 256)
-            copy(f_ref.at[:, at], out_ref.at[:, pl.ds(m * 256, 256)])
+    rows, pieces = f_ref.shape[0], f_ref.shape[1] // 256
     half = q_ref.shape[1] // 2
-    copy(q_ref.at[:, pl.ds(pl.multiple_of((1 - core) * half, 128), half)], qo_ref)
+    mine = pl.ds(pl.multiple_of(core * HD, HD), HD)
+    other = pl.ds(pl.multiple_of((1 - core) * HD, HD), HD)
+    at = 0
+    for k in range(pieces):
+        for ref, own in ((out_ref, 1 - core), (xm_ref, core)):
+            lane = pl.multiple_of((k // 2 * 2 + own) * 256 + k % 2 * HD, HD)
+            copy(f_ref.at[:, pl.ds(lane, HD)], ref.at[pl.ds(k * rows, rows), :])
+    at = pieces * rows
+    for h in range(half // HD):
+        lane = pl.multiple_of((1 - core) * half + h * HD, HD)
+        copy(q_ref.at[:, pl.ds(lane, HD)], out_ref.at[pl.ds(at, rows), :])
+        at += rows
+    for n, ref in enumerate((kp_ref, vp_ref)):
+        copy(ref.at[pl.ds(0, old), :, mine], kvm_ref.at[pl.ds(n * old, old)])
+        for p in range(old):
+            copy(ref.at[p, :, other], out_ref.at[pl.ds(at, PAGE), :])
+            at += PAGE
     for c in copies:
         c.wait()
 
 
-def merge_kernel(q_ref, qg_ref, qs_ref):
+def stack_kernel(wk_ref, wv_ref, out_ref, sems):
+    rows = wk_ref.shape[0]
+    copies = [
+        pltpu.make_async_copy(ref, out_ref.at[pl.ds(n * rows, rows), :], sems.at[n])
+        for n, ref in enumerate((wk_ref, wv_ref))
+    ]
+    for c in copies:
+        c.start()
+    for c in copies:
+        c.wait()
+
+
+def merge_kernel(xm_ref, kvm_ref, got_ref, q_ref, x_ref, kv_ref, qs_ref):
     core = lax.axis_index("dp") % 2
-    rows, group = q_ref.shape[0], qg_ref.shape[1] // HD
+    size, count = xm_ref.shape[0], kvm_ref.shape[0]
+    x_ref[:size, :] = xm_ref[...]
+    x_ref[size:, :] = got_ref[:size, :]
+    rows, group = q_ref.shape[0], q_ref.shape[1] // (2 * HD)
     for h in range(group):
         mine = pl.ds(pl.multiple_of((2 * h + core) * rows, rows), rows)
         other = pl.ds(pl.multiple_of((2 * h + 1 - core) * rows, rows), rows)
         qs_ref[mine, :] = q_ref[:, pl.ds(pl.multiple_of((core * group + h) * HD, HD), HD)]
-        qs_ref[other, :] = qg_ref[:, h * HD : (h + 1) * HD]
-
-
-def scale_kernel(
-    chips, lens_ref, tr_ref, inv_ref, gain_ref, a_ref, b_ref, c_ref, d_ref, xs_ref, ss_ref, cos_ref, sin_ref
-):
+        qs_ref[other, :] = got_ref[size + h * rows : size + (h + 1) * rows, :]
+    kv_ref[:count] = kvm_ref[...]
+    first = size + group * rows
+    for n in range(count):
+        kv_ref[count + n] = got_ref[first + n * PAGE : first + (n + 1) * PAGE, :]
+
+
+def scale_kernel(chips, lens_ref, tr_ref, inv_ref, gain_ref, x_ref, got_ref, xs_ref, ss_ref, cos_ref, sin_ref):
     dp = lax.axis_index("dp")
     mp = lax.axis_index("mp")
     chip, core = dp // 2, dp % 2
-    rows = a_ref.shape[0]
-    per_half = a_ref.shape[1] // 256
-    for first, second, owner in ((a_ref, b_ref, core), (c_ref, d_ref, 1 - core)):
+    rows = xs_ref.shape[1] // 2
+    pieces = x_ref.shape[0] // (2 * rows)
+    for n, owner in enumerate((core, 1 - core)):
         at = pl.ds(pl.multiple_of(owner * rows, rows), rows)
-        total = jnp.zeros((rows, 256), jnp.float32)
-        for ref, half in ((first, mp), (second, 1 - mp)):
-            for m in range(per_half):
-                wide = ref[:, m * 256 : (m + 1) * 256].astype(jnp.float32)
-                block = half * (2 * per_half) + 2 * m + core
-                gain = gain_ref[:, pl.ds(pl.multiple_of(block * 256, 256), 256)].astype(jnp.float32)
+        total = jnp.zeros((rows, HD), jnp.float32)
+        for ref, half in ((x_ref, mp), (got_ref, 1 - mp)):
+            for k in range(pieces):
+                first = (n * pieces + k) * rows
+                wide = ref[first : first + rows, :].astype(jnp.float32)
+                lane = (half * pieces + k // 2 * 2 + core) * 256 + k % 2 * HD
+                gain = gain_ref[:, pl.ds(pl.multiple_of(lane, HD), HD)].astype(jnp.float32)
                 total = total + wide * wide
-                xs_ref[half * per_half + m, at, :] = (wide * gain).astype(jnp.bfloat16)
-        ss_ref[at, :] = jnp.broadcast_to(jnp.sum(total, axis=1, keepdims=True), (rows, 128))
+                xs_ref[half * (pieces // 2) + k // 2, at, k % 2 * HD : (k % 2 + 1) * HD] = (
+                    wide * gain
+                ).astype(jnp.bfloat16)
+        ss_ref[at, :] = jnp.broadcast_to(jnp.sum(total, axis=1, keepdims=True), (rows, HD))
     requests = lens_ref.shape[0]
     starts = request_starts(tr_ref, requests)
     tokens = chip * (2 * rows) + lax.broadcasted_iota(jnp.int32, (2 * rows, 128), 0)
@@ -328,8 +357,10 @@
 
 
 def project_kernel(chips, xs_ref, ss_ref, *refs):
-    keys, values = refs[:chips], refs[chips : 2 * chips]
-    send_ref, keep_ref, acc_ref = refs[2 * chips :]
+    rows = xs_ref.shape[2]
+    keys = [ref.at[pl.ds(0, rows), :] for ref in refs[: chips - 1]] + [refs[chips - 1]]
+    values = [ref.at[pl.ds(rows, rows), :] for ref in refs[: chips - 1]] + [refs[chips]]
+    send_ref, keep_ref, acc_ref = refs[chips + 1 :]
     dp = lax.axis_index("dp")
     chip, core = dp // 2, dp % 2
     place = ring_place(chip, chips)
@@ -382,8 +413,8 @@
 
 def cached_kernel(chips, pages_dev, old, away, lens_ref, table_ref, tr_ref, qs_ref, *refs):
     members = chips // 2
-    near, far = refs[:members], refs[members : 2 * members]
-    outs, (kbuf, vbuf, m_ref, l_ref, acc_ref, slot_of) = refs[2 * members : -6], refs[-6:]
+    blocks = refs[:members]
+    outs, (kbuf, vbuf, m_ref, l_ref, acc_ref, slot_of) = refs[members:-6], refs[-6:]
     dp = lax.axis_index("dp")
     chip, core = dp // 2, dp % 2
     who = chip ^ away
@@ -428,15 +459,15 @@
 
     for e in range(members):
         source = chip ^ e
-        for block, owner in ((near[e], 2 * source + core), (far[e], 2 * source + 1 - core)):
+        for part, owner in ((0, 2 * source + core), (2 * old, 2 * source + 1 - core)):
             for s in range(old):
                 slot = slot_of[owner * pages_dev + s]
 
                 @pl.when(slot >= 0)
-                def _(block=block, s=s, slot=slot):
+                def _(e=e, part=part, s=s, slot=slot):
                     at = pl.ds(pl.multiple_of(slot * PAGE, PAGE), PAGE)
-                    kbuf[at, :] = block[s]
-                    vbuf[at, :] = block[old + s]
+                    kbuf[at, :] = blocks[e][part + s]
+                    vbuf[at, :] = blocks[e][part + old + s]
 
     step_pages = STEP_PAGES
     pad = pl.ds(pl.multiple_of(base * PAGE, PAGE), (step_pages - 1) * PAGE)
@@ -469,8 +500,8 @@
     chips, pages_dev, lens_ref, table_ref, tr_ref, qs_ref, m0_ref, l0_ref, acc0_ref, back_ref, *refs
 ):
     fresh = refs[:chips]
-    atto_ref, attc_ref, no_ref, nc_ref, info_ref = refs[chips : chips + 5]
-    nbuf, m_ref, l_ref, acc_ref, out_ref, new_at, new_lo, new_hi = refs[chips + 5 :]
+    send_ref, attc_ref, nc_ref, info_ref = refs[chips : chips + 4]
+    nbuf, m_ref, l_ref, acc_ref, out_ref, new_at, new_lo, new_hi = refs[chips + 4 :]
     dp = lax.axis_index("dp")
     chip, core = dp // 2, dp % 2
     place = ring_place(chip, chips)
@@ -532,11 +563,14 @@
     for h in range(group):
         out_ref[:, h * HD : (h + 1) * HD] = result[:, h * toks : (h + 1) * toks].T.astype(jnp.bfloat16)
     attc_ref[...] = out_ref[pl.ds(pl.multiple_of(core * rows, rows), rows), :]
-    atto_ref[...] = out_ref[pl.ds(pl.multiple_of((1 - core) * rows, rows), rows), :]
+    other = pl.ds(pl.multiple_of((1 - core) * rows, rows), rows)
+    for h in range(group):
+        first = 2 * pages_dev * PAGE + h * rows
+        send_ref[first : first + rows, :] = out_ref[other, h * HD : (h + 1) * HD]
 
     row = lax.broadcasted_iota(jnp.int32, (PAGE, 2 * toks), 0)
     column = lax.broadcasted_iota(jnp.int32, (PAGE, 2 * toks), 1)
-    for ref, owner in ((no_ref, dp + 1 - 2 * core), (nc_ref, dp)):
+    for ref, owner in ((send_ref, dp + 1 - 2 * core), (nc_ref, dp)):
         for s in range(pages_dev):
             page = owner * pages_dev + s
             at, low_row, high_row = new_at[page], new_lo[page], new_hi[page]
@@ -546,29 +580,36 @@
                 shifted = at + toks
                 first = pl.multiple_of(shifted // toks * toks, toks)
                 chosen = (column + first == row + shifted) & (row >= low_row) & (row < high_row)
-                ref[s] = jnp.dot(
+                found = jnp.dot(
                     jnp.where(chosen, 1.0, 0.0).astype(jnp.bfloat16),
                     nbuf[pl.ds(first, 2 * toks), :],
                     preferred_element_type=jnp.float32,
                 ).astype(jnp.bfloat16)
+                ref[2 * s * PAGE : (2 * s + 1) * PAGE, :] = found[:, :HD]
+                ref[(2 * s + 1) * PAGE : (2 * s + 2) * PAGE, :] = found[:, HD:]
 
     for s in range(pages_dev):
         info_ref[2 * s] = new_lo[dp * pages_dev + s]
         info_ref[2 * s + 1] = new_hi[dp * pages_dev + s]
 
 
-def join_kernel(info_ref, attc_ref, attr_ref, nc_ref, nr_ref, kp_ref, vp_ref, att_ref, ko_ref, vo_ref):
+def join_kernel(info_ref, attc_ref, nc_ref, got_ref, kp_ref, vp_ref, att_ref, ko_ref, vo_ref):
     core = lax.axis_index("dp") % 2
-    half = attc_ref.shape[1]
+    rows, half = attc_ref.shape
+    pages = kp_ref.shape[0]
     att_ref[:, pl.ds(pl.multiple_of(core * half, HD), half)] = attc_ref[...]
-    att_ref[:, pl.ds(pl.multiple_of((1 - core) * half, HD), half)] = attr_ref[...]
+    for h in range(half // HD):
+        first = 2 * pages * PAGE + h * rows
+        lane = pl.multiple_of((1 - core) * half + h * HD, HD)
+        att_ref[:, pl.ds(lane, HD)] = got_ref[first : first + rows, :]
     row = lax.broadcasted_iota(jnp.int32, (PAGE, HD), 0)
-    for s in range(kp_ref.shape[0]):
+    for s in range(pages):
         chosen = (row >= info_ref[2 * s]) & (row < info_ref[2 * s + 1])
-        for ref, head in ((nc_ref, core), (nr_ref, 1 - core)):
+        for ref, head in ((nc_ref, core), (got_ref, 1 - core)):
             at = pl.ds(pl.multiple_of(head * HD, HD), HD)
-            ko_ref[s, :, at] = jnp.where(chosen, ref[s, :, :HD], kp_ref[s, :, at])
-            vo_ref[s, :, at] = jnp.where(chosen, ref[s, :, HD:], vp_ref[s, :, at])
+            first = 2 * s * PAGE
+            ko_ref[s, :, at] = jnp.where(chosen, ref[first : first + PAGE, :], kp_ref[s, :, at])
+            vo_ref[s, :, at] = jnp.where(chosen, ref[first + PAGE : first + 2 * PAGE, :], vp_ref[s, :, at])
 
 
 def call(
@@ -617,76 +658,72 @@
     columns = group * toks
     core_pairs = [(i, i ^ 1) for i in range(dp_count)]
     mp_pairs = [(0, 1), (1, 0)]
-    both_pairs = [(2 * i + j, 2 * (i ^ 1) + (1 - j)) for i in range(dp_count) for j in range(2)]
     requests_tile = token_request.reshape(-1, 128)
 
     def exchange(array, e, swap=0):
         return lax.ppermute(array, "dp", [(i, i ^ (2 * e) ^ swap) for i in range(dp_count)])
 
-    w_got = {0: [w_key, w_value]}
-    right, left = ring_send(chips, [w_key, w_value], 1), ring_send(chips, [w_key, w_value], -1)
-    w_got[-1], w_got[1] = right, left
-    x_mine, x_other, q_other, kv_mine, kv_other = call(
+    last = chips // 2
+    w_rows = w_key.shape[0]
+    (w_both,) = call(
+        stack_kernel,
+        [((2 * w_rows, w_key.shape[1]), bf)],
+        scratch=[pltpu.SemaphoreType.DMA((2,))],
+        ins=2,
+        far=(0, 1),
+        limit=SPLIT_LIMIT,
+        name="stack",
+    )(w_key, w_value)
+
+    def hop(array, step):
+        return ring_send(chips, [array], step)[0]
+
+    w_got = {0: w_both, -1: hop(w_both, 1), 1: hop(w_both, -1)}
+    pieces = half_width // 256
+    bundle = (pieces + group) * rows + 2 * old * PAGE
+    x_mine, kv_mine, core_send = call(
         functools.partial(split_kernel, old),
-        [
-            ((rows, half_width // 2), bf),
-            ((rows, half_width // 2), bf),
-            ((rows, group * HD), bf),
-            ((2 * old, PAGE, HD), bf),
-            ((2 * old, PAGE, HD), bf),
-        ],
-        scratch=[pltpu.SemaphoreType.DMA((4 + 2 * (half_width // 512) + 1,))],
+        [((pieces * rows, HD), bf), ((2 * old, PAGE, HD), bf), ((bundle, HD), bf)],
+        scratch=[pltpu.SemaphoreType.DMA((2 * pieces + group + 2 + 2 * old,))],
         ins=4,
         far=(0, 1, 2, 3),
         limit=SPLIT_LIMIT,
         name="split",
     )(features, queries, key_pool, value_pool)
-    x_b = lax.ppermute(x_mine, "mp", mp_pairs)
-    x_c = lax.ppermute(x_other, "dp", core_pairs)
-    x_d = lax.ppermute(x_other, ("dp", "mp"), both_pairs)
-    q_got = lax.ppermute(q_other, "dp", core_pairs)
-    kv_got = lax.ppermute(kv_other, "dp", core_pairs)
-    z_near, z_far = exchange(kv_mine, 2), exchange(kv_other, 2, 1)
-    y_near, y_far = exchange(kv_mine, 1), exchange(kv_other, 1, 1)
-    for d in range(2, chips // 2):
-        if d == chips // 2 - 1:
-            w_first, z_near, z_far, y_near, y_far, q_got = lax.optimization_barrier(
-                (right[0], z_near, z_far, y_near, y_far, q_got)
-            )
-            right = [w_first, right[1]]
-        right, left = ring_send(chips, right, 1), ring_send(chips, left, -1)
-        w_got[-d], w_got[d] = right, left
-    near = [kv_mine, y_near, z_near, exchange(y_near, 2)]
-    far = [kv_got, y_far, z_far, exchange(z_far, 1)]
-
-    (q_rows,) = call(merge_kernel, [((columns, HD), bf)], ins=2, name="merge")(queries, q_got)
-    q_away = exchange(q_rows, chips // 2)
+    core_got = lax.ppermute(core_send, "dp", core_pairs)
+    x_here, kv, q_rows = call(
+        merge_kernel,
+        [((2 * pieces * rows, HD), bf), ((4 * old, PAGE, HD), bf), ((columns, HD), bf)],
+        ins=4,
+        name="merge",
+    )(x_mine, kv_mine, core_got, queries)
+    x_there = lax.ppermute(x_here, "mp", mp_pairs)
+    q_away = exchange(q_rows, last)
+    kv_z, kv_y = exchange(kv, 2), exchange(kv, 1)
+
+    right, x_here = lax.optimization_barrier((w_got[-1], x_here))
+    w_got[-2], w_got[2] = hop(right, 1), hop(w_got[1], -1)
+    right, x_there, kv_y = lax.optimization_barrier((w_got[-2], x_there, kv_y))
+    w_got[-3], w_got[3] = hop(right, 1), hop(w_got[2], -1)
+    kv_d = exchange(kv_y, 2)
     inverse = (THETA ** (-(np.arange(HD) % (HD // 2)) * 2.0 / HD)).astype(np.float32)[None, :]
     scaled, squares, cosine, sine = call(
         functools.partial(scale_kernel, chips),
-        [((chips, toks, 256), bf), ((toks, 128), f32), ((toks, HD), f32), ((toks, HD), f32)],
-        ins=8,
+        [((chips, toks, w_rows), bf), ((toks, HD), f32), ((toks, HD), f32), ((toks, HD), f32)],
+        ins=6,
         smem=(0,),
         name="scale",
-    )(
-        cache_lens,
-        requests_tile,
-        jnp.asarray(inverse),
-        norm_gain.reshape(1, -1),
-        x_mine,
-        x_b,
-        x_c,
-        x_d,
-    )
-    w_got[chips // 2] = ring_send(chips, right[:1], 1) + ring_send(chips, left[1:], -1)
-    scaled, near[3], far[3], q_away = lax.optimization_barrier((scaled, near[3], far[3], q_away))
+    )(cache_lens, requests_tile, jnp.asarray(inverse), norm_gain.reshape(1, -1), x_here, x_there)
+    right, kv_z, q_away = lax.optimization_barrier((w_got[-3], kv_z, q_away))
+    w_last = [hop(right[:w_rows], 1), hop(w_got[3][w_rows:], -1)]
+    scaled, kv_d = lax.optimization_barrier((scaled, kv_d))
     part_send, part_keep = call(
         functools.partial(project_kernel, chips),
         [((toks, 3 * HD), f32), ((toks, 3 * HD), f32)],
         scratch=[pltpu.VMEM((toks, 4 * HD), f32)],
-        ins=2 + 2 * chips,
+        ins=2 + chips + 1,
         name="project",
-    )(scaled, squares, *[w_got[o][0] for o in offsets], *[w_got[o][1] for o in offsets])
+    )(scaled, squares, *[w_got[o] for o in offsets[:-1]], *w_last)
     part_got = lax.ppermute(part_send, "dp", core_pairs)
 
     (fresh,) = call(
@@ -712,10 +749,10 @@
                 pltpu.VMEM((HD, columns), f32),
                 table,
             ],
-            ins=4 + chips,
+            ins=4 + chips // 2,
             smem=(0, 1),
             name=name,
-        )(cache_lens, page_table, requests_tile, q, *near, *far)
+        )(cache_lens, page_table, requests_tile, q, kv, kv_y, kv_z, kv_d)
 
     (away,) = cached(q_away, chips // 2, [((HD + 16, columns), bf)], "attend_cached_away")
     here = cached(
@@ -729,13 +766,13 @@
     back = exchange(beside[2], chips // 2)
     top, total, acc = beside[3]
 
-    att_other, att_mine, rows_other, rows_mine, info = call(
+    rows_bundle = 2 * pages_dev * PAGE
+    last_send, att_mine, rows_mine, info = call(
         functools.partial(fresh_kernel, chips, pages_dev),
         [
+            ((rows_bundle + group * rows, HD), bf),
             ((rows, group * HD), bf),
-            ((rows, group * HD), bf),
-            ((pages_dev, PAGE, 2 * HD), bf),
-            ((pages_dev, PAGE, 2 * HD), bf),
+            ((rows_bundle, HD), bf),
             ((2 * pages_dev,), i32),
         ],
         scratch=[
@@ -750,7 +787,7 @@
         ],
         ins=8 + chips,
         smem=(0, 1),
-        out_smem=(4,),
+        out_smem=(3,),
         name="attend_new",
     )(
         cache_lens,
@@ -763,15 +800,14 @@
         back,
         *[new[o] for o in offsets],
     )
-    rows_got = lax.ppermute(rows_other, "dp", core_pairs)
-    att_got = lax.ppermute(att_other, "dp", core_pairs)
+    last_got = lax.ppermute(last_send, "dp", core_pairs)
     attended, keys_out, values_out = call(
         join_kernel,
         [(queries.shape, bf), (key_pool.shape, bf), (value_pool.shape, bf)],
-        ins=7,
+        ins=6,
         smem=(0,),
         name="join",
-    )(info, att_mine, att_got, rows_mine, rows_got, key_pool, value_pool)
+    )(info, att_mine, rows_mine, last_got, key_pool, value_pool)
     return attended, keys_out, values_out
 
 

time: 75 us -> 78.5 us (1.047)
  waiting for transfers between devices: 15 us -> 31.2 us
  starting transfers between devices: 43.8 us -> 29.2 us
  Pallas kernels: 13.8 us -> 15.6 us
    ppermute x21 -> x15, starting transfers between devices: 27.5 us -> 16.3 us  [ring_send(): lax.ppermute(a, 'dp', ring_pairs(chips, step, swap * n))]
    ppermute x21 -> x15, waiting for transfers between devices: 9.12 us -> 19.8 us  [ring_send(): lax.ppermute(a, 'dp', ring_pairs(chips, step, swap * n))]
    ppermute x8 -> x5, waiting for transfers between devices: 2.79 us -> 8.48 us  [exchange(): lax.ppermute(array, 'dp', [(i, i ^ 2 * e ^ swap) for i in range(dp_count)])]
    ppermute x7 -> x3, starting transfers between devices: 4.01 us -> 2.08 us  [the longest x1 1.49 us: ring_body(): x_there = lax.ppermute(x_here, 'mp', mp_pairs)]
    pallas_call x4 -> x5, Pallas kernels: 5.88 us -> 7.71 us  [the longest x1 2.77 us: ring_body(): call(functools.partial(fresh_kernel, chips, pages_dev), [((rows_bundle +...]
    ppermute x8 -> x5, starting transfers between devices: 12.2 us -> 10.7 us  [exchange(): lax.ppermute(array, 'dp', [(i, i ^ 2 * e ^ swap) for i in range(dp_count)])]
    ppermute x7 -> x3, waiting for transfers between devices: 2.15 us -> 1.53 us  [the longest x1 1.52 us: ring_body(): last_got = lax.ppermute(last_send, 'dp', core_pairs)]
  transfers between devices with their start and end apart: 37 -> 24, of which waited for: 12 -> 15; matrix products, arithmetic and copies ran while one was open for 0% -> 0% of each run, Pallas kernels for 9% -> 11%
where the time goes in v3:
time: 78.5 us; the launch traced here: 77.6 us
  waiting for transfers between devices  31.2 us (40%)
  starting transfers between devices  29.2 us (37%)
  Pallas kernels  15.6 us (20%)
  between operations  0.86 us (1%)
    ppermute x15, waiting for transfers between devices, ring_send(): lax.ppermute(a, 'dp', ring_pairs(chips, step, swap * n))  19.8 us
    ppermute x15, starting transfers between devices, ring_send(): lax.ppermute(a, 'dp', ring_pairs(chips, step, swap * n))  16.3 us
    ppermute x5, starting transfers between devices, exchange(): lax.ppermute(array, 'dp', [(i, i ^ 2 * e ^ swap) for i in range(dp_count)])  10.7 us
    ppermute x5, waiting for transfers between devices, exchange(): lax.ppermute(array, 'dp', [(i, i ^ 2 * e ^ swap) for i in range(dp_count)])  8.48 us
    pallas_call x2, Pallas kernels, cached(): call(functools.partial(cached_kernel, chips, pages_dev, old, away), outs,...  5.89 us
    pallas_call x1, Pallas kernels, ring_body(): call(functools.partial(fresh_kernel, chips, pages_dev), [((rows_bundle +...  2.77 us
    pallas_call x1, Pallas kernels, ring_body(): call(functools.partial(split_kernel, old), [((pieces * rows, HD), bf), ((...  2.18 us
    pallas_call x1, Pallas kernels, ring_body(): call(stack_kernel, [((2 * w_rows, w_key.shape[1]), bf)], scratch=[pltpu.S...  1.7 us
  transfers between devices with their start and end apart: 24, of which 15 were waited for; matrix products, arithmetic and copies ran while one was open for 0% of the time, Pallas kernels for 11%

profile of v3, /device:TPU:0, one launch (start us, length us, event | category | flops | bytes accessed | tf_op | source)
XLA Modules:
  0.0 77.6 jit_solution(9259641333453288686)
XLA Ops:
  0.6 2.2 %split.1 = (bf16[512,128]{1,0:T(8,128)(2,1)}, bf16[4,128,128]{2,1,0:T(8,128)(2,1)}, bf16[1280,128]{1,0:T(8,128)(2,1)}) custom-call(bf16[64,2048]{1,0:T(8,128)(2,1)} %f_ref.1, bf16[64,1024]{1,0:T(8,128)(2,1)} %q_ref.3, bf16[3,128,256]{2,1,0:T(8,128)(2,1)} %kp_ref.3, bf16[3,128,256]{2,1,0:T(8,128)(2,1)} %vp_ref.3), custom_call_target="tpu_custom_call" | custom-call | tf_op jit(solution)/shard_map/split/pallas_call | solution.py:684
  3.4 1.7 %stack.1.refs_0_ = bf16[512,256]{1,0:T(8,128)(2,1)} custom-call(bf16[256,256]{1,0:T(8,128)(2,1)} %wk_ref.1, bf16[256,256]{1,0:T(8,128)(2,1)} %wv_ref.1), custom_call_target="tpu_custom_call" | custom-call | tf_op jit(solution)/shard_map/stack/pallas_call | solution.py:668
  5.1 2.7 %collective-permute-start.6 = (bf16[512,256]{1,0:T(8,128)(2,1)}, bf16[512,256]{1,0:T(8,128)(2,1)S(1)}, u32[]{:S(2)}, u32[]{:S(2)}) collective-permute-start(bf16[512,256]{1,0:T(8,128)(2,1)} %stack.1.refs_0_), channel_id=1, source_target_pairs={{0,4},{2,6},{8,0},{10,2},{16,8},{18,10},{24,16},{26,18},{28,24},{3... | collective-permute-start | bytes 786440 | tf_op jit(solution)/shard_map/ppermute | solution.py:632
  7.9 7.0 %collective-permute-done.6.refs_1_ = bf16[512,256]{1,0:T(8,128)(2,1)S(1)} collective-permute-done((bf16[512,256]{1,0:T(8,128)(2,1)}, bf16[512,256]{1,0:T(8,128)(2,1)S(1)}, u32[]{:S(2)}, u32[]{:S(2)}) %collective-permute-start.6) | collective-permute-done | bytes 262176 | tf_op jit(solution)/shard_map/ppermute | solution.py:632
  14.9 1.7 %collective-permute-start.7 = (bf16[512,256]{1,0:T(8,128)(2,1)S(1)}, bf16[512,256]{1,0:T(8,128)(2,1)S(1)}, u32[]{:S(2)}, u32[]{:S(2)}) collective-permute-start(bf16[512,256]{1,0:T(8,128)(2,1)S(1)} %collective-permute-done.6.refs_1_), channel_id=1, source_target_pairs={{0,4},{2,6},{8,0},{10,2},{16,8},{18,10},{24,16},{26,18},{28,24},{3... | collective-permute-start | bytes 786440 | tf_op jit(solution)/shard_map/ppermute | solution.py:632
  17.1 1.7 %collective-permute-start.4 = (bf16[8,128,128]{2,1,0:T(8,128)(2,1)S(1)}, bf16[8,128,128]{2,1,0:T(8,128)(2,1)S(1)}, u32[]{:S(2)}, u32[]{:S(2)}) collective-permute-start(bf16[8,128,128]{2,1,0:T(8,128)(2,1)S(1)} %get-tuple-element.47.refs_0_), channel_id=1, source_target_pairs={{0,4},{2,6},{4,0},{6,2},{8,12},{10,14},{12,8},{14,10},{16,20},{18,... | collective-permute-start | bytes 786440 | tf_op jit(solution)/shard_map/ppermute | solution.py:664
  18.8 1.5 %collective-permute-start.3 = (bf16[1024,128]{1,0:T(8,128)(2,1)S(1)}, bf16[1024,128]{1,0:T(8,128)(2,1)S(1)}, u32[]{:S(2)}, u32[]{:S(2)}) collective-permute-start(bf16[1024,128]{1,0:T(8,128)(2,1)S(1)} %get-tuple-element.45.x_ref), channel_id=1, source_target_pairs={{0,1},{1,0},{2,3},{3,2},{4,5},{5,4},{6,7},{7,6},{8,9},{9,8},{10,11... | collective-permute-start | bytes 786440 | tf_op jit(solution)/shard_map/ppermute | solution.py:700
  20.2 1.6 %collective-permute-start.10 = (bf16[8,128,128]{2,1,0:T(8,128)(2,1)S(1)}, bf16[8,128,128]{2,1,0:T(8,128)(2,1)S(1)}, u32[]{:S(2)}, u32[]{:S(2)}) collective-permute-start(bf16[8,128,128]{2,1,0:T(8,128)(2,1)S(1)} %get-tuple-element.47.refs_0_), channel_id=1, source_target_pairs={{0,8},{2,10},{4,12},{6,14},{8,0},{10,2},{12,4},{14,6},{16,24},{18,... | collective-permute-start | bytes 786440 | tf_op jit(solution)/shard_map/ppermute | solution.py:664
  21.8 2.3 %collective-permute-done.7.refs_3_ = bf16[512,256]{1,0:T(8,128)(2,1)S(1)} collective-permute-done((bf16[512,256]{1,0:T(8,128)(2,1)S(1)}, bf16[512,256]{1,0:T(8,128)(2,1)S(1)}, u32[]{:S(2)}, u32[]{:S(2)}) %collective-permute-start.7) | collective-permute-done | bytes 262176 | tf_op jit(solution)/shard_map/ppermute | solution.py:632
  24.1 1.7 %collective-permute-start.8 = (bf16[512,256]{1,0:T(8,128)(2,1)S(1)}, bf16[512,256]{1,0:T(8,128)(2,1)S(1)}, u32[]{:S(2)}, u32[]{:S(2)}) collective-permute-start(bf16[512,256]{1,0:T(8,128)(2,1)S(1)} %collective-permute-done.7.refs_3_), channel_id=1, source_target_pairs={{0,4},{2,6},{8,0},{10,2},{16,8},{18,10},{24,16},{26,18},{28,24},{3... | collective-permute-start | bytes 786440 | tf_op jit(solution)/shard_map/ppermute | solution.py:632
  26.0 3.9 %collective-permute-done.4.refs_1_ = bf16[8,128,128]{2,1,0:T(8,128)(2,1)S(1)} collective-permute-done((bf16[8,128,128]{2,1,0:T(8,128)(2,1)S(1)}, bf16[8,128,128]{2,1,0:T(8,128)(2,1)S(1)}, u32[]{:S(2)}, u32[]{:S(2)}) %collective-permute-start.4) | collective-permute-done | bytes 262176 | tf_op jit(solution)/shard_map/ppermute | solution.py:664
  29.9 4.1 %collective-permute-start.11 = (bf16[512,128]{1,0:T(8,128)(2,1)S(1)}, bf16[512,128]{1,0:T(8,128)(2,1)S(1)}, u32[]{:S(2)}, u32[]{:S(2)}) collective-permute-start(bf16[512,128]{1,0:T(8,128)(2,1)S(1)} %get-tuple-element.43.qs_ref), channel_id=1, source_target_pairs={{0,16},{2,18},{4,20},{6,22},{8,24},{10,26},{12,28},{14,30},{16,0},... | collective-permute-start | bytes 393224 | tf_op jit(solution)/shard_map/ppermute | solution.py:664
  34.6 2.7 %collective-permute-done.8.refs_5_ = bf16[512,256]{1,0:T(8,128)(2,1)S(1)} collective-permute-done((bf16[512,256]{1,0:T(8,128)(2,1)S(1)}, bf16[512,256]{1,0:T(8,128)(2,1)S(1)}, u32[]{:S(2)}, u32[]{:S(2)}) %collective-permute-start.8) | collective-permute-done | bytes 262176 | tf_op jit(solution)/shard_map/ppermute | solution.py:632
  37.4 3.0 %collective-permute-done.11.qs_ref = bf16[512,128]{1,0:T(8,128)(2,1)S(1)} collective-permute-done((bf16[512,128]{1,0:T(8,128)(2,1)S(1)}, bf16[512,128]{1,0:T(8,128)(2,1)S(1)}, u32[]{:S(2)}, u32[]{:S(2)}) %collective-permute-start.11) | collective-permute-done | bytes 131104 | tf_op jit(solution)/shard_map/ppermute | solution.py:664
  41.7 1.0 %scale.1 = (bf16[8,128,256]{2,1,0:T(8,128)(2,1)S(1)}, f32[128,128]{1,0:T(8,128)S(1)}, f32[128,128]{1,0:T(8,128)S(1)}, f32[128,128]{1,0:T(8,128)S(1)}) custom-call(s32[3]{0:T(128)S(1)} %copy-done.8, s32[8,128]{1,0:T(8,128)S(1)} %bitcast.1, f32[1,128]{1,0:T(1,128)S(1)} %copy-done.9, bf16[1,4096]{1,0:T(2,128)(2,1)S(1)} %reshape.13.gain_ref, ...), custom_call_target="tpu_custom_call" | custom-call | tf_op jit(solution)/shard_map/scale/pallas_call | solution.py:710
  42.7 1.5 %collective-permute-done.5.refs_3_ = bf16[8,128,128]{2,1,0:T(8,128)(2,1)S(1)} collective-permute-done((bf16[8,128,128]{2,1,0:T(8,128)(2,1)S(1)}, bf16[8,128,128]{2,1,0:T(8,128)(2,1)S(1)}, u32[]{:S(2)}, u32[]{:S(2)}) %collective-permute-start.5) | collective-permute-done | bytes 262176 | tf_op jit(solution)/shard_map/ppermute | solution.py:664
  44.2 1.2 %collective-permute-done.13.refs_8_ = bf16[256,256]{1,0:T(8,128)(2,1)S(1)} collective-permute-done((bf16[256,256]{1,0:T(8,128)(2,1)S(1)}, bf16[256,256]{1,0:T(8,128)(2,1)S(1)}, u32[]{:S(2)}, u32[]{:S(2)}) %collective-permute-start.13) | collective-permute-done | bytes 131104 | tf_op jit(solution)/shard_map/ppermute | solution.py:632
  46.4 1.4 %collective-permute-done.14.got_ref = f32[128,384]{1,0:T(8,128)S(1)} collective-permute-done((f32[128,384]{1,0:T(8,128)S(1)}, f32[128,384]{1,0:T(8,128)S(1)}, u32[]{:S(2)}, u32[]{:S(2)}) %collective-permute-start.14) | collective-permute-done | bytes 196640 | tf_op jit(solution)/shard_map/ppermute | solution.py:727
  47.9 2.3 %collective-permute-start.15 = (bf16[128,256]{1,0:T(8,128)(2,1)S(1)}, bf16[128,256]{1,0:T(8,128)(2,1)S(1)}, u32[]{:S(2)}, u32[]{:S(2)}) collective-permute-start(bf16[128,256]{1,0:T(8,128)(2,1)S(1)} %rotary.1.refs_0_), channel_id=1, source_target_pairs={{0,8},{2,10},{8,16},{10,18},{16,24},{18,26},{24,28},{26,30},{28,20... | collective-permute-start | bytes 196616 | tf_op jit(solution)/shard_map/ppermute | solution.py:632
  50.6 2.1 %attend_cached_away.1 = bf16[144,512]{1,0:T(8,128)(2,1)S(1)} custom-call(s32[3]{0:T(128)S(1)} %copy-done.8, s32[3,25]{1,0:T(4,128)S(1)} %copy-done.7, s32[8,128]{1,0:T(8,128)S(1)} %bitcast.2, bf16[512,128]{1,0:T(8,128)(2,1)S(1)} %collective-permute-done.11.qs_ref, bf16[8,128,128]{2,1,0:T(8,128)(2,1)S(1)} %get-tuple-element.47.refs_0_, ...), custom_call_target="tpu_custom_call" | custom-call | tf_op jit(solution)/shard_map/attend_cached_away/pallas_call | solution.py:741
  52.9 1.6 %collective-permute-done.16.refs_1_ = bf16[128,256]{1,0:T(8,128)(2,1)S(1)} collective-permute-done((bf16[128,256]{1,0:T(8,128)(2,1)S(1)}, bf16[128,256]{1,0:T(8,128)(2,1)S(1)}, u32[]{:S(2)}, u32[]{:S(2)}) %collective-permute-start.16) | collective-permute-done | bytes 65568 | tf_op jit(solution)/shard_map/ppermute | solution.py:632
  54.5 1.3 %collective-permute-start.17 = (bf16[128,256]{1,0:T(8,128)(2,1)S(1)}, bf16[128,256]{1,0:T(8,128)(2,1)S(1)}, u32[]{:S(2)}, u32[]{:S(2)}) collective-permute-start(bf16[128,256]{1,0:T(8,128)(2,1)S(1)} %collective-permute-done.15.refs_2_), channel_id=1, source_target_pairs={{0,8},{2,10},{8,16},{10,18},{16,24},{18,26},{24,28},{26,30},{28,20... | collective-permute-start | bytes 196616 | tf_op jit(solution)/shard_map/ppermute | solution.py:632
  55.9 0.7 collective-permute-start.18
  56.6 2.8 %collective-permute-start.19 = (bf16[144,512]{1,0:T(8,128)(2,1)S(1)}, bf16[144,512]{1,0:T(8,128)(2,1)S(1)}, u32[]{:S(2)}, u32[]{:S(2)}) collective-permute-start(bf16[144,512]{1,0:T(8,128)(2,1)S(1)} %attend_cached_away.1), channel_id=1, source_target_pairs={{0,16},{2,18},{4,20},{6,22},{8,24},{10,26},{12,28},{14,30},{16,0},... | collective-permute-start | bytes 442376 | tf_op jit(solution)/shard_map/ppermute | solution.py:664
  59.4 3.7 %attend_cached_here.1 = (f32[1,512]{1,0:T(1,128)S(1)}, f32[1,512]{1,0:T(1,128)S(1)}, f32[128,512]{1,0:T(8,128)S(1)}) custom-call(s32[3]{0:T(128)S(1)} %copy-done.8, s32[3,25]{1,0:T(4,128)S(1)} %copy-done.7, s32[8,128]{1,0:T(8,128)S(1)} %bitcast.3, bf16[512,128]{1,0:T(8,128)(2,1)S(1)} %get-tuple-element.43.qs_ref, ...), custom_call_target="tpu_custom_call" | custom-call | tf_op jit(solution)/shard_map/attend_cached_here/pallas_call | solution.py:741
  63.2 2.2 %collective-permute-start.21 = (bf16[128,256]{1,0:T(8,128)(2,1)S(1)}, bf16[128,256]{1,0:T(8,128)(2,1)S(1)}, u32[]{:S(2)}, u32[]{:S(2)}) collective-permute-start(bf16[128,256]{1,0:T(8,128)(2,1)S(1)} %collective-permute-done.17.refs_4_), channel_id=1, source_target_pairs={{0,8},{2,10},{8,16},{10,18},{16,24},{18,26},{24,28},{26,30},{28,20... | collective-permute-start | bytes 196616 | tf_op jit(solution)/shard_map/ppermute | solution.py:632
  65.4 2.1 %collective-permute-done.21.refs_6_ = bf16[128,256]{1,0:T(8,128)(2,1)S(1)} collective-permute-done((bf16[128,256]{1,0:T(8,128)(2,1)S(1)}, bf16[128,256]{1,0:T(8,128)(2,1)S(1)}, u32[]{:S(2)}, u32[]{:S(2)}) %collective-permute-start.21) | collective-permute-done | bytes 65568 | tf_op jit(solution)/shard_map/ppermute | solution.py:632
  67.5 2.2 %collective-permute-start.22 = (bf16[128,256]{1,0:T(8,128)(2,1)S(1)}, bf16[128,256]{1,0:T(8,128)(2,1)S(1)}, u32[]{:S(2)}, u32[]{:S(2)}) collective-permute-start(bf16[128,256]{1,0:T(8,128)(2,1)S(1)} %collective-permute-done.21.refs_6_), channel_id=1, source_target_pairs={{0,8},{2,10},{8,16},{10,18},{16,24},{18,26},{24,28},{26,30},{28,20... | collective-permute-start | bytes 196616 | tf_op jit(solution)/shard_map/ppermute | solution.py:632
  69.7 2.1 %collective-permute-done.22.refs_7_ = bf16[128,256]{1,0:T(8,128)(2,1)S(1)} collective-permute-done((bf16[128,256]{1,0:T(8,128)(2,1)S(1)}, bf16[128,256]{1,0:T(8,128)(2,1)S(1)}, u32[]{:S(2)}, u32[]{:S(2)}) %collective-permute-start.22) | collective-permute-done | bytes 65568 | tf_op jit(solution)/shard_map/ppermute | solution.py:632
  71.7 2.8 %attend_new.1 = (bf16[1024,128]{1,0:T(8,128)(2,1)S(1)}, bf16[64,512]{1,0:T(8,128)(2,1)S(1)}, bf16[768,128]{1,0:T(8,128)(2,1)S(1)}, s32[6]{0:T(128)S(1)}) custom-call(s32[3]{0:T(128)S(1)} %copy-done.8, s32[3,25]{1,0:T(4,128)S(1)} %copy-done.7, s32[8,128]{1,0:T(8,128)S(1)} %bitcast.4, bf16[512,128]{1,0:T(8,128)(2,1)S(1)} %get-tuple-element.43.qs_ref, ...), custom_call_target="tpu_custom_call" | custom-call | tf_op jit(solution)/shard_map/attend_new/pallas_call | solution.py:770
  74.6 1.5 %collective-permute-done.23.got_ref = bf16[1024,128]{1,0:T(8,128)(2,1)S(1)} collective-permute-done((bf16[1024,128]{1,0:T(8,128)(2,1)S(1)}, bf16[1024,128]{1,0:T(8,128)(2,1)S(1)}, u32[]{:S(2)}, u32[]{:S(2)}) %collective-permute-start.23) | collective-permute-done | bytes 262176 | tf_op jit(solution)/shard_map/ppermute | solution.py:803
  76.1 1.5 %join.1 = (bf16[64,1024]{1,0:T(8,128)(2,1)}, bf16[3,128,256]{2,1,0:T(8,128)(2,1)}, bf16[3,128,256]{2,1,0:T(8,128)(2,1)}) custom-call(s32[6]{0:T(128)S(1)} %get-tuple-element.73.info_ref, bf16[64,512]{1,0:T(8,128)(2,1)S(1)} %get-tuple-element.74.attc_ref, bf16[768,128]{1,0:T(8,128)(2,1)S(1)} %get-tuple-element.75.nc_ref, ...), custom_call_target="tpu_custom_call" | custom-call | tf_op jit(solution)/shard_map/join/pallas_call | solution.py:804
  (51 shorter events, 4.8 us)
Async XLA Ops:
  2.8 13.8 %copy-start.3 = (bf16[64,1024]{1,0:T(8,128)(2,1)S(1)}, bf16[64,1024]{1,0:T(8,128)(2,1)}, u32[]{:S(2)}) copy-start(bf16[64,1024]{1,0:T(8,128)(2,1)} %q_ref.3) | copy-start | bytes 393220
  2.8 13.8 %copy-start.4 = (bf16[512,128]{1,0:T(8,128)(2,1)S(1)}, bf16[512,128]{1,0:T(8,128)(2,1)}, u32[]{:S(2)}) copy-start(bf16[512,128]{1,0:T(8,128)(2,1)} %get-tuple-element.40.xm_ref) | copy-start | bytes 393220
  2.8 13.8 %copy-start.5 = (bf16[4,128,128]{2,1,0:T(8,128)(2,1)S(1)}, bf16[4,128,128]{2,1,0:T(8,128)(2,1)}, u32[]{:S(2)}) copy-start(bf16[4,128,128]{2,1,0:T(8,128)(2,1)} %get-tuple-element.41.kvm_ref) | copy-start | bytes 393220
  2.9 13.7 %collective-permute-start = (bf16[1280,128]{1,0:T(8,128)(2,1)}, bf16[1280,128]{1,0:T(8,128)(2,1)S(1)}, u32[]{:S(2)}, u32[]{:S(2)}) collective-permute-start(bf16[1280,128]{1,0:T(8,128)(2,1)} %get-tuple-element.42), channel_id=1, source_target_pairs={{0,2},{2,0},{4,6},{6,4},{8,10},{10,8},{12,14},{14,12},{16,18},{18,... | collective-permute-start | bytes 983048 | tf_op jit(solution)/shard_map/ppermute | solution.py:693
  5.1 9.8 %collective-permute-start.6 = (bf16[512,256]{1,0:T(8,128)(2,1)}, bf16[512,256]{1,0:T(8,128)(2,1)S(1)}, u32[]{:S(2)}, u32[]{:S(2)}) collective-permute-start(bf16[512,256]{1,0:T(8,128)(2,1)} %stack.1.refs_0_), channel_id=1, source_target_pairs={{0,4},{2,6},{8,0},{10,2},{16,8},{18,10},{24,16},{26,18},{28,24},{3... | collective-permute-start | bytes 786440 | tf_op jit(solution)/shard_map/ppermute | solution.py:632
  7.7 8.9 %collective-permute-start.1 = (bf16[512,256]{1,0:T(8,128)(2,1)}, bf16[512,256]{1,0:T(8,128)(2,1)S(1)}, u32[]{:S(2)}, u32[]{:S(2)}) collective-permute-start(bf16[512,256]{1,0:T(8,128)(2,1)} %stack.1.refs_0_), channel_id=1, source_target_pairs={{0,8},{2,10},{8,16},{10,18},{16,24},{18,26},{24,28},{26,30},{28,20... | collective-permute-start | bytes 786440 | tf_op jit(solution)/shard_map/ppermute | solution.py:632
  14.9 9.2 %collective-permute-start.7 = (bf16[512,256]{1,0:T(8,128)(2,1)S(1)}, bf16[512,256]{1,0:T(8,128)(2,1)S(1)}, u32[]{:S(2)}, u32[]{:S(2)}) collective-permute-start(bf16[512,256]{1,0:T(8,128)(2,1)S(1)} %collective-permute-done.6.refs_1_), channel_id=1, source_target_pairs={{0,4},{2,6},{8,0},{10,2},{16,8},{18,10},{24,16},{26,18},{28,24},{3... | collective-permute-start | bytes 786440 | tf_op jit(solution)/shard_map/ppermute | solution.py:632
  16.7 9.3 %collective-permute-start.2 = (bf16[512,256]{1,0:T(8,128)(2,1)S(1)}, bf16[512,256]{1,0:T(8,128)(2,1)S(1)}, u32[]{:S(2)}, u32[]{:S(2)}) collective-permute-start(bf16[512,256]{1,0:T(8,128)(2,1)S(1)} %collective-permute-done.1.refs_2_), channel_id=1, source_target_pairs={{0,8},{2,10},{8,16},{10,18},{16,24},{18,26},{24,28},{26,30},{28,20... | collective-permute-start | bytes 786440 | tf_op jit(solution)/shard_map/ppermute | solution.py:632
  17.1 12.9 %collective-permute-start.4 = (bf16[8,128,128]{2,1,0:T(8,128)(2,1)S(1)}, bf16[8,128,128]{2,1,0:T(8,128)(2,1)S(1)}, u32[]{:S(2)}, u32[]{:S(2)}) collective-permute-start(bf16[8,128,128]{2,1,0:T(8,128)(2,1)S(1)} %get-tuple-element.47.refs_0_), channel_id=1, source_target_pairs={{0,4},{2,6},{4,0},{6,2},{8,12},{10,14},{12,8},{14,10},{16,20},{18,... | collective-permute-start | bytes 786440 | tf_op jit(solution)/shard_map/ppermute | solution.py:664
  18.8 11.2 %collective-permute-start.3 = (bf16[1024,128]{1,0:T(8,128)(2,1)S(1)}, bf16[1024,128]{1,0:T(8,128)(2,1)S(1)}, u32[]{:S(2)}, u32[]{:S(2)}) collective-permute-start(bf16[1024,128]{1,0:T(8,128)(2,1)S(1)} %get-tuple-element.45.x_ref), channel_id=1, source_target_pairs={{0,1},{1,0},{2,3},{3,2},{4,5},{5,4},{6,7},{7,6},{8,9},{9,8},{10,11... | collective-permute-start | bytes 786440 | tf_op jit(solution)/shard_map/ppermute | solution.py:700
  20.2 20.2 %collective-permute-start.10 = (bf16[8,128,128]{2,1,0:T(8,128)(2,1)S(1)}, bf16[8,128,128]{2,1,0:T(8,128)(2,1)S(1)}, u32[]{:S(2)}, u32[]{:S(2)}) collective-permute-start(bf16[8,128,128]{2,1,0:T(8,128)(2,1)S(1)} %get-tuple-element.47.refs_0_), channel_id=1, source_target_pairs={{0,8},{2,10},{4,12},{6,14},{8,0},{10,2},{12,4},{14,6},{16,24},{18,... | collective-permute-start | bytes 786440 | tf_op jit(solution)/shard_map/ppermute | solution.py:664
  24.1 13.3 %collective-permute-start.8 = (bf16[512,256]{1,0:T(8,128)(2,1)S(1)}, bf16[512,256]{1,0:T(8,128)(2,1)S(1)}, u32[]{:S(2)}, u32[]{:S(2)}) collective-permute-start(bf16[512,256]{1,0:T(8,128)(2,1)S(1)} %collective-permute-done.7.refs_3_), channel_id=1, source_target_pairs={{0,4},{2,6},{8,0},{10,2},{16,8},{18,10},{24,16},{26,18},{28,24},{3... | collective-permute-start | bytes 786440 | tf_op jit(solution)/shard_map/ppermute | solution.py:632
  29.9 10.5 %collective-permute-start.9 = (bf16[512,256]{1,0:T(8,128)(2,1)S(1)}, bf16[512,256]{1,0:T(8,128)(2,1)S(1)}, u32[]{:S(2)}, u32[]{:S(2)}) collective-permute-start(bf16[512,256]{1,0:T(8,128)(2,1)S(1)} %collective-permute-done.2.refs_4_), channel_id=1, source_target_pairs={{0,8},{2,10},{8,16},{10,18},{16,24},{18,26},{24,28},{26,30},{28,20... | collective-permute-start | bytes 786440 | tf_op jit(solution)/shard_map/ppermute | solution.py:632
  29.9 10.5 %collective-permute-start.11 = (bf16[512,128]{1,0:T(8,128)(2,1)S(1)}, bf16[512,128]{1,0:T(8,128)(2,1)S(1)}, u32[]{:S(2)}, u32[]{:S(2)}) collective-permute-start(bf16[512,128]{1,0:T(8,128)(2,1)S(1)} %get-tuple-element.43.qs_ref), channel_id=1, source_target_pairs={{0,16},{2,18},{4,20},{6,22},{8,24},{10,26},{12,28},{14,30},{16,0},... | collective-permute-start | bytes 393224 | tf_op jit(solution)/shard_map/ppermute | solution.py:664
  34.1 10.1 %collective-permute-start.5 = (bf16[8,128,128]{2,1,0:T(8,128)(2,1)S(1)}, bf16[8,128,128]{2,1,0:T(8,128)(2,1)S(1)}, u32[]{:S(2)}, u32[]{:S(2)}) collective-permute-start(bf16[8,128,128]{2,1,0:T(8,128)(2,1)S(1)} %collective-permute-done.4.refs_1_), channel_id=1, source_target_pairs={{0,8},{2,10},{4,12},{6,14},{8,0},{10,2},{12,4},{14,6},{16,24},{18,... | collective-permute-start | bytes 786440 | tf_op jit(solution)/shard_map/ppermute | solution.py:664
  37.4 3.7 %copy-start.10 = (bf16[4096]{0:T(1024)(128)(2,1)S(1)}, bf16[4096]{0:T(1024)(128)(2,1)}, u32[]{:S(2)}) copy-start(bf16[4096]{0:T(1024)(128)(2,1)} %param.12) | copy-start | bytes 24580
  37.4 8.0 %collective-permute-start.13 = (bf16[256,256]{1,0:T(8,128)(2,1)S(1)}, bf16[256,256]{1,0:T(8,128)(2,1)S(1)}, u32[]{:S(2)}, u32[]{:S(2)}) collective-permute-start(bf16[256,256]{1,0:T(8,128)(2,1)S(1)} %slice.8), channel_id=1, source_target_pairs={{0,4},{2,6},{8,0},{10,2},{16,8},{18,10},{24,16},{26,18},{28,24},{3... | collective-permute-start | bytes 393224 | tf_op jit(solution)/shard_map/ppermute | solution.py:632
  40.5 5.4 %collective-permute-start.12 = (bf16[256,256]{1,0:T(8,128)(2,1)S(1)}, bf16[256,256]{1,0:T(8,128)(2,1)S(1)}, u32[]{:S(2)}, u32[]{:S(2)}) collective-permute-start(bf16[256,256]{1,0:T(8,128)(2,1)S(1)} %slice.6), channel_id=1, source_target_pairs={{0,8},{2,10},{8,16},{10,18},{16,24},{18,26},{24,28},{26,30},{28,20... | collective-permute-start | bytes 393224 | tf_op jit(solution)/shard_map/ppermute | solution.py:632
  41.7 4.1 %copy-start = (bf16[512,256]{1,0:T(8,128)(2,1)S(1)}, bf16[512,256]{1,0:T(8,128)(2,1)}, u32[]{:S(2)}) copy-start(bf16[512,256]{1,0:T(8,128)(2,1)} %stack.1.refs_0_) | copy-start | bytes 786436
  46.3 1.5 %collective-permute-start.14 = (f32[128,384]{1,0:T(8,128)S(1)}, f32[128,384]{1,0:T(8,128)S(1)}, u32[]{:S(2)}, u32[]{:S(2)}) collective-permute-start(f32[128,384]{1,0:T(8,128)S(1)} %get-tuple-element.56), channel_id=1, source_target_pairs={{0,2},{2,0},{4,6},{6,4},{8,10},{10,8},{12,14},{14,12},{16,18},{18,... | collective-permute-start | bytes 589832 | tf_op jit(solution)/shard_map/ppermute | solution.py:727
  47.8 2.7 %copy-start.7 = (s32[3,25]{1,0:T(4,128)S(1)}, s32[3,25]{1,0:T(4,128)}, u32[]{:S(2)}) copy-start(s32[3,25]{1,0:T(4,128)} %table_ref.5) | copy-start | bytes 904
  47.9 5.0 %collective-permute-start.15 = (bf16[128,256]{1,0:T(8,128)(2,1)S(1)}, bf16[128,256]{1,0:T(8,128)(2,1)S(1)}, u32[]{:S(2)}, u32[]{:S(2)}) collective-permute-start(bf16[128,256]{1,0:T(8,128)(2,1)S(1)} %rotary.1.refs_0_), channel_id=1, source_target_pairs={{0,8},{2,10},{8,16},{10,18},{16,24},{18,26},{24,28},{26,30},{28,20... | collective-permute-start | bytes 196616 | tf_op jit(solution)/shard_map/ppermute | solution.py:632
  50.3 4.3 %collective-permute-start.16 = (bf16[128,256]{1,0:T(8,128)(2,1)S(1)}, bf16[128,256]{1,0:T(8,128)(2,1)S(1)}, u32[]{:S(2)}, u32[]{:S(2)}) collective-permute-start(bf16[128,256]{1,0:T(8,128)(2,1)S(1)} %rotary.1.refs_0_), channel_id=1, source_target_pairs={{0,4},{2,6},{8,0},{10,2},{16,8},{18,10},{24,16},{26,18},{28,24},{3... | collective-permute-start | bytes 196616 | tf_op jit(solution)/shard_map/ppermute | solution.py:632
  54.5 8.6 %collective-permute-start.17 = (bf16[128,256]{1,0:T(8,128)(2,1)S(1)}, bf16[128,256]{1,0:T(8,128)(2,1)S(1)}, u32[]{:S(2)}, u32[]{:S(2)}) collective-permute-start(bf16[128,256]{1,0:T(8,128)(2,1)S(1)} %collective-permute-done.15.refs_2_), channel_id=1, source_target_pairs={{0,8},{2,10},{8,16},{10,18},{16,24},{18,26},{24,28},{26,30},{28,20... | collective-permute-start | bytes 196616 | tf_op jit(solution)/shard_map/ppermute | solution.py:632
  55.9 7.3 %collective-permute-start.18 = (bf16[128,256]{1,0:T(8,128)(2,1)S(1)}, bf16[128,256]{1,0:T(8,128)(2,1)S(1)}, u32[]{:S(2)}, u32[]{:S(2)}) collective-permute-start(bf16[128,256]{1,0:T(8,128)(2,1)S(1)} %collective-permute-done.16.refs_1_), channel_id=1, source_target_pairs={{0,4},{2,6},{8,0},{10,2},{16,8},{18,10},{24,16},{26,18},{28,24},{3... | collective-permute-start | bytes 196616 | tf_op jit(solution)/shard_map/ppermute | solution.py:632
  56.6 13.1 %collective-permute-start.19 = (bf16[144,512]{1,0:T(8,128)(2,1)S(1)}, bf16[144,512]{1,0:T(8,128)(2,1)S(1)}, u32[]{:S(2)}, u32[]{:S(2)}) collective-permute-start(bf16[144,512]{1,0:T(8,128)(2,1)S(1)} %attend_cached_away.1), channel_id=1, source_target_pairs={{0,16},{2,18},{4,20},{6,22},{8,24},{10,26},{12,28},{14,30},{16,0},... | collective-permute-start | bytes 442376 | tf_op jit(solution)/shard_map/ppermute | solution.py:664
  63.1 13.0 %copy-start.1 = (bf16[3,128,256]{2,1,0:T(8,128)(2,1)S(1)}, bf16[3,128,256]{2,1,0:T(8,128)(2,1)}, u32[]{:S(2)}) copy-start(bf16[3,128,256]{2,1,0:T(8,128)(2,1)} %kp_ref.3) | copy-start | bytes 589828
  63.1 13.0 %copy-start.2 = (bf16[3,128,256]{2,1,0:T(8,128)(2,1)S(1)}, bf16[3,128,256]{2,1,0:T(8,128)(2,1)}, u32[]{:S(2)}) copy-start(bf16[3,128,256]{2,1,0:T(8,128)(2,1)} %vp_ref.3) | copy-start | bytes 589828
  63.2 4.3 %collective-permute-start.21 = (bf16[128,256]{1,0:T(8,128)(2,1)S(1)}, bf16[128,256]{1,0:T(8,128)(2,1)S(1)}, u32[]{:S(2)}, u32[]{:S(2)}) collective-permute-start(bf16[128,256]{1,0:T(8,128)(2,1)S(1)} %collective-permute-done.17.refs_4_), channel_id=1, source_target_pairs={{0,8},{2,10},{8,16},{10,18},{16,24},{18,26},{24,28},{26,30},{28,20... | collective-permute-start | bytes 196616 | tf_op jit(solution)/shard_map/ppermute | solution.py:632
  65.4 4.3 %collective-permute-start.20 = (bf16[128,256]{1,0:T(8,128)(2,1)S(1)}, bf16[128,256]{1,0:T(8,128)(2,1)S(1)}, u32[]{:S(2)}, u32[]{:S(2)}) collective-permute-start(bf16[128,256]{1,0:T(8,128)(2,1)S(1)} %collective-permute-done.18.refs_3_), channel_id=1, source_target_pairs={{0,4},{2,6},{8,0},{10,2},{16,8},{18,10},{24,16},{26,18},{28,24},{3... | collective-permute-start | bytes 196616 | tf_op jit(solution)/shard_map/ppermute | solution.py:632
  67.5 4.3 %collective-permute-start.22 = (bf16[128,256]{1,0:T(8,128)(2,1)S(1)}, bf16[128,256]{1,0:T(8,128)(2,1)S(1)}, u32[]{:S(2)}, u32[]{:S(2)}) collective-permute-start(bf16[128,256]{1,0:T(8,128)(2,1)S(1)} %collective-permute-done.21.refs_6_), channel_id=1, source_target_pairs={{0,8},{2,10},{8,16},{10,18},{16,24},{18,26},{24,28},{26,30},{28,20... | collective-permute-start | bytes 196616 | tf_op jit(solution)/shard_map/ppermute | solution.py:632
  74.5 1.6 %collective-permute-start.23 = (bf16[1024,128]{1,0:T(8,128)(2,1)S(1)}, bf16[1024,128]{1,0:T(8,128)(2,1)S(1)}, u32[]{:S(2)}, u32[]{:S(2)}) collective-permute-start(bf16[1024,128]{1,0:T(8,128)(2,1)S(1)} %get-tuple-element.76), channel_id=1, source_target_pairs={{0,2},{2,0},{4,6},{6,4},{8,10},{10,8},{12,14},{14,12},{16,18},{18,... | collective-permute-start | bytes 786440 | tf_op jit(solution)/shard_map/ppermute | solution.py:803
  (3 other events, 2.0 us)

commit v4 on v2

--- a/solution.py
+++ b/solution.py
@@ -265,7 +265,7 @@
     return first, last
 
 
-def split_kernel(old, f_ref, q_ref, kp_ref, vp_ref, xc_ref, xo_ref, qo_ref, kvc_ref, kvo_ref, sems):
+def split_kernel(old, f_ref, q_ref, kp_ref, vp_ref, xc_ref, xo_ref, kvc_ref, out_ref, sems):
     core = lax.axis_index("dp") % 2
     copies = []
 
@@ -273,28 +273,40 @@
         copies.append(pltpu.make_async_copy(source, target, sems.at[len(copies)]))
         copies[-1].start()
 
-    for page_ref, first in ((kp_ref, 0), (vp_ref, old)):
-        for out_ref, head in ((kvo_ref, 1 - core), (kvc_ref, core)):
-            at = pl.ds(pl.multiple_of(head * HD, HD), HD)
-            copy(page_ref.at[pl.ds(0, old), :, at], out_ref.at[pl.ds(first, old)])
-    for out_ref, own in ((xo_ref, 1 - core), (xc_ref, core)):
+    rows = f_ref.shape[0]
+    half = q_ref.shape[1] // 2
+    mine = pl.ds(pl.multiple_of(core * HD, HD), HD)
+    other = pl.ds(pl.multiple_of((1 - core) * HD, HD), HD)
+    for out, own in ((xo_ref, 1 - core), (xc_ref, core)):
         for m in range(f_ref.shape[1] // 512):
             at = pl.ds(pl.multiple_of((2 * m + own) * 256, 256), 256)
-            copy(f_ref.at[:, at], out_ref.at[:, pl.ds(m * 256, 256)])
-    half = q_ref.shape[1] // 2
-    copy(q_ref.at[:, pl.ds(pl.multiple_of((1 - core) * half, 128), half)], qo_ref)
+            copy(f_ref.at[:, at], out.at[:, pl.ds(m * 256, 256)])
+    at = 0
+    for n, ref in enumerate((kp_ref, vp_ref)):
+        copy(ref.at[pl.ds(0, old), :, mine], kvc_ref.at[pl.ds(n * old, old)])
+        for p in range(old):
+            copy(ref.at[p, :, other], out_ref.at[pl.ds(at, PAGE), :])
+            at += PAGE
+    for h in range(half // HD):
+        lane = pl.multiple_of((1 - core) * half + h * HD, HD)
+        copy(q_ref.at[:, pl.ds(lane, HD)], out_ref.at[pl.ds(at, rows), :])
+        at += rows
     for c in copies:
         c.wait()
 
 
-def merge_kernel(q_ref, qg_ref, qs_ref):
+def merge_kernel(q_ref, got_ref, qs_ref, kv_ref):
     core = lax.axis_index("dp") % 2
-    rows, group = q_ref.shape[0], qg_ref.shape[1] // HD
+    count = kv_ref.shape[0]
+    rows, group = q_ref.shape[0], q_ref.shape[1] // (2 * HD)
+    for n in range(count):
+        kv_ref[n] = got_ref[n * PAGE : (n + 1) * PAGE, :]
     for h in range(group):
         mine = pl.ds(pl.multiple_of((2 * h + core) * rows, rows), rows)
         other = pl.ds(pl.multiple_of((2 * h + 1 - core) * rows, rows), rows)
         qs_ref[mine, :] = q_ref[:, pl.ds(pl.multiple_of((core * group + h) * HD, HD), HD)]
-        qs_ref[other, :] = qg_ref[:, h * HD : (h + 1) * HD]
+        first = count * PAGE + h * rows
+        qs_ref[other, :] = got_ref[first : first + rows, :]
 
 
 def scale_kernel(
@@ -626,41 +638,45 @@
     w_got = {0: [w_key, w_value]}
     right, left = ring_send(chips, [w_key, w_value], 1), ring_send(chips, [w_key, w_value], -1)
     w_got[-1], w_got[1] = right, left
-    x_mine, x_other, q_other, kv_mine, kv_other = call(
+    bundle = 2 * old * PAGE + group * rows
+    x_mine, x_other, kv_mine, core_send = call(
         functools.partial(split_kernel, old),
         [
             ((rows, half_width // 2), bf),
             ((rows, half_width // 2), bf),
-            ((rows, group * HD), bf),
             ((2 * old, PAGE, HD), bf),
-            ((2 * old, PAGE, HD), bf),
+            ((bundle, HD), bf),
         ],
-        scratch=[pltpu.SemaphoreType.DMA((4 + 2 * (half_width // 512) + 1,))],
+        scratch=[pltpu.SemaphoreType.DMA((2 * (half_width // 512) + 2 + 2 * old + group,))],
         ins=4,
         far=(0, 1, 2, 3),
         limit=SPLIT_LIMIT,
         name="split",
     )(features, queries, key_pool, value_pool)
+    core_got = lax.ppermute(core_send, "dp", core_pairs)
     x_b = lax.ppermute(x_mine, "mp", mp_pairs)
     x_c = lax.ppermute(x_other, "dp", core_pairs)
     x_d = lax.ppermute(x_other, ("dp", "mp"), both_pairs)
-    q_got = lax.ppermute(q_other, "dp", core_pairs)
-    kv_got = lax.ppermute(kv_other, "dp", core_pairs)
-    z_near, z_far = exchange(kv_mine, 2), exchange(kv_other, 2, 1)
-    y_near, y_far = exchange(kv_mine, 1), exchange(kv_other, 1, 1)
+    q_rows, kv_other = call(
+        merge_kernel,
+        [((columns, HD), bf), ((2 * old, PAGE, HD), bf)],
+        ins=2,
+        name="merge",
+    )(queries, core_got)
+    q_away = exchange(q_rows, chips // 2)
+    z_near, z_far = exchange(kv_mine, 2), exchange(kv_other, 2)
+    y_near, y_far = exchange(kv_mine, 1), exchange(kv_other, 1)
     for d in range(2, chips // 2):
         if d == chips // 2 - 1:
-            w_first, z_near, z_far, y_near, y_far, q_got = lax.optimization_barrier(
-                (right[0], z_near, z_far, y_near, y_far, q_got)
+            (w_first, w_second), z_near, z_far, y_near, y_far = lax.optimization_barrier(
+                (right, z_near, z_far, y_near, y_far)
             )
-            right = [w_first, right[1]]
+            right = [w_first, w_second]
         right, left = ring_send(chips, right, 1), ring_send(chips, left, -1)
         w_got[-d], w_got[d] = right, left
     near = [kv_mine, y_near, z_near, exchange(y_near, 2)]
-    far = [kv_got, y_far, z_far, exchange(z_far, 1)]
-
-    (q_rows,) = call(merge_kernel, [((columns, HD), bf)], ins=2, name="merge")(queries, q_got)
-    q_away = exchange(q_rows, chips // 2)
+    far = [kv_other, y_far, z_far, exchange(z_far, 1)]
+
     inverse = (THETA ** (-(np.arange(HD) % (HD // 2)) * 2.0 / HD)).astype(np.float32)[None, :]
     scaled, squares, cosine, sine = call(
         functools.partial(scale_kernel, chips),
@@ -679,7 +695,7 @@
         x_d,
     )
     w_got[chips // 2] = ring_send(chips, right[:1], 1) + ring_send(chips, left[1:], -1)
-    scaled, near[3], far[3], q_away = lax.optimization_barrier((scaled, near[3], far[3], q_away))
+    scaled, q_away = lax.optimization_barrier((scaled, q_away))
     part_send, part_keep = call(
         functools.partial(project_kernel, chips),
         [((toks, 3 * HD), f32), ((toks, 3 * HD), f32)],
@@ -723,8 +739,8 @@
     )
     beside = {2: away, 3: here}
     for d in range(2, chips // 2):
-        right, left, beside[d] = lax.optimization_barrier((new[1 - d], new[d - 1], beside[d]))
-        new[-d], new[d] = ring_send(chips, [right], 1)[0], ring_send(chips, [left], -1)[0]
+        right, beside[d] = lax.optimization_barrier((new[1 - d], beside[d]))
+        new[-d], new[d] = ring_send(chips, [right], 1)[0], ring_send(chips, [new[d - 1]], -1)[0]
     (new[chips // 2],) = ring_send(chips, [new[1 - chips // 2]], 1)
     back = exchange(beside[2], chips // 2)
     top, total, acc = beside[3]

time: 75 us -> 78.2 us (1.043)
  waiting for transfers between devices: 15 us -> 21.8 us
  starting transfers between devices: 43.8 us -> 39.8 us
    ppermute x21, starting transfers between devices: 27.5 us -> 22.1 us  [ring_send(): lax.ppermute(a, 'dp', ring_pairs(chips, step, swap * n))]
    ppermute x21, waiting for transfers between devices: 9.12 us -> 14 us  [ring_send(): lax.ppermute(a, 'dp', ring_pairs(chips, step, swap * n))]
    ppermute x8, waiting for transfers between devices: 2.79 us -> 6.78 us  [exchange(): lax.ppermute(array, 'dp', [(i, i ^ 2 * e ^ swap) for i in range(dp_count)])]
    ppermute x8, starting transfers between devices: 12.2 us -> 13.5 us  [exchange(): lax.ppermute(array, 'dp', [(i, i ^ 2 * e ^ swap) for i in range(dp_count)])]
    ppermute x2 -> x1, waiting for transfers between devices: 1.12 us -> 0.01 us  [ring_body(): core_got = lax.ppermute(core_send, 'dp', core_pairs)]
    ppermute x1, starting transfers between devices: 0.6 us -> 1.6 us  [ring_body(): x_d = lax.ppermute(x_other, ('dp', 'mp'), both_pairs)]
    ppermute x1, waiting for transfers between devices: 0.93 us -> 0.01 us  [ring_body(): part_got = lax.ppermute(part_send, 'dp', core_pairs)]
  transfers between devices with their start and end apart: 37 -> 36, of which waited for: 12 -> 16; matrix products, arithmetic and copies ran while one was open for 0% -> 0% of each run, Pallas kernels for 9% -> 9%
where the time goes in v4:
time: 78.2 us; the launch traced here: 77 us
  starting transfers between devices  39.8 us (51%)
  waiting for transfers between devices  21.8 us (28%)
  Pallas kernels  13.8 us (18%)
  between operations  0.82 us (1%)
    ppermute x21, starting transfers between devices, ring_send(): lax.ppermute(a, 'dp', ring_pairs(chips, step, swap * n))  22.1 us
    ppermute x21, waiting for transfers between devices, ring_send(): lax.ppermute(a, 'dp', ring_pairs(chips, step, swap * n))  14 us
    ppermute x8, starting transfers between devices, exchange(): lax.ppermute(array, 'dp', [(i, i ^ 2 * e ^ swap) for i in range(dp_count)])  13.5 us
    ppermute x8, waiting for transfers between devices, exchange(): lax.ppermute(array, 'dp', [(i, i ^ 2 * e ^ swap) for i in range(dp_count)])  6.78 us
    pallas_call x2, Pallas kernels, cached(): call(functools.partial(cached_kernel, chips, pages_dev, old, away), outs,...  5.91 us
    pallas_call x1, Pallas kernels, ring_body(): call(functools.partial(fresh_kernel, chips, pages_dev), [((rows, group *...  2.75 us
    pallas_call x1, Pallas kernels, ring_body(): call(functools.partial(split_kernel, old), [((rows, half_width // 2), bf)...  2.09 us
    ppermute x1, starting transfers between devices, ring_body(): x_d = lax.ppermute(x_other, ('dp', 'mp'), both_pairs)  1.6 us
  transfers between devices with their start and end apart: 36, of which 16 were waited for; matrix products, arithmetic and copies ran while one was open for 0% of the time, Pallas kernels for 9%

profile of v4, /device:TPU:0, one launch (start us, length us, event | category | flops | bytes accessed | tf_op | source)
XLA Modules:
  0.0 77.0 jit_solution(18342820681228103524)
XLA Ops:
  0.7 2.1 %split.1 = (bf16[64,1024]{1,0:T(8,128)(2,1)}, bf16[64,1024]{1,0:T(8,128)(2,1)}, bf16[4,128,128]{2,1,0:T(8,128)(2,1)}, bf16[768,128]{1,0:T(8,128)(2,1)}) custom-call(bf16[64,2048]{1,0:T(8,128)(2,1)} %f_ref.1, bf16[64,1024]{1,0:T(8,128)(2,1)} %q_ref.3, bf16[3,128,256]{2,1,0:T(8,128)(2,1)} %kp_ref.3, bf16[3,128,256]{2,1,0:T(8,128)(2,1)} %vp_ref.3), custom_call_target="tpu_custom_call" | custom-call | tf_op jit(solution)/shard_map/split/pallas_call | solution.py:642
  3.3 2.7 %collective-permute-start.12 = (bf16[4,128,128]{2,1,0:T(8,128)(2,1)}, bf16[4,128,128]{2,1,0:T(8,128)(2,1)S(1)}, u32[]{:S(2)}, u32[]{:S(2)}) collective-permute-start(bf16[4,128,128]{2,1,0:T(8,128)(2,1)} %get-tuple-element.44.refs_0_), channel_id=1, source_target_pairs={{0,8},{2,10},{4,12},{6,14},{8,0},{10,2},{12,4},{14,6},{16,24},{18,... | collective-permute-start | bytes 393224 | tf_op jit(solution)/shard_map/ppermute | solution.py:636
  6.0 3.1 %collective-permute-start.6 = (bf16[256,256]{1,0:T(8,128)(2,1)S(1)}, bf16[256,256]{1,0:T(8,128)(2,1)S(1)}, u32[]{:S(2)}, u32[]{:S(2)}) collective-permute-start(bf16[256,256]{1,0:T(8,128)(2,1)S(1)} %copy-done.5), channel_id=1, source_target_pairs={{0,8},{2,10},{8,16},{10,18},{16,24},{18,26},{24,28},{26,30},{28,20... | collective-permute-start | bytes 393224 | tf_op jit(solution)/shard_map/ppermute | solution.py:603
  9.1 1.1 %collective-permute-done.12.refs_2_ = bf16[4,128,128]{2,1,0:T(8,128)(2,1)S(1)} collective-permute-done((bf16[4,128,128]{2,1,0:T(8,128)(2,1)}, bf16[4,128,128]{2,1,0:T(8,128)(2,1)S(1)}, u32[]{:S(2)}, u32[]{:S(2)}) %collective-permute-start.12) | collective-permute-done | bytes 131104 | tf_op jit(solution)/shard_map/ppermute | solution.py:636
  10.2 2.2 %collective-permute-start.14 = (bf16[4,128,128]{2,1,0:T(8,128)(2,1)}, bf16[4,128,128]{2,1,0:T(8,128)(2,1)S(1)}, u32[]{:S(2)}, u32[]{:S(2)}) collective-permute-start(bf16[4,128,128]{2,1,0:T(8,128)(2,1)} %get-tuple-element.44.refs_0_), channel_id=1, source_target_pairs={{0,4},{2,6},{4,0},{6,2},{8,12},{10,14},{12,8},{14,10},{16,20},{18,... | collective-permute-start | bytes 393224 | tf_op jit(solution)/shard_map/ppermute | solution.py:636
  12.8 2.4 %collective-permute-start.5 = (bf16[256,256]{1,0:T(8,128)(2,1)S(1)}, bf16[256,256]{1,0:T(8,128)(2,1)S(1)}, u32[]{:S(2)}, u32[]{:S(2)}) collective-permute-start(bf16[256,256]{1,0:T(8,128)(2,1)S(1)} %copy-done.5), channel_id=1, source_target_pairs={{0,4},{2,6},{8,0},{10,2},{16,8},{18,10},{24,16},{26,18},{28,24},{3... | collective-permute-start | bytes 393224 | tf_op jit(solution)/shard_map/ppermute | solution.py:603
  15.6 2.5 %collective-permute-start.8 = (bf16[256,256]{1,0:T(8,128)(2,1)S(1)}, bf16[256,256]{1,0:T(8,128)(2,1)S(1)}, u32[]{:S(2)}, u32[]{:S(2)}) collective-permute-start(bf16[256,256]{1,0:T(8,128)(2,1)S(1)} %collective-permute-done.6.refs_2_), channel_id=1, source_target_pairs={{0,8},{2,10},{8,16},{10,18},{16,24},{18,26},{24,28},{26,30},{28,20... | collective-permute-start | bytes 393224 | tf_op jit(solution)/shard_map/ppermute | solution.py:603
  18.1 2.0 %collective-permute-start.13 = (bf16[4,128,128]{2,1,0:T(8,128)(2,1)S(1)}, bf16[4,128,128]{2,1,0:T(8,128)(2,1)S(1)}, u32[]{:S(2)}, u32[]{:S(2)}) collective-permute-start(bf16[4,128,128]{2,1,0:T(8,128)(2,1)S(1)} %get-tuple-element.45.refs_4_), channel_id=1, source_target_pairs={{0,8},{2,10},{4,12},{6,14},{8,0},{10,2},{12,4},{14,6},{16,24},{18,... | collective-permute-start | bytes 393224 | tf_op jit(solution)/shard_map/ppermute | solution.py:636
  20.1 1.1 %collective-permute-start.15 = (bf16[4,128,128]{2,1,0:T(8,128)(2,1)S(1)}, bf16[4,128,128]{2,1,0:T(8,128)(2,1)S(1)}, u32[]{:S(2)}, u32[]{:S(2)}) collective-permute-start(bf16[4,128,128]{2,1,0:T(8,128)(2,1)S(1)} %get-tuple-element.45.refs_4_), channel_id=1, source_target_pairs={{0,4},{2,6},{4,0},{6,2},{8,12},{10,14},{12,8},{14,10},{16,20},{18,... | collective-permute-start | bytes 393224 | tf_op jit(solution)/shard_map/ppermute | solution.py:636
  21.6 1.5 %collective-permute-start.1 = (bf16[64,1024]{1,0:T(8,128)(2,1)S(1)}, bf16[64,1024]{1,0:T(8,128)(2,1)S(1)}, u32[]{:S(2)}, u32[]{:S(2)}) collective-permute-start(bf16[64,1024]{1,0:T(8,128)(2,1)S(1)} %copy-done.4), channel_id=1, source_target_pairs={{0,1},{1,0},{2,3},{3,2},{4,5},{5,4},{6,7},{7,6},{8,9},{9,8},{10,11... | collective-permute-start | bytes 393224 | tf_op jit(solution)/shard_map/ppermute | solution.py:657
  23.1 1.1 %collective-permute-done.8.refs_4_ = bf16[256,256]{1,0:T(8,128)(2,1)S(1)} collective-permute-done((bf16[256,256]{1,0:T(8,128)(2,1)S(1)}, bf16[256,256]{1,0:T(8,128)(2,1)S(1)}, u32[]{:S(2)}, u32[]{:S(2)}) %collective-permute-start.8) | collective-permute-done | bytes 131104 | tf_op jit(solution)/shard_map/ppermute | solution.py:603
  24.2 1.6 %collective-permute-start.3 = (bf16[64,1024]{1,0:T(8,128)(2,1)S(1)}, bf16[64,1024]{1,0:T(8,128)(2,1)S(1)}, u32[]{:S(2)}, u32[]{:S(2)}) collective-permute-start(bf16[64,1024]{1,0:T(8,128)(2,1)S(1)} %copy-done.12), channel_id=1, source_target_pairs={{0,3},{1,2},{2,1},{3,0},{4,7},{5,6},{6,5},{7,4},{8,11},{9,10},{10,... | collective-permute-start | bytes 393224 | tf_op jit(solution)/shard_map/ppermute | solution.py:659
  25.8 1.3 %collective-permute-start.7 = (bf16[256,256]{1,0:T(8,128)(2,1)S(1)}, bf16[256,256]{1,0:T(8,128)(2,1)S(1)}, u32[]{:S(2)}, u32[]{:S(2)}) collective-permute-start(bf16[256,256]{1,0:T(8,128)(2,1)S(1)} %collective-permute-done.5.refs_1_), channel_id=1, source_target_pairs={{0,4},{2,6},{8,0},{10,2},{16,8},{18,10},{24,16},{26,18},{28,24},{3... | collective-permute-start | bytes 393224 | tf_op jit(solution)/shard_map/ppermute | solution.py:603
  27.2 1.9 %collective-permute-start.16 = (bf16[256,256]{1,0:T(8,128)(2,1)S(1)}, bf16[256,256]{1,0:T(8,128)(2,1)S(1)}, u32[]{:S(2)}, u32[]{:S(2)}) collective-permute-start(bf16[256,256]{1,0:T(8,128)(2,1)S(1)} %collective-permute-done.8.refs_4_), channel_id=1, source_target_pairs={{0,8},{2,10},{8,16},{10,18},{16,24},{18,26},{24,28},{26,30},{28,20... | collective-permute-start | bytes 393224 | tf_op jit(solution)/shard_map/ppermute | solution.py:603
  29.9 2.2 %collective-permute-done.7.refs_3_ = bf16[256,256]{1,0:T(8,128)(2,1)S(1)} collective-permute-done((bf16[256,256]{1,0:T(8,128)(2,1)S(1)}, bf16[256,256]{1,0:T(8,128)(2,1)S(1)}, u32[]{:S(2)}, u32[]{:S(2)}) %collective-permute-start.7) | collective-permute-done | bytes 131104 | tf_op jit(solution)/shard_map/ppermute | solution.py:603
  32.1 1.3 %collective-permute-start.9 = (bf16[256,256]{1,0:T(8,128)(2,1)S(1)}, bf16[256,256]{1,0:T(8,128)(2,1)S(1)}, u32[]{:S(2)}, u32[]{:S(2)}) collective-permute-start(bf16[256,256]{1,0:T(8,128)(2,1)S(1)} %collective-permute-done.7.refs_3_), channel_id=1, source_target_pairs={{0,4},{2,6},{8,0},{10,2},{16,8},{18,10},{24,16},{26,18},{28,24},{3... | collective-permute-start | bytes 393224 | tf_op jit(solution)/shard_map/ppermute | solution.py:603
  34.1 1.7 %collective-permute-done.20.refs_13_ = bf16[256,256]{1,0:T(8,128)(2,1)S(1)} collective-permute-done((bf16[256,256]{1,0:T(8,128)(2,1)S(1)}, bf16[256,256]{1,0:T(8,128)(2,1)S(1)}, u32[]{:S(2)}, u32[]{:S(2)}) %collective-permute-start.20) | collective-permute-done | bytes 131104 | tf_op jit(solution)/shard_map/ppermute | solution.py:603
  36.2 1.7 %collective-permute-start.17 = (bf16[256,256]{1,0:T(8,128)(2,1)S(1)}, bf16[256,256]{1,0:T(8,128)(2,1)S(1)}, u32[]{:S(2)}, u32[]{:S(2)}) collective-permute-start(bf16[256,256]{1,0:T(8,128)(2,1)S(1)} %collective-permute-done.16.refs_6_), channel_id=1, source_target_pairs={{0,8},{2,10},{8,16},{10,18},{16,24},{18,26},{24,28},{26,30},{28,20... | collective-permute-start | bytes 393224 | tf_op jit(solution)/shard_map/ppermute | solution.py:603
  40.5 1.9 %collective-permute-done.22.refs_15_ = bf16[256,256]{1,0:T(8,128)(2,1)S(1)} collective-permute-done((bf16[256,256]{1,0:T(8,128)(2,1)S(1)}, bf16[256,256]{1,0:T(8,128)(2,1)S(1)}, u32[]{:S(2)}, u32[]{:S(2)}) %collective-permute-start.22) | collective-permute-done | bytes 131104 | tf_op jit(solution)/shard_map/ppermute | solution.py:603
  43.1 3.8 %collective-permute-start.25 = (bf16[4,128,128]{2,1,0:T(8,128)(2,1)S(1)}, bf16[4,128,128]{2,1,0:T(8,128)(2,1)S(1)}, u32[]{:S(2)}, u32[]{:S(2)}) collective-permute-start(bf16[4,128,128]{2,1,0:T(8,128)(2,1)S(1)} %collective-permute-done.14.refs_1_), channel_id=1, source_target_pairs={{0,8},{2,10},{4,12},{6,14},{8,0},{10,2},{12,4},{14,6},{16,24},{18,... | collective-permute-start | bytes 393224 | tf_op jit(solution)/shard_map/ppermute | solution.py:636
  48.4 2.6 %collective-permute-done.25.refs_3_ = bf16[4,128,128]{2,1,0:T(8,128)(2,1)S(1)} collective-permute-done((bf16[4,128,128]{2,1,0:T(8,128)(2,1)S(1)}, bf16[4,128,128]{2,1,0:T(8,128)(2,1)S(1)}, u32[]{:S(2)}, u32[]{:S(2)}) %collective-permute-start.25) | collective-permute-done | bytes 131104 | tf_op jit(solution)/shard_map/ppermute | solution.py:636
  51.0 2.2 %collective-permute-done.26.refs_7_ = bf16[4,128,128]{2,1,0:T(8,128)(2,1)S(1)} collective-permute-done((bf16[4,128,128]{2,1,0:T(8,128)(2,1)S(1)}, bf16[4,128,128]{2,1,0:T(8,128)(2,1)S(1)}, u32[]{:S(2)}, u32[]{:S(2)}) %collective-permute-start.26) | collective-permute-done | bytes 131104 | tf_op jit(solution)/shard_map/ppermute | solution.py:636
  53.2 3.9 %attend_cached_away.1 = bf16[144,512]{1,0:T(8,128)(2,1)S(1)} custom-call(s32[3]{0:T(128)S(1)} %copy-done.9, s32[3,25]{1,0:T(4,128)S(1)} %copy-done.8, s32[8,128]{1,0:T(8,128)S(1)} %bitcast.2, bf16[512,128]{1,0:T(8,128)(2,1)S(1)} %collective-permute-done.4.qs_ref, bf16[4,128,128]{2,1,0:T(8,128)(2,1)S(1)} %copy-done.2, ...), custom_call_target="tpu_custom_call" | custom-call | tf_op jit(solution)/shard_map/attend_cached_away/pallas_call | solution.py:720
  57.1 2.0 %collective-permute-start.27 = (bf16[128,256]{1,0:T(8,128)(2,1)S(1)}, bf16[128,256]{1,0:T(8,128)(2,1)S(1)}, u32[]{:S(2)}, u32[]{:S(2)}) collective-permute-start(bf16[128,256]{1,0:T(8,128)(2,1)S(1)} %collective-permute-done.24.refs_2_), channel_id=1, source_target_pairs={{0,8},{2,10},{8,16},{10,18},{16,24},{18,26},{24,28},{26,30},{28,20... | collective-permute-start | bytes 196616 | tf_op jit(solution)/shard_map/ppermute | solution.py:603
  59.1 2.0 %attend_cached_here.1 = (f32[1,512]{1,0:T(1,128)S(1)}, f32[1,512]{1,0:T(1,128)S(1)}, f32[128,512]{1,0:T(8,128)S(1)}) custom-call(s32[3]{0:T(128)S(1)} %copy-done.9, s32[3,25]{1,0:T(4,128)S(1)} %copy-done.8, s32[8,128]{1,0:T(8,128)S(1)} %bitcast.3, bf16[512,128]{1,0:T(8,128)(2,1)S(1)} %get-tuple-element.38.qs_ref, bf16[4,128,128]{2,1,0:T(8,128)(2,1)S(1)} %copy-done.2, ...), custom_call_target="tpu_custom_call" | custom-call | tf_op jit(solution)/shard_map/attend_cached_here/pallas_call | solution.py:720
  61.5 2.0 %collective-permute-start.32 = (bf16[128,256]{1,0:T(8,128)(2,1)S(1)}, bf16[128,256]{1,0:T(8,128)(2,1)S(1)}, u32[]{:S(2)}, u32[]{:S(2)}) collective-permute-start(bf16[128,256]{1,0:T(8,128)(2,1)S(1)} %collective-permute-done.27.refs_4_), channel_id=1, source_target_pairs={{0,8},{2,10},{8,16},{10,18},{16,24},{18,26},{24,28},{26,30},{28,20... | collective-permute-start | bytes 196616 | tf_op jit(solution)/shard_map/ppermute | solution.py:603
  63.5 3.5 %collective-permute-done.30.refs_3_ = bf16[128,256]{1,0:T(8,128)(2,1)S(1)} collective-permute-done((bf16[128,256]{1,0:T(8,128)(2,1)S(1)}, bf16[128,256]{1,0:T(8,128)(2,1)S(1)}, u32[]{:S(2)}, u32[]{:S(2)}) %collective-permute-start.30) | collective-permute-done | bytes 65568 | tf_op jit(solution)/shard_map/ppermute | solution.py:603
  66.9 2.0 %collective-permute-start.33 = (bf16[128,256]{1,0:T(8,128)(2,1)S(1)}, bf16[128,256]{1,0:T(8,128)(2,1)S(1)}, u32[]{:S(2)}, u32[]{:S(2)}) collective-permute-start(bf16[128,256]{1,0:T(8,128)(2,1)S(1)} %collective-permute-done.32.refs_6_), channel_id=1, source_target_pairs={{0,8},{2,10},{8,16},{10,18},{16,24},{18,26},{24,28},{26,30},{28,20... | collective-permute-start | bytes 196616 | tf_op jit(solution)/shard_map/ppermute | solution.py:603
  69.0 2.2 %collective-permute-done.31.refs_5_ = bf16[128,256]{1,0:T(8,128)(2,1)S(1)} collective-permute-done((bf16[128,256]{1,0:T(8,128)(2,1)S(1)}, bf16[128,256]{1,0:T(8,128)(2,1)S(1)}, u32[]{:S(2)}, u32[]{:S(2)}) %collective-permute-start.31) | collective-permute-done | bytes 65568 | tf_op jit(solution)/shard_map/ppermute | solution.py:603
  71.2 2.7 %attend_new.1 = (bf16[64,512]{1,0:T(8,128)(2,1)S(1)}, bf16[64,512]{1,0:T(8,128)(2,1)S(1)}, bf16[3,128,256]{2,1,0:T(8,128)(2,1)S(1)}, bf16[3,128,256]{2,1,0:T(8,128)(2,1)S(1)}, s32[6]{0:T(128)S(1)}) custom-call(s32[3]{0:T(128)S(1)} %copy-done.9, s32[3,25]{1,0:T(4,128)S(1)} %copy-done.8, s32[8,128]{1,0:T(8,128)S(1)} %bitcast.4, ...), custom_call_target="tpu_custom_call" | custom-call | tf_op jit(solution)/shard_map/attend_new/pallas_call | solution.py:748
  74.5 1.0 %collective-permute-done.34.attr_ref = bf16[64,512]{1,0:T(8,128)(2,1)S(1)} collective-permute-done((bf16[64,512]{1,0:T(8,128)(2,1)S(1)}, bf16[64,512]{1,0:T(8,128)(2,1)S(1)}, u32[]{:S(2)}, u32[]{:S(2)}) %collective-permute-start.34) | collective-permute-done | bytes 65568 | tf_op jit(solution)/shard_map/ppermute | solution.py:783
  75.6 1.5 %join.1 = (bf16[64,1024]{1,0:T(8,128)(2,1)}, bf16[3,128,256]{2,1,0:T(8,128)(2,1)}, bf16[3,128,256]{2,1,0:T(8,128)(2,1)}) custom-call(s32[6]{0:T(128)S(1)} %get-tuple-element.66.info_ref, bf16[64,512]{1,0:T(8,128)(2,1)S(1)} %get-tuple-element.67.attc_ref, bf16[64,512]{1,0:T(8,128)(2,1)S(1)} %collective-permute-done.34.attr_ref, ...), custom_call_target="tpu_custom_call" | custom-call | tf_op jit(solution)/shard_map/join/pallas_call | solution.py:784
  (76 shorter events, 9.5 us)
Async XLA Ops:
  2.8 12.5 %collective-permute-start = (bf16[768,128]{1,0:T(8,128)(2,1)}, bf16[768,128]{1,0:T(8,128)(2,1)S(1)}, u32[]{:S(2)}, u32[]{:S(2)}) collective-permute-start(bf16[768,128]{1,0:T(8,128)(2,1)} %get-tuple-element.37), channel_id=1, source_target_pairs={{0,2},{2,0},{4,6},{6,4},{8,10},{10,8},{12,14},{14,12},{16,18},{18,... | collective-permute-start | bytes 589832 | tf_op jit(solution)/shard_map/ppermute | solution.py:656
  3.3 7.0 %collective-permute-start.12 = (bf16[4,128,128]{2,1,0:T(8,128)(2,1)}, bf16[4,128,128]{2,1,0:T(8,128)(2,1)S(1)}, u32[]{:S(2)}, u32[]{:S(2)}) collective-permute-start(bf16[4,128,128]{2,1,0:T(8,128)(2,1)} %get-tuple-element.44.refs_0_), channel_id=1, source_target_pairs={{0,8},{2,10},{4,12},{6,14},{8,0},{10,2},{12,4},{14,6},{16,24},{18,... | collective-permute-start | bytes 393224 | tf_op jit(solution)/shard_map/ppermute | solution.py:636
  6.0 6.8 %collective-permute-start.10 = (bf16[256,256]{1,0:T(8,128)(2,1)S(1)}, bf16[256,256]{1,0:T(8,128)(2,1)S(1)}, u32[]{:S(2)}, u32[]{:S(2)}) collective-permute-start(bf16[256,256]{1,0:T(8,128)(2,1)S(1)} %copy-done.6), channel_id=1, source_target_pairs={{0,8},{2,10},{8,16},{10,18},{16,24},{18,26},{24,28},{26,30},{28,20... | collective-permute-start | bytes 393224 | tf_op jit(solution)/shard_map/ppermute | solution.py:603
  6.0 9.6 %collective-permute-start.6 = (bf16[256,256]{1,0:T(8,128)(2,1)S(1)}, bf16[256,256]{1,0:T(8,128)(2,1)S(1)}, u32[]{:S(2)}, u32[]{:S(2)}) collective-permute-start(bf16[256,256]{1,0:T(8,128)(2,1)S(1)} %copy-done.5), channel_id=1, source_target_pairs={{0,8},{2,10},{8,16},{10,18},{16,24},{18,26},{24,28},{26,30},{28,20... | collective-permute-start | bytes 393224 | tf_op jit(solution)/shard_map/ppermute | solution.py:603
  9.1 9.0 %collective-permute-start.18 = (bf16[256,256]{1,0:T(8,128)(2,1)S(1)}, bf16[256,256]{1,0:T(8,128)(2,1)S(1)}, u32[]{:S(2)}, u32[]{:S(2)}) collective-permute-start(bf16[256,256]{1,0:T(8,128)(2,1)S(1)} %copy-done.6), channel_id=1, source_target_pairs={{0,4},{2,6},{8,0},{10,2},{16,8},{18,10},{24,16},{26,18},{28,24},{3... | collective-permute-start | bytes 393224 | tf_op jit(solution)/shard_map/ppermute | solution.py:603
  10.2 7.9 %collective-permute-start.14 = (bf16[4,128,128]{2,1,0:T(8,128)(2,1)}, bf16[4,128,128]{2,1,0:T(8,128)(2,1)S(1)}, u32[]{:S(2)}, u32[]{:S(2)}) collective-permute-start(bf16[4,128,128]{2,1,0:T(8,128)(2,1)} %get-tuple-element.44.refs_0_), channel_id=1, source_target_pairs={{0,4},{2,6},{4,0},{6,2},{8,12},{10,14},{12,8},{14,10},{16,20},{18,... | collective-permute-start | bytes 393224 | tf_op jit(solution)/shard_map/ppermute | solution.py:636
  12.8 7.3 %collective-permute-start.5 = (bf16[256,256]{1,0:T(8,128)(2,1)S(1)}, bf16[256,256]{1,0:T(8,128)(2,1)S(1)}, u32[]{:S(2)}, u32[]{:S(2)}) collective-permute-start(bf16[256,256]{1,0:T(8,128)(2,1)S(1)} %copy-done.5), channel_id=1, source_target_pairs={{0,4},{2,6},{8,0},{10,2},{16,8},{18,10},{24,16},{26,18},{28,24},{3... | collective-permute-start | bytes 393224 | tf_op jit(solution)/shard_map/ppermute | solution.py:603
  15.2 6.3 %collective-permute-start.11 = (bf16[256,256]{1,0:T(8,128)(2,1)S(1)}, bf16[256,256]{1,0:T(8,128)(2,1)S(1)}, u32[]{:S(2)}, u32[]{:S(2)}) collective-permute-start(bf16[256,256]{1,0:T(8,128)(2,1)S(1)} %collective-permute-done.10.refs_10_), channel_id=1, source_target_pairs={{0,8},{2,10},{8,16},{10,18},{16,24},{18,26},{24,28},{26,30},{28,20... | collective-permute-start | bytes 393224 | tf_op jit(solution)/shard_map/ppermute | solution.py:603
  15.6 8.5 %collective-permute-start.8 = (bf16[256,256]{1,0:T(8,128)(2,1)S(1)}, bf16[256,256]{1,0:T(8,128)(2,1)S(1)}, u32[]{:S(2)}, u32[]{:S(2)}) collective-permute-start(bf16[256,256]{1,0:T(8,128)(2,1)S(1)} %collective-permute-done.6.refs_2_), channel_id=1, source_target_pairs={{0,8},{2,10},{8,16},{10,18},{16,24},{18,26},{24,28},{26,30},{28,20... | collective-permute-start | bytes 393224 | tf_op jit(solution)/shard_map/ppermute | solution.py:603
  18.1 6.1 %collective-permute-start.19 = (bf16[256,256]{1,0:T(8,128)(2,1)S(1)}, bf16[256,256]{1,0:T(8,128)(2,1)S(1)}, u32[]{:S(2)}, u32[]{:S(2)}) collective-permute-start(bf16[256,256]{1,0:T(8,128)(2,1)S(1)} %collective-permute-done.18.refs_9_), channel_id=1, source_target_pairs={{0,4},{2,6},{8,0},{10,2},{16,8},{18,10},{24,16},{26,18},{28,24},{3... | collective-permute-start | bytes 393224 | tf_op jit(solution)/shard_map/ppermute | solution.py:603
  18.1 7.7 %collective-permute-start.13 = (bf16[4,128,128]{2,1,0:T(8,128)(2,1)S(1)}, bf16[4,128,128]{2,1,0:T(8,128)(2,1)S(1)}, u32[]{:S(2)}, u32[]{:S(2)}) collective-permute-start(bf16[4,128,128]{2,1,0:T(8,128)(2,1)S(1)} %get-tuple-element.45.refs_4_), channel_id=1, source_target_pairs={{0,8},{2,10},{4,12},{6,14},{8,0},{10,2},{12,4},{14,6},{16,24},{18,... | collective-permute-start | bytes 393224 | tf_op jit(solution)/shard_map/ppermute | solution.py:636
  20.1 6.9 %collective-permute-start.15 = (bf16[4,128,128]{2,1,0:T(8,128)(2,1)S(1)}, bf16[4,128,128]{2,1,0:T(8,128)(2,1)S(1)}, u32[]{:S(2)}, u32[]{:S(2)}) collective-permute-start(bf16[4,128,128]{2,1,0:T(8,128)(2,1)S(1)} %get-tuple-element.45.refs_4_), channel_id=1, source_target_pairs={{0,4},{2,6},{4,0},{6,2},{8,12},{10,14},{12,8},{14,10},{16,20},{18,... | collective-permute-start | bytes 393224 | tf_op jit(solution)/shard_map/ppermute | solution.py:636
  21.6 5.6 %collective-permute-start.1 = (bf16[64,1024]{1,0:T(8,128)(2,1)S(1)}, bf16[64,1024]{1,0:T(8,128)(2,1)S(1)}, u32[]{:S(2)}, u32[]{:S(2)}) collective-permute-start(bf16[64,1024]{1,0:T(8,128)(2,1)S(1)} %copy-done.4), channel_id=1, source_target_pairs={{0,1},{1,0},{2,3},{3,2},{4,5},{5,4},{6,7},{7,6},{8,9},{9,8},{10,11... | collective-permute-start | bytes 393224 | tf_op jit(solution)/shard_map/ppermute | solution.py:657
  24.2 4.9 %collective-permute-start.2 = (bf16[64,1024]{1,0:T(8,128)(2,1)S(1)}, bf16[64,1024]{1,0:T(8,128)(2,1)S(1)}, u32[]{:S(2)}, u32[]{:S(2)}) collective-permute-start(bf16[64,1024]{1,0:T(8,128)(2,1)S(1)} %copy-done.12), channel_id=1, source_target_pairs={{0,2},{2,0},{4,6},{6,4},{8,10},{10,8},{12,14},{14,12},{16,18},{18,... | collective-permute-start | bytes 393224 | tf_op jit(solution)/shard_map/ppermute | solution.py:658
  24.2 9.2 %collective-permute-start.3 = (bf16[64,1024]{1,0:T(8,128)(2,1)S(1)}, bf16[64,1024]{1,0:T(8,128)(2,1)S(1)}, u32[]{:S(2)}, u32[]{:S(2)}) collective-permute-start(bf16[64,1024]{1,0:T(8,128)(2,1)S(1)} %copy-done.12), channel_id=1, source_target_pairs={{0,3},{1,2},{2,1},{3,0},{4,7},{5,6},{6,5},{7,4},{8,11},{9,10},{10,... | collective-permute-start | bytes 393224 | tf_op jit(solution)/shard_map/ppermute | solution.py:659
  25.8 6.4 %collective-permute-start.7 = (bf16[256,256]{1,0:T(8,128)(2,1)S(1)}, bf16[256,256]{1,0:T(8,128)(2,1)S(1)}, u32[]{:S(2)}, u32[]{:S(2)}) collective-permute-start(bf16[256,256]{1,0:T(8,128)(2,1)S(1)} %collective-permute-done.5.refs_1_), channel_id=1, source_target_pairs={{0,4},{2,6},{8,0},{10,2},{16,8},{18,10},{24,16},{26,18},{28,24},{3... | collective-permute-start | bytes 393224 | tf_op jit(solution)/shard_map/ppermute | solution.py:603
  27.0 8.8 %collective-permute-start.20 = (bf16[256,256]{1,0:T(8,128)(2,1)S(1)}, bf16[256,256]{1,0:T(8,128)(2,1)S(1)}, u32[]{:S(2)}, u32[]{:S(2)}) collective-permute-start(bf16[256,256]{1,0:T(8,128)(2,1)S(1)} %collective-permute-done.19.refs_11_), channel_id=1, source_target_pairs={{0,4},{2,6},{8,0},{10,2},{16,8},{18,10},{24,16},{26,18},{28,24},{3... | collective-permute-start | bytes 393224 | tf_op jit(solution)/shard_map/ppermute | solution.py:603
  27.2 9.0 %collective-permute-start.16 = (bf16[256,256]{1,0:T(8,128)(2,1)S(1)}, bf16[256,256]{1,0:T(8,128)(2,1)S(1)}, u32[]{:S(2)}, u32[]{:S(2)}) collective-permute-start(bf16[256,256]{1,0:T(8,128)(2,1)S(1)} %collective-permute-done.8.refs_4_), channel_id=1, source_target_pairs={{0,8},{2,10},{8,16},{10,18},{16,24},{18,26},{24,28},{26,30},{28,20... | collective-permute-start | bytes 393224 | tf_op jit(solution)/shard_map/ppermute | solution.py:603
  29.1 11.4 %collective-permute-start.4 = (bf16[512,128]{1,0:T(8,128)(2,1)S(1)}, bf16[512,128]{1,0:T(8,128)(2,1)S(1)}, u32[]{:S(2)}, u32[]{:S(2)}) collective-permute-start(bf16[512,128]{1,0:T(8,128)(2,1)S(1)} %get-tuple-element.38.qs_ref), channel_id=1, source_target_pairs={{0,16},{2,18},{4,20},{6,22},{8,24},{10,26},{12,28},{14,30},{16,0},... | collective-permute-start | bytes 393224 | tf_op jit(solution)/shard_map/ppermute | solution.py:636
  32.1 8.4 %collective-permute-start.9 = (bf16[256,256]{1,0:T(8,128)(2,1)S(1)}, bf16[256,256]{1,0:T(8,128)(2,1)S(1)}, u32[]{:S(2)}, u32[]{:S(2)}) collective-permute-start(bf16[256,256]{1,0:T(8,128)(2,1)S(1)} %collective-permute-done.7.refs_3_), channel_id=1, source_target_pairs={{0,4},{2,6},{8,0},{10,2},{16,8},{18,10},{24,16},{26,18},{28,24},{3... | collective-permute-start | bytes 393224 | tf_op jit(solution)/shard_map/ppermute | solution.py:603
  33.4 7.2 %collective-permute-start.21 = (bf16[256,256]{1,0:T(8,128)(2,1)S(1)}, bf16[256,256]{1,0:T(8,128)(2,1)S(1)}, u32[]{:S(2)}, u32[]{:S(2)}) collective-permute-start(bf16[256,256]{1,0:T(8,128)(2,1)S(1)} %collective-permute-done.11.refs_12_), channel_id=1, source_target_pairs={{0,8},{2,10},{8,16},{10,18},{16,24},{18,26},{24,28},{26,30},{28,20... | collective-permute-start | bytes 393224 | tf_op jit(solution)/shard_map/ppermute | solution.py:603
  35.8 6.6 %collective-permute-start.22 = (bf16[256,256]{1,0:T(8,128)(2,1)S(1)}, bf16[256,256]{1,0:T(8,128)(2,1)S(1)}, u32[]{:S(2)}, u32[]{:S(2)}) collective-permute-start(bf16[256,256]{1,0:T(8,128)(2,1)S(1)} %collective-permute-done.20.refs_13_), channel_id=1, source_target_pairs={{0,4},{2,6},{8,0},{10,2},{16,8},{18,10},{24,16},{26,18},{28,24},{3... | collective-permute-start | bytes 393224 | tf_op jit(solution)/shard_map/ppermute | solution.py:603
  36.2 6.3 %collective-permute-start.17 = (bf16[256,256]{1,0:T(8,128)(2,1)S(1)}, bf16[256,256]{1,0:T(8,128)(2,1)S(1)}, u32[]{:S(2)}, u32[]{:S(2)}) collective-permute-start(bf16[256,256]{1,0:T(8,128)(2,1)S(1)} %collective-permute-done.16.refs_6_), channel_id=1, source_target_pairs={{0,8},{2,10},{8,16},{10,18},{16,24},{18,26},{24,28},{26,30},{28,20... | collective-permute-start | bytes 393224 | tf_op jit(solution)/shard_map/ppermute | solution.py:603
  43.0 4.8 %collective-permute-start.23 = (f32[128,384]{1,0:T(8,128)S(1)}, f32[128,384]{1,0:T(8,128)S(1)}, u32[]{:S(2)}, u32[]{:S(2)}) collective-permute-start(f32[128,384]{1,0:T(8,128)S(1)} %get-tuple-element.49), channel_id=1, source_target_pairs={{0,2},{2,0},{4,6},{6,4},{8,10},{10,8},{12,14},{14,12},{16,18},{18,... | collective-permute-start | bytes 589832 | tf_op jit(solution)/shard_map/ppermute | solution.py:706
  43.1 7.9 %collective-permute-start.25 = (bf16[4,128,128]{2,1,0:T(8,128)(2,1)S(1)}, bf16[4,128,128]{2,1,0:T(8,128)(2,1)S(1)}, u32[]{:S(2)}, u32[]{:S(2)}) collective-permute-start(bf16[4,128,128]{2,1,0:T(8,128)(2,1)S(1)} %collective-permute-done.14.refs_1_), channel_id=1, source_target_pairs={{0,8},{2,10},{4,12},{6,14},{8,0},{10,2},{12,4},{14,6},{16,24},{18,... | collective-permute-start | bytes 393224 | tf_op jit(solution)/shard_map/ppermute | solution.py:636
  46.9 6.3 %collective-permute-start.26 = (bf16[4,128,128]{2,1,0:T(8,128)(2,1)S(1)}, bf16[4,128,128]{2,1,0:T(8,128)(2,1)S(1)}, u32[]{:S(2)}, u32[]{:S(2)}) collective-permute-start(bf16[4,128,128]{2,1,0:T(8,128)(2,1)S(1)} %collective-permute-done.13.refs_6_), channel_id=1, source_target_pairs={{0,4},{2,6},{4,0},{6,2},{8,12},{10,14},{12,8},{14,10},{16,20},{18,... | collective-permute-start | bytes 393224 | tf_op jit(solution)/shard_map/ppermute | solution.py:636
  47.9 9.3 %collective-permute-start.24 = (bf16[128,256]{1,0:T(8,128)(2,1)S(1)}, bf16[128,256]{1,0:T(8,128)(2,1)S(1)}, u32[]{:S(2)}, u32[]{:S(2)}) collective-permute-start(bf16[128,256]{1,0:T(8,128)(2,1)S(1)} %rotary.1.refs_0_), channel_id=1, source_target_pairs={{0,8},{2,10},{8,16},{10,18},{16,24},{18,26},{24,28},{26,30},{28,20... | collective-permute-start | bytes 196616 | tf_op jit(solution)/shard_map/ppermute | solution.py:603
  57.1 4.4 %collective-permute-start.29 = (bf16[128,256]{1,0:T(8,128)(2,1)S(1)}, bf16[128,256]{1,0:T(8,128)(2,1)S(1)}, u32[]{:S(2)}, u32[]{:S(2)}) collective-permute-start(bf16[128,256]{1,0:T(8,128)(2,1)S(1)} %rotary.1.refs_0_), channel_id=1, source_target_pairs={{0,4},{2,6},{8,0},{10,2},{16,8},{18,10},{24,16},{26,18},{28,24},{3... | collective-permute-start | bytes 196616 | tf_op jit(solution)/shard_map/ppermute | solution.py:603
  57.1 4.3 %collective-permute-start.27 = (bf16[128,256]{1,0:T(8,128)(2,1)S(1)}, bf16[128,256]{1,0:T(8,128)(2,1)S(1)}, u32[]{:S(2)}, u32[]{:S(2)}) collective-permute-start(bf16[128,256]{1,0:T(8,128)(2,1)S(1)} %collective-permute-done.24.refs_2_), channel_id=1, source_target_pairs={{0,8},{2,10},{8,16},{10,18},{16,24},{18,26},{24,28},{26,30},{28,20... | collective-permute-start | bytes 196616 | tf_op jit(solution)/shard_map/ppermute | solution.py:603
  59.1 12.1 %collective-permute-start.28 = (bf16[144,512]{1,0:T(8,128)(2,1)S(1)}, bf16[144,512]{1,0:T(8,128)(2,1)S(1)}, u32[]{:S(2)}, u32[]{:S(2)}) collective-permute-start(bf16[144,512]{1,0:T(8,128)(2,1)S(1)} %attend_cached_away.1), channel_id=1, source_target_pairs={{0,16},{2,18},{4,20},{6,22},{8,24},{10,26},{12,28},{14,30},{16,0},... | collective-permute-start | bytes 442376 | tf_op jit(solution)/shard_map/ppermute | solution.py:636
  61.4 5.5 %collective-permute-start.30 = (bf16[128,256]{1,0:T(8,128)(2,1)S(1)}, bf16[128,256]{1,0:T(8,128)(2,1)S(1)}, u32[]{:S(2)}, u32[]{:S(2)}) collective-permute-start(bf16[128,256]{1,0:T(8,128)(2,1)S(1)} %collective-permute-done.29.refs_1_), channel_id=1, source_target_pairs={{0,4},{2,6},{8,0},{10,2},{16,8},{18,10},{24,16},{26,18},{28,24},{3... | collective-permute-start | bytes 196616 | tf_op jit(solution)/shard_map/ppermute | solution.py:603
  61.5 5.5 %collective-permute-start.32 = (bf16[128,256]{1,0:T(8,128)(2,1)S(1)}, bf16[128,256]{1,0:T(8,128)(2,1)S(1)}, u32[]{:S(2)}, u32[]{:S(2)}) collective-permute-start(bf16[128,256]{1,0:T(8,128)(2,1)S(1)} %collective-permute-done.27.refs_4_), channel_id=1, source_target_pairs={{0,8},{2,10},{8,16},{10,18},{16,24},{18,26},{24,28},{26,30},{28,20... | collective-permute-start | bytes 196616 | tf_op jit(solution)/shard_map/ppermute | solution.py:603
  (17 other events, 139.8 us)

commit v5 on v4

--- a/solution.py
+++ b/solution.py
@@ -663,20 +663,9 @@
         ins=2,
         name="merge",
     )(queries, core_got)
-    q_away = exchange(q_rows, chips // 2)
-    z_near, z_far = exchange(kv_mine, 2), exchange(kv_other, 2)
-    y_near, y_far = exchange(kv_mine, 1), exchange(kv_other, 1)
     for d in range(2, chips // 2):
-        if d == chips // 2 - 1:
-            (w_first, w_second), z_near, z_far, y_near, y_far = lax.optimization_barrier(
-                (right, z_near, z_far, y_near, y_far)
-            )
-            right = [w_first, w_second]
         right, left = ring_send(chips, right, 1), ring_send(chips, left, -1)
         w_got[-d], w_got[d] = right, left
-    near = [kv_mine, y_near, z_near, exchange(y_near, 2)]
-    far = [kv_other, y_far, z_far, exchange(z_far, 1)]
-
     inverse = (THETA ** (-(np.arange(HD) % (HD // 2)) * 2.0 / HD)).astype(np.float32)[None, :]
     scaled, squares, cosine, sine = call(
         functools.partial(scale_kernel, chips),
@@ -695,7 +684,7 @@
         x_d,
     )
     w_got[chips // 2] = ring_send(chips, right[:1], 1) + ring_send(chips, left[1:], -1)
-    scaled, q_away = lax.optimization_barrier((scaled, q_away))
+    scaled, q_rows, kv_other = lax.optimization_barrier((scaled, q_rows, kv_other))
     part_send, part_keep = call(
         functools.partial(project_kernel, chips),
         [((toks, 3 * HD), f32), ((toks, 3 * HD), f32)],
@@ -705,6 +694,9 @@
     )(scaled, squares, *[w_got[o][0] for o in offsets], *[w_got[o][1] for o in offsets])
     part_got = lax.ppermute(part_send, "dp", core_pairs)
 
+    first_near, first_far, _ = lax.optimization_barrier((kv_mine, kv_other, part_send))
+    z_near, z_far = exchange(first_near, 2), exchange(first_far, 2)
+    y_near, y_far = exchange(first_near, 1), exchange(first_far, 1)
     (fresh,) = call(
         functools.partial(rotate_kernel, width),
         [((toks, 2 * HD), bf)],
@@ -713,6 +705,10 @@
     )(part_keep, part_got, cosine, sine)
     new = {0: fresh}
     new[-1], new[1] = ring_send(chips, [fresh], 1)[0], ring_send(chips, [fresh], -1)[0]
+    late_y, late_z, late_q, _ = lax.optimization_barrier((y_near, z_far, q_rows, fresh))
+    q_away = exchange(late_q, chips // 2)
+    near = [kv_mine, y_near, z_near, exchange(late_y, 2)]
+    far = [kv_other, y_far, z_far, exchange(late_z, 1)]
     slots = dp_count // 2 * old + STEP_PAGES
     table = pltpu.SMEM((dp_count * pages_dev,), i32)
 
@@ -739,8 +735,8 @@
     )
     beside = {2: away, 3: here}
     for d in range(2, chips // 2):
-        right, beside[d] = lax.optimization_barrier((new[1 - d], beside[d]))
-        new[-d], new[d] = ring_send(chips, [right], 1)[0], ring_send(chips, [new[d - 1]], -1)[0]
+        right, left, beside[d] = lax.optimization_barrier((new[1 - d], new[d - 1], beside[d]))
+        new[-d], new[d] = ring_send(chips, [right], 1)[0], ring_send(chips, [left], -1)[0]
     (new[chips // 2],) = ring_send(chips, [new[1 - chips // 2]], 1)
     back = exchange(beside[2], chips // 2)
     top, total, acc = beside[3]

time: 78.2 us -> 72.9 us (0.932)
  waiting for transfers between devices: 21.8 us -> 19.1 us
  starting transfers between devices: 39.8 us -> 37.2 us
  local copies, waits for them, and re-layouts: 0.71 us -> 1.93 us
  Pallas kernels: 13.8 us -> 12.9 us
    ppermute x8, starting transfers between devices: 13.5 us -> 9.95 us  [exchange(): lax.ppermute(array, 'dp', [(i, i ^ 2 * e ^ swap) for i in range(dp_count)])]
    ppermute x21, waiting for transfers between devices: 14 us -> 11.9 us  [ring_send(): lax.ppermute(a, 'dp', ring_pairs(chips, step, swap * n))]
    ppermute x1, starting transfers between devices: 1.6 us -> 0.01 us  [ring_body(): x_d = lax.ppermute(x_other, ('dp', 'mp'), both_pairs)]
    ppermute x1, starting transfers between devices: 1.49 us -> 3 us  [ring_body(): x_b = lax.ppermute(x_mine, 'mp', mp_pairs)]
    ppermute x21, starting transfers between devices: 22.1 us -> 23.5 us  [ring_send(): lax.ppermute(a, 'dp', ring_pairs(chips, step, swap * n))]
    unnamed x26 -> x24, local copies, waits for them, and re-layouts: 0.7 us -> 1.92 us
    ppermute x8, waiting for transfers between devices: 6.78 us -> 5.93 us  [exchange(): lax.ppermute(array, 'dp', [(i, i ^ 2 * e ^ swap) for i in range(dp_count)])]
  transfers between devices with their start and end apart: 36 -> 36, of which waited for: 16 -> 17; matrix products, arithmetic and copies ran while one was open for 0% -> 0% of each run, Pallas kernels for 9% -> 9%
where the time goes in v5:
time: 72.9 us; the launch traced here: 72 us
  starting transfers between devices  37.2 us (51%)
  waiting for transfers between devices  19.1 us (26%)
  Pallas kernels  12.9 us (18%)
  local copies, waits for them, and re-layouts  1.93 us (3%)
  between operations  0.84 us (1%)
    ppermute x21, starting transfers between devices, ring_send(): lax.ppermute(a, 'dp', ring_pairs(chips, step, swap * n))  23.5 us
    ppermute x21, waiting for transfers between devices, ring_send(): lax.ppermute(a, 'dp', ring_pairs(chips, step, swap * n))  11.9 us
    ppermute x8, starting transfers between devices, exchange(): lax.ppermute(array, 'dp', [(i, i ^ 2 * e ^ swap) for i in range(dp_count)])  9.95 us
    ppermute x8, waiting for transfers between devices, exchange(): lax.ppermute(array, 'dp', [(i, i ^ 2 * e ^ swap) for i in range(dp_count)])  5.93 us
    pallas_call x2, Pallas kernels, cached(): call(functools.partial(cached_kernel, chips, pages_dev, old, away), outs,...  5.17 us
    ppermute x1, starting transfers between devices, ring_body(): x_b = lax.ppermute(x_mine, 'mp', mp_pairs)  3 us
    pallas_call x1, Pallas kernels, ring_body(): call(functools.partial(fresh_kernel, chips, pages_dev), [((rows, group *...  2.58 us
    pallas_call x1, Pallas kernels, ring_body(): call(functools.partial(split_kernel, old), [((rows, half_width // 2), bf)...  2.1 us
  transfers between devices with their start and end apart: 36, of which 17 were waited for; matrix products, arithmetic and copies ran while one was open for 0% of the time, Pallas kernels for 9%

profile of v5, /device:TPU:0, one launch (start us, length us, event | category | flops | bytes accessed | tf_op | source)
XLA Modules:
  0.0 72.0 jit_solution(6306733878309175121)
XLA Ops:
  0.7 2.1 %split.1 = (bf16[64,1024]{1,0:T(8,128)(2,1)}, bf16[64,1024]{1,0:T(8,128)(2,1)}, bf16[4,128,128]{2,1,0:T(8,128)(2,1)}, bf16[768,128]{1,0:T(8,128)(2,1)}) custom-call(bf16[64,2048]{1,0:T(8,128)(2,1)} %f_ref.1, bf16[64,1024]{1,0:T(8,128)(2,1)} %q_ref.3, bf16[3,128,256]{2,1,0:T(8,128)(2,1)} %kp_ref.3, bf16[3,128,256]{2,1,0:T(8,128)(2,1)} %vp_ref.3), custom_call_target="tpu_custom_call" | custom-call | tf_op jit(solution)/shard_map/split/pallas_call | solution.py:642
  2.8 3.0 %collective-permute-start = (bf16[64,1024]{1,0:T(8,128)(2,1)}, bf16[64,1024]{1,0:T(8,128)(2,1)S(1)}, u32[]{:S(2)}, u32[]{:S(2)}) collective-permute-start(bf16[64,1024]{1,0:T(8,128)(2,1)} %get-tuple-element.39.a_ref), channel_id=1, source_target_pairs={{0,1},{1,0},{2,3},{3,2},{4,5},{5,4},{6,7},{7,6},{8,9},{9,8},{10,11... | collective-permute-start | bytes 393224 | tf_op jit(solution)/shard_map/ppermute | solution.py:657
  5.8 1.6 %collective-permute-start.5 = (bf16[256,256]{1,0:T(8,128)(2,1)S(1)}, bf16[256,256]{1,0:T(8,128)(2,1)S(1)}, u32[]{:S(2)}, u32[]{:S(2)}) collective-permute-start(bf16[256,256]{1,0:T(8,128)(2,1)S(1)} %copy-done.5), channel_id=1, source_target_pairs={{0,8},{2,10},{8,16},{10,18},{16,24},{18,26},{24,28},{26,30},{28,20... | collective-permute-start | bytes 393224 | tf_op jit(solution)/shard_map/ppermute | solution.py:603
  7.8 1.6 %collective-permute-start.12 = (bf16[256,256]{1,0:T(8,128)(2,1)S(1)}, bf16[256,256]{1,0:T(8,128)(2,1)S(1)}, u32[]{:S(2)}, u32[]{:S(2)}) collective-permute-start(bf16[256,256]{1,0:T(8,128)(2,1)S(1)} %copy-done.6), channel_id=1, source_target_pairs={{0,8},{2,10},{8,16},{10,18},{16,24},{18,26},{24,28},{26,30},{28,20... | collective-permute-start | bytes 393224 | tf_op jit(solution)/shard_map/ppermute | solution.py:603
  9.5 1.8 %collective-permute-start.4 = (bf16[256,256]{1,0:T(8,128)(2,1)S(1)}, bf16[256,256]{1,0:T(8,128)(2,1)S(1)}, u32[]{:S(2)}, u32[]{:S(2)}) collective-permute-start(bf16[256,256]{1,0:T(8,128)(2,1)S(1)} %copy-done.5), channel_id=1, source_target_pairs={{0,4},{2,6},{8,0},{10,2},{16,8},{18,10},{24,16},{26,18},{28,24},{3... | collective-permute-start | bytes 393224 | tf_op jit(solution)/shard_map/ppermute | solution.py:603
  11.2 1.1 %collective-permute-start.7 = (bf16[256,256]{1,0:T(8,128)(2,1)S(1)}, bf16[256,256]{1,0:T(8,128)(2,1)S(1)}, u32[]{:S(2)}, u32[]{:S(2)}) collective-permute-start(bf16[256,256]{1,0:T(8,128)(2,1)S(1)} %collective-permute-done.5.refs_2_), channel_id=1, source_target_pairs={{0,8},{2,10},{8,16},{10,18},{16,24},{18,26},{24,28},{26,30},{28,20... | collective-permute-start | bytes 393224 | tf_op jit(solution)/shard_map/ppermute | solution.py:603
  14.1 1.6 %collective-permute-start.14 = (bf16[256,256]{1,0:T(8,128)(2,1)S(1)}, bf16[256,256]{1,0:T(8,128)(2,1)S(1)}, u32[]{:S(2)}, u32[]{:S(2)}) collective-permute-start(bf16[256,256]{1,0:T(8,128)(2,1)S(1)} %collective-permute-done.12.refs_10_), channel_id=1, source_target_pairs={{0,8},{2,10},{8,16},{10,18},{16,24},{18,26},{24,28},{26,30},{28,20... | collective-permute-start | bytes 393224 | tf_op jit(solution)/shard_map/ppermute | solution.py:603
  15.8 1.3 %collective-permute-start.6 = (bf16[256,256]{1,0:T(8,128)(2,1)S(1)}, bf16[256,256]{1,0:T(8,128)(2,1)S(1)}, u32[]{:S(2)}, u32[]{:S(2)}) collective-permute-start(bf16[256,256]{1,0:T(8,128)(2,1)S(1)} %collective-permute-done.4.refs_1_), channel_id=1, source_target_pairs={{0,4},{2,6},{8,0},{10,2},{16,8},{18,10},{24,16},{26,18},{28,24},{3... | collective-permute-start | bytes 393224 | tf_op jit(solution)/shard_map/ppermute | solution.py:603
  17.1 1.0 %collective-permute-start.9 = (bf16[256,256]{1,0:T(8,128)(2,1)S(1)}, bf16[256,256]{1,0:T(8,128)(2,1)S(1)}, u32[]{:S(2)}, u32[]{:S(2)}) collective-permute-start(bf16[256,256]{1,0:T(8,128)(2,1)S(1)} %collective-permute-done.7.refs_4_), channel_id=1, source_target_pairs={{0,8},{2,10},{8,16},{10,18},{16,24},{18,26},{24,28},{26,30},{28,20... | collective-permute-start | bytes 393224 | tf_op jit(solution)/shard_map/ppermute | solution.py:603
  19.4 1.1 %collective-permute-done.14.refs_12_ = bf16[256,256]{1,0:T(8,128)(2,1)S(1)} collective-permute-done((bf16[256,256]{1,0:T(8,128)(2,1)S(1)}, bf16[256,256]{1,0:T(8,128)(2,1)S(1)}, u32[]{:S(2)}, u32[]{:S(2)}) %collective-permute-start.14) | collective-permute-done | bytes 131104 | tf_op jit(solution)/shard_map/ppermute | solution.py:603
  20.5 1.2 %collective-permute-start.16 = (bf16[256,256]{1,0:T(8,128)(2,1)S(1)}, bf16[256,256]{1,0:T(8,128)(2,1)S(1)}, u32[]{:S(2)}, u32[]{:S(2)}) collective-permute-start(bf16[256,256]{1,0:T(8,128)(2,1)S(1)} %collective-permute-done.14.refs_12_), channel_id=1, source_target_pairs={{0,8},{2,10},{8,16},{10,18},{16,24},{18,26},{24,28},{26,30},{28,20... | collective-permute-start | bytes 393224 | tf_op jit(solution)/shard_map/ppermute | solution.py:603
  21.8 1.6 %collective-permute-start.8 = (bf16[256,256]{1,0:T(8,128)(2,1)S(1)}, bf16[256,256]{1,0:T(8,128)(2,1)S(1)}, u32[]{:S(2)}, u32[]{:S(2)}) collective-permute-start(bf16[256,256]{1,0:T(8,128)(2,1)S(1)} %collective-permute-done.6.refs_3_), channel_id=1, source_target_pairs={{0,4},{2,6},{8,0},{10,2},{16,8},{18,10},{24,16},{26,18},{28,24},{3... | collective-permute-start | bytes 393224 | tf_op jit(solution)/shard_map/ppermute | solution.py:603
  24.1 1.3 %collective-permute-start.17 = (bf16[256,256]{1,0:T(8,128)(2,1)S(1)}, bf16[256,256]{1,0:T(8,128)(2,1)S(1)}, u32[]{:S(2)}, u32[]{:S(2)}) collective-permute-start(bf16[256,256]{1,0:T(8,128)(2,1)S(1)} %collective-permute-done.15.refs_13_), channel_id=1, source_target_pairs={{0,4},{2,6},{8,0},{10,2},{16,8},{18,10},{24,16},{26,18},{28,24},{3... | collective-permute-start | bytes 393224 | tf_op jit(solution)/shard_map/ppermute | solution.py:603
  30.5 1.6 %collective-permute-start.21 = (bf16[4,128,128]{2,1,0:T(8,128)(2,1)S(1)}, bf16[4,128,128]{2,1,0:T(8,128)(2,1)S(1)}, u32[]{:S(2)}, u32[]{:S(2)}) collective-permute-start(bf16[4,128,128]{2,1,0:T(8,128)(2,1)S(1)} %copy-done.2), channel_id=1, source_target_pairs={{0,4},{2,6},{4,0},{6,2},{8,12},{10,14},{12,8},{14,10},{16,20},{18,... | collective-permute-start | bytes 393224 | tf_op jit(solution)/shard_map/ppermute | solution.py:636
  32.1 1.6 %collective-permute-start.22 = (bf16[4,128,128]{2,1,0:T(8,128)(2,1)S(1)}, bf16[4,128,128]{2,1,0:T(8,128)(2,1)S(1)}, u32[]{:S(2)}, u32[]{:S(2)}) collective-permute-start(bf16[4,128,128]{2,1,0:T(8,128)(2,1)S(1)} %get-tuple-element.55.refs_4_), channel_id=1, source_target_pairs={{0,8},{2,10},{4,12},{6,14},{8,0},{10,2},{12,4},{14,6},{16,24},{18,... | collective-permute-start | bytes 393224 | tf_op jit(solution)/shard_map/ppermute | solution.py:636
  34.7 1.4 %collective-permute-done.21.refs_1_ = bf16[4,128,128]{2,1,0:T(8,128)(2,1)S(1)} collective-permute-done((bf16[4,128,128]{2,1,0:T(8,128)(2,1)S(1)}, bf16[4,128,128]{2,1,0:T(8,128)(2,1)S(1)}, u32[]{:S(2)}, u32[]{:S(2)}) %collective-permute-start.21) | collective-permute-done | bytes 131104 | tf_op jit(solution)/shard_map/ppermute | solution.py:636
  36.1 2.4 %collective-permute-done.22.refs_6_ = bf16[4,128,128]{2,1,0:T(8,128)(2,1)S(1)} collective-permute-done((bf16[4,128,128]{2,1,0:T(8,128)(2,1)S(1)}, bf16[4,128,128]{2,1,0:T(8,128)(2,1)S(1)}, u32[]{:S(2)}, u32[]{:S(2)}) %collective-permute-start.22) | collective-permute-done | bytes 131104 | tf_op jit(solution)/shard_map/ppermute | solution.py:636
  38.5 1.6 %collective-permute-start.25 = (bf16[4,128,128]{2,1,0:T(8,128)(2,1)S(1)}, bf16[4,128,128]{2,1,0:T(8,128)(2,1)S(1)}, u32[]{:S(2)}, u32[]{:S(2)}) collective-permute-start(bf16[4,128,128]{2,1,0:T(8,128)(2,1)S(1)} %collective-permute-done.21.refs_1_), channel_id=1, source_target_pairs={{0,8},{2,10},{4,12},{6,14},{8,0},{10,2},{12,4},{14,6},{16,24},{18,... | collective-permute-start | bytes 393224 | tf_op jit(solution)/shard_map/ppermute | solution.py:636
  40.5 2.6 %collective-permute-start.23 = (bf16[512,128]{1,0:T(8,128)(2,1)S(1)}, bf16[512,128]{1,0:T(8,128)(2,1)S(1)}, u32[]{:S(2)}, u32[]{:S(2)}) collective-permute-start(bf16[512,128]{1,0:T(8,128)(2,1)S(1)} %get-tuple-element.56.qs_ref), channel_id=1, source_target_pairs={{0,16},{2,18},{4,20},{6,22},{8,24},{10,26},{12,28},{14,30},{16,0},... | collective-permute-start | bytes 393224 | tf_op jit(solution)/shard_map/ppermute | solution.py:636
  43.6 1.6 %collective-permute-start.20 = (bf16[128,256]{1,0:T(8,128)(2,1)S(1)}, bf16[128,256]{1,0:T(8,128)(2,1)S(1)}, u32[]{:S(2)}, u32[]{:S(2)}) collective-permute-start(bf16[128,256]{1,0:T(8,128)(2,1)S(1)} %rotary.1.refs_0_), channel_id=1, source_target_pairs={{0,4},{2,6},{8,0},{10,2},{16,8},{18,10},{24,16},{26,18},{28,24},{3... | collective-permute-start | bytes 196616 | tf_op jit(solution)/shard_map/ppermute | solution.py:603
  45.2 2.1 %collective-permute-done.23.qs_ref = bf16[512,128]{1,0:T(8,128)(2,1)S(1)} collective-permute-done((bf16[512,128]{1,0:T(8,128)(2,1)S(1)}, bf16[512,128]{1,0:T(8,128)(2,1)S(1)}, u32[]{:S(2)}, u32[]{:S(2)}) %collective-permute-start.23) | collective-permute-done | bytes 131104 | tf_op jit(solution)/shard_map/ppermute | solution.py:636
  47.3 3.9 %attend_cached_away.1 = bf16[144,512]{1,0:T(8,128)(2,1)S(1)} custom-call(s32[3]{0:T(128)S(1)} %copy-done.9, s32[3,25]{1,0:T(4,128)S(1)} %copy-done.8, s32[8,128]{1,0:T(8,128)S(1)} %bitcast.2, bf16[512,128]{1,0:T(8,128)(2,1)S(1)} %collective-permute-done.23.qs_ref, bf16[4,128,128]{2,1,0:T(8,128)(2,1)S(1)} %copy-done.2, ...), custom_call_target="tpu_custom_call" | custom-call | tf_op jit(solution)/shard_map/attend_cached_away/pallas_call | solution.py:716
  51.2 1.8 %collective-permute-start.28 = (bf16[128,256]{1,0:T(8,128)(2,1)S(1)}, bf16[128,256]{1,0:T(8,128)(2,1)S(1)}, u32[]{:S(2)}, u32[]{:S(2)}) collective-permute-start(bf16[128,256]{1,0:T(8,128)(2,1)S(1)} %collective-permute-done.19.refs_2_), channel_id=1, source_target_pairs={{0,8},{2,10},{8,16},{10,18},{16,24},{18,26},{24,28},{26,30},{28,20... | collective-permute-start | bytes 196616 | tf_op jit(solution)/shard_map/ppermute | solution.py:603
  53.3 1.2 %collective-permute-start.30 = (bf16[144,512]{1,0:T(8,128)(2,1)S(1)}, bf16[144,512]{1,0:T(8,128)(2,1)S(1)}, u32[]{:S(2)}, u32[]{:S(2)}) collective-permute-start(bf16[144,512]{1,0:T(8,128)(2,1)S(1)} %attend_cached_away.1), channel_id=1, source_target_pairs={{0,16},{2,18},{4,20},{6,22},{8,24},{10,26},{12,28},{14,30},{16,0},... | collective-permute-start | bytes 442376 | tf_op jit(solution)/shard_map/ppermute | solution.py:636
  54.5 1.3 %attend_cached_here.1 = (f32[1,512]{1,0:T(1,128)S(1)}, f32[1,512]{1,0:T(1,128)S(1)}, f32[128,512]{1,0:T(8,128)S(1)}) custom-call(s32[3]{0:T(128)S(1)} %copy-done.9, s32[3,25]{1,0:T(4,128)S(1)} %copy-done.8, s32[8,128]{1,0:T(8,128)S(1)} %bitcast.3, bf16[512,128]{1,0:T(8,128)(2,1)S(1)} %get-tuple-element.56.qs_ref, bf16[4,128,128]{2,1,0:T(8,128)(2,1)S(1)} %copy-done.2, ...), custom_call_target="tpu_custom_call" | custom-call | tf_op jit(solution)/shard_map/attend_cached_here/pallas_call | solution.py:716
  55.8 2.0 %collective-permute-done.29.refs_3_ = bf16[128,256]{1,0:T(8,128)(2,1)S(1)} collective-permute-done((bf16[128,256]{1,0:T(8,128)(2,1)S(1)}, bf16[128,256]{1,0:T(8,128)(2,1)S(1)}, u32[]{:S(2)}, u32[]{:S(2)}) %collective-permute-start.29) | collective-permute-done | bytes 65568 | tf_op jit(solution)/shard_map/ppermute | solution.py:603
  57.9 2.0 %collective-permute-start.31 = (bf16[128,256]{1,0:T(8,128)(2,1)S(1)}, bf16[128,256]{1,0:T(8,128)(2,1)S(1)}, u32[]{:S(2)}, u32[]{:S(2)}) collective-permute-start(bf16[128,256]{1,0:T(8,128)(2,1)S(1)} %collective-permute-done.29.refs_3_), channel_id=1, source_target_pairs={{0,4},{2,6},{8,0},{10,2},{16,8},{18,10},{24,16},{26,18},{28,24},{3... | collective-permute-start | bytes 196616 | tf_op jit(solution)/shard_map/ppermute | solution.py:603
  59.9 2.2 %collective-permute-done.32.refs_6_ = bf16[128,256]{1,0:T(8,128)(2,1)S(1)} collective-permute-done((bf16[128,256]{1,0:T(8,128)(2,1)S(1)}, bf16[128,256]{1,0:T(8,128)(2,1)S(1)}, u32[]{:S(2)}, u32[]{:S(2)}) %collective-permute-start.32) | collective-permute-done | bytes 65568 | tf_op jit(solution)/shard_map/ppermute | solution.py:603
  62.4 4.0 %collective-permute-done.33.refs_7_ = bf16[128,256]{1,0:T(8,128)(2,1)S(1)} collective-permute-done((bf16[128,256]{1,0:T(8,128)(2,1)S(1)}, bf16[128,256]{1,0:T(8,128)(2,1)S(1)}, u32[]{:S(2)}, u32[]{:S(2)}) %collective-permute-start.33) | collective-permute-done | bytes 65568 | tf_op jit(solution)/shard_map/ppermute | solution.py:603
  66.4 2.6 %attend_new.1 = (bf16[64,512]{1,0:T(8,128)(2,1)S(1)}, bf16[64,512]{1,0:T(8,128)(2,1)S(1)}, bf16[3,128,256]{2,1,0:T(8,128)(2,1)S(1)}, bf16[3,128,256]{2,1,0:T(8,128)(2,1)S(1)}, s32[6]{0:T(128)S(1)}) custom-call(s32[3]{0:T(128)S(1)} %copy-done.9, s32[3,25]{1,0:T(4,128)S(1)} %copy-done.8, s32[8,128]{1,0:T(8,128)S(1)} %bitcast.4, ...), custom_call_target="tpu_custom_call" | custom-call | tf_op jit(solution)/shard_map/attend_new/pallas_call | solution.py:744
  69.5 1.0 %collective-permute-done.34.attr_ref = bf16[64,512]{1,0:T(8,128)(2,1)S(1)} collective-permute-done((bf16[64,512]{1,0:T(8,128)(2,1)S(1)}, bf16[64,512]{1,0:T(8,128)(2,1)S(1)}, u32[]{:S(2)}, u32[]{:S(2)}) %collective-permute-start.34) | collective-permute-done | bytes 65568 | tf_op jit(solution)/shard_map/ppermute | solution.py:779
  70.6 1.5 %join.1 = (bf16[64,1024]{1,0:T(8,128)(2,1)}, bf16[3,128,256]{2,1,0:T(8,128)(2,1)}, bf16[3,128,256]{2,1,0:T(8,128)(2,1)}) custom-call(s32[6]{0:T(128)S(1)} %get-tuple-element.70.info_ref, bf16[64,512]{1,0:T(8,128)(2,1)S(1)} %get-tuple-element.71.attc_ref, bf16[64,512]{1,0:T(8,128)(2,1)S(1)} %collective-permute-done.34.attr_ref, ...), custom_call_target="tpu_custom_call" | custom-call | tf_op jit(solution)/shard_map/join/pallas_call | solution.py:780
  (74 shorter events, 12.8 us)
Async XLA Ops:
  2.8 6.7 %collective-permute-start = (bf16[64,1024]{1,0:T(8,128)(2,1)}, bf16[64,1024]{1,0:T(8,128)(2,1)S(1)}, u32[]{:S(2)}, u32[]{:S(2)}) collective-permute-start(bf16[64,1024]{1,0:T(8,128)(2,1)} %get-tuple-element.39.a_ref), channel_id=1, source_target_pairs={{0,1},{1,0},{2,3},{3,2},{4,5},{5,4},{6,7},{7,6},{8,9},{9,8},{10,11... | collective-permute-start | bytes 393224 | tf_op jit(solution)/shard_map/ppermute | solution.py:657
  5.8 5.5 %collective-permute-start.5 = (bf16[256,256]{1,0:T(8,128)(2,1)S(1)}, bf16[256,256]{1,0:T(8,128)(2,1)S(1)}, u32[]{:S(2)}, u32[]{:S(2)}) collective-permute-start(bf16[256,256]{1,0:T(8,128)(2,1)S(1)} %copy-done.5), channel_id=1, source_target_pairs={{0,8},{2,10},{8,16},{10,18},{16,24},{18,26},{24,28},{26,30},{28,20... | collective-permute-start | bytes 393224 | tf_op jit(solution)/shard_map/ppermute | solution.py:603
  7.4 5.0 %collective-permute-start.11 = (bf16[256,256]{1,0:T(8,128)(2,1)S(1)}, bf16[256,256]{1,0:T(8,128)(2,1)S(1)}, u32[]{:S(2)}, u32[]{:S(2)}) collective-permute-start(bf16[256,256]{1,0:T(8,128)(2,1)S(1)} %copy-done.6), channel_id=1, source_target_pairs={{0,4},{2,6},{8,0},{10,2},{16,8},{18,10},{24,16},{26,18},{28,24},{3... | collective-permute-start | bytes 393224 | tf_op jit(solution)/shard_map/ppermute | solution.py:603
  7.8 5.5 %collective-permute-start.1 = (bf16[64,1024]{1,0:T(8,128)(2,1)}, bf16[64,1024]{1,0:T(8,128)(2,1)S(1)}, u32[]{:S(2)}, u32[]{:S(2)}) collective-permute-start(bf16[64,1024]{1,0:T(8,128)(2,1)} %get-tuple-element.40), channel_id=1, source_target_pairs={{0,2},{2,0},{4,6},{6,4},{8,10},{10,8},{12,14},{14,12},{16,18},{18,... | collective-permute-start | bytes 393224 | tf_op jit(solution)/shard_map/ppermute | solution.py:658
  7.8 6.3 %collective-permute-start.12 = (bf16[256,256]{1,0:T(8,128)(2,1)S(1)}, bf16[256,256]{1,0:T(8,128)(2,1)S(1)}, u32[]{:S(2)}, u32[]{:S(2)}) collective-permute-start(bf16[256,256]{1,0:T(8,128)(2,1)S(1)} %copy-done.6), channel_id=1, source_target_pairs={{0,8},{2,10},{8,16},{10,18},{16,24},{18,26},{24,28},{26,30},{28,20... | collective-permute-start | bytes 393224 | tf_op jit(solution)/shard_map/ppermute | solution.py:603
  9.5 6.3 %collective-permute-start.4 = (bf16[256,256]{1,0:T(8,128)(2,1)S(1)}, bf16[256,256]{1,0:T(8,128)(2,1)S(1)}, u32[]{:S(2)}, u32[]{:S(2)}) collective-permute-start(bf16[256,256]{1,0:T(8,128)(2,1)S(1)} %copy-done.5), channel_id=1, source_target_pairs={{0,4},{2,6},{8,0},{10,2},{16,8},{18,10},{24,16},{26,18},{28,24},{3... | collective-permute-start | bytes 393224 | tf_op jit(solution)/shard_map/ppermute | solution.py:603
  11.2 5.8 %collective-permute-start.7 = (bf16[256,256]{1,0:T(8,128)(2,1)S(1)}, bf16[256,256]{1,0:T(8,128)(2,1)S(1)}, u32[]{:S(2)}, u32[]{:S(2)}) collective-permute-start(bf16[256,256]{1,0:T(8,128)(2,1)S(1)} %collective-permute-done.5.refs_2_), channel_id=1, source_target_pairs={{0,8},{2,10},{8,16},{10,18},{16,24},{18,26},{24,28},{26,30},{28,20... | collective-permute-start | bytes 393224 | tf_op jit(solution)/shard_map/ppermute | solution.py:603
  12.4 5.8 %collective-permute-start.13 = (bf16[256,256]{1,0:T(8,128)(2,1)S(1)}, bf16[256,256]{1,0:T(8,128)(2,1)S(1)}, u32[]{:S(2)}, u32[]{:S(2)}) collective-permute-start(bf16[256,256]{1,0:T(8,128)(2,1)S(1)} %collective-permute-done.11.refs_9_), channel_id=1, source_target_pairs={{0,4},{2,6},{8,0},{10,2},{16,8},{18,10},{24,16},{26,18},{28,24},{3... | collective-permute-start | bytes 393224 | tf_op jit(solution)/shard_map/ppermute | solution.py:603
  13.3 6.0 %collective-permute-start.2 = (bf16[64,1024]{1,0:T(8,128)(2,1)}, bf16[64,1024]{1,0:T(8,128)(2,1)S(1)}, u32[]{:S(2)}, u32[]{:S(2)}) collective-permute-start(bf16[64,1024]{1,0:T(8,128)(2,1)} %get-tuple-element.40), channel_id=1, source_target_pairs={{0,3},{1,2},{2,1},{3,0},{4,7},{5,6},{6,5},{7,4},{8,11},{9,10},{10,... | collective-permute-start | bytes 393224 | tf_op jit(solution)/shard_map/ppermute | solution.py:659
  14.1 6.4 %collective-permute-start.14 = (bf16[256,256]{1,0:T(8,128)(2,1)S(1)}, bf16[256,256]{1,0:T(8,128)(2,1)S(1)}, u32[]{:S(2)}, u32[]{:S(2)}) collective-permute-start(bf16[256,256]{1,0:T(8,128)(2,1)S(1)} %collective-permute-done.12.refs_10_), channel_id=1, source_target_pairs={{0,8},{2,10},{8,16},{10,18},{16,24},{18,26},{24,28},{26,30},{28,20... | collective-permute-start | bytes 393224 | tf_op jit(solution)/shard_map/ppermute | solution.py:603
  15.8 6.0 %collective-permute-start.6 = (bf16[256,256]{1,0:T(8,128)(2,1)S(1)}, bf16[256,256]{1,0:T(8,128)(2,1)S(1)}, u32[]{:S(2)}, u32[]{:S(2)}) collective-permute-start(bf16[256,256]{1,0:T(8,128)(2,1)S(1)} %collective-permute-done.4.refs_1_), channel_id=1, source_target_pairs={{0,4},{2,6},{8,0},{10,2},{16,8},{18,10},{24,16},{26,18},{28,24},{3... | collective-permute-start | bytes 393224 | tf_op jit(solution)/shard_map/ppermute | solution.py:603
  17.1 6.3 %collective-permute-start.9 = (bf16[256,256]{1,0:T(8,128)(2,1)S(1)}, bf16[256,256]{1,0:T(8,128)(2,1)S(1)}, u32[]{:S(2)}, u32[]{:S(2)}) collective-permute-start(bf16[256,256]{1,0:T(8,128)(2,1)S(1)} %collective-permute-done.7.refs_4_), channel_id=1, source_target_pairs={{0,8},{2,10},{8,16},{10,18},{16,24},{18,26},{24,28},{26,30},{28,20... | collective-permute-start | bytes 393224 | tf_op jit(solution)/shard_map/ppermute | solution.py:603
  18.1 6.0 %collective-permute-start.15 = (bf16[256,256]{1,0:T(8,128)(2,1)S(1)}, bf16[256,256]{1,0:T(8,128)(2,1)S(1)}, u32[]{:S(2)}, u32[]{:S(2)}) collective-permute-start(bf16[256,256]{1,0:T(8,128)(2,1)S(1)} %collective-permute-done.13.refs_11_), channel_id=1, source_target_pairs={{0,4},{2,6},{8,0},{10,2},{16,8},{18,10},{24,16},{26,18},{28,24},{3... | collective-permute-start | bytes 393224 | tf_op jit(solution)/shard_map/ppermute | solution.py:603
  19.2 8.8 %collective-permute-start.3 = (bf16[768,128]{1,0:T(8,128)(2,1)}, bf16[768,128]{1,0:T(8,128)(2,1)S(1)}, u32[]{:S(2)}, u32[]{:S(2)}) collective-permute-start(bf16[768,128]{1,0:T(8,128)(2,1)} %get-tuple-element.42), channel_id=1, source_target_pairs={{0,2},{2,0},{4,6},{6,4},{8,10},{10,8},{12,14},{14,12},{16,18},{18,... | collective-permute-start | bytes 589832 | tf_op jit(solution)/shard_map/ppermute | solution.py:656
  20.5 7.6 %collective-permute-start.16 = (bf16[256,256]{1,0:T(8,128)(2,1)S(1)}, bf16[256,256]{1,0:T(8,128)(2,1)S(1)}, u32[]{:S(2)}, u32[]{:S(2)}) collective-permute-start(bf16[256,256]{1,0:T(8,128)(2,1)S(1)} %collective-permute-done.14.refs_12_), channel_id=1, source_target_pairs={{0,8},{2,10},{8,16},{10,18},{16,24},{18,26},{24,28},{26,30},{28,20... | collective-permute-start | bytes 393224 | tf_op jit(solution)/shard_map/ppermute | solution.py:603
  21.8 6.4 %collective-permute-start.8 = (bf16[256,256]{1,0:T(8,128)(2,1)S(1)}, bf16[256,256]{1,0:T(8,128)(2,1)S(1)}, u32[]{:S(2)}, u32[]{:S(2)}) collective-permute-start(bf16[256,256]{1,0:T(8,128)(2,1)S(1)} %collective-permute-done.6.refs_3_), channel_id=1, source_target_pairs={{0,4},{2,6},{8,0},{10,2},{16,8},{18,10},{24,16},{26,18},{28,24},{3... | collective-permute-start | bytes 393224 | tf_op jit(solution)/shard_map/ppermute | solution.py:603
  23.4 5.3 %collective-permute-start.10 = (bf16[256,256]{1,0:T(8,128)(2,1)S(1)}, bf16[256,256]{1,0:T(8,128)(2,1)S(1)}, u32[]{:S(2)}, u32[]{:S(2)}) collective-permute-start(bf16[256,256]{1,0:T(8,128)(2,1)S(1)} %collective-permute-done.9.refs_6_), channel_id=1, source_target_pairs={{0,8},{2,10},{8,16},{10,18},{16,24},{18,26},{24,28},{26,30},{28,20... | collective-permute-start | bytes 393224 | tf_op jit(solution)/shard_map/ppermute | solution.py:603
  24.1 5.5 %collective-permute-start.17 = (bf16[256,256]{1,0:T(8,128)(2,1)S(1)}, bf16[256,256]{1,0:T(8,128)(2,1)S(1)}, u32[]{:S(2)}, u32[]{:S(2)}) collective-permute-start(bf16[256,256]{1,0:T(8,128)(2,1)S(1)} %collective-permute-done.15.refs_13_), channel_id=1, source_target_pairs={{0,4},{2,6},{8,0},{10,2},{16,8},{18,10},{24,16},{26,18},{28,24},{3... | collective-permute-start | bytes 393224 | tf_op jit(solution)/shard_map/ppermute | solution.py:603
  30.1 4.5 %collective-permute-start.18 = (f32[128,384]{1,0:T(8,128)S(1)}, f32[128,384]{1,0:T(8,128)S(1)}, u32[]{:S(2)}, u32[]{:S(2)}) collective-permute-start(f32[128,384]{1,0:T(8,128)S(1)} %get-tuple-element.49), channel_id=1, source_target_pairs={{0,2},{2,0},{4,6},{6,4},{8,10},{10,8},{12,14},{14,12},{16,18},{18,... | collective-permute-start | bytes 589832 | tf_op jit(solution)/shard_map/ppermute | solution.py:695
  30.5 5.6 %collective-permute-start.21 = (bf16[4,128,128]{2,1,0:T(8,128)(2,1)S(1)}, bf16[4,128,128]{2,1,0:T(8,128)(2,1)S(1)}, u32[]{:S(2)}, u32[]{:S(2)}) collective-permute-start(bf16[4,128,128]{2,1,0:T(8,128)(2,1)S(1)} %copy-done.2), channel_id=1, source_target_pairs={{0,4},{2,6},{4,0},{6,2},{8,12},{10,14},{12,8},{14,10},{16,20},{18,... | collective-permute-start | bytes 393224 | tf_op jit(solution)/shard_map/ppermute | solution.py:636
  32.1 6.4 %collective-permute-start.22 = (bf16[4,128,128]{2,1,0:T(8,128)(2,1)S(1)}, bf16[4,128,128]{2,1,0:T(8,128)(2,1)S(1)}, u32[]{:S(2)}, u32[]{:S(2)}) collective-permute-start(bf16[4,128,128]{2,1,0:T(8,128)(2,1)S(1)} %get-tuple-element.55.refs_4_), channel_id=1, source_target_pairs={{0,8},{2,10},{4,12},{6,14},{8,0},{10,2},{12,4},{14,6},{16,24},{18,... | collective-permute-start | bytes 393224 | tf_op jit(solution)/shard_map/ppermute | solution.py:636
  33.7 9.5 %collective-permute-start.24 = (bf16[4,128,128]{2,1,0:T(8,128)(2,1)S(1)}, bf16[4,128,128]{2,1,0:T(8,128)(2,1)S(1)}, u32[]{:S(2)}, u32[]{:S(2)}) collective-permute-start(bf16[4,128,128]{2,1,0:T(8,128)(2,1)S(1)} %copy-done.2), channel_id=1, source_target_pairs={{0,8},{2,10},{4,12},{6,14},{8,0},{10,2},{12,4},{14,6},{16,24},{18,... | collective-permute-start | bytes 393224 | tf_op jit(solution)/shard_map/ppermute | solution.py:636
  34.1 9.5 %collective-permute-start.26 = (bf16[4,128,128]{2,1,0:T(8,128)(2,1)S(1)}, bf16[4,128,128]{2,1,0:T(8,128)(2,1)S(1)}, u32[]{:S(2)}, u32[]{:S(2)}) collective-permute-start(bf16[4,128,128]{2,1,0:T(8,128)(2,1)S(1)} %get-tuple-element.55.refs_4_), channel_id=1, source_target_pairs={{0,4},{2,6},{4,0},{6,2},{8,12},{10,14},{12,8},{14,10},{16,20},{18,... | collective-permute-start | bytes 393224 | tf_op jit(solution)/shard_map/ppermute | solution.py:636
  38.5 6.7 %collective-permute-start.25 = (bf16[4,128,128]{2,1,0:T(8,128)(2,1)S(1)}, bf16[4,128,128]{2,1,0:T(8,128)(2,1)S(1)}, u32[]{:S(2)}, u32[]{:S(2)}) collective-permute-start(bf16[4,128,128]{2,1,0:T(8,128)(2,1)S(1)} %collective-permute-done.21.refs_1_), channel_id=1, source_target_pairs={{0,8},{2,10},{4,12},{6,14},{8,0},{10,2},{12,4},{14,6},{16,24},{18,... | collective-permute-start | bytes 393224 | tf_op jit(solution)/shard_map/ppermute | solution.py:636
  40.0 5.2 %collective-permute-start.27 = (bf16[4,128,128]{2,1,0:T(8,128)(2,1)S(1)}, bf16[4,128,128]{2,1,0:T(8,128)(2,1)S(1)}, u32[]{:S(2)}, u32[]{:S(2)}) collective-permute-start(bf16[4,128,128]{2,1,0:T(8,128)(2,1)S(1)} %collective-permute-done.22.refs_6_), channel_id=1, source_target_pairs={{0,4},{2,6},{4,0},{6,2},{8,12},{10,14},{12,8},{14,10},{16,20},{18,... | collective-permute-start | bytes 393224 | tf_op jit(solution)/shard_map/ppermute | solution.py:636
  40.5 6.8 %collective-permute-start.23 = (bf16[512,128]{1,0:T(8,128)(2,1)S(1)}, bf16[512,128]{1,0:T(8,128)(2,1)S(1)}, u32[]{:S(2)}, u32[]{:S(2)}) collective-permute-start(bf16[512,128]{1,0:T(8,128)(2,1)S(1)} %get-tuple-element.56.qs_ref), channel_id=1, source_target_pairs={{0,16},{2,18},{4,20},{6,22},{8,24},{10,26},{12,28},{14,30},{16,0},... | collective-permute-start | bytes 393224 | tf_op jit(solution)/shard_map/ppermute | solution.py:636
  43.2 8.1 %collective-permute-start.19 = (bf16[128,256]{1,0:T(8,128)(2,1)S(1)}, bf16[128,256]{1,0:T(8,128)(2,1)S(1)}, u32[]{:S(2)}, u32[]{:S(2)}) collective-permute-start(bf16[128,256]{1,0:T(8,128)(2,1)S(1)} %rotary.1.refs_0_), channel_id=1, source_target_pairs={{0,8},{2,10},{8,16},{10,18},{16,24},{18,26},{24,28},{26,30},{28,20... | collective-permute-start | bytes 196616 | tf_op jit(solution)/shard_map/ppermute | solution.py:603
  43.6 7.6 %collective-permute-start.20 = (bf16[128,256]{1,0:T(8,128)(2,1)S(1)}, bf16[128,256]{1,0:T(8,128)(2,1)S(1)}, u32[]{:S(2)}, u32[]{:S(2)}) collective-permute-start(bf16[128,256]{1,0:T(8,128)(2,1)S(1)} %rotary.1.refs_0_), channel_id=1, source_target_pairs={{0,4},{2,6},{8,0},{10,2},{16,8},{18,10},{24,16},{26,18},{28,24},{3... | collective-permute-start | bytes 196616 | tf_op jit(solution)/shard_map/ppermute | solution.py:603
  51.2 4.6 %collective-permute-start.28 = (bf16[128,256]{1,0:T(8,128)(2,1)S(1)}, bf16[128,256]{1,0:T(8,128)(2,1)S(1)}, u32[]{:S(2)}, u32[]{:S(2)}) collective-permute-start(bf16[128,256]{1,0:T(8,128)(2,1)S(1)} %collective-permute-done.19.refs_2_), channel_id=1, source_target_pairs={{0,8},{2,10},{8,16},{10,18},{16,24},{18,26},{24,28},{26,30},{28,20... | collective-permute-start | bytes 196616 | tf_op jit(solution)/shard_map/ppermute | solution.py:603
  53.0 4.9 %collective-permute-start.29 = (bf16[128,256]{1,0:T(8,128)(2,1)S(1)}, bf16[128,256]{1,0:T(8,128)(2,1)S(1)}, u32[]{:S(2)}, u32[]{:S(2)}) collective-permute-start(bf16[128,256]{1,0:T(8,128)(2,1)S(1)} %collective-permute-done.20.refs_1_), channel_id=1, source_target_pairs={{0,4},{2,6},{8,0},{10,2},{16,8},{18,10},{24,16},{26,18},{28,24},{3... | collective-permute-start | bytes 196616 | tf_op jit(solution)/shard_map/ppermute | solution.py:603
  53.3 9.1 %collective-permute-start.30 = (bf16[144,512]{1,0:T(8,128)(2,1)S(1)}, bf16[144,512]{1,0:T(8,128)(2,1)S(1)}, u32[]{:S(2)}, u32[]{:S(2)}) collective-permute-start(bf16[144,512]{1,0:T(8,128)(2,1)S(1)} %attend_cached_away.1), channel_id=1, source_target_pairs={{0,16},{2,18},{4,20},{6,22},{8,24},{10,26},{12,28},{14,30},{16,0},... | collective-permute-start | bytes 442376 | tf_op jit(solution)/shard_map/ppermute | solution.py:636
  57.9 4.5 %collective-permute-start.31 = (bf16[128,256]{1,0:T(8,128)(2,1)S(1)}, bf16[128,256]{1,0:T(8,128)(2,1)S(1)}, u32[]{:S(2)}, u32[]{:S(2)}) collective-permute-start(bf16[128,256]{1,0:T(8,128)(2,1)S(1)} %collective-permute-done.29.refs_3_), channel_id=1, source_target_pairs={{0,4},{2,6},{8,0},{10,2},{16,8},{18,10},{24,16},{26,18},{28,24},{3... | collective-permute-start | bytes 196616 | tf_op jit(solution)/shard_map/ppermute | solution.py:603
  (16 other events, 91.4 us)

commit v6 on v5

--- a/solution.py
+++ b/solution.py
@@ -653,6 +653,7 @@
         limit=SPLIT_LIMIT,
         name="split",
     )(features, queries, key_pool, value_pool)
+    core_send, _ = lax.optimization_barrier((core_send, w_got[-1]))
     core_got = lax.ppermute(core_send, "dp", core_pairs)
     x_b = lax.ppermute(x_mine, "mp", mp_pairs)
     x_c = lax.ppermute(x_other, "dp", core_pairs)
@@ -705,7 +706,7 @@
     )(part_keep, part_got, cosine, sine)
     new = {0: fresh}
     new[-1], new[1] = ring_send(chips, [fresh], 1)[0], ring_send(chips, [fresh], -1)[0]
-    late_y, late_z, late_q, _ = lax.optimization_barrier((y_near, z_far, q_rows, fresh))
+    late_y, late_z, late_q, _ = lax.optimization_barrier((y_near, z_far, q_rows, (new[-1], new[1])))
     q_away = exchange(late_q, chips // 2)
     near = [kv_mine, y_near, z_near, exchange(late_y, 2)]
     far = [kv_other, y_far, z_far, exchange(late_z, 1)]
@@ -733,13 +734,13 @@
     here = cached(
         q_rows, 0, [((1, columns), f32), ((1, columns), f32), ((HD, columns), f32)], "attend_cached_here"
     )
-    beside = {2: away, 3: here}
-    for d in range(2, chips // 2):
-        right, left, beside[d] = lax.optimization_barrier((new[1 - d], new[d - 1], beside[d]))
-        new[-d], new[d] = ring_send(chips, [right], 1)[0], ring_send(chips, [left], -1)[0]
-    (new[chips // 2],) = ring_send(chips, [new[1 - chips // 2]], 1)
-    back = exchange(beside[2], chips // 2)
-    top, total, acc = beside[3]
+    new[-2], new[2] = ring_send(chips, [new[-1]], 1)[0], ring_send(chips, [new[1]], -1)[0]
+    right, left, away = lax.optimization_barrier((new[-2], new[2], away))
+    new[-3], new[3] = ring_send(chips, [right], 1)[0], ring_send(chips, [left], -1)[0]
+    right, here = lax.optimization_barrier((new[-3], here))
+    (new[chips // 2],) = ring_send(chips, [right], 1)
+    back = exchange(away, chips // 2)
+    top, total, acc = here
 
     att_other, att_mine, rows_other, rows_mine, info = call(
         functools.partial(fresh_kernel, chips, pages_dev),

time: 72.9 us -> 69.4 us (0.952)
  the two profiles are of different devices: /device:TPU:0 before, /device:TPU:13 now
where the time goes in v6:
time: 69.4 us; the launch traced here: 69.5 us
  starting transfers between devices  34.7 us (50%)
  waiting for transfers between devices  19.1 us (28%)
  Pallas kernels  13.3 us (19%)
  local copies, waits for them, and re-layouts  1.61 us (2%)
  between operations  0.84 us (1%)
    ppermute x21, starting transfers between devices, ring_send(): lax.ppermute(a, 'dp', ring_pairs(chips, step, swap * n))  15.3 us
    ppermute x21, waiting for transfers between devices, ring_send(): lax.ppermute(a, 'dp', ring_pairs(chips, step, swap * n))  10.9 us
    ppermute x1, starting transfers between devices, ring_body(): rows_got = lax.ppermute(rows_other, 'dp', core_pairs)  6.37 us
    pallas_call x2, Pallas kernels, cached(): call(functools.partial(cached_kernel, chips, pages_dev, old, away), outs,...  5.1 us
    ppermute x8, starting transfers between devices, exchange(): lax.ppermute(array, 'dp', [(i, i ^ 2 * e ^ swap) for i in range(dp_count)])  4.62 us
    ppermute x8, waiting for transfers between devices, exchange(): lax.ppermute(array, 'dp', [(i, i ^ 2 * e ^ swap) for i in range(dp_count)])  4.57 us
    ppermute x1, starting transfers between devices, ring_body(): x_d = lax.ppermute(x_other, ('dp', 'mp'), both_pairs)  3.48 us
    pallas_call x1, Pallas kernels, ring_body(): call(functools.partial(fresh_kernel, chips, pages_dev), [((rows, group *...  3.01 us
  transfers between devices with their start and end apart: 36, of which 15 were waited for; matrix products, arithmetic and copies ran while one was open for 0% of the time, Pallas kernels for 9%

profile of v6, /device:TPU:13, one launch (start us, length us, event | category | flops | bytes accessed | tf_op | source)
XLA Modules:
  0.0 69.5 jit_solution(15736354787542232026)
XLA Ops:
  0.7 2.1 %split.1 = (bf16[64,1024]{1,0:T(8,128)(2,1)}, bf16[64,1024]{1,0:T(8,128)(2,1)}, bf16[4,128,128]{2,1,0:T(8,128)(2,1)}, bf16[768,128]{1,0:T(8,128)(2,1)}) custom-call(bf16[64,2048]{1,0:T(8,128)(2,1)} %f_ref.1, bf16[64,1024]{1,0:T(8,128)(2,1)} %q_ref.3, bf16[3,128,256]{2,1,0:T(8,128)(2,1)} %kp_ref.3, bf16[3,128,256]{2,1,0:T(8,128)(2,1)} %vp_ref.3), custom_call_target="tpu_custom_call" | custom-call | tf_op jit(solution)/shard_map/split/pallas_call | solution.py:642
  2.8 1.3 %collective-permute-start = (bf16[64,1024]{1,0:T(8,128)(2,1)}, bf16[64,1024]{1,0:T(8,128)(2,1)S(1)}, u32[]{:S(2)}, u32[]{:S(2)}) collective-permute-start(bf16[64,1024]{1,0:T(8,128)(2,1)} %get-tuple-element.39.a_ref), channel_id=1, source_target_pairs={{0,1},{1,0},{2,3},{3,2},{4,5},{5,4},{6,7},{7,6},{8,9},{9,8},{10,11... | collective-permute-start | bytes 393224 | tf_op jit(solution)/shard_map/ppermute | solution.py:658
  4.2 1.3 %collective-permute-start.12 = (bf16[256,256]{1,0:T(8,128)(2,1)S(1)}, bf16[256,256]{1,0:T(8,128)(2,1)S(1)}, u32[]{:S(2)}, u32[]{:S(2)}) collective-permute-start(bf16[256,256]{1,0:T(8,128)(2,1)S(1)} %copy-done.6), channel_id=1, source_target_pairs={{0,4},{2,6},{8,0},{10,2},{16,8},{18,10},{24,16},{26,18},{28,24},{3... | collective-permute-start | bytes 393224 | tf_op jit(solution)/shard_map/ppermute | solution.py:603
  5.5 1.5 %collective-permute-start.1 = (bf16[64,1024]{1,0:T(8,128)(2,1)}, bf16[64,1024]{1,0:T(8,128)(2,1)S(1)}, u32[]{:S(2)}, u32[]{:S(2)}) collective-permute-start(bf16[64,1024]{1,0:T(8,128)(2,1)} %get-tuple-element.40), channel_id=1, source_target_pairs={{0,2},{2,0},{4,6},{6,4},{8,10},{10,8},{12,14},{14,12},{16,18},{18,... | collective-permute-start | bytes 393224 | tf_op jit(solution)/shard_map/ppermute | solution.py:659
  7.4 1.3 %collective-permute-start.6 = (bf16[256,256]{1,0:T(8,128)(2,1)S(1)}, bf16[256,256]{1,0:T(8,128)(2,1)S(1)}, u32[]{:S(2)}, u32[]{:S(2)}) collective-permute-start(bf16[256,256]{1,0:T(8,128)(2,1)S(1)} %copy-done.5), channel_id=1, source_target_pairs={{0,4},{2,6},{8,0},{10,2},{16,8},{18,10},{24,16},{26,18},{28,24},{3... | collective-permute-start | bytes 393224 | tf_op jit(solution)/shard_map/ppermute | solution.py:603
  8.9 1.3 %collective-permute-start.13 = (bf16[256,256]{1,0:T(8,128)(2,1)S(1)}, bf16[256,256]{1,0:T(8,128)(2,1)S(1)}, u32[]{:S(2)}, u32[]{:S(2)}) collective-permute-start(bf16[256,256]{1,0:T(8,128)(2,1)S(1)} %collective-permute-done.12.refs_9_), channel_id=1, source_target_pairs={{0,4},{2,6},{8,0},{10,2},{16,8},{18,10},{24,16},{26,18},{28,24},{3... | collective-permute-start | bytes 393224 | tf_op jit(solution)/shard_map/ppermute | solution.py:603
  10.2 3.5 %collective-permute-start.2 = (bf16[64,1024]{1,0:T(8,128)(2,1)}, bf16[64,1024]{1,0:T(8,128)(2,1)S(1)}, u32[]{:S(2)}, u32[]{:S(2)}) collective-permute-start(bf16[64,1024]{1,0:T(8,128)(2,1)} %get-tuple-element.40), channel_id=1, source_target_pairs={{0,3},{1,2},{2,1},{3,0},{4,7},{5,6},{6,5},{7,4},{8,11},{9,10},{10,... | collective-permute-start | bytes 393224 | tf_op jit(solution)/shard_map/ppermute | solution.py:660
  13.8 1.3 %collective-permute-start.7 = (bf16[256,256]{1,0:T(8,128)(2,1)S(1)}, bf16[256,256]{1,0:T(8,128)(2,1)S(1)}, u32[]{:S(2)}, u32[]{:S(2)}) collective-permute-start(bf16[256,256]{1,0:T(8,128)(2,1)S(1)} %collective-permute-done.6.refs_1_), channel_id=1, source_target_pairs={{0,4},{2,6},{8,0},{10,2},{16,8},{18,10},{24,16},{26,18},{28,24},{3... | collective-permute-start | bytes 393224 | tf_op jit(solution)/shard_map/ppermute | solution.py:603
  15.3 1.3 %collective-permute-start.15 = (bf16[256,256]{1,0:T(8,128)(2,1)S(1)}, bf16[256,256]{1,0:T(8,128)(2,1)S(1)}, u32[]{:S(2)}, u32[]{:S(2)}) collective-permute-start(bf16[256,256]{1,0:T(8,128)(2,1)S(1)} %collective-permute-done.13.refs_11_), channel_id=1, source_target_pairs={{0,4},{2,6},{8,0},{10,2},{16,8},{18,10},{24,16},{26,18},{28,24},{3... | collective-permute-start | bytes 393224 | tf_op jit(solution)/shard_map/ppermute | solution.py:603
  16.6 1.6 %collective-permute-done.2.d_ref = bf16[64,1024]{1,0:T(8,128)(2,1)S(1)} collective-permute-done((bf16[64,1024]{1,0:T(8,128)(2,1)}, bf16[64,1024]{1,0:T(8,128)(2,1)S(1)}, u32[]{:S(2)}, u32[]{:S(2)}) %collective-permute-start.2) | collective-permute-done | bytes 131104 | tf_op jit(solution)/shard_map/ppermute | solution.py:660
  19.2 1.3 %collective-permute-start.9 = (bf16[256,256]{1,0:T(8,128)(2,1)S(1)}, bf16[256,256]{1,0:T(8,128)(2,1)S(1)}, u32[]{:S(2)}, u32[]{:S(2)}) collective-permute-start(bf16[256,256]{1,0:T(8,128)(2,1)S(1)} %collective-permute-done.7.refs_3_), channel_id=1, source_target_pairs={{0,4},{2,6},{8,0},{10,2},{16,8},{18,10},{24,16},{26,18},{28,24},{3... | collective-permute-start | bytes 393224 | tf_op jit(solution)/shard_map/ppermute | solution.py:603
  20.5 1.0 %collective-permute-done.10.refs_6_ = bf16[256,256]{1,0:T(8,128)(2,1)S(1)} collective-permute-done((bf16[256,256]{1,0:T(8,128)(2,1)S(1)}, bf16[256,256]{1,0:T(8,128)(2,1)S(1)}, u32[]{:S(2)}, u32[]{:S(2)}) %collective-permute-start.10) | collective-permute-done | bytes 131104 | tf_op jit(solution)/shard_map/ppermute | solution.py:603
  21.7 1.3 %collective-permute-start.17 = (bf16[256,256]{1,0:T(8,128)(2,1)S(1)}, bf16[256,256]{1,0:T(8,128)(2,1)S(1)}, u32[]{:S(2)}, u32[]{:S(2)}) collective-permute-start(bf16[256,256]{1,0:T(8,128)(2,1)S(1)} %collective-permute-done.15.refs_13_), channel_id=1, source_target_pairs={{0,4},{2,6},{8,0},{10,2},{16,8},{18,10},{24,16},{26,18},{28,24},{3... | collective-permute-start | bytes 393224 | tf_op jit(solution)/shard_map/ppermute | solution.py:603
  23.7 0.9 %copy-done.4 = bf16[64,1024]{1,0:T(8,128)(2,1)S(1)} copy-done((bf16[64,1024]{1,0:T(8,128)(2,1)S(1)}, bf16[64,1024]{1,0:T(8,128)(2,1)}, u32[]{:S(2)}) %copy-start.4) | copy-done | bytes 131096
  24.6 1.0 %scale.1 = (bf16[8,128,256]{2,1,0:T(8,128)(2,1)S(1)}, f32[128,128]{1,0:T(8,128)S(1)}, f32[128,128]{1,0:T(8,128)S(1)}, f32[128,128]{1,0:T(8,128)S(1)}) custom-call(s32[3]{0:T(128)S(1)} %copy-done.9, s32[8,128]{1,0:T(8,128)S(1)} %bitcast.1, f32[1,128]{1,0:T(1,128)S(1)} %copy-done.10, bf16[1,4096]{1,0:T(2,128)(2,1)S(1)} %reshape.13.gain_ref, ...), custom_call_target="tpu_custom_call" | custom-call | tf_op jit(solution)/shard_map/scale/pallas_call | solution.py:671
  27.8 1.7 %collective-permute-start.18 = (f32[128,384]{1,0:T(8,128)S(1)}, f32[128,384]{1,0:T(8,128)S(1)}, u32[]{:S(2)}, u32[]{:S(2)}) collective-permute-start(f32[128,384]{1,0:T(8,128)S(1)} %get-tuple-element.50), channel_id=1, source_target_pairs={{0,2},{2,0},{4,6},{6,4},{8,10},{10,8},{12,14},{14,12},{16,18},{18,... | collective-permute-start | bytes 589832 | tf_op jit(solution)/shard_map/ppermute | solution.py:696
  31.3 1.2 %collective-permute-start.21 = (bf16[128,256]{1,0:T(8,128)(2,1)S(1)}, bf16[128,256]{1,0:T(8,128)(2,1)S(1)}, u32[]{:S(2)}, u32[]{:S(2)}) collective-permute-start(bf16[128,256]{1,0:T(8,128)(2,1)S(1)} %rotary.1.refs_0_), channel_id=1, source_target_pairs={{0,4},{2,6},{8,0},{10,2},{16,8},{18,10},{24,16},{26,18},{28,24},{3... | collective-permute-start | bytes 196616 | tf_op jit(solution)/shard_map/ppermute | solution.py:603
  32.8 1.4 %collective-permute-done.23.refs_1_ = bf16[4,128,128]{2,1,0:T(8,128)(2,1)S(1)} collective-permute-done((bf16[4,128,128]{2,1,0:T(8,128)(2,1)S(1)}, bf16[4,128,128]{2,1,0:T(8,128)(2,1)S(1)}, u32[]{:S(2)}, u32[]{:S(2)}) %collective-permute-start.23) | collective-permute-done | bytes 131104 | tf_op jit(solution)/shard_map/ppermute | solution.py:636
  34.4 1.1 %collective-permute-done.21.refs_1_ = bf16[128,256]{1,0:T(8,128)(2,1)S(1)} collective-permute-done((bf16[128,256]{1,0:T(8,128)(2,1)S(1)}, bf16[128,256]{1,0:T(8,128)(2,1)S(1)}, u32[]{:S(2)}, u32[]{:S(2)}) %collective-permute-start.21) | collective-permute-done | bytes 65568 | tf_op jit(solution)/shard_map/ppermute | solution.py:603
  35.9 1.4 %collective-permute-start.29 = (bf16[4,128,128]{2,1,0:T(8,128)(2,1)S(1)}, bf16[4,128,128]{2,1,0:T(8,128)(2,1)S(1)}, u32[]{:S(2)}, u32[]{:S(2)}) collective-permute-start(bf16[4,128,128]{2,1,0:T(8,128)(2,1)S(1)} %collective-permute-done.24.refs_6_), channel_id=1, source_target_pairs={{0,4},{2,6},{4,0},{6,2},{8,12},{10,14},{12,8},{14,10},{16,20},{18,... | collective-permute-start | bytes 393224 | tf_op jit(solution)/shard_map/ppermute | solution.py:636
  37.3 1.9 %collective-permute-start.25 = (bf16[512,128]{1,0:T(8,128)(2,1)S(1)}, bf16[512,128]{1,0:T(8,128)(2,1)S(1)}, u32[]{:S(2)}, u32[]{:S(2)}) collective-permute-start(bf16[512,128]{1,0:T(8,128)(2,1)S(1)} %get-tuple-element.57.qs_ref), channel_id=1, source_target_pairs={{0,16},{2,18},{4,20},{6,22},{8,24},{10,26},{12,28},{14,30},{16,0},... | collective-permute-start | bytes 393224 | tf_op jit(solution)/shard_map/ppermute | solution.py:636
  39.2 1.3 %collective-permute-start.20 = (bf16[128,256]{1,0:T(8,128)(2,1)S(1)}, bf16[128,256]{1,0:T(8,128)(2,1)S(1)}, u32[]{:S(2)}, u32[]{:S(2)}) collective-permute-start(bf16[128,256]{1,0:T(8,128)(2,1)S(1)} %collective-permute-done.19.refs_2_), channel_id=1, source_target_pairs={{0,8},{2,10},{8,16},{10,18},{16,24},{18,26},{24,28},{26,30},{28,20... | collective-permute-start | bytes 196616 | tf_op jit(solution)/shard_map/ppermute | solution.py:603
  41.3 2.5 %collective-permute-done.25.qs_ref = bf16[512,128]{1,0:T(8,128)(2,1)S(1)} collective-permute-done((bf16[512,128]{1,0:T(8,128)(2,1)S(1)}, bf16[512,128]{1,0:T(8,128)(2,1)S(1)}, u32[]{:S(2)}, u32[]{:S(2)}) %collective-permute-start.25) | collective-permute-done | bytes 131104 | tf_op jit(solution)/shard_map/ppermute | solution.py:636
  43.8 3.1 %attend_cached_away.1 = bf16[144,512]{1,0:T(8,128)(2,1)S(1)} custom-call(s32[3]{0:T(128)S(1)} %copy-done.9, s32[3,25]{1,0:T(4,128)S(1)} %copy-done.8, s32[8,128]{1,0:T(8,128)S(1)} %bitcast.2, bf16[512,128]{1,0:T(8,128)(2,1)S(1)} %collective-permute-done.25.qs_ref, bf16[4,128,128]{2,1,0:T(8,128)(2,1)S(1)} %copy-done.2, ...), custom_call_target="tpu_custom_call" | custom-call | tf_op jit(solution)/shard_map/attend_cached_away/pallas_call | solution.py:717
  47.0 1.4 %collective-permute-start.30 = (bf16[128,256]{1,0:T(8,128)(2,1)S(1)}, bf16[128,256]{1,0:T(8,128)(2,1)S(1)}, u32[]{:S(2)}, u32[]{:S(2)}) collective-permute-start(bf16[128,256]{1,0:T(8,128)(2,1)S(1)} %collective-permute-done.20.refs_4_), channel_id=1, source_target_pairs={{0,8},{2,10},{8,16},{10,18},{16,24},{18,26},{24,28},{26,30},{28,20... | collective-permute-start | bytes 196616 | tf_op jit(solution)/shard_map/ppermute | solution.py:603
  48.7 2.0 %attend_cached_here.1 = (f32[1,512]{1,0:T(1,128)S(1)}, f32[1,512]{1,0:T(1,128)S(1)}, f32[128,512]{1,0:T(8,128)S(1)}) custom-call(s32[3]{0:T(128)S(1)} %copy-done.9, s32[3,25]{1,0:T(4,128)S(1)} %copy-done.8, s32[8,128]{1,0:T(8,128)S(1)} %bitcast.3, bf16[512,128]{1,0:T(8,128)(2,1)S(1)} %get-tuple-element.57.qs_ref, bf16[4,128,128]{2,1,0:T(8,128)(2,1)S(1)} %copy-done.2, ...), custom_call_target="tpu_custom_call" | custom-call | tf_op jit(solution)/shard_map/attend_cached_here/pallas_call | solution.py:717
  50.7 2.8 %collective-permute-done.30.refs_6_ = bf16[128,256]{1,0:T(8,128)(2,1)S(1)} collective-permute-done((bf16[128,256]{1,0:T(8,128)(2,1)S(1)}, bf16[128,256]{1,0:T(8,128)(2,1)S(1)}, u32[]{:S(2)}, u32[]{:S(2)}) %collective-permute-start.30) | collective-permute-done | bytes 65568 | tf_op jit(solution)/shard_map/ppermute | solution.py:603
  53.5 3.9 %collective-permute-done.33.refs_7_ = bf16[128,256]{1,0:T(8,128)(2,1)S(1)} collective-permute-done((bf16[128,256]{1,0:T(8,128)(2,1)S(1)}, bf16[128,256]{1,0:T(8,128)(2,1)S(1)}, u32[]{:S(2)}, u32[]{:S(2)}) %collective-permute-start.33) | collective-permute-done | bytes 65568 | tf_op jit(solution)/shard_map/ppermute | solution.py:603
  57.4 3.0 %attend_new.1 = (bf16[64,512]{1,0:T(8,128)(2,1)S(1)}, bf16[64,512]{1,0:T(8,128)(2,1)S(1)}, bf16[3,128,256]{2,1,0:T(8,128)(2,1)S(1)}, bf16[3,128,256]{2,1,0:T(8,128)(2,1)S(1)}, s32[6]{0:T(128)S(1)}) custom-call(s32[3]{0:T(128)S(1)} %copy-done.9, s32[3,25]{1,0:T(4,128)S(1)} %copy-done.8, s32[8,128]{1,0:T(8,128)S(1)} %bitcast.4, ...), custom_call_target="tpu_custom_call" | custom-call | tf_op jit(solution)/shard_map/attend_new/pallas_call | solution.py:745
  60.4 6.4 %collective-permute-start.35 = (bf16[3,128,256]{2,1,0:T(8,128)(2,1)S(1)}, bf16[3,128,256]{2,1,0:T(8,128)(2,1)S(1)}, u32[]{:S(2)}, u32[]{:S(2)}) collective-permute-start(bf16[3,128,256]{2,1,0:T(8,128)(2,1)S(1)} %get-tuple-element.74), channel_id=1, source_target_pairs={{0,2},{2,0},{4,6},{6,4},{8,10},{10,8},{12,14},{14,12},{16,18},{18,... | collective-permute-start | bytes 589832 | tf_op jit(solution)/shard_map/ppermute | solution.py:779
  66.9 1.2 %collective-permute-done.34.attr_ref = bf16[64,512]{1,0:T(8,128)(2,1)S(1)} collective-permute-done((bf16[64,512]{1,0:T(8,128)(2,1)S(1)}, bf16[64,512]{1,0:T(8,128)(2,1)S(1)}, u32[]{:S(2)}, u32[]{:S(2)}) %collective-permute-start.34) | collective-permute-done | bytes 65568 | tf_op jit(solution)/shard_map/ppermute | solution.py:780
  68.0 1.5 %join.1 = (bf16[64,1024]{1,0:T(8,128)(2,1)}, bf16[3,128,256]{2,1,0:T(8,128)(2,1)}, bf16[3,128,256]{2,1,0:T(8,128)(2,1)}) custom-call(s32[6]{0:T(128)S(1)} %get-tuple-element.70.info_ref, bf16[64,512]{1,0:T(8,128)(2,1)S(1)} %get-tuple-element.71.attc_ref, bf16[64,512]{1,0:T(8,128)(2,1)S(1)} %collective-permute-done.34.attr_ref, ...), custom_call_target="tpu_custom_call" | custom-call | tf_op jit(solution)/shard_map/join/pallas_call | solution.py:781
  (74 shorter events, 9.1 us)
Async XLA Ops:
  2.8 4.6 %collective-permute-start = (bf16[64,1024]{1,0:T(8,128)(2,1)}, bf16[64,1024]{1,0:T(8,128)(2,1)S(1)}, u32[]{:S(2)}, u32[]{:S(2)}) collective-permute-start(bf16[64,1024]{1,0:T(8,128)(2,1)} %get-tuple-element.39.a_ref), channel_id=1, source_target_pairs={{0,1},{1,0},{2,3},{3,2},{4,5},{5,4},{6,7},{7,6},{8,9},{9,8},{10,11... | collective-permute-start | bytes 393224 | tf_op jit(solution)/shard_map/ppermute | solution.py:658
  4.0 4.7 %collective-permute-start.3 = (bf16[256,256]{1,0:T(8,128)(2,1)S(1)}, bf16[256,256]{1,0:T(8,128)(2,1)S(1)}, u32[]{:S(2)}, u32[]{:S(2)}) collective-permute-start(bf16[256,256]{1,0:T(8,128)(2,1)S(1)} %copy-done.5), channel_id=1, source_target_pairs={{0,8},{2,10},{8,16},{10,18},{16,24},{18,26},{24,28},{26,30},{28,20... | collective-permute-start | bytes 393224 | tf_op jit(solution)/shard_map/ppermute | solution.py:603
  4.2 4.7 %collective-permute-start.12 = (bf16[256,256]{1,0:T(8,128)(2,1)S(1)}, bf16[256,256]{1,0:T(8,128)(2,1)S(1)}, u32[]{:S(2)}, u32[]{:S(2)}) collective-permute-start(bf16[256,256]{1,0:T(8,128)(2,1)S(1)} %copy-done.6), channel_id=1, source_target_pairs={{0,4},{2,6},{8,0},{10,2},{16,8},{18,10},{24,16},{26,18},{28,24},{3... | collective-permute-start | bytes 393224 | tf_op jit(solution)/shard_map/ppermute | solution.py:603
  5.5 4.7 %collective-permute-start.1 = (bf16[64,1024]{1,0:T(8,128)(2,1)}, bf16[64,1024]{1,0:T(8,128)(2,1)S(1)}, u32[]{:S(2)}, u32[]{:S(2)}) collective-permute-start(bf16[64,1024]{1,0:T(8,128)(2,1)} %get-tuple-element.40), channel_id=1, source_target_pairs={{0,2},{2,0},{4,6},{6,4},{8,10},{10,8},{12,14},{14,12},{16,18},{18,... | collective-permute-start | bytes 393224 | tf_op jit(solution)/shard_map/ppermute | solution.py:659
  7.0 6.6 %collective-permute-start.4 = (bf16[256,256]{1,0:T(8,128)(2,1)S(1)}, bf16[256,256]{1,0:T(8,128)(2,1)S(1)}, u32[]{:S(2)}, u32[]{:S(2)}) collective-permute-start(bf16[256,256]{1,0:T(8,128)(2,1)S(1)} %copy-done.6), channel_id=1, source_target_pairs={{0,8},{2,10},{8,16},{10,18},{16,24},{18,26},{24,28},{26,30},{28,20... | collective-permute-start | bytes 393224 | tf_op jit(solution)/shard_map/ppermute | solution.py:603
  7.4 6.4 %collective-permute-start.6 = (bf16[256,256]{1,0:T(8,128)(2,1)S(1)}, bf16[256,256]{1,0:T(8,128)(2,1)S(1)}, u32[]{:S(2)}, u32[]{:S(2)}) collective-permute-start(bf16[256,256]{1,0:T(8,128)(2,1)S(1)} %copy-done.5), channel_id=1, source_target_pairs={{0,4},{2,6},{8,0},{10,2},{16,8},{18,10},{24,16},{26,18},{28,24},{3... | collective-permute-start | bytes 393224 | tf_op jit(solution)/shard_map/ppermute | solution.py:603
  8.7 6.4 %collective-permute-start.8 = (bf16[256,256]{1,0:T(8,128)(2,1)S(1)}, bf16[256,256]{1,0:T(8,128)(2,1)S(1)}, u32[]{:S(2)}, u32[]{:S(2)}) collective-permute-start(bf16[256,256]{1,0:T(8,128)(2,1)S(1)} %collective-permute-done.3.refs_2_), channel_id=1, source_target_pairs={{0,8},{2,10},{8,16},{10,18},{16,24},{18,26},{24,28},{26,30},{28,20... | collective-permute-start | bytes 393224 | tf_op jit(solution)/shard_map/ppermute | solution.py:603
  8.9 6.4 %collective-permute-start.13 = (bf16[256,256]{1,0:T(8,128)(2,1)S(1)}, bf16[256,256]{1,0:T(8,128)(2,1)S(1)}, u32[]{:S(2)}, u32[]{:S(2)}) collective-permute-start(bf16[256,256]{1,0:T(8,128)(2,1)S(1)} %collective-permute-done.12.refs_9_), channel_id=1, source_target_pairs={{0,4},{2,6},{8,0},{10,2},{16,8},{18,10},{24,16},{26,18},{28,24},{3... | collective-permute-start | bytes 393224 | tf_op jit(solution)/shard_map/ppermute | solution.py:603
  10.2 8.0 %collective-permute-start.2 = (bf16[64,1024]{1,0:T(8,128)(2,1)}, bf16[64,1024]{1,0:T(8,128)(2,1)S(1)}, u32[]{:S(2)}, u32[]{:S(2)}) collective-permute-start(bf16[64,1024]{1,0:T(8,128)(2,1)} %get-tuple-element.40), channel_id=1, source_target_pairs={{0,3},{1,2},{2,1},{3,0},{4,7},{5,6},{6,5},{7,4},{8,11},{9,10},{10,... | collective-permute-start | bytes 393224 | tf_op jit(solution)/shard_map/ppermute | solution.py:660
  13.7 5.4 %collective-permute-start.14 = (bf16[256,256]{1,0:T(8,128)(2,1)S(1)}, bf16[256,256]{1,0:T(8,128)(2,1)S(1)}, u32[]{:S(2)}, u32[]{:S(2)}) collective-permute-start(bf16[256,256]{1,0:T(8,128)(2,1)S(1)} %collective-permute-done.4.refs_10_), channel_id=1, source_target_pairs={{0,8},{2,10},{8,16},{10,18},{16,24},{18,26},{24,28},{26,30},{28,20... | collective-permute-start | bytes 393224 | tf_op jit(solution)/shard_map/ppermute | solution.py:603
  13.8 5.4 %collective-permute-start.7 = (bf16[256,256]{1,0:T(8,128)(2,1)S(1)}, bf16[256,256]{1,0:T(8,128)(2,1)S(1)}, u32[]{:S(2)}, u32[]{:S(2)}) collective-permute-start(bf16[256,256]{1,0:T(8,128)(2,1)S(1)} %collective-permute-done.6.refs_1_), channel_id=1, source_target_pairs={{0,4},{2,6},{8,0},{10,2},{16,8},{18,10},{24,16},{26,18},{28,24},{3... | collective-permute-start | bytes 393224 | tf_op jit(solution)/shard_map/ppermute | solution.py:603
  15.1 6.4 %collective-permute-start.10 = (bf16[256,256]{1,0:T(8,128)(2,1)S(1)}, bf16[256,256]{1,0:T(8,128)(2,1)S(1)}, u32[]{:S(2)}, u32[]{:S(2)}) collective-permute-start(bf16[256,256]{1,0:T(8,128)(2,1)S(1)} %collective-permute-done.8.refs_4_), channel_id=1, source_target_pairs={{0,8},{2,10},{8,16},{10,18},{16,24},{18,26},{24,28},{26,30},{28,20... | collective-permute-start | bytes 393224 | tf_op jit(solution)/shard_map/ppermute | solution.py:603
  15.3 6.4 %collective-permute-start.15 = (bf16[256,256]{1,0:T(8,128)(2,1)S(1)}, bf16[256,256]{1,0:T(8,128)(2,1)S(1)}, u32[]{:S(2)}, u32[]{:S(2)}) collective-permute-start(bf16[256,256]{1,0:T(8,128)(2,1)S(1)} %collective-permute-done.13.refs_11_), channel_id=1, source_target_pairs={{0,4},{2,6},{8,0},{10,2},{16,8},{18,10},{24,16},{26,18},{28,24},{3... | collective-permute-start | bytes 393224 | tf_op jit(solution)/shard_map/ppermute | solution.py:603
  18.2 7.5 %collective-permute-start.5 = (bf16[768,128]{1,0:T(8,128)(2,1)}, bf16[768,128]{1,0:T(8,128)(2,1)S(1)}, u32[]{:S(2)}, u32[]{:S(2)}) collective-permute-start(bf16[768,128]{1,0:T(8,128)(2,1)} %get-tuple-element.43), channel_id=1, source_target_pairs={{0,2},{2,0},{4,6},{6,4},{8,10},{10,8},{12,14},{14,12},{16,18},{18,... | collective-permute-start | bytes 589832 | tf_op jit(solution)/shard_map/ppermute | solution.py:657
  19.1 6.7 %collective-permute-start.16 = (bf16[256,256]{1,0:T(8,128)(2,1)S(1)}, bf16[256,256]{1,0:T(8,128)(2,1)S(1)}, u32[]{:S(2)}, u32[]{:S(2)}) collective-permute-start(bf16[256,256]{1,0:T(8,128)(2,1)S(1)} %collective-permute-done.14.refs_12_), channel_id=1, source_target_pairs={{0,8},{2,10},{8,16},{10,18},{16,24},{18,26},{24,28},{26,30},{28,20... | collective-permute-start | bytes 393224 | tf_op jit(solution)/shard_map/ppermute | solution.py:603
  19.2 6.5 %collective-permute-start.9 = (bf16[256,256]{1,0:T(8,128)(2,1)S(1)}, bf16[256,256]{1,0:T(8,128)(2,1)S(1)}, u32[]{:S(2)}, u32[]{:S(2)}) collective-permute-start(bf16[256,256]{1,0:T(8,128)(2,1)S(1)} %collective-permute-done.7.refs_3_), channel_id=1, source_target_pairs={{0,4},{2,6},{8,0},{10,2},{16,8},{18,10},{24,16},{26,18},{28,24},{3... | collective-permute-start | bytes 393224 | tf_op jit(solution)/shard_map/ppermute | solution.py:603
  21.6 4.9 %collective-permute-start.11 = (bf16[256,256]{1,0:T(8,128)(2,1)S(1)}, bf16[256,256]{1,0:T(8,128)(2,1)S(1)}, u32[]{:S(2)}, u32[]{:S(2)}) collective-permute-start(bf16[256,256]{1,0:T(8,128)(2,1)S(1)} %collective-permute-done.10.refs_6_), channel_id=1, source_target_pairs={{0,8},{2,10},{8,16},{10,18},{16,24},{18,26},{24,28},{26,30},{28,20... | collective-permute-start | bytes 393224 | tf_op jit(solution)/shard_map/ppermute | solution.py:603
  21.7 5.5 %collective-permute-start.17 = (bf16[256,256]{1,0:T(8,128)(2,1)S(1)}, bf16[256,256]{1,0:T(8,128)(2,1)S(1)}, u32[]{:S(2)}, u32[]{:S(2)}) collective-permute-start(bf16[256,256]{1,0:T(8,128)(2,1)S(1)} %collective-permute-done.15.refs_13_), channel_id=1, source_target_pairs={{0,4},{2,6},{8,0},{10,2},{16,8},{18,10},{24,16},{26,18},{28,24},{3... | collective-permute-start | bytes 393224 | tf_op jit(solution)/shard_map/ppermute | solution.py:603
  29.4 4.7 %collective-permute-start.23 = (bf16[4,128,128]{2,1,0:T(8,128)(2,1)S(1)}, bf16[4,128,128]{2,1,0:T(8,128)(2,1)S(1)}, u32[]{:S(2)}, u32[]{:S(2)}) collective-permute-start(bf16[4,128,128]{2,1,0:T(8,128)(2,1)S(1)} %copy-done.2), channel_id=1, source_target_pairs={{0,4},{2,6},{4,0},{6,2},{8,12},{10,14},{12,8},{14,10},{16,20},{18,... | collective-permute-start | bytes 393224 | tf_op jit(solution)/shard_map/ppermute | solution.py:636
  29.7 4.8 %collective-permute-start.24 = (bf16[4,128,128]{2,1,0:T(8,128)(2,1)S(1)}, bf16[4,128,128]{2,1,0:T(8,128)(2,1)S(1)}, u32[]{:S(2)}, u32[]{:S(2)}) collective-permute-start(bf16[4,128,128]{2,1,0:T(8,128)(2,1)S(1)} %get-tuple-element.56.refs_4_), channel_id=1, source_target_pairs={{0,8},{2,10},{4,12},{6,14},{8,0},{10,2},{12,4},{14,6},{16,24},{18,... | collective-permute-start | bytes 393224 | tf_op jit(solution)/shard_map/ppermute | solution.py:636
  31.3 4.2 %collective-permute-start.21 = (bf16[128,256]{1,0:T(8,128)(2,1)S(1)}, bf16[128,256]{1,0:T(8,128)(2,1)S(1)}, u32[]{:S(2)}, u32[]{:S(2)}) collective-permute-start(bf16[128,256]{1,0:T(8,128)(2,1)S(1)} %rotary.1.refs_0_), channel_id=1, source_target_pairs={{0,4},{2,6},{8,0},{10,2},{16,8},{18,10},{24,16},{26,18},{28,24},{3... | collective-permute-start | bytes 196616 | tf_op jit(solution)/shard_map/ppermute | solution.py:603
  32.5 6.7 %collective-permute-start.26 = (bf16[4,128,128]{2,1,0:T(8,128)(2,1)S(1)}, bf16[4,128,128]{2,1,0:T(8,128)(2,1)S(1)}, u32[]{:S(2)}, u32[]{:S(2)}) collective-permute-start(bf16[4,128,128]{2,1,0:T(8,128)(2,1)S(1)} %copy-done.2), channel_id=1, source_target_pairs={{0,8},{2,10},{4,12},{6,14},{8,0},{10,2},{12,4},{14,6},{16,24},{18,... | collective-permute-start | bytes 393224 | tf_op jit(solution)/shard_map/ppermute | solution.py:636
  34.2 6.3 %collective-permute-start.28 = (bf16[4,128,128]{2,1,0:T(8,128)(2,1)S(1)}, bf16[4,128,128]{2,1,0:T(8,128)(2,1)S(1)}, u32[]{:S(2)}, u32[]{:S(2)}) collective-permute-start(bf16[4,128,128]{2,1,0:T(8,128)(2,1)S(1)} %get-tuple-element.56.refs_4_), channel_id=1, source_target_pairs={{0,4},{2,6},{4,0},{6,2},{8,12},{10,14},{12,8},{14,10},{16,20},{18,... | collective-permute-start | bytes 393224 | tf_op jit(solution)/shard_map/ppermute | solution.py:636
  35.5 5.3 %collective-permute-start.27 = (bf16[4,128,128]{2,1,0:T(8,128)(2,1)S(1)}, bf16[4,128,128]{2,1,0:T(8,128)(2,1)S(1)}, u32[]{:S(2)}, u32[]{:S(2)}) collective-permute-start(bf16[4,128,128]{2,1,0:T(8,128)(2,1)S(1)} %collective-permute-done.23.refs_1_), channel_id=1, source_target_pairs={{0,8},{2,10},{4,12},{6,14},{8,0},{10,2},{12,4},{14,6},{16,24},{18,... | collective-permute-start | bytes 393224 | tf_op jit(solution)/shard_map/ppermute | solution.py:636
  35.9 5.4 %collective-permute-start.29 = (bf16[4,128,128]{2,1,0:T(8,128)(2,1)S(1)}, bf16[4,128,128]{2,1,0:T(8,128)(2,1)S(1)}, u32[]{:S(2)}, u32[]{:S(2)}) collective-permute-start(bf16[4,128,128]{2,1,0:T(8,128)(2,1)S(1)} %collective-permute-done.24.refs_6_), channel_id=1, source_target_pairs={{0,4},{2,6},{4,0},{6,2},{8,12},{10,14},{12,8},{14,10},{16,20},{18,... | collective-permute-start | bytes 393224 | tf_op jit(solution)/shard_map/ppermute | solution.py:636
  37.3 6.5 %collective-permute-start.25 = (bf16[512,128]{1,0:T(8,128)(2,1)S(1)}, bf16[512,128]{1,0:T(8,128)(2,1)S(1)}, u32[]{:S(2)}, u32[]{:S(2)}) collective-permute-start(bf16[512,128]{1,0:T(8,128)(2,1)S(1)} %get-tuple-element.57.qs_ref), channel_id=1, source_target_pairs={{0,16},{2,18},{4,20},{6,22},{8,24},{10,26},{12,28},{14,30},{16,0},... | collective-permute-start | bytes 393224 | tf_op jit(solution)/shard_map/ppermute | solution.py:636
  39.2 7.7 %collective-permute-start.20 = (bf16[128,256]{1,0:T(8,128)(2,1)S(1)}, bf16[128,256]{1,0:T(8,128)(2,1)S(1)}, u32[]{:S(2)}, u32[]{:S(2)}) collective-permute-start(bf16[128,256]{1,0:T(8,128)(2,1)S(1)} %collective-permute-done.19.refs_2_), channel_id=1, source_target_pairs={{0,8},{2,10},{8,16},{10,18},{16,24},{18,26},{24,28},{26,30},{28,20... | collective-permute-start | bytes 196616 | tf_op jit(solution)/shard_map/ppermute | solution.py:603
  40.5 6.4 %collective-permute-start.22 = (bf16[128,256]{1,0:T(8,128)(2,1)S(1)}, bf16[128,256]{1,0:T(8,128)(2,1)S(1)}, u32[]{:S(2)}, u32[]{:S(2)}) collective-permute-start(bf16[128,256]{1,0:T(8,128)(2,1)S(1)} %collective-permute-done.21.refs_1_), channel_id=1, source_target_pairs={{0,4},{2,6},{8,0},{10,2},{16,8},{18,10},{24,16},{26,18},{28,24},{3... | collective-permute-start | bytes 196616 | tf_op jit(solution)/shard_map/ppermute | solution.py:603
  46.9 10.5 %collective-permute-start.31 = (bf16[144,512]{1,0:T(8,128)(2,1)S(1)}, bf16[144,512]{1,0:T(8,128)(2,1)S(1)}, u32[]{:S(2)}, u32[]{:S(2)}) collective-permute-start(bf16[144,512]{1,0:T(8,128)(2,1)S(1)} %attend_cached_away.1), channel_id=1, source_target_pairs={{0,16},{2,18},{4,20},{6,22},{8,24},{10,26},{12,28},{14,30},{16,0},... | collective-permute-start | bytes 442376 | tf_op jit(solution)/shard_map/ppermute | solution.py:636
  47.0 6.5 %collective-permute-start.30 = (bf16[128,256]{1,0:T(8,128)(2,1)S(1)}, bf16[128,256]{1,0:T(8,128)(2,1)S(1)}, u32[]{:S(2)}, u32[]{:S(2)}) collective-permute-start(bf16[128,256]{1,0:T(8,128)(2,1)S(1)} %collective-permute-done.20.refs_4_), channel_id=1, source_target_pairs={{0,8},{2,10},{8,16},{10,18},{16,24},{18,26},{24,28},{26,30},{28,20... | collective-permute-start | bytes 196616 | tf_op jit(solution)/shard_map/ppermute | solution.py:603
  48.4 5.1 %collective-permute-start.32 = (bf16[128,256]{1,0:T(8,128)(2,1)S(1)}, bf16[128,256]{1,0:T(8,128)(2,1)S(1)}, u32[]{:S(2)}, u32[]{:S(2)}) collective-permute-start(bf16[128,256]{1,0:T(8,128)(2,1)S(1)} %collective-permute-done.22.refs_3_), channel_id=1, source_target_pairs={{0,4},{2,6},{8,0},{10,2},{16,8},{18,10},{24,16},{26,18},{28,24},{3... | collective-permute-start | bytes 196616 | tf_op jit(solution)/shard_map/ppermute | solution.py:603
  60.4 7.6 %collective-permute-start.35 = (bf16[3,128,256]{2,1,0:T(8,128)(2,1)S(1)}, bf16[3,128,256]{2,1,0:T(8,128)(2,1)S(1)}, u32[]{:S(2)}, u32[]{:S(2)}) collective-permute-start(bf16[3,128,256]{2,1,0:T(8,128)(2,1)S(1)} %get-tuple-element.74), channel_id=1, source_target_pairs={{0,2},{2,0},{4,6},{6,4},{8,10},{10,8},{12,14},{14,12},{16,18},{18,... | collective-permute-start | bytes 589832 | tf_op jit(solution)/shard_map/ppermute | solution.py:779
  (16 other events, 89.7 us)

commit v7 on v6

--- a/solution.py
+++ b/solution.py
@@ -706,8 +706,9 @@
     )(part_keep, part_got, cosine, sine)
     new = {0: fresh}
     new[-1], new[1] = ring_send(chips, [fresh], 1)[0], ring_send(chips, [fresh], -1)[0]
-    late_y, late_z, late_q, _ = lax.optimization_barrier((y_near, z_far, q_rows, (new[-1], new[1])))
+    late_q, right = lax.optimization_barrier((q_rows, new[-1]))
     q_away = exchange(late_q, chips // 2)
+    late_y, late_z, q_away, _ = lax.optimization_barrier((y_near, z_far, q_away, (new[-1], new[1])))
     near = [kv_mine, y_near, z_near, exchange(late_y, 2)]
     far = [kv_other, y_far, z_far, exchange(late_z, 1)]
     slots = dp_count // 2 * old + STEP_PAGES
@@ -735,9 +736,9 @@
         q_rows, 0, [((1, columns), f32), ((1, columns), f32), ((HD, columns), f32)], "attend_cached_here"
     )
     new[-2], new[2] = ring_send(chips, [new[-1]], 1)[0], ring_send(chips, [new[1]], -1)[0]
-    right, left, away = lax.optimization_barrier((new[-2], new[2], away))
+    right, left = lax.optimization_barrier((new[-2], new[2]))
     new[-3], new[3] = ring_send(chips, [right], 1)[0], ring_send(chips, [left], -1)[0]
-    right, here = lax.optimization_barrier((new[-3], here))
+    right, new[3], away = lax.optimization_barrier((new[-3], new[3], away))
     (new[chips // 2],) = ring_send(chips, [right], 1)
     back = exchange(away, chips // 2)
     top, total, acc = here

time: 69.4 us -> 70.2 us (1.012)
  the two profiles are of different devices: /device:TPU:13 before, /device:TPU:0 now
where the time goes in v7:
time: 70.2 us; the launch traced here: 69.7 us
  starting transfers between devices  39.4 us (56%)
  waiting for transfers between devices  15 us (21%)
  Pallas kernels  12.7 us (18%)
  local copies, waits for them, and re-layouts  1.61 us (2%)
  between operations  0.85 us (1%)
    ppermute x21, starting transfers between devices, ring_send(): lax.ppermute(a, 'dp', ring_pairs(chips, step, swap * n))  24.8 us
    ppermute x8, starting transfers between devices, exchange(): lax.ppermute(array, 'dp', [(i, i ^ 2 * e ^ swap) for i in range(dp_count)])  11 us
    ppermute x21, waiting for transfers between devices, ring_send(): lax.ppermute(a, 'dp', ring_pairs(chips, step, swap * n))  10.6 us
    pallas_call x2, Pallas kernels, cached(): call(functools.partial(cached_kernel, chips, pages_dev, old, away), outs,...  5.16 us
    ppermute x1, starting transfers between devices, ring_body(): x_b = lax.ppermute(x_mine, 'mp', mp_pairs)  3 us
    pallas_call x1, Pallas kernels, ring_body(): call(functools.partial(fresh_kernel, chips, pages_dev), [((rows, group *...  2.42 us
    pallas_call x1, Pallas kernels, ring_body(): call(functools.partial(split_kernel, old), [((rows, half_width // 2), bf)...  2.1 us
    ppermute x8, waiting for transfers between devices, exchange(): lax.ppermute(array, 'dp', [(i, i ^ 2 * e ^ swap) for i in range(dp_count)])  1.84 us
  transfers between devices with their start and end apart: 36, of which 14 were waited for; matrix products, arithmetic and copies ran while one was open for 0% of the time, Pallas kernels for 9%

profile of v7, /device:TPU:0, one launch (start us, length us, event | category | flops | bytes accessed | tf_op | source)
XLA Modules:
  0.0 69.7 jit_solution(3997663252795570381)
XLA Ops:
  0.7 2.1 %split.1 = (bf16[64,1024]{1,0:T(8,128)(2,1)}, bf16[64,1024]{1,0:T(8,128)(2,1)}, bf16[4,128,128]{2,1,0:T(8,128)(2,1)}, bf16[768,128]{1,0:T(8,128)(2,1)}) custom-call(bf16[64,2048]{1,0:T(8,128)(2,1)} %f_ref.1, bf16[64,1024]{1,0:T(8,128)(2,1)} %q_ref.3, bf16[3,128,256]{2,1,0:T(8,128)(2,1)} %kp_ref.3, bf16[3,128,256]{2,1,0:T(8,128)(2,1)} %vp_ref.3), custom_call_target="tpu_custom_call" | custom-call | tf_op jit(solution)/shard_map/split/pallas_call | solution.py:642
  2.8 3.0 %collective-permute-start = (bf16[64,1024]{1,0:T(8,128)(2,1)}, bf16[64,1024]{1,0:T(8,128)(2,1)S(1)}, u32[]{:S(2)}, u32[]{:S(2)}) collective-permute-start(bf16[64,1024]{1,0:T(8,128)(2,1)} %get-tuple-element.38.a_ref), channel_id=1, source_target_pairs={{0,1},{1,0},{2,3},{3,2},{4,5},{5,4},{6,7},{7,6},{8,9},{9,8},{10,11... | collective-permute-start | bytes 393224 | tf_op jit(solution)/shard_map/ppermute | solution.py:658
  5.8 1.6 %collective-permute-start.3 = (bf16[256,256]{1,0:T(8,128)(2,1)S(1)}, bf16[256,256]{1,0:T(8,128)(2,1)S(1)}, u32[]{:S(2)}, u32[]{:S(2)}) collective-permute-start(bf16[256,256]{1,0:T(8,128)(2,1)S(1)} %copy-done.5), channel_id=1, source_target_pairs={{0,8},{2,10},{8,16},{10,18},{16,24},{18,26},{24,28},{26,30},{28,20... | collective-permute-start | bytes 393224 | tf_op jit(solution)/shard_map/ppermute | solution.py:603
  7.8 1.5 %collective-permute-start.6 = (bf16[256,256]{1,0:T(8,128)(2,1)S(1)}, bf16[256,256]{1,0:T(8,128)(2,1)S(1)}, u32[]{:S(2)}, u32[]{:S(2)}) collective-permute-start(bf16[256,256]{1,0:T(8,128)(2,1)S(1)} %copy-done.5), channel_id=1, source_target_pairs={{0,4},{2,6},{8,0},{10,2},{16,8},{18,10},{24,16},{26,18},{28,24},{3... | collective-permute-start | bytes 393224 | tf_op jit(solution)/shard_map/ppermute | solution.py:603
  9.5 1.8 %collective-permute-start.4 = (bf16[256,256]{1,0:T(8,128)(2,1)S(1)}, bf16[256,256]{1,0:T(8,128)(2,1)S(1)}, u32[]{:S(2)}, u32[]{:S(2)}) collective-permute-start(bf16[256,256]{1,0:T(8,128)(2,1)S(1)} %copy-done.6), channel_id=1, source_target_pairs={{0,8},{2,10},{8,16},{10,18},{16,24},{18,26},{24,28},{26,30},{28,20... | collective-permute-start | bytes 393224 | tf_op jit(solution)/shard_map/ppermute | solution.py:603
  11.3 1.6 %collective-permute-start.8 = (bf16[256,256]{1,0:T(8,128)(2,1)S(1)}, bf16[256,256]{1,0:T(8,128)(2,1)S(1)}, u32[]{:S(2)}, u32[]{:S(2)}) collective-permute-start(bf16[256,256]{1,0:T(8,128)(2,1)S(1)} %collective-permute-done.3.refs_2_), channel_id=1, source_target_pairs={{0,8},{2,10},{8,16},{10,18},{16,24},{18,26},{24,28},{26,30},{28,20... | collective-permute-start | bytes 393224 | tf_op jit(solution)/shard_map/ppermute | solution.py:603
  13.7 2.6 %collective-permute-done.6.refs_1_ = bf16[256,256]{1,0:T(8,128)(2,1)S(1)} collective-permute-done((bf16[256,256]{1,0:T(8,128)(2,1)S(1)}, bf16[256,256]{1,0:T(8,128)(2,1)S(1)}, u32[]{:S(2)}, u32[]{:S(2)}) %collective-permute-start.6) | collective-permute-done | bytes 131104 | tf_op jit(solution)/shard_map/ppermute | solution.py:603
  16.3 2.0 %collective-permute-start.14 = (bf16[256,256]{1,0:T(8,128)(2,1)S(1)}, bf16[256,256]{1,0:T(8,128)(2,1)S(1)}, u32[]{:S(2)}, u32[]{:S(2)}) collective-permute-start(bf16[256,256]{1,0:T(8,128)(2,1)S(1)} %collective-permute-done.4.refs_10_), channel_id=1, source_target_pairs={{0,8},{2,10},{8,16},{10,18},{16,24},{18,26},{24,28},{26,30},{28,20... | collective-permute-start | bytes 393224 | tf_op jit(solution)/shard_map/ppermute | solution.py:603
  18.3 1.6 %collective-permute-start.10 = (bf16[256,256]{1,0:T(8,128)(2,1)S(1)}, bf16[256,256]{1,0:T(8,128)(2,1)S(1)}, u32[]{:S(2)}, u32[]{:S(2)}) collective-permute-start(bf16[256,256]{1,0:T(8,128)(2,1)S(1)} %collective-permute-done.8.refs_4_), channel_id=1, source_target_pairs={{0,8},{2,10},{8,16},{10,18},{16,24},{18,26},{24,28},{26,30},{28,20... | collective-permute-start | bytes 393224 | tf_op jit(solution)/shard_map/ppermute | solution.py:603
  20.4 2.3 %collective-permute-done.7.refs_3_ = bf16[256,256]{1,0:T(8,128)(2,1)S(1)} collective-permute-done((bf16[256,256]{1,0:T(8,128)(2,1)S(1)}, bf16[256,256]{1,0:T(8,128)(2,1)S(1)}, u32[]{:S(2)}, u32[]{:S(2)}) %collective-permute-start.7) | collective-permute-done | bytes 131104 | tf_op jit(solution)/shard_map/ppermute | solution.py:603
  22.7 2.0 %collective-permute-start.16 = (bf16[256,256]{1,0:T(8,128)(2,1)S(1)}, bf16[256,256]{1,0:T(8,128)(2,1)S(1)}, u32[]{:S(2)}, u32[]{:S(2)}) collective-permute-start(bf16[256,256]{1,0:T(8,128)(2,1)S(1)} %collective-permute-done.14.refs_12_), channel_id=1, source_target_pairs={{0,8},{2,10},{8,16},{10,18},{16,24},{18,26},{24,28},{26,30},{28,20... | collective-permute-start | bytes 393224 | tf_op jit(solution)/shard_map/ppermute | solution.py:603
  24.7 1.6 %collective-permute-start.11 = (bf16[256,256]{1,0:T(8,128)(2,1)S(1)}, bf16[256,256]{1,0:T(8,128)(2,1)S(1)}, u32[]{:S(2)}, u32[]{:S(2)}) collective-permute-start(bf16[256,256]{1,0:T(8,128)(2,1)S(1)} %collective-permute-done.10.refs_6_), channel_id=1, source_target_pairs={{0,8},{2,10},{8,16},{10,18},{16,24},{18,26},{24,28},{26,30},{28,20... | collective-permute-start | bytes 393224 | tf_op jit(solution)/shard_map/ppermute | solution.py:603
  29.8 1.4 %collective-permute-done.17.refs_15_ = bf16[256,256]{1,0:T(8,128)(2,1)S(1)} collective-permute-done((bf16[256,256]{1,0:T(8,128)(2,1)S(1)}, bf16[256,256]{1,0:T(8,128)(2,1)S(1)}, u32[]{:S(2)}, u32[]{:S(2)}) %collective-permute-start.17) | collective-permute-done | bytes 131104 | tf_op jit(solution)/shard_map/ppermute | solution.py:603
  31.8 1.4 %collective-permute-done.21.got_ref = f32[128,384]{1,0:T(8,128)S(1)} collective-permute-done((f32[128,384]{1,0:T(8,128)S(1)}, f32[128,384]{1,0:T(8,128)S(1)}, u32[]{:S(2)}, u32[]{:S(2)}) %collective-permute-start.21) | collective-permute-done | bytes 196640 | tf_op jit(solution)/shard_map/ppermute | solution.py:696
  33.4 1.7 %collective-permute-start.22 = (bf16[128,256]{1,0:T(8,128)(2,1)S(1)}, bf16[128,256]{1,0:T(8,128)(2,1)S(1)}, u32[]{:S(2)}, u32[]{:S(2)}) collective-permute-start(bf16[128,256]{1,0:T(8,128)(2,1)S(1)} %rotary.1.refs_0_), channel_id=1, source_target_pairs={{0,8},{2,10},{8,16},{10,18},{16,24},{18,26},{24,28},{26,30},{28,20... | collective-permute-start | bytes 196616 | tf_op jit(solution)/shard_map/ppermute | solution.py:603
  35.4 1.2 %collective-permute-start.20 = (bf16[4,128,128]{2,1,0:T(8,128)(2,1)S(1)}, bf16[4,128,128]{2,1,0:T(8,128)(2,1)S(1)}, u32[]{:S(2)}, u32[]{:S(2)}) collective-permute-start(bf16[4,128,128]{2,1,0:T(8,128)(2,1)S(1)} %get-tuple-element.52.refs_4_), channel_id=1, source_target_pairs={{0,8},{2,10},{4,12},{6,14},{8,0},{10,2},{12,4},{14,6},{16,24},{18,... | collective-permute-start | bytes 393224 | tf_op jit(solution)/shard_map/ppermute | solution.py:636
  36.6 1.3 %collective-permute-done.22.refs_2_ = bf16[128,256]{1,0:T(8,128)(2,1)S(1)} collective-permute-done((bf16[128,256]{1,0:T(8,128)(2,1)S(1)}, bf16[128,256]{1,0:T(8,128)(2,1)S(1)}, u32[]{:S(2)}, u32[]{:S(2)}) %collective-permute-start.22) | collective-permute-done | bytes 65568 | tf_op jit(solution)/shard_map/ppermute | solution.py:603
  37.9 2.4 %collective-permute-start.23 = (bf16[512,128]{1,0:T(8,128)(2,1)S(1)}, bf16[512,128]{1,0:T(8,128)(2,1)S(1)}, u32[]{:S(2)}, u32[]{:S(2)}) collective-permute-start(bf16[512,128]{1,0:T(8,128)(2,1)S(1)} %get-tuple-element.56.qs_ref), channel_id=1, source_target_pairs={{0,16},{2,18},{4,20},{6,22},{8,24},{10,26},{12,28},{14,30},{16,0},... | collective-permute-start | bytes 393224 | tf_op jit(solution)/shard_map/ppermute | solution.py:636
  40.8 1.6 %collective-permute-start.28 = (bf16[128,256]{1,0:T(8,128)(2,1)S(1)}, bf16[128,256]{1,0:T(8,128)(2,1)S(1)}, u32[]{:S(2)}, u32[]{:S(2)}) collective-permute-start(bf16[128,256]{1,0:T(8,128)(2,1)S(1)} %collective-permute-done.22.refs_2_), channel_id=1, source_target_pairs={{0,8},{2,10},{8,16},{10,18},{16,24},{18,26},{24,28},{26,30},{28,20... | collective-permute-start | bytes 196616 | tf_op jit(solution)/shard_map/ppermute | solution.py:603
  42.3 1.6 %collective-permute-start.19 = (bf16[4,128,128]{2,1,0:T(8,128)(2,1)S(1)}, bf16[4,128,128]{2,1,0:T(8,128)(2,1)S(1)}, u32[]{:S(2)}, u32[]{:S(2)}) collective-permute-start(bf16[4,128,128]{2,1,0:T(8,128)(2,1)S(1)} %copy-done.2), channel_id=1, source_target_pairs={{0,8},{2,10},{4,12},{6,14},{8,0},{10,2},{12,4},{14,6},{16,24},{18,... | collective-permute-start | bytes 393224 | tf_op jit(solution)/shard_map/ppermute | solution.py:636
  44.6 1.4 %collective-permute-done.24.refs_1_ = bf16[128,256]{1,0:T(8,128)(2,1)S(1)} collective-permute-done((bf16[128,256]{1,0:T(8,128)(2,1)S(1)}, bf16[128,256]{1,0:T(8,128)(2,1)S(1)}, u32[]{:S(2)}, u32[]{:S(2)}) %collective-permute-start.24) | collective-permute-done | bytes 65568 | tf_op jit(solution)/shard_map/ppermute | solution.py:603
  46.7 1.4 %collective-permute-start.25 = (bf16[4,128,128]{2,1,0:T(8,128)(2,1)S(1)}, bf16[4,128,128]{2,1,0:T(8,128)(2,1)S(1)}, u32[]{:S(2)}, u32[]{:S(2)}) collective-permute-start(bf16[4,128,128]{2,1,0:T(8,128)(2,1)S(1)} %collective-permute-done.18.refs_1_), channel_id=1, source_target_pairs={{0,8},{2,10},{4,12},{6,14},{8,0},{10,2},{12,4},{14,6},{16,24},{18,... | collective-permute-start | bytes 393224 | tf_op jit(solution)/shard_map/ppermute | solution.py:636
  48.0 2.4 %collective-permute-start.27 = (bf16[4,128,128]{2,1,0:T(8,128)(2,1)S(1)}, bf16[4,128,128]{2,1,0:T(8,128)(2,1)S(1)}, u32[]{:S(2)}, u32[]{:S(2)}) collective-permute-start(bf16[4,128,128]{2,1,0:T(8,128)(2,1)S(1)} %collective-permute-done.20.refs_6_), channel_id=1, source_target_pairs={{0,4},{2,6},{4,0},{6,2},{8,12},{10,14},{12,8},{14,10},{16,20},{18,... | collective-permute-start | bytes 393224 | tf_op jit(solution)/shard_map/ppermute | solution.py:636
  50.7 1.4 %collective-permute-start.30 = (bf16[128,256]{1,0:T(8,128)(2,1)S(1)}, bf16[128,256]{1,0:T(8,128)(2,1)S(1)}, u32[]{:S(2)}, u32[]{:S(2)}) collective-permute-start(bf16[128,256]{1,0:T(8,128)(2,1)S(1)} %collective-permute-done.28.refs_4_), channel_id=1, source_target_pairs={{0,8},{2,10},{8,16},{10,18},{16,24},{18,26},{24,28},{26,30},{28,20... | collective-permute-start | bytes 196616 | tf_op jit(solution)/shard_map/ppermute | solution.py:603
  53.4 3.1 %attend_cached_away.1 = bf16[144,512]{1,0:T(8,128)(2,1)S(1)} custom-call(s32[3]{0:T(128)S(1)} %copy-done.9, s32[3,25]{1,0:T(4,128)S(1)} %copy-done.8, s32[8,128]{1,0:T(8,128)S(1)} %bitcast.2, bf16[512,128]{1,0:T(8,128)(2,1)S(1)} %collective-permute-done.23.qs_ref, bf16[4,128,128]{2,1,0:T(8,128)(2,1)S(1)} %copy-done.2, ...), custom_call_target="tpu_custom_call" | custom-call | tf_op jit(solution)/shard_map/attend_cached_away/pallas_call | solution.py:718
  56.5 1.1 %collective-permute-start.32 = (bf16[144,512]{1,0:T(8,128)(2,1)S(1)}, bf16[144,512]{1,0:T(8,128)(2,1)S(1)}, u32[]{:S(2)}, u32[]{:S(2)}) collective-permute-start(bf16[144,512]{1,0:T(8,128)(2,1)S(1)} %attend_cached_away.1), channel_id=1, source_target_pairs={{0,16},{2,18},{4,20},{6,22},{8,24},{10,26},{12,28},{14,30},{16,0},... | collective-permute-start | bytes 442376 | tf_op jit(solution)/shard_map/ppermute | solution.py:636
  57.6 3.4 %collective-permute-start.33 = (bf16[128,256]{1,0:T(8,128)(2,1)S(1)}, bf16[128,256]{1,0:T(8,128)(2,1)S(1)}, u32[]{:S(2)}, u32[]{:S(2)}) collective-permute-start(bf16[128,256]{1,0:T(8,128)(2,1)S(1)} %collective-permute-done.30.refs_6_), channel_id=1, source_target_pairs={{0,8},{2,10},{8,16},{10,18},{16,24},{18,26},{24,28},{26,30},{28,20... | collective-permute-start | bytes 196616 | tf_op jit(solution)/shard_map/ppermute | solution.py:603
  60.9 2.1 %attend_cached_here.1 = (f32[1,512]{1,0:T(1,128)S(1)}, f32[1,512]{1,0:T(1,128)S(1)}, f32[128,512]{1,0:T(8,128)S(1)}) custom-call(s32[3]{0:T(128)S(1)} %copy-done.9, s32[3,25]{1,0:T(4,128)S(1)} %copy-done.8, s32[8,128]{1,0:T(8,128)S(1)} %bitcast.3, bf16[512,128]{1,0:T(8,128)(2,1)S(1)} %get-tuple-element.56.qs_ref, bf16[4,128,128]{2,1,0:T(8,128)(2,1)S(1)} %copy-done.2, ...), custom_call_target="tpu_custom_call" | custom-call | tf_op jit(solution)/shard_map/attend_cached_here/pallas_call | solution.py:718
  63.0 1.2 %collective-permute-done.32.back_ref = bf16[144,512]{1,0:T(8,128)(2,1)S(1)} collective-permute-done((bf16[144,512]{1,0:T(8,128)(2,1)S(1)}, bf16[144,512]{1,0:T(8,128)(2,1)S(1)}, u32[]{:S(2)}, u32[]{:S(2)}) %collective-permute-start.32) | collective-permute-done | bytes 147488 | tf_op jit(solution)/shard_map/ppermute | solution.py:636
  64.2 2.4 %attend_new.1 = (bf16[64,512]{1,0:T(8,128)(2,1)S(1)}, bf16[64,512]{1,0:T(8,128)(2,1)S(1)}, bf16[3,128,256]{2,1,0:T(8,128)(2,1)S(1)}, bf16[3,128,256]{2,1,0:T(8,128)(2,1)S(1)}, s32[6]{0:T(128)S(1)}) custom-call(s32[3]{0:T(128)S(1)} %copy-done.9, s32[3,25]{1,0:T(4,128)S(1)} %copy-done.8, s32[8,128]{1,0:T(8,128)S(1)} %bitcast.4, ...), custom_call_target="tpu_custom_call" | custom-call | tf_op jit(solution)/shard_map/attend_new/pallas_call | solution.py:746
  67.2 1.0 %collective-permute-done.34.attr_ref = bf16[64,512]{1,0:T(8,128)(2,1)S(1)} collective-permute-done((bf16[64,512]{1,0:T(8,128)(2,1)S(1)}, bf16[64,512]{1,0:T(8,128)(2,1)S(1)}, u32[]{:S(2)}, u32[]{:S(2)}) %collective-permute-start.34) | collective-permute-done | bytes 65568 | tf_op jit(solution)/shard_map/ppermute | solution.py:781
  68.2 1.5 %join.1 = (bf16[64,1024]{1,0:T(8,128)(2,1)}, bf16[3,128,256]{2,1,0:T(8,128)(2,1)}, bf16[3,128,256]{2,1,0:T(8,128)(2,1)}) custom-call(s32[6]{0:T(128)S(1)} %get-tuple-element.68.info_ref, bf16[64,512]{1,0:T(8,128)(2,1)S(1)} %get-tuple-element.69.attc_ref, bf16[64,512]{1,0:T(8,128)(2,1)S(1)} %collective-permute-done.34.attr_ref, ...), custom_call_target="tpu_custom_call" | custom-call | tf_op jit(solution)/shard_map/join/pallas_call | solution.py:782
  (74 shorter events, 10.4 us)
Async XLA Ops:
  2.8 6.7 %collective-permute-start = (bf16[64,1024]{1,0:T(8,128)(2,1)}, bf16[64,1024]{1,0:T(8,128)(2,1)S(1)}, u32[]{:S(2)}, u32[]{:S(2)}) collective-permute-start(bf16[64,1024]{1,0:T(8,128)(2,1)} %get-tuple-element.38.a_ref), channel_id=1, source_target_pairs={{0,1},{1,0},{2,3},{3,2},{4,5},{5,4},{6,7},{7,6},{8,9},{9,8},{10,11... | collective-permute-start | bytes 393224 | tf_op jit(solution)/shard_map/ppermute | solution.py:658
  5.8 5.5 %collective-permute-start.3 = (bf16[256,256]{1,0:T(8,128)(2,1)S(1)}, bf16[256,256]{1,0:T(8,128)(2,1)S(1)}, u32[]{:S(2)}, u32[]{:S(2)}) collective-permute-start(bf16[256,256]{1,0:T(8,128)(2,1)S(1)} %copy-done.5), channel_id=1, source_target_pairs={{0,8},{2,10},{8,16},{10,18},{16,24},{18,26},{24,28},{26,30},{28,20... | collective-permute-start | bytes 393224 | tf_op jit(solution)/shard_map/ppermute | solution.py:603
  7.4 6.4 %collective-permute-start.12 = (bf16[256,256]{1,0:T(8,128)(2,1)S(1)}, bf16[256,256]{1,0:T(8,128)(2,1)S(1)}, u32[]{:S(2)}, u32[]{:S(2)}) collective-permute-start(bf16[256,256]{1,0:T(8,128)(2,1)S(1)} %copy-done.6), channel_id=1, source_target_pairs={{0,4},{2,6},{8,0},{10,2},{16,8},{18,10},{24,16},{26,18},{28,24},{3... | collective-permute-start | bytes 393224 | tf_op jit(solution)/shard_map/ppermute | solution.py:603
  7.8 5.9 %collective-permute-start.1 = (bf16[64,1024]{1,0:T(8,128)(2,1)}, bf16[64,1024]{1,0:T(8,128)(2,1)S(1)}, u32[]{:S(2)}, u32[]{:S(2)}) collective-permute-start(bf16[64,1024]{1,0:T(8,128)(2,1)} %get-tuple-element.39), channel_id=1, source_target_pairs={{0,2},{2,0},{4,6},{6,4},{8,10},{10,8},{12,14},{14,12},{16,18},{18,... | collective-permute-start | bytes 393224 | tf_op jit(solution)/shard_map/ppermute | solution.py:659
  7.8 8.5 %collective-permute-start.6 = (bf16[256,256]{1,0:T(8,128)(2,1)S(1)}, bf16[256,256]{1,0:T(8,128)(2,1)S(1)}, u32[]{:S(2)}, u32[]{:S(2)}) collective-permute-start(bf16[256,256]{1,0:T(8,128)(2,1)S(1)} %copy-done.5), channel_id=1, source_target_pairs={{0,4},{2,6},{8,0},{10,2},{16,8},{18,10},{24,16},{26,18},{28,24},{3... | collective-permute-start | bytes 393224 | tf_op jit(solution)/shard_map/ppermute | solution.py:603
  9.5 6.8 %collective-permute-start.4 = (bf16[256,256]{1,0:T(8,128)(2,1)S(1)}, bf16[256,256]{1,0:T(8,128)(2,1)S(1)}, u32[]{:S(2)}, u32[]{:S(2)}) collective-permute-start(bf16[256,256]{1,0:T(8,128)(2,1)S(1)} %copy-done.6), channel_id=1, source_target_pairs={{0,8},{2,10},{8,16},{10,18},{16,24},{18,26},{24,28},{26,30},{28,20... | collective-permute-start | bytes 393224 | tf_op jit(solution)/shard_map/ppermute | solution.py:603
  11.3 7.0 %collective-permute-start.8 = (bf16[256,256]{1,0:T(8,128)(2,1)S(1)}, bf16[256,256]{1,0:T(8,128)(2,1)S(1)}, u32[]{:S(2)}, u32[]{:S(2)}) collective-permute-start(bf16[256,256]{1,0:T(8,128)(2,1)S(1)} %collective-permute-done.3.refs_2_), channel_id=1, source_target_pairs={{0,8},{2,10},{8,16},{10,18},{16,24},{18,26},{24,28},{26,30},{28,20... | collective-permute-start | bytes 393224 | tf_op jit(solution)/shard_map/ppermute | solution.py:603
  13.7 6.2 %collective-permute-start.13 = (bf16[256,256]{1,0:T(8,128)(2,1)S(1)}, bf16[256,256]{1,0:T(8,128)(2,1)S(1)}, u32[]{:S(2)}, u32[]{:S(2)}) collective-permute-start(bf16[256,256]{1,0:T(8,128)(2,1)S(1)} %collective-permute-done.12.refs_9_), channel_id=1, source_target_pairs={{0,4},{2,6},{8,0},{10,2},{16,8},{18,10},{24,16},{26,18},{28,24},{3... | collective-permute-start | bytes 393224 | tf_op jit(solution)/shard_map/ppermute | solution.py:603
  13.7 6.6 %collective-permute-start.2 = (bf16[64,1024]{1,0:T(8,128)(2,1)}, bf16[64,1024]{1,0:T(8,128)(2,1)S(1)}, u32[]{:S(2)}, u32[]{:S(2)}) collective-permute-start(bf16[64,1024]{1,0:T(8,128)(2,1)} %get-tuple-element.39), channel_id=1, source_target_pairs={{0,3},{1,2},{2,1},{3,0},{4,7},{5,6},{6,5},{7,4},{8,11},{9,10},{10,... | collective-permute-start | bytes 393224 | tf_op jit(solution)/shard_map/ppermute | solution.py:660
  16.3 6.4 %collective-permute-start.7 = (bf16[256,256]{1,0:T(8,128)(2,1)S(1)}, bf16[256,256]{1,0:T(8,128)(2,1)S(1)}, u32[]{:S(2)}, u32[]{:S(2)}) collective-permute-start(bf16[256,256]{1,0:T(8,128)(2,1)S(1)} %collective-permute-done.6.refs_1_), channel_id=1, source_target_pairs={{0,4},{2,6},{8,0},{10,2},{16,8},{18,10},{24,16},{26,18},{28,24},{3... | collective-permute-start | bytes 393224 | tf_op jit(solution)/shard_map/ppermute | solution.py:603
  16.3 6.4 %collective-permute-start.14 = (bf16[256,256]{1,0:T(8,128)(2,1)S(1)}, bf16[256,256]{1,0:T(8,128)(2,1)S(1)}, u32[]{:S(2)}, u32[]{:S(2)}) collective-permute-start(bf16[256,256]{1,0:T(8,128)(2,1)S(1)} %collective-permute-done.4.refs_10_), channel_id=1, source_target_pairs={{0,8},{2,10},{8,16},{10,18},{16,24},{18,26},{24,28},{26,30},{28,20... | collective-permute-start | bytes 393224 | tf_op jit(solution)/shard_map/ppermute | solution.py:603
  18.3 6.4 %collective-permute-start.10 = (bf16[256,256]{1,0:T(8,128)(2,1)S(1)}, bf16[256,256]{1,0:T(8,128)(2,1)S(1)}, u32[]{:S(2)}, u32[]{:S(2)}) collective-permute-start(bf16[256,256]{1,0:T(8,128)(2,1)S(1)} %collective-permute-done.8.refs_4_), channel_id=1, source_target_pairs={{0,8},{2,10},{8,16},{10,18},{16,24},{18,26},{24,28},{26,30},{28,20... | collective-permute-start | bytes 393224 | tf_op jit(solution)/shard_map/ppermute | solution.py:603
  19.9 6.4 %collective-permute-start.15 = (bf16[256,256]{1,0:T(8,128)(2,1)S(1)}, bf16[256,256]{1,0:T(8,128)(2,1)S(1)}, u32[]{:S(2)}, u32[]{:S(2)}) collective-permute-start(bf16[256,256]{1,0:T(8,128)(2,1)S(1)} %collective-permute-done.13.refs_11_), channel_id=1, source_target_pairs={{0,4},{2,6},{8,0},{10,2},{16,8},{18,10},{24,16},{26,18},{28,24},{3... | collective-permute-start | bytes 393224 | tf_op jit(solution)/shard_map/ppermute | solution.py:603
  20.4 9.0 %collective-permute-start.5 = (bf16[768,128]{1,0:T(8,128)(2,1)}, bf16[768,128]{1,0:T(8,128)(2,1)S(1)}, u32[]{:S(2)}, u32[]{:S(2)}) collective-permute-start(bf16[768,128]{1,0:T(8,128)(2,1)} %get-tuple-element.42), channel_id=1, source_target_pairs={{0,2},{2,0},{4,6},{6,4},{8,10},{10,8},{12,14},{14,12},{16,18},{18,... | collective-permute-start | bytes 589832 | tf_op jit(solution)/shard_map/ppermute | solution.py:657
  22.7 6.7 %collective-permute-start.9 = (bf16[256,256]{1,0:T(8,128)(2,1)S(1)}, bf16[256,256]{1,0:T(8,128)(2,1)S(1)}, u32[]{:S(2)}, u32[]{:S(2)}) collective-permute-start(bf16[256,256]{1,0:T(8,128)(2,1)S(1)} %collective-permute-done.7.refs_3_), channel_id=1, source_target_pairs={{0,4},{2,6},{8,0},{10,2},{16,8},{18,10},{24,16},{26,18},{28,24},{3... | collective-permute-start | bytes 393224 | tf_op jit(solution)/shard_map/ppermute | solution.py:603
  22.7 6.7 %collective-permute-start.16 = (bf16[256,256]{1,0:T(8,128)(2,1)S(1)}, bf16[256,256]{1,0:T(8,128)(2,1)S(1)}, u32[]{:S(2)}, u32[]{:S(2)}) collective-permute-start(bf16[256,256]{1,0:T(8,128)(2,1)S(1)} %collective-permute-done.14.refs_12_), channel_id=1, source_target_pairs={{0,8},{2,10},{8,16},{10,18},{16,24},{18,26},{24,28},{26,30},{28,20... | collective-permute-start | bytes 393224 | tf_op jit(solution)/shard_map/ppermute | solution.py:603
  24.7 5.1 %collective-permute-start.11 = (bf16[256,256]{1,0:T(8,128)(2,1)S(1)}, bf16[256,256]{1,0:T(8,128)(2,1)S(1)}, u32[]{:S(2)}, u32[]{:S(2)}) collective-permute-start(bf16[256,256]{1,0:T(8,128)(2,1)S(1)} %collective-permute-done.10.refs_6_), channel_id=1, source_target_pairs={{0,8},{2,10},{8,16},{10,18},{16,24},{18,26},{24,28},{26,30},{28,20... | collective-permute-start | bytes 393224 | tf_op jit(solution)/shard_map/ppermute | solution.py:603
  26.3 5.0 %collective-permute-start.17 = (bf16[256,256]{1,0:T(8,128)(2,1)S(1)}, bf16[256,256]{1,0:T(8,128)(2,1)S(1)}, u32[]{:S(2)}, u32[]{:S(2)}) collective-permute-start(bf16[256,256]{1,0:T(8,128)(2,1)S(1)} %collective-permute-done.15.refs_13_), channel_id=1, source_target_pairs={{0,4},{2,6},{8,0},{10,2},{16,8},{18,10},{24,16},{26,18},{28,24},{3... | collective-permute-start | bytes 393224 | tf_op jit(solution)/shard_map/ppermute | solution.py:603
  33.4 4.6 %collective-permute-start.22 = (bf16[128,256]{1,0:T(8,128)(2,1)S(1)}, bf16[128,256]{1,0:T(8,128)(2,1)S(1)}, u32[]{:S(2)}, u32[]{:S(2)}) collective-permute-start(bf16[128,256]{1,0:T(8,128)(2,1)S(1)} %rotary.1.refs_0_), channel_id=1, source_target_pairs={{0,8},{2,10},{8,16},{10,18},{16,24},{18,26},{24,28},{26,30},{28,20... | collective-permute-start | bytes 196616 | tf_op jit(solution)/shard_map/ppermute | solution.py:603
  35.0 7.3 %collective-permute-start.18 = (bf16[4,128,128]{2,1,0:T(8,128)(2,1)S(1)}, bf16[4,128,128]{2,1,0:T(8,128)(2,1)S(1)}, u32[]{:S(2)}, u32[]{:S(2)}) collective-permute-start(bf16[4,128,128]{2,1,0:T(8,128)(2,1)S(1)} %copy-done.2), channel_id=1, source_target_pairs={{0,4},{2,6},{4,0},{6,2},{8,12},{10,14},{12,8},{14,10},{16,20},{18,... | collective-permute-start | bytes 393224 | tf_op jit(solution)/shard_map/ppermute | solution.py:636
  35.4 8.5 %collective-permute-start.20 = (bf16[4,128,128]{2,1,0:T(8,128)(2,1)S(1)}, bf16[4,128,128]{2,1,0:T(8,128)(2,1)S(1)}, u32[]{:S(2)}, u32[]{:S(2)}) collective-permute-start(bf16[4,128,128]{2,1,0:T(8,128)(2,1)S(1)} %get-tuple-element.52.refs_4_), channel_id=1, source_target_pairs={{0,8},{2,10},{4,12},{6,14},{8,0},{10,2},{12,4},{14,6},{16,24},{18,... | collective-permute-start | bytes 393224 | tf_op jit(solution)/shard_map/ppermute | solution.py:636
  37.9 8.8 %collective-permute-start.23 = (bf16[512,128]{1,0:T(8,128)(2,1)S(1)}, bf16[512,128]{1,0:T(8,128)(2,1)S(1)}, u32[]{:S(2)}, u32[]{:S(2)}) collective-permute-start(bf16[512,128]{1,0:T(8,128)(2,1)S(1)} %get-tuple-element.56.qs_ref), channel_id=1, source_target_pairs={{0,16},{2,18},{4,20},{6,22},{8,24},{10,26},{12,28},{14,30},{16,0},... | collective-permute-start | bytes 393224 | tf_op jit(solution)/shard_map/ppermute | solution.py:636
  40.3 5.7 %collective-permute-start.24 = (bf16[128,256]{1,0:T(8,128)(2,1)S(1)}, bf16[128,256]{1,0:T(8,128)(2,1)S(1)}, u32[]{:S(2)}, u32[]{:S(2)}) collective-permute-start(bf16[128,256]{1,0:T(8,128)(2,1)S(1)} %rotary.1.refs_0_), channel_id=1, source_target_pairs={{0,4},{2,6},{8,0},{10,2},{16,8},{18,10},{24,16},{26,18},{28,24},{3... | collective-permute-start | bytes 196616 | tf_op jit(solution)/shard_map/ppermute | solution.py:603
  40.8 7.3 %collective-permute-start.28 = (bf16[128,256]{1,0:T(8,128)(2,1)S(1)}, bf16[128,256]{1,0:T(8,128)(2,1)S(1)}, u32[]{:S(2)}, u32[]{:S(2)}) collective-permute-start(bf16[128,256]{1,0:T(8,128)(2,1)S(1)} %collective-permute-done.22.refs_2_), channel_id=1, source_target_pairs={{0,8},{2,10},{8,16},{10,18},{16,24},{18,26},{24,28},{26,30},{28,20... | collective-permute-start | bytes 196616 | tf_op jit(solution)/shard_map/ppermute | solution.py:603
  42.3 9.8 %collective-permute-start.19 = (bf16[4,128,128]{2,1,0:T(8,128)(2,1)S(1)}, bf16[4,128,128]{2,1,0:T(8,128)(2,1)S(1)}, u32[]{:S(2)}, u32[]{:S(2)}) collective-permute-start(bf16[4,128,128]{2,1,0:T(8,128)(2,1)S(1)} %copy-done.2), channel_id=1, source_target_pairs={{0,8},{2,10},{4,12},{6,14},{8,0},{10,2},{12,4},{14,6},{16,24},{18,... | collective-permute-start | bytes 393224 | tf_op jit(solution)/shard_map/ppermute | solution.py:636
  44.0 8.8 %collective-permute-start.26 = (bf16[4,128,128]{2,1,0:T(8,128)(2,1)S(1)}, bf16[4,128,128]{2,1,0:T(8,128)(2,1)S(1)}, u32[]{:S(2)}, u32[]{:S(2)}) collective-permute-start(bf16[4,128,128]{2,1,0:T(8,128)(2,1)S(1)} %get-tuple-element.52.refs_4_), channel_id=1, source_target_pairs={{0,4},{2,6},{4,0},{6,2},{8,12},{10,14},{12,8},{14,10},{16,20},{18,... | collective-permute-start | bytes 393224 | tf_op jit(solution)/shard_map/ppermute | solution.py:636
  46.0 4.7 %collective-permute-start.29 = (bf16[128,256]{1,0:T(8,128)(2,1)S(1)}, bf16[128,256]{1,0:T(8,128)(2,1)S(1)}, u32[]{:S(2)}, u32[]{:S(2)}) collective-permute-start(bf16[128,256]{1,0:T(8,128)(2,1)S(1)} %collective-permute-done.24.refs_1_), channel_id=1, source_target_pairs={{0,4},{2,6},{8,0},{10,2},{16,8},{18,10},{24,16},{26,18},{28,24},{3... | collective-permute-start | bytes 196616 | tf_op jit(solution)/shard_map/ppermute | solution.py:603
  46.7 6.1 %collective-permute-start.25 = (bf16[4,128,128]{2,1,0:T(8,128)(2,1)S(1)}, bf16[4,128,128]{2,1,0:T(8,128)(2,1)S(1)}, u32[]{:S(2)}, u32[]{:S(2)}) collective-permute-start(bf16[4,128,128]{2,1,0:T(8,128)(2,1)S(1)} %collective-permute-done.18.refs_1_), channel_id=1, source_target_pairs={{0,8},{2,10},{4,12},{6,14},{8,0},{10,2},{12,4},{14,6},{16,24},{18,... | collective-permute-start | bytes 393224 | tf_op jit(solution)/shard_map/ppermute | solution.py:636
  48.0 5.3 %collective-permute-start.27 = (bf16[4,128,128]{2,1,0:T(8,128)(2,1)S(1)}, bf16[4,128,128]{2,1,0:T(8,128)(2,1)S(1)}, u32[]{:S(2)}, u32[]{:S(2)}) collective-permute-start(bf16[4,128,128]{2,1,0:T(8,128)(2,1)S(1)} %collective-permute-done.20.refs_6_), channel_id=1, source_target_pairs={{0,4},{2,6},{4,0},{6,2},{8,12},{10,14},{12,8},{14,10},{16,20},{18,... | collective-permute-start | bytes 393224 | tf_op jit(solution)/shard_map/ppermute | solution.py:636
  50.7 5.7 %collective-permute-start.30 = (bf16[128,256]{1,0:T(8,128)(2,1)S(1)}, bf16[128,256]{1,0:T(8,128)(2,1)S(1)}, u32[]{:S(2)}, u32[]{:S(2)}) collective-permute-start(bf16[128,256]{1,0:T(8,128)(2,1)S(1)} %collective-permute-done.28.refs_4_), channel_id=1, source_target_pairs={{0,8},{2,10},{8,16},{10,18},{16,24},{18,26},{24,28},{26,30},{28,20... | collective-permute-start | bytes 196616 | tf_op jit(solution)/shard_map/ppermute | solution.py:603
  56.5 7.7 %collective-permute-start.32 = (bf16[144,512]{1,0:T(8,128)(2,1)S(1)}, bf16[144,512]{1,0:T(8,128)(2,1)S(1)}, u32[]{:S(2)}, u32[]{:S(2)}) collective-permute-start(bf16[144,512]{1,0:T(8,128)(2,1)S(1)} %attend_cached_away.1), channel_id=1, source_target_pairs={{0,16},{2,18},{4,20},{6,22},{8,24},{10,26},{12,28},{14,30},{16,0},... | collective-permute-start | bytes 442376 | tf_op jit(solution)/shard_map/ppermute | solution.py:636
  57.6 5.5 %collective-permute-start.33 = (bf16[128,256]{1,0:T(8,128)(2,1)S(1)}, bf16[128,256]{1,0:T(8,128)(2,1)S(1)}, u32[]{:S(2)}, u32[]{:S(2)}) collective-permute-start(bf16[128,256]{1,0:T(8,128)(2,1)S(1)} %collective-permute-done.30.refs_6_), channel_id=1, source_target_pairs={{0,8},{2,10},{8,16},{10,18},{16,24},{18,26},{24,28},{26,30},{28,20... | collective-permute-start | bytes 196616 | tf_op jit(solution)/shard_map/ppermute | solution.py:603
  (16 other events, 80.9 us)
